TPU v7x, 128 devices: a whole 4x4x4 slice. The times are simulated.
128 devices in a mesh: section: 2 (over core), dp: 64 (over z, y, x).
Axes of the slice: x: 4, y: 4, z: 4, core: 2. Of those that a mesh axis runs over, the one named last changes fastest.
Arguments:
- activations: bfloat16 [128, 6, 192, 2560], P(('section', 'dp')), parts along dimension 0, may hold values from -16 to 16
- cotangents: bfloat16 [128, 6, 192, 2560], P(('section', 'dp')), parts along dimension 0, may hold values from -1.5 to 1.5
- failed: int32 [1], replicated, may hold values from 0 to 63
- counts: int32 [64], P('dp'), may hold values from 1 to 6, as said below
- order: int32 [64, 6], P('dp'), may hold values from 0 to 5, each once within a row
Outputs:
- gradient: float32 [5120, 2560], P(('section', 'dp')), parts along dimension 0
There are 2 independent parts, one for each index of `section`. A program takes and returns all parts, laid end to end along the dimension named above; an argument that names none is the same for every part. Nothing has to cross between parts.
Inputs may be any that keep to these rules, and one draw needn't show every extreme that they name: `counts`: each replica reports 1 to 6 micro-batches; some replica reports exactly 6.
All inputs are finite; a program needn't handle non-finite values.
Results may differ from a plain program's by a relative error of at most 0.0003.
Values sent between devices are 32-bit elements; how exact they have to be, the bound alone decides.
No kernel may reach another device: no remote copies, remote signals or barrier semaphores. Data moves between devices by JAX's collectives and lax.ppermute only.
A program may use at most 320 MiB of HBM per device.

v0:
```python
import jax
import jax.numpy as jnp
from jax import lax
from jax.sharding import PartitionSpec as P


def total_of_pieces(value, axis):
    tiles = lax.all_gather(value, axis)
    return tiles.sum(axis=0)


def shards(activations, cotangents, failed, counts, order):
    my_index = lax.axis_index("dp")
    alive_replica_count = jnp.where(my_index == failed[0], 0, counts[0])
    remaining_replica_total = total_of_pieces(alive_replica_count.astype(jnp.float32), "dp")
    act_all = activations[0]
    cot_all = cotangents[0]
    permuted = order[0]
    slot_count = permuted.shape[0]
    out_width = cot_all.shape[2]
    empty_sum = jnp.zeros((act_all.shape[2], out_width), jnp.float32)
    partial_gradient = empty_sum
    for position in range(slot_count):
        selected_replica = permuted[position]
        weight_live = jnp.where(position < alive_replica_count, 1.0, 0.0).astype(jnp.bfloat16)
        act_rows = lax.dynamic_index_in_dim(act_all, selected_replica, 0, keepdims=False)
        cot_rows = (
            lax.dynamic_index_in_dim(cot_all, selected_replica, 0, keepdims=False) * weight_live
        )
        partial_gradient = partial_gradient + lax.dot_general(
            act_rows, cot_rows, (((0,), (0,)), ((), ())), preferred_element_type=jnp.float32
        )
    gradient_sum = lax.psum_scatter(partial_gradient, "dp", scatter_dimension=0, tiled=True)
    return gradient_sum / remaining_replica_total


def solution(mesh):
    in_specs = (
        P(("section", "dp"), None, None, None),
        P(("section", "dp"), None, None, None),
        P(),
        P("dp"),
        P("dp", None),
    )
    out_specs = P(("section", "dp"), None)
    return jax.shard_map(shards, mesh=mesh, in_specs=in_specs, out_specs=out_specs, check_vma=False)
```

profile of v0, /device:TPU:0, one launch (start us, length us, event | category | flops | bytes accessed | tf_op | source)
XLA Modules:
  0.0 550.5 jit_solution(12159529300730511617)
XLA Ops:
  6.5 0.0 reduce-scatter.2.cloned.1.call-start
  6.5 1.5 fusion.47
  20.7 0.0 copy-start
  20.8 0.0 copy-start.1
  20.8 13.9 %fusion.5 = f32[2560,2560]{1,0:T(8,128)} fusion(bf16[1,6,192,2560]{3,2,1,0:T(8,128)(2,1)} %param.6, s32[]{:T(128)S(6)} %select_n.55, bf16[1,6,192,2560]{3,2,1,0:T(8,128)(2,1)} %param.5, bf16[]{:T(256)S(6)} %select_n.56), kind=kOutput, calls=%fused_computation.6 | convolution fusion | flops 2517073920 | bytes 28182016 | tf_op jit(solution)/shard_map/dot_general | solution.py:30
  34.7 0.0 copy-done
  34.7 0.0 copy-done.1
  34.7 10.9 %fusion.8 = f32[2560,2560]{1,0:T(8,128)} fusion(bf16[1,6,192,2560]{3,2,1,0:T(8,128)(2,1)S(1)} %copy-done, s32[]{:T(128)S(6)} %select_n.53, bf16[1,6,192,2560]{3,2,1,0:T(8,128)(2,1)S(1)} %copy-done.1, bf16[]{:T(256)S(6)} %select_n.54), kind=kOutput, calls=%fused_computation.9 | convolution fusion | flops 2517073920 | bytes 28182016 | tf_op jit(solution)/shard_map/dot_general | solution.py:30
  45.6 10.8 %fusion.11 = f32[2560,2560]{1,0:T(8,128)} fusion(bf16[1,6,192,2560]{3,2,1,0:T(8,128)(2,1)S(1)} %copy-done, s32[]{:T(128)S(6)} %select_n.51, bf16[1,6,192,2560]{3,2,1,0:T(8,128)(2,1)S(1)} %copy-done.1, bf16[]{:T(256)S(6)} %select_n.52), kind=kOutput, calls=%fused_computation.12 | convolution fusion | flops 2517073920 | bytes 28182016 | tf_op jit(solution)/shard_map/dot_general | solution.py:30
  56.3 10.6 %fusion.14 = f32[2560,2560]{1,0:T(8,128)} fusion(bf16[1,6,192,2560]{3,2,1,0:T(8,128)(2,1)S(1)} %copy-done, s32[]{:T(128)S(6)} %select_n.48, bf16[1,6,192,2560]{3,2,1,0:T(8,128)(2,1)S(1)} %copy-done.1, bf16[]{:T(256)S(6)} %select_n.50), kind=kOutput, calls=%fused_computation.15 | convolution fusion | flops 2517073920 | bytes 28182016 | tf_op jit(solution)/shard_map/dot_general | solution.py:30
  67.0 10.7 %fusion.2 = f32[2560,2560]{1,0:T(8,128)} fusion(bf16[1,6,192,2560]{3,2,1,0:T(8,128)(2,1)S(1)} %copy-done, s32[]{:T(128)S(6)} %select_n.57, bf16[1,6,192,2560]{3,2,1,0:T(8,128)(2,1)S(1)} %copy-done.1, bf16[]{:T(256)S(6)} %select_n.58), kind=kOutput, calls=%fused_computation.3 | convolution fusion | flops 2517073920 | bytes 28182016 | tf_op jit(solution)/shard_map/dot_general | solution.py:30
  77.6 50.8 %add_add_fusion = f32[2560,2560]{1,0:T(8,128)} fusion(f32[2560,2560]{1,0:T(8,128)} %fusion.2, f32[2560,2560]{1,0:T(8,128)} %fusion.5, f32[2560,2560]{1,0:T(8,128)} %fusion.8, f32[2560,2560]{1,0:T(8,128)} %fusion.14, f32[2560,2560]{1,0:T(8,128)} %fusion.11, bf16[1,6,192,2560]{3,2,1,0:T(8,128)(2,1)} %param.6, s32[]{:T(128)S(6)} %select_n.59, ...), kind=kOutput, calls=%fused_computation | convolution fusion | flops 2549841920 | bytes 159254016 | tf_op jit(solution)/shard_map/dot_general | solution.py:30
  128.4 0.0 copy-start.2
  128.4 0.0 reduce-scatter.2.cloned.1.call-update
  128.4 0.6 copy-done.2
  129.1 0.6 dynamic-slice.12
  129.7 0.7 dynamic-update-slice
  130.4 180.9 %all-reduce = f32[64]{0:T(128)S(1)} all-reduce(f32[64]{0:T(128)S(1)} %dynamic-update-slice), channel_id=1, replica_groups=mesh['section'=2,'dp'=64] {'dp'}, use_global_device_ids=true, to_apply=%add | all-reduce | flops 64 | bytes 512
  311.3 0.6 reduce_sum.9
  311.9 229.3 %reduce-scatter.2.cloned.1.call-done = f32[40,2560]{1,0:T(8,128)} async-done(((f32[2560,2560]{1,0:T(8,128)}), f32[40,2560]{1,0:T(8,128)}) %reduce-scatter.2.cloned.1.call-update) | async-done | bytes 409616 | tf_op jit(solution)/shard_map/reduce_scatter | solution.py:33
  541.2 2.4 broadcast_divide_fusion
  (1 shorter events, 0.0 us)
Async XLA Ops:
  6.5 534.7 %reduce-scatter.2.cloned.1.call-start = ((), (), s32[]{:S(2)}) async-start(), calls=%async_computation.1 | async-start | bytes 26624000 | tf_op jit(solution)/shard_map/reduce_scatter | solution.py:33
  20.7 13.9 %copy-start = (bf16[1,6,192,2560]{3,2,1,0:T(8,128)(2,1)S(1)}, bf16[1,6,192,2560]{3,2,1,0:T(8,128)(2,1)}, u32[]{:S(2)}) copy-start(bf16[1,6,192,2560]{3,2,1,0:T(8,128)(2,1)} %param.6) | copy-start | bytes 17694724
  20.8 13.9 %copy-start.1 = (bf16[1,6,192,2560]{3,2,1,0:T(8,128)(2,1)S(1)}, bf16[1,6,192,2560]{3,2,1,0:T(8,128)(2,1)}, u32[]{:S(2)}) copy-start(bf16[1,6,192,2560]{3,2,1,0:T(8,128)(2,1)} %param.5) | copy-start | bytes 17694724
  128.4 0.7 copy-start.2
Sparse Core Ops, SparseCore 0:
  128.6 412.5 reduce-scatter.1
where the time goes:
time: 551 us; the launch traced here: 550 us
  waiting for transfers between devices  229 us (42%)
  blocking collectives  181 us (33%)
  matrix products  108 us (20%)
  between operations  26.1 us (5%)
    reduce_scatter x1, waiting for transfers between devices, shards(): lax.psum_scatter(partial_gradient, 'dp', scatter_dimension=0, tiled=True)  229 us
    unnamed x1, blocking collectives  181 us
    dot_general x6, matrix products, shards(): lax.dot_general(act_rows, cot_rows, (((0,), (0,)), ((), ())), preferred_e...  108 us
  transfers between devices with their start and end apart: 1, of which 1 were waited for; matrix products, arithmetic and copies ran while one was open for 0% of the time, Pallas kernels for 0%

commit v1 on v0

v1 whole, which is shorter than its diff:
```python
import functools

import jax
import jax.numpy as jnp
from jax import lax
from jax.experimental import pallas as pl
from jax.experimental.pallas import tpu as pltpu
from jax.sharding import PartitionSpec as P

SLOTS, TOKENS, ROWS = 6, 192, 40
K = SLOTS * TOKENS
TILE = 16 * ROWS
STRIDE = {"x": 1, "y": 4, "z": 16}
COLOURS = ((0, 896, "xyz"), (896, 640, "yxz"), (1536, 1024, "zyx"))


def exchange(value, axis, turn):
    pairs = []
    for section in range(2):
        flip = 1 if section == turn else 3
        for d in range(64):
            p = d // STRIDE[axis] % 4
            pairs.append((section * 64 + d, section * 64 + d + ((p ^ flip) - p) * STRIDE[axis]))
    return lax.ppermute(value, ("section", "dp"), pairs)


def masked(place, cot_ref, cotm):
    for k in range(SLOTS):
        live = (place[12 + k] > 0).astype(jnp.float32)
        cotm[k * TOKENS:(k + 1) * TOKENS, :] = (cot_ref[0, k].astype(jnp.float32) * live).astype(jnp.bfloat16)


def z_first(place, act_ref, cot_ref, one_ref, two_ref, cotm, total):
    @pl.when(pl.program_id(0) == 0)
    def _():
        masked(place, cot_ref, cotm)
    total[...] = lax.dot_general(
        act_ref[...].reshape(K, TILE), cotm[...], (((0,), (0,)), ((), ())), preferred_element_type=jnp.float32)
    for sy in range(4):
        for sx in range(4):
            start = pl.multiple_of(place[4 + sy] * 160 + place[sx] * 40, 8)
            (two_ref if sx < 2 else one_ref)[0, sy, sx % 2] = total[pl.ds(start, ROWS), :]


def z_last(first, place, act_ref, cot_ref, send_ref, keep_ref, cotm, total):
    @pl.when(pl.program_id(0) == 0)
    def _():
        masked(place, cot_ref, cotm)
    total[...] = lax.dot_general(
        act_ref[...].reshape(K, TILE), cotm[...], (((0,), (0,)), ((), ())), preferred_element_type=jnp.float32)
    for sy in range(4):
        for sx in range(4):
            start = pl.multiple_of(place[4 + sy] * 160 + place[sx] * 40, 8)
            major, minor = (sx, sy) if first == "x" else (sy, sx)
            (keep_ref if major < 2 else send_ref)[major % 2, minor, 0] = total[pl.ds(start, ROWS), :]


def partials(colour, half, activations, cotangents, place):
    column, columns, axes = COLOURS[colour]
    if axes[0] == "z":
        kernel = z_first
        shape = (2, 4, 2, ROWS, columns)
        out = pl.BlockSpec((1, 4, 2, ROWS, columns), lambda g, s: (g, 0, 0, 0, 0))
    else:
        kernel = functools.partial(z_last, axes[0])
        shape = (2, 4, 2, ROWS, columns)
        out = pl.BlockSpec((2, 4, 1, ROWS, columns), lambda g, s: (0, 0, g, 0, 0))
    return pl.pallas_call(
        kernel,
        out_shape=[jax.ShapeDtypeStruct(shape, jnp.float32)] * 2,
        grid_spec=pltpu.PrefetchScalarGridSpec(
            num_scalar_prefetch=1,
            grid=(2,),
            in_specs=[
                pl.BlockSpec((1, SLOTS, TOKENS, TILE), lambda g, s: (0, 0, 0, s[8 + half + g])),
                pl.BlockSpec(tuple(map(pl.Element, (1, SLOTS, TOKENS, columns))), lambda g, s: (0, 0, 0, column)),
            ],
            out_specs=[out] * 2,
            scratch_shapes=[pltpu.VMEM((K, columns), jnp.bfloat16), pltpu.VMEM((TILE, columns), jnp.float32)],
        ),
        compiler_params=pltpu.CompilerParams(vmem_limit_bytes=40 << 20),
        cost_estimate=pl.CostEstimate(
            flops=2 * K * 2 * TILE * columns,
            bytes_accessed=K * 2 * TILE * 2 + K * columns * 2 + 2 * TILE * columns * 4,
            transcendentals=0,
        ),
    )(place, activations, cotangents)


def scattered(axes, halves):
    after_first = []
    for send, keep in halves:
        got = exchange(send, axes[0], 0)
        late = exchange(keep[1] + got[1], axes[0], 1)
        after_first.append((keep[0] + got[0]) + late)
    after_second = []
    for whole in after_first:
        got = exchange(whole[2:4], axes[1], 0)
        late = exchange(whole[1] + got[1], axes[1], 1)
        after_second.append((whole[0] + got[0]) + late)
    far, near = after_second
    got = exchange(far, axes[2], 0)
    late = exchange(near[1] + got[1], axes[2], 1)
    return (near[0] + got[0]) + late


def shards(activations, cotangents, failed, counts, order):
    section, me = lax.axis_index("section"), lax.axis_index("dp")
    alive = jnp.where(me == failed[0], 0, counts[0])
    live = jnp.zeros((SLOTS,), jnp.int32).at[order[0]].set((jnp.arange(SLOTS) < alive).astype(jnp.int32))
    flips = jnp.where(section == 0, jnp.array([0, 3, 1, 2]), jnp.array([0, 1, 3, 2])).astype(jnp.int32)
    place = jnp.concatenate([me % 4 ^ flips, me // 4 % 4 ^ flips, me // 16 ^ flips, live])
    total = lax.psum(alive.astype(jnp.float32), "dp")

    run = lambda colour, half: partials(colour, half, activations, cotangents, place)
    a_far = run(0, 2)
    b_far = run(1, 2)
    c_send = run(2, 2)
    a_near = run(0, 0)
    b_near = run(1, 0)
    c_keep = run(2, 0)
    a = scattered(COLOURS[0][2], (a_far, a_near))
    b = scattered(COLOURS[1][2], (b_far, b_near))
    c = scattered(COLOURS[2][2], ((c_send[0], c_keep[0]), (c_send[1], c_keep[1])))
    return jnp.concatenate([a, b, c], axis=1) / total


def solution(mesh):
    in_specs = (
        P(("section", "dp"), None, None, None),
        P(("section", "dp"), None, None, None),
        P(),
        P("dp"),
        P("dp", None),
    )
    out_specs = P(("section", "dp"), None)
    return jax.shard_map(shards, mesh=mesh, in_specs=in_specs, out_specs=out_specs, check_vma=False)
```

time: 551 us -> 378 us (0.69)
  waiting for transfers between devices: 229 us -> 89 us
  matrix products: 108 us -> 0 us
  Pallas kernels: 0 us -> 43.6 us
  between operations: 26.1 us -> 1.73 us
  starting transfers between devices: 0.01 us -> 19.9 us
  other arithmetic: 3.02 us -> 18.6 us
  blocking collectives: 181 us -> 194 us
  local copies, waits for them, and re-layouts: 3.5 us -> 10.2 us
    reduce_scatter x1 -> x0, waiting for transfers between devices: 229 us -> none  [shards(): lax.psum_scatter(partial_gradient, 'dp', scatter_dimension=0, tiled=True)]
    psum x0 -> x1, blocking collectives: none -> 194 us  [shards(): total = lax.psum(alive.astype(jnp.float32), 'dp')]
    unnamed x1 -> x0, blocking collectives: 181 us -> none
    dot_general x6 -> x0, matrix products: 108 us -> none  [shards(): lax.dot_general(act_rows, cot_rows, (((0,), (0,)), ((), ())), preferred_e...]
    ppermute x0 -> x30, waiting for transfers between devices: none -> 89 us  [exchange(): return lax.ppermute(value, ('section', 'dp'), pairs)]
    pallas_call x0 -> x6, Pallas kernels: none -> 43.6 us  [partials(): pl.pallas_call(kernel, out_shape=[jax.ShapeDtypeStruct(shape, jnp.float32...]
    ppermute x0 -> x30, starting transfers between devices: none -> 19.9 us  [exchange(): return lax.ppermute(value, ('section', 'dp'), pairs)]
    add x0 -> x30, other arithmetic: none -> 15.8 us  [the longest x6 7.83 us: scattered(): after_first.append(keep[0] + got[0] + late)]
  transfers between devices with their start and end apart: 1 -> 30, of which waited for: 1 -> 19; matrix products, arithmetic and copies ran while one was open for 0% -> 4% of each run, Pallas kernels for 0% -> 10%
where the time goes in v1:
time: 378 us; the launch traced here: 377 us
  blocking collectives  194 us (51%)
  waiting for transfers between devices  89 us (24%)
  Pallas kernels  43.6 us (12%)
  starting transfers between devices  19.9 us (5%)
  other arithmetic  18.6 us (5%)
  local copies, waits for them, and re-layouts  10.2 us (3%)
    psum x1, blocking collectives, shards(): total = lax.psum(alive.astype(jnp.float32), 'dp')  194 us
    ppermute x30, waiting for transfers between devices, exchange(): return lax.ppermute(value, ('section', 'dp'), pairs)  89 us
    pallas_call x6, Pallas kernels, partials(): pl.pallas_call(kernel, out_shape=[jax.ShapeDtypeStruct(shape, jnp.float32...  43.6 us
    ppermute x30, starting transfers between devices, exchange(): return lax.ppermute(value, ('section', 'dp'), pairs)  19.9 us
    unnamed x20, local copies, waits for them, and re-layouts  9.35 us
    add x6, other arithmetic, scattered(): after_first.append(keep[0] + got[0] + late)  7.83 us
  transfers between devices with their start and end apart: 30, of which 19 were waited for; matrix products, arithmetic and copies ran while one was open for 4% of the time, Pallas kernels for 10%

profile of v1, /device:TPU:0, one launch (start us, length us, event | category | flops | bytes accessed | tf_op | source)
XLA Modules:
  0.0 376.8 jit_solution(10649938962867397439)
XLA Ops:
  3.4 2.7 copy-done
  6.0 6.4 %shard_map.76 = (f32[2,4,2,40,640]{4,3,2,1,0:T(8,128)}, f32[2,4,2,40,640]{4,3,2,1,0:T(8,128)S(1)}) custom-call(s32[18]{0:T(128)S(1)} %pad_add_fusion.place, bf16[1,6,192,2560]{3,2,1,0:T(8,128)(2,1)S(1)} %copy-done, bf16[1,6,192,2560]{3,2,1,0:T(8,128)(2,1)} %cot_ref.11), custom_call_target="tpu_custom_call" | custom-call | flops 1887436800 | bytes 7700480 | tf_op jit(solution)/shard_map/pallas_call | solution.py:68
  13.7 1.7 collective-permute-start.14
  15.3 7.8 %shard_map.74 = (f32[2,4,2,40,896]{4,3,2,1,0:T(8,128)}, f32[2,4,2,40,896]{4,3,2,1,0:T(8,128)S(1)}) custom-call(s32[18]{0:T(128)S(1)} %pad_add_fusion.place, bf16[1,6,192,2560]{3,2,1,0:T(8,128)(2,1)S(1)} %copy-done, bf16[1,6,192,2560]{3,2,1,0:T(8,128)(2,1)} %cot_ref.11), custom_call_target="tpu_custom_call" | custom-call | flops 2642411520 | bytes 9601024 | tf_op jit(solution)/shard_map/pallas_call | solution.py:68
  24.6 7.8 %shard_map.73 = (f32[2,4,2,40,896]{4,3,2,1,0:T(8,128)}, f32[2,4,2,40,896]{4,3,2,1,0:T(8,128)S(1)}) custom-call(s32[18]{0:T(128)S(1)} %pad_add_fusion.place, bf16[1,6,192,2560]{3,2,1,0:T(8,128)(2,1)S(1)} %copy-done, bf16[1,6,192,2560]{3,2,1,0:T(8,128)(2,1)} %cot_ref.11), custom_call_target="tpu_custom_call" | custom-call | flops 2642411520 | bytes 9601024 | tf_op jit(solution)/shard_map/pallas_call | solution.py:68
  32.9 6.5 %shard_map.75 = (f32[2,4,2,40,640]{4,3,2,1,0:T(8,128)}, f32[2,4,2,40,640]{4,3,2,1,0:T(8,128)S(1)}) custom-call(s32[18]{0:T(128)S(1)} %pad_add_fusion.place, bf16[1,6,192,2560]{3,2,1,0:T(8,128)(2,1)S(1)} %copy-done, bf16[1,6,192,2560]{3,2,1,0:T(8,128)(2,1)} %cot_ref.11), custom_call_target="tpu_custom_call" | custom-call | flops 1887436800 | bytes 7700480 | tf_op jit(solution)/shard_map/pallas_call | solution.py:68
  40.9 8.0 %shard_map.78 = (f32[2,4,2,40,1024]{4,3,2,1,0:T(8,128)}, f32[2,4,2,40,1024]{4,3,2,1,0:T(8,128)S(1)}) custom-call(s32[18]{0:T(128)S(1)} %pad_add_fusion.place, bf16[1,6,192,2560]{3,2,1,0:T(8,128)(2,1)S(1)} %copy-done, bf16[1,6,192,2560]{3,2,1,0:T(8,128)(2,1)} %cot_ref.11), custom_call_target="tpu_custom_call" | custom-call | flops 3019898880 | bytes 10551296 | tf_op jit(solution)/shard_map/pallas_call | solution.py:68
  50.4 2.0 collective-permute-start.24
  52.4 193.7 %psum.7 = f32[]{:T(128)} all-reduce(f32[]{:T(128)S(6)} %convert_element_type.7), channel_id=1, replica_groups=mesh['section'=2,'dp'=64] {'dp'}, use_global_device_ids=true, to_apply=%region_1.2 | all-reduce | flops 1 | bytes 8 | tf_op jit(solution)/shard_map/psum | solution.py:113
  246.2 2.7 copy-done.1
  248.8 7.2 %shard_map.77 = (f32[2,4,2,40,1024]{4,3,2,1,0:T(8,128)S(1)}, f32[2,4,2,40,1024]{4,3,2,1,0:T(8,128)S(1)}) custom-call(s32[18]{0:T(128)S(1)} %pad_add_fusion.place, bf16[1,6,192,2560]{3,2,1,0:T(8,128)(2,1)S(1)} %copy-done.1, bf16[1,6,192,2560]{3,2,1,0:T(8,128)(2,1)} %cot_ref.11), custom_call_target="tpu_custom_call" | custom-call | flops 3019898880 | bytes 10551296 | tf_op jit(solution)/shard_map/pallas_call | solution.py:68
  259.1 3.1 collective-permute-start.11
  265.2 6.1 %collective-permute-done.15 = f32[4,2,40,640]{3,2,1,0:T(8,128)S(1)} collective-permute-done((f32[4,2,40,640]{3,2,1,0:T(8,128)S(1)}, f32[4,2,40,640]{3,2,1,0:T(8,128)S(1)}, u32[]{:S(2)}, u32[]{:S(2)}) %collective-permute-start.15) | collective-permute-done | bytes 819232 | tf_op jit(solution)/shard_map/ppermute | solution.py:24
  272.6 7.4 %collective-permute-done.11 = f32[4,2,40,640]{3,2,1,0:T(8,128)S(1)} collective-permute-done((f32[4,2,40,640]{3,2,1,0:T(8,128)S(1)}, f32[4,2,40,640]{3,2,1,0:T(8,128)S(1)}, u32[]{:S(2)}, u32[]{:S(2)}) %collective-permute-start.11) | collective-permute-done | bytes 819232 | tf_op jit(solution)/shard_map/ppermute | solution.py:24
  281.4 2.1 collective-permute-start.12
  285.0 2.9 collective-permute-done.16
  288.0 4.4 %collective-permute-done.12 = f32[2,2,40,640]{3,2,1,0:T(8,128)S(1)} collective-permute-done((f32[2,2,40,640]{3,2,1,0:T(8,128)S(1)}, f32[2,2,40,640]{3,2,1,0:T(8,128)S(1)}, u32[]{:S(2)}, u32[]{:S(2)}) %collective-permute-start.12) | collective-permute-done | bytes 409632 | tf_op jit(solution)/shard_map/ppermute | solution.py:24
  292.4 6.9 %collective-permute-done.17 = f32[2,40,640]{2,1,0:T(8,128)S(1)} collective-permute-done((f32[2,40,640]{2,1,0:T(8,128)S(1)}, f32[2,40,640]{2,1,0:T(8,128)S(1)}, u32[]{:S(2)}, u32[]{:S(2)}) %collective-permute-start.17) | collective-permute-done | bytes 204832 | tf_op jit(solution)/shard_map/ppermute | solution.py:24
  299.4 6.9 %collective-permute-done.13 = f32[2,40,640]{2,1,0:T(8,128)S(1)} collective-permute-done((f32[2,40,640]{2,1,0:T(8,128)S(1)}, f32[2,40,640]{2,1,0:T(8,128)S(1)}, u32[]{:S(2)}, u32[]{:S(2)}) %collective-permute-start.13) | collective-permute-done | bytes 204832 | tf_op jit(solution)/shard_map/ppermute | solution.py:24
  306.3 1.9 collective-permute-start.18
  308.2 10.1 %collective-permute-done.18 = f32[2,40,640]{2,1,0:T(8,128)S(1)} collective-permute-done((f32[2,40,640]{2,1,0:T(8,128)S(1)}, f32[2,40,640]{2,1,0:T(8,128)S(1)}, u32[]{:S(2)}, u32[]{:S(2)}) %collective-permute-start.18) | collective-permute-done | bytes 204832 | tf_op jit(solution)/shard_map/ppermute | solution.py:24
  318.7 3.3 collective-permute-start.21
  322.0 3.0 collective-permute-done.19
  328.3 2.1 collective-permute-start.2
  330.4 1.7 fusion.2
  332.3 7.3 %collective-permute-done.6 = f32[2,2,40,896]{3,2,1,0:T(8,128)S(1)} collective-permute-done((f32[2,2,40,896]{3,2,1,0:T(8,128)S(1)}, f32[2,2,40,896]{3,2,1,0:T(8,128)S(1)}, u32[]{:S(2)}, u32[]{:S(2)}) %collective-permute-start.6) | collective-permute-done | bytes 573472 | tf_op jit(solution)/shard_map/ppermute | solution.py:24
  339.7 1.8 collective-permute-done.21
  341.9 4.1 %collective-permute-done.2 = f32[2,2,40,896]{3,2,1,0:T(8,128)S(1)} collective-permute-done((f32[2,2,40,896]{3,2,1,0:T(8,128)S(1)}, f32[2,2,40,896]{3,2,1,0:T(8,128)S(1)}, u32[]{:S(2)}, u32[]{:S(2)}) %collective-permute-start.2) | collective-permute-done | bytes 573472 | tf_op jit(solution)/shard_map/ppermute | solution.py:24
  347.6 5.4 %collective-permute-done.26 = f32[2,2,40,1024]{3,2,1,0:T(8,128)S(1)} collective-permute-done((f32[2,2,40,1024]{3,2,1,0:T(8,128)S(1)}, f32[2,2,40,1024]{3,2,1,0:T(8,128)S(1)}, u32[]{:S(2)}, u32[]{:S(2)}) %collective-permute-start.26) | collective-permute-done | bytes 655392 | tf_op jit(solution)/shard_map/ppermute | solution.py:24
  354.1 6.0 %collective-permute-done.22 = f32[2,2,40,1024]{3,2,1,0:T(8,128)S(1)} collective-permute-done((f32[2,2,40,1024]{3,2,1,0:T(8,128)S(1)}, f32[2,2,40,1024]{3,2,1,0:T(8,128)S(1)}, u32[]{:S(2)}, u32[]{:S(2)}) %collective-permute-start.22) | collective-permute-done | bytes 655392 | tf_op jit(solution)/shard_map/ppermute | solution.py:24
  361.8 6.7 %collective-permute-done.23 = f32[2,40,1024]{2,1,0:T(8,128)S(1)} collective-permute-done((f32[2,40,1024]{2,1,0:T(8,128)S(1)}, f32[2,40,1024]{2,1,0:T(8,128)S(1)}, u32[]{:S(2)}, u32[]{:S(2)}) %collective-permute-start.23) | collective-permute-done | bytes 327712 | tf_op jit(solution)/shard_map/ppermute | solution.py:24
  368.9 6.5 %collective-permute-done.29 = f32[40,1024]{1,0:T(8,128)S(1)} collective-permute-done((f32[40,1024]{1,0:T(8,128)S(1)}, f32[40,1024]{1,0:T(8,128)S(1)}, u32[]{:S(2)}, u32[]{:S(2)}) %collective-permute-start.29) | collective-permute-done | bytes 163872 | tf_op jit(solution)/shard_map/ppermute | solution.py:24
  (97 shorter events, 28.9 us)
Async XLA Ops:
  13.7 242.4 %collective-permute-start.14 = (f32[2,4,2,40,640]{4,3,2,1,0:T(8,128)}, f32[2,4,2,40,640]{4,3,2,1,0:T(8,128)}, u32[]{:S(2)}, u32[]{:S(2)}) collective-permute-start(f32[2,4,2,40,640]{4,3,2,1,0:T(8,128)} %get-tuple-element.24), channel_id=1, source_target_pairs={{0,4},{1,5},{2,6},{3,7},{4,0},{5,1},{6,2},{7,3},{8,12},{9,13},{10,... | collective-permute-start | bytes 4915208 | tf_op jit(solution)/shard_map/ppermute | solution.py:24
  23.1 9.3 %copy-start.2 = (f32[2,4,2,40,896]{4,3,2,1,0:T(8,128)}, f32[2,4,2,40,896]{4,3,2,1,0:T(8,128)S(1)}, u32[]{:S(2)}) copy-start(f32[2,4,2,40,896]{4,3,2,1,0:T(8,128)S(1)} %get-tuple-element.19) | copy-start | bytes 6881284
  23.1 236.1 %collective-permute-start.4 = (f32[2,4,2,40,896]{4,3,2,1,0:T(8,128)}, f32[2,4,2,40,896]{4,3,2,1,0:T(8,128)}, u32[]{:S(2)}, u32[]{:S(2)}) collective-permute-start(f32[2,4,2,40,896]{4,3,2,1,0:T(8,128)} %get-tuple-element.20), channel_id=1, source_target_pairs={{0,1},{1,0},{2,3},{3,2},{4,5},{5,4},{6,7},{7,6},{8,9},{9,8},{10,11... | collective-permute-start | bytes 6881288 | tf_op jit(solution)/shard_map/ppermute | solution.py:24
  32.4 231.3 %collective-permute-start = (f32[2,4,2,40,896]{4,3,2,1,0:T(8,128)}, f32[2,4,2,40,896]{4,3,2,1,0:T(8,128)}, u32[]{:S(2)}, u32[]{:S(2)}) collective-permute-start(f32[2,4,2,40,896]{4,3,2,1,0:T(8,128)} %get-tuple-element.18), channel_id=1, source_target_pairs={{0,1},{1,0},{2,3},{3,2},{4,5},{5,4},{6,7},{7,6},{8,9},{9,8},{10,11... | collective-permute-start | bytes 6881288 | tf_op jit(solution)/shard_map/ppermute | solution.py:24
  40.6 217.0 %collective-permute-start.10 = (f32[2,4,2,40,640]{4,3,2,1,0:T(8,128)}, f32[2,4,2,40,640]{4,3,2,1,0:T(8,128)}, u32[]{:S(2)}, u32[]{:S(2)}) collective-permute-start(f32[2,4,2,40,640]{4,3,2,1,0:T(8,128)} %get-tuple-element.22), channel_id=1, source_target_pairs={{0,4},{1,5},{2,6},{3,7},{4,0},{5,1},{6,2},{7,3},{8,12},{9,13},{10,... | collective-permute-start | bytes 4915208 | tf_op jit(solution)/shard_map/ppermute | solution.py:24
  50.4 231.0 %collective-permute-start.24 = (f32[2,4,2,40,1024]{4,3,2,1,0:T(8,128)}, f32[2,4,2,40,1024]{4,3,2,1,0:T(8,128)}, u32[]{:S(2)}, u32[]{:S(2)}) collective-permute-start(f32[2,4,2,40,1024]{4,3,2,1,0:T(8,128)} %get-tuple-element.28), channel_id=1, source_target_pairs={{0,16},{1,17},{2,18},{3,19},{4,20},{5,21},{6,22},{7,23},{8,24},{9,... | collective-permute-start | bytes 7864328 | tf_op jit(solution)/shard_map/ppermute | solution.py:24
  248.8 7.4 %copy-start.5 = (f32[2,4,2,40,640]{4,3,2,1,0:T(8,128)S(1)}, f32[2,4,2,40,640]{4,3,2,1,0:T(8,128)}, u32[]{:S(2)}) copy-start(f32[2,4,2,40,640]{4,3,2,1,0:T(8,128)} %copy-done.4) | copy-start | bytes 4915204
  256.1 62.3 %collective-permute-start.20 = (f32[2,4,2,40,1024]{4,3,2,1,0:T(8,128)S(1)}, f32[2,4,2,40,1024]{4,3,2,1,0:T(8,128)S(1)}, u32[]{:S(2)}, u32[]{:S(2)}) collective-permute-start(f32[2,4,2,40,1024]{4,3,2,1,0:T(8,128)S(1)} %copy-done.9), channel_id=1, source_target_pairs={{0,16},{1,17},{2,18},{3,19},{4,20},{5,21},{6,22},{7,23},{8,24},{9,... | collective-permute-start | bytes 7864328 | tf_op jit(solution)/shard_map/ppermute | solution.py:24
  257.6 13.6 %collective-permute-start.15 = (f32[4,2,40,640]{3,2,1,0:T(8,128)S(1)}, f32[4,2,40,640]{3,2,1,0:T(8,128)S(1)}, u32[]{:S(2)}, u32[]{:S(2)}) collective-permute-start(f32[4,2,40,640]{3,2,1,0:T(8,128)S(1)} %fusion.12), channel_id=1, source_target_pairs={{0,12},{1,13},{2,14},{3,15},{4,8},{5,9},{6,10},{7,11},{8,4},{9,5},... | collective-permute-start | bytes 2457608 | tf_op jit(solution)/shard_map/ppermute | solution.py:24
  259.1 20.8 %collective-permute-start.11 = (f32[4,2,40,640]{3,2,1,0:T(8,128)S(1)}, f32[4,2,40,640]{3,2,1,0:T(8,128)S(1)}, u32[]{:S(2)}, u32[]{:S(2)}) collective-permute-start(f32[4,2,40,640]{3,2,1,0:T(8,128)S(1)} %fusion.15), channel_id=1, source_target_pairs={{0,12},{1,13},{2,14},{3,15},{4,8},{5,9},{6,10},{7,11},{8,4},{9,5},... | collective-permute-start | bytes 2457608 | tf_op jit(solution)/shard_map/ppermute | solution.py:24
  263.7 61.4 %collective-permute-start.5 = (f32[4,2,40,896]{3,2,1,0:T(8,128)S(1)}, f32[4,2,40,896]{3,2,1,0:T(8,128)S(1)}, u32[]{:S(2)}, u32[]{:S(2)}) collective-permute-start(f32[4,2,40,896]{3,2,1,0:T(8,128)S(1)} %fusion.6), channel_id=1, source_target_pairs={{0,3},{1,2},{2,1},{3,0},{4,7},{5,6},{6,5},{7,4},{8,11},{9,10},{10,... | collective-permute-start | bytes 3440648 | tf_op jit(solution)/shard_map/ppermute | solution.py:24
  271.2 55.5 %collective-permute-start.1 = (f32[4,2,40,896]{3,2,1,0:T(8,128)S(1)}, f32[4,2,40,896]{3,2,1,0:T(8,128)S(1)}, u32[]{:S(2)}, u32[]{:S(2)}) collective-permute-start(f32[4,2,40,896]{3,2,1,0:T(8,128)S(1)} %fusion.9), channel_id=1, source_target_pairs={{0,3},{1,2},{2,1},{3,0},{4,7},{5,6},{6,5},{7,4},{8,11},{9,10},{10,... | collective-permute-start | bytes 3440648 | tf_op jit(solution)/shard_map/ppermute | solution.py:24
  280.0 8.0 %collective-permute-start.16 = (f32[2,2,40,640]{3,2,1,0:T(8,128)S(1)}, f32[2,2,40,640]{3,2,1,0:T(8,128)S(1)}, u32[]{:S(2)}, u32[]{:S(2)}) collective-permute-start(f32[2,2,40,640]{3,2,1,0:T(8,128)S(1)} %slice.293), channel_id=1, source_target_pairs={{0,1},{1,0},{2,3},{3,2},{4,5},{5,4},{6,7},{7,6},{8,9},{9,8},{10,11... | collective-permute-start | bytes 1228808 | tf_op jit(solution)/shard_map/ppermute | solution.py:24
  281.4 10.9 %collective-permute-start.12 = (f32[2,2,40,640]{3,2,1,0:T(8,128)S(1)}, f32[2,2,40,640]{3,2,1,0:T(8,128)S(1)}, u32[]{:S(2)}, u32[]{:S(2)}) collective-permute-start(f32[2,2,40,640]{3,2,1,0:T(8,128)S(1)} %slice.285), channel_id=1, source_target_pairs={{0,1},{1,0},{2,3},{3,2},{4,5},{5,4},{6,7},{7,6},{8,9},{9,8},{10,11... | collective-permute-start | bytes 1228808 | tf_op jit(solution)/shard_map/ppermute | solution.py:24
  288.0 42.4 %collective-permute-start.25 = (f32[4,2,40,1024]{3,2,1,0:T(8,128)S(1)}, f32[4,2,40,1024]{3,2,1,0:T(8,128)S(1)}, u32[]{:S(2)}, u32[]{:S(2)}) collective-permute-start(f32[4,2,40,1024]{3,2,1,0:T(8,128)S(1)} %fusion), channel_id=1, source_target_pairs={{0,48},{1,49},{2,50},{3,51},{4,52},{5,53},{6,54},{7,55},{8,56},{9,... | collective-permute-start | bytes 3932168 | tf_op jit(solution)/shard_map/ppermute | solution.py:24
  292.3 7.0 %collective-permute-start.17 = (f32[2,40,640]{2,1,0:T(8,128)S(1)}, f32[2,40,640]{2,1,0:T(8,128)S(1)}, u32[]{:S(2)}, u32[]{:S(2)}) collective-permute-start(f32[2,40,640]{2,1,0:T(8,128)S(1)} %fusion.30), channel_id=1, source_target_pairs={{0,3},{1,2},{2,1},{3,0},{4,7},{5,6},{6,5},{7,4},{8,11},{9,10},{10,... | collective-permute-start | bytes 614408 | tf_op jit(solution)/shard_map/ppermute | solution.py:24
  299.3 7.0 %collective-permute-start.13 = (f32[2,40,640]{2,1,0:T(8,128)S(1)}, f32[2,40,640]{2,1,0:T(8,128)S(1)}, u32[]{:S(2)}, u32[]{:S(2)}) collective-permute-start(f32[2,40,640]{2,1,0:T(8,128)S(1)} %fusion.33), channel_id=1, source_target_pairs={{0,3},{1,2},{2,1},{3,0},{4,7},{5,6},{6,5},{7,4},{8,11},{9,10},{10,... | collective-permute-start | bytes 614408 | tf_op jit(solution)/shard_map/ppermute | solution.py:24
  306.3 12.1 %collective-permute-start.18 = (f32[2,40,640]{2,1,0:T(8,128)S(1)}, f32[2,40,640]{2,1,0:T(8,128)S(1)}, u32[]{:S(2)}, u32[]{:S(2)}) collective-permute-start(f32[2,40,640]{2,1,0:T(8,128)S(1)} %fusion.32), channel_id=1, source_target_pairs={{0,16},{1,17},{2,18},{3,19},{4,20},{5,21},{6,22},{7,23},{8,24},{9,... | collective-permute-start | bytes 614408 | tf_op jit(solution)/shard_map/ppermute | solution.py:24
  318.4 6.7 %collective-permute-start.19 = (f32[40,640]{1,0:T(8,128)S(1)}, f32[40,640]{1,0:T(8,128)S(1)}, u32[]{:S(2)}, u32[]{:S(2)}) collective-permute-start(f32[40,640]{1,0:T(8,128)S(1)} %fusion.42), channel_id=1, source_target_pairs={{0,48},{1,49},{2,50},{3,51},{4,52},{5,53},{6,54},{7,55},{8,56},{9,... | collective-permute-start | bytes 307208 | tf_op jit(solution)/shard_map/ppermute | solution.py:24
  318.7 22.7 %collective-permute-start.21 = (f32[4,2,40,1024]{3,2,1,0:T(8,128)S(1)}, f32[4,2,40,1024]{3,2,1,0:T(8,128)S(1)}, u32[]{:S(2)}, u32[]{:S(2)}) collective-permute-start(f32[4,2,40,1024]{3,2,1,0:T(8,128)S(1)} %fusion.3), channel_id=1, source_target_pairs={{0,48},{1,49},{2,50},{3,51},{4,52},{5,53},{6,54},{7,55},{8,56},{9,... | collective-permute-start | bytes 3932168 | tf_op jit(solution)/shard_map/ppermute | solution.py:24
  326.6 12.9 %collective-permute-start.6 = (f32[2,2,40,896]{3,2,1,0:T(8,128)S(1)}, f32[2,2,40,896]{3,2,1,0:T(8,128)S(1)}, u32[]{:S(2)}, u32[]{:S(2)}) collective-permute-start(f32[2,2,40,896]{3,2,1,0:T(8,128)S(1)} %slice.275), channel_id=1, source_target_pairs={{0,4},{1,5},{2,6},{3,7},{4,0},{5,1},{6,2},{7,3},{8,12},{9,13},{10,... | collective-permute-start | bytes 1720328 | tf_op jit(solution)/shard_map/ppermute | solution.py:24
  328.3 17.8 %collective-permute-start.2 = (f32[2,2,40,896]{3,2,1,0:T(8,128)S(1)}, f32[2,2,40,896]{3,2,1,0:T(8,128)S(1)}, u32[]{:S(2)}, u32[]{:S(2)}) collective-permute-start(f32[2,2,40,896]{3,2,1,0:T(8,128)S(1)} %slice.267), channel_id=1, source_target_pairs={{0,4},{1,5},{2,6},{3,7},{4,0},{5,1},{6,2},{7,3},{8,12},{9,13},{10,... | collective-permute-start | bytes 1720328 | tf_op jit(solution)/shard_map/ppermute | solution.py:24
  332.2 20.9 %collective-permute-start.26 = (f32[2,2,40,1024]{3,2,1,0:T(8,128)S(1)}, f32[2,2,40,1024]{3,2,1,0:T(8,128)S(1)}, u32[]{:S(2)}, u32[]{:S(2)}) collective-permute-start(f32[2,2,40,1024]{3,2,1,0:T(8,128)S(1)} %slice.311), channel_id=1, source_target_pairs={{0,4},{1,5},{2,6},{3,7},{4,0},{5,1},{6,2},{7,3},{8,12},{9,13},{10,... | collective-permute-start | bytes 1966088 | tf_op jit(solution)/shard_map/ppermute | solution.py:24
  339.6 7.9 %collective-permute-start.7 = (f32[2,40,896]{2,1,0:T(8,128)S(1)}, f32[2,40,896]{2,1,0:T(8,128)S(1)}, u32[]{:S(2)}, u32[]{:S(2)}) collective-permute-start(f32[2,40,896]{2,1,0:T(8,128)S(1)} %fusion.24), channel_id=1, source_target_pairs={{0,12},{1,13},{2,14},{3,15},{4,8},{5,9},{6,10},{7,11},{8,4},{9,5},... | collective-permute-start | bytes 860168 | tf_op jit(solution)/shard_map/ppermute | solution.py:24
  341.9 18.3 %collective-permute-start.22 = (f32[2,2,40,1024]{3,2,1,0:T(8,128)S(1)}, f32[2,2,40,1024]{3,2,1,0:T(8,128)S(1)}, u32[]{:S(2)}, u32[]{:S(2)}) collective-permute-start(f32[2,2,40,1024]{3,2,1,0:T(8,128)S(1)} %slice.303), channel_id=1, source_target_pairs={{0,4},{1,5},{2,6},{3,7},{4,0},{5,1},{6,2},{7,3},{8,12},{9,13},{10,... | collective-permute-start | bytes 1966088 | tf_op jit(solution)/shard_map/ppermute | solution.py:24
  346.1 7.9 %collective-permute-start.3 = (f32[2,40,896]{2,1,0:T(8,128)S(1)}, f32[2,40,896]{2,1,0:T(8,128)S(1)}, u32[]{:S(2)}, u32[]{:S(2)}) collective-permute-start(f32[2,40,896]{2,1,0:T(8,128)S(1)} %fusion.27), channel_id=1, source_target_pairs={{0,12},{1,13},{2,14},{3,15},{4,8},{5,9},{6,10},{7,11},{8,4},{9,5},... | collective-permute-start | bytes 860168 | tf_op jit(solution)/shard_map/ppermute | solution.py:24
  347.6 14.1 %collective-permute-start.8 = (f32[2,40,896]{2,1,0:T(8,128)S(1)}, f32[2,40,896]{2,1,0:T(8,128)S(1)}, u32[]{:S(2)}, u32[]{:S(2)}) collective-permute-start(f32[2,40,896]{2,1,0:T(8,128)S(1)} %fusion.26), channel_id=1, source_target_pairs={{0,16},{1,17},{2,18},{3,19},{4,20},{5,21},{6,22},{7,23},{8,24},{9,... | collective-permute-start | bytes 860168 | tf_op jit(solution)/shard_map/ppermute | solution.py:24
  353.1 8.4 %collective-permute-start.27 = (f32[2,40,1024]{2,1,0:T(8,128)S(1)}, f32[2,40,1024]{2,1,0:T(8,128)S(1)}, u32[]{:S(2)}, u32[]{:S(2)}) collective-permute-start(f32[2,40,1024]{2,1,0:T(8,128)S(1)} %fusion.18), channel_id=1, source_target_pairs={{0,12},{1,13},{2,14},{3,15},{4,8},{5,9},{6,10},{7,11},{8,4},{9,5},... | collective-permute-start | bytes 983048 | tf_op jit(solution)/shard_map/ppermute | solution.py:24
  360.2 8.4 %collective-permute-start.23 = (f32[2,40,1024]{2,1,0:T(8,128)S(1)}, f32[2,40,1024]{2,1,0:T(8,128)S(1)}, u32[]{:S(2)}, u32[]{:S(2)}) collective-permute-start(f32[2,40,1024]{2,1,0:T(8,128)S(1)} %fusion.21), channel_id=1, source_target_pairs={{0,12},{1,13},{2,14},{3,15},{4,8},{5,9},{6,10},{7,11},{8,4},{9,5},... | collective-permute-start | bytes 983048 | tf_op jit(solution)/shard_map/ppermute | solution.py:24
  361.6 7.2 %collective-permute-start.28 = (f32[2,40,1024]{2,1,0:T(8,128)S(1)}, f32[2,40,1024]{2,1,0:T(8,128)S(1)}, u32[]{:S(2)}, u32[]{:S(2)}) collective-permute-start(f32[2,40,1024]{2,1,0:T(8,128)S(1)} %fusion.20), channel_id=1, source_target_pairs={{0,1},{1,0},{2,3},{3,2},{4,5},{5,4},{6,7},{7,6},{8,9},{9,8},{10,11... | collective-permute-start | bytes 983048 | tf_op jit(solution)/shard_map/ppermute | solution.py:24
  361.7 7.1 %collective-permute-start.9 = (f32[40,896]{1,0:T(8,128)S(1)}, f32[40,896]{1,0:T(8,128)S(1)}, u32[]{:S(2)}, u32[]{:S(2)}) collective-permute-start(f32[40,896]{1,0:T(8,128)S(1)} %fusion.39), channel_id=1, source_target_pairs={{0,48},{1,49},{2,50},{3,51},{4,52},{5,53},{6,54},{7,55},{8,56},{9,... | collective-permute-start | bytes 430088 | tf_op jit(solution)/shard_map/ppermute | solution.py:24
  368.7 6.6 %collective-permute-start.29 = (f32[40,1024]{1,0:T(8,128)S(1)}, f32[40,1024]{1,0:T(8,128)S(1)}, u32[]{:S(2)}, u32[]{:S(2)}) collective-permute-start(f32[40,1024]{1,0:T(8,128)S(1)} %fusion.36), channel_id=1, source_target_pairs={{0,3},{1,2},{2,1},{3,0},{4,7},{5,6},{6,5},{7,4},{8,11},{9,10},{10,... | collective-permute-start | bytes 491528 | tf_op jit(solution)/shard_map/ppermute | solution.py:24
  (8 other events, 22.9 us)

commit v2 on v0

v2 whole, which is shorter than its diff:
```python
import functools

import jax
import jax.numpy as jnp
from jax import lax
from jax.experimental import pallas as pl
from jax.experimental.pallas import tpu as pltpu
from jax.sharding import PartitionSpec as P

SLOTS, TOKENS, ROWS = 6, 192, 40
K = SLOTS * TOKENS
TILE = 16 * ROWS
STRIDE = {"x": 1, "y": 4, "z": 16}
COLOURS = ((0, 768, ("xyz", "xyz")), (768, 768, ("yxz", "yxz")), (1536, 1024, ("zyx", "zxy")))


def exchange(value, axes, turn):
    pairs = []
    for section in range(2):
        flip, stride = 1 if section == turn else 3, STRIDE[axes[section]]
        for d in range(64):
            p = d // stride % 4
            pairs.append((section * 64 + d, section * 64 + d + ((p ^ flip) - p) * stride))
    return lax.ppermute(value, ("section", "dp"), pairs)


def products(half, failed, counts, order, act, cot, *refs):
    outs, (acts, cots, total, sems) = refs[:-4], refs[-4:]
    section, me = lax.axis_index("section"), lax.axis_index("dp")
    flips = (0, 3 - 2 * section, 1 + 2 * section, 2)
    xs, ys, zs = ([place ^ flip for flip in flips] for place in (me % 4, me // 4 % 4, me // 16))
    fetch = [
        pltpu.make_async_copy(
            act.at[0, :, :, pl.ds(pl.multiple_of(zs[half + g] * TILE, 128), TILE)], acts.at[g], sems.at[g])
        for g in range(2)
    ]
    load = [
        pltpu.make_async_copy(cot.at[0, :, :, pl.ds(column, columns)], cots.at[:, :, pl.ds(column, columns)], sems.at[2 + c])
        for c, (column, columns, _) in enumerate(COLOURS)
    ]
    fetch[0].start()
    for copy in load:
        copy.start()
    fetch[1].start()
    alive = jnp.where(me == failed[0], 0, counts[0])
    live = [jnp.float32(0)] * SLOTS
    for position in range(SLOTS):
        for k in range(SLOTS):
            live[k] = jnp.where((order[0, position] == k) & (position < alive), jnp.float32(1), live[k])
    if half == 2:
        outs[5][...] = jnp.full((8, 128), alive.astype(jnp.float32))
    for g in range(2):
        fetch[g].wait()
        rows = acts[g].reshape(K, TILE)
        for c, (column, columns, _) in enumerate(COLOURS):
            span = slice(column, column + columns)
            if g == 0:
                load[c].wait()
                for k in range(SLOTS):
                    cots[k, :, span] = cots[k, :, span] * live[k].astype(jnp.bfloat16)
            total[:, :columns] = lax.dot_general(
                rows, cots[:, :, span].reshape(K, columns), (((0,), (0,)), ((), ())),
                preferred_element_type=jnp.float32)
            for i in range(4):
                for j in range(4):
                    if c == 0:
                        start = xs[i] * ROWS + ys[j] * 160
                    elif c == 1:
                        start = ys[i] * 160 + xs[j] * ROWS
                    else:
                        start = jnp.where(section == 0, ys[i] * 160 + xs[j] * ROWS, xs[i] * ROWS + ys[j] * 160)
                    block = total[pl.ds(pl.multiple_of(start, 8), ROWS), :columns]
                    if c == 2:
                        outs[4][g, i, j] = block
                    else:
                        outs[2 * c + i // 2][i % 2, j, g] = block


def partials(half, activations, cotangents, failed, counts, order):
    shapes = [jax.ShapeDtypeStruct((2, 4, 2, ROWS, 768), jnp.float32)] * 4
    shapes.append(jax.ShapeDtypeStruct((2, 4, 4, ROWS, 1024), jnp.float32))
    if half == 2:
        shapes.append(jax.ShapeDtypeStruct((8, 128), jnp.float32))
    return pl.pallas_call(
        functools.partial(products, half),
        out_shape=shapes,
        in_specs=[pl.BlockSpec(memory_space=pltpu.SMEM)] * 3 + [pl.BlockSpec(memory_space=pltpu.HBM)] * 2,
        out_specs=[pl.BlockSpec(memory_space=pltpu.VMEM)] * len(shapes),
        scratch_shapes=[
            pltpu.VMEM((2, SLOTS, TOKENS, TILE), jnp.bfloat16),
            pltpu.VMEM((SLOTS, TOKENS, 2560), jnp.bfloat16),
            pltpu.VMEM((TILE, 1024), jnp.float32),
            pltpu.SemaphoreType.DMA((5,)),
        ],
        compiler_params=pltpu.CompilerParams(vmem_limit_bytes=26 << 20),
        cost_estimate=pl.CostEstimate(flops=1024, bytes_accessed=1024, transcendentals=0),
    )(failed, counts, order, *(pltpu.with_memory_space_constraint(x, pltpu.HBM) for x in (activations, cotangents)))


def together(values):
    return list(lax.optimization_barrier(tuple(values)))


def shards(activations, cotangents, failed, counts, order):
    axes = [[(colour[2][0][phase], colour[2][1][phase]) for colour in COLOURS] for phase in range(3)]

    def step(values, turn, phase):
        return [exchange(v, a, turn) for v, a in zip(values, axes[phase])]

    one = partials(2, activations, cotangents, failed, counts, order)
    activations, cotangents, *one = together([activations, cotangents, *one])
    two = partials(0, activations, cotangents, failed, counts, order)
    count = one[5]

    def counted(values, turn, axis):
        nonlocal count
        *values, got = together([*values, exchange(count, (axis, axis), turn)])
        count = count + got
        return values

    got_far = step([one[1], one[3]], 0, 0)
    got_near = step([two[1], two[3], one[4]], 0, 0)
    keep_far = [one[0], one[2], two[4][:, :, 2:4]]
    keep_near = [two[0], two[2], two[4][:, :, 0:2]]
    got_far = counted(got_far, 0, "x")
    got_near = counted(got_near, 1, "x")
    got_far.append(got_near[2][:, :, 2:4])
    got_near[2] = got_near[2][:, :, 0:2]
    keep, got = [keep_far, keep_near], [got_far, got_near]
    late = [step([k[1] + r[1] for k, r in zip(keep[i], got[i])], 1, 0) for i in range(2)]
    late = [counted(late[i], i, "y") for i in range(2)]
    whole = [[k[0] + r[0] + s for k, r, s in zip(keep[i], got[i], late[i])] for i in range(2)]
    send = [[w[2:4] for w in whole[i]] for i in range(2)]
    keep = [[w[0:2] for w in whole[i]] for i in range(2)]
    got = [counted(step(send[i], 0, 1), i, "z") for i in range(2)]
    late = [together(step([k[1] + r[1] for k, r in zip(keep[i], got[i])], 1, 1)) for i in range(2)]
    far, near = [[k[0] + r[0] + s for k, r, s in zip(keep[i], got[i], late[i])] for i in range(2)]
    got = together(step(far, 0, 2))
    late = together(step([k[1] + r[1] for k, r in zip(near, got)], 1, 2))
    total = count[0, 0]
    return jnp.concatenate([(k[0] + r[0] + s) / total for k, r, s in zip(near, got, late)], axis=1)


def solution(mesh):
    in_specs = (
        P(("section", "dp"), None, None, None),
        P(("section", "dp"), None, None, None),
        P(),
        P("dp"),
        P("dp", None),
    )
    out_specs = P(("section", "dp"), None)
    return jax.shard_map(shards, mesh=mesh, in_specs=in_specs, out_specs=out_specs, check_vma=False)
```

time: 551 us -> 178 us (0.32)
  blocking collectives: 181 us -> 0 us
  waiting for transfers between devices: 229 us -> 77.3 us
  matrix products: 108 us -> 0 us
  starting transfers between devices: 0.01 us -> 62.3 us
  Pallas kernels: 0 us -> 26.8 us
  between operations: 26.1 us -> 1.55 us
    reduce_scatter x1 -> x0, waiting for transfers between devices: 229 us -> none  [shards(): lax.psum_scatter(partial_gradient, 'dp', scatter_dimension=0, tiled=True)]
    unnamed x1 -> x0, blocking collectives: 181 us -> none
    dot_general x6 -> x0, matrix products: 108 us -> none  [shards(): lax.dot_general(act_rows, cot_rows, (((0,), (0,)), ((), ())), preferred_e...]
    ppermute x0 -> x35, waiting for transfers between devices: none -> 77.3 us  [exchange(): return lax.ppermute(value, ('section', 'dp'), pairs)]
    ppermute x0 -> x35, starting transfers between devices: none -> 62.3 us  [exchange(): return lax.ppermute(value, ('section', 'dp'), pairs)]
    pallas_call x0 -> x2, Pallas kernels: none -> 26.8 us  [partials(): pl.pallas_call(functools.partial(products, half), out_shape=shapes, in_sp...]
    add x0 -> x31, other arithmetic: none -> 6.11 us  [the longest x11 3.41 us: shards(): k[0] + r[0] + s]
  transfers between devices with their start and end apart: 1 -> 35, of which waited for: 1 -> 16; matrix products, arithmetic and copies ran while one was open for 0% -> 4% of each run, Pallas kernels for 0% -> 8%
where the time goes in v2:
time: 178 us
  waiting for transfers between devices  77.3 us (43%)
  starting transfers between devices  62.3 us (35%)
  Pallas kernels  26.8 us (15%)
  other arithmetic  8.27 us (5%)
    ppermute x35, waiting for transfers between devices, exchange(): return lax.ppermute(value, ('section', 'dp'), pairs)  77.3 us
    ppermute x35, starting transfers between devices, exchange(): return lax.ppermute(value, ('section', 'dp'), pairs)  62.3 us
    pallas_call x2, Pallas kernels, partials(): pl.pallas_call(functools.partial(products, half), out_shape=shapes, in_sp...  26.8 us
  transfers between devices with their start and end apart: 35, of which 16 were waited for; matrix products, arithmetic and copies ran while one was open for 4% of the time, Pallas kernels for 8%

profile of v2, /device:TPU:0, one launch (start us, length us, event | category | flops | bytes accessed | tf_op | source)
XLA Modules:
  0.0 177.6 jit_solution(6496839659763116193)
XLA Ops:
  2.0 13.4 %shard_map.55 = (f32[2,4,2,40,768]{4,3,2,1,0:T(8,128)S(1)}, f32[2,4,2,40,768]{4,3,2,1,0:T(8,128)S(1)}, f32[2,4,2,40,768]{4,3,2,1,0:T(8,128)S(1)}, f32[2,4,2,40,7...) custom-call(s32[1]{0:T(128)S(6)} %copy.6.failed, s32[1]{0:T(128)S(6)} %copy.7.counts, ...), custom_call_target="tpu_custom_call" | custom-call | flops 1024 | bytes 1024 | tf_op jit(solution)/shard_map/pallas_call | solution.py:84
  15.4 2.1 %collective-permute-start.2 = (f32[2,4,4,40,1024]{4,3,2,1,0:T(8,128)S(1)}, f32[2,4,4,40,1024]{4,3,2,1,0:T(8,128)S(1)}, u32[]{:S(2)}, u32[]{:S(2)}) collective-permute-start(f32[2,4,4,40,1024]{4,3,2,1,0:T(8,128)S(1)} %get-tuple-element.70), channel_id=1, source_target_pairs={{0,16},{1,17},{2,18},{3,19},{4,20},{5,21},{6,22},{7,23},{8,24},{9,... | collective-permute-start | bytes 15728648 | tf_op jit(solution)/shard_map/ppermute | solution.py:24
  21.0 13.4 %shard_map.56 = (f32[2,4,2,40,768]{4,3,2,1,0:T(8,128)S(1)}, f32[2,4,2,40,768]{4,3,2,1,0:T(8,128)S(1)}, f32[2,4,2,40,768]{4,3,2,1,0:T(8,128)S(1)}, f32[2,4,2,40,7...) custom-call(s32[1]{0:T(128)S(6)} %copy.6.failed, s32[1]{0:T(128)S(6)} %copy.7.counts, s32[1,6]{1,0:T(1,128)S(1)} %copy-done, ...), custom_call_target="tpu_custom_call" | custom-call | flops 1024 | bytes 1024 | tf_op jit(solution)/shard_map/pallas_call | solution.py:84
  36.0 6.1 %collective-permute-done.5 = f32[8,128]{1,0:T(8,128)S(1)} collective-permute-done((f32[8,128]{1,0:T(8,128)S(1)}, f32[8,128]{1,0:T(8,128)S(1)}, u32[]{:S(2)}, u32[]{:S(2)}) %collective-permute-start.5) | collective-permute-done | bytes 4128 | tf_op jit(solution)/shard_map/ppermute | solution.py:24
  43.7 2.8 %collective-permute-start.6 = (f32[8,128]{1,0:T(8,128)S(1)}, f32[8,128]{1,0:T(8,128)S(1)}, u32[]{:S(2)}, u32[]{:S(2)}) collective-permute-start(f32[8,128]{1,0:T(8,128)S(1)} %add.243), channel_id=1, source_target_pairs={{0,3},{1,2},{2,1},{3,0},{4,7},{5,6},{6,5},{7,4},{8,11},{9,10},{10,... | collective-permute-start | bytes 12296 | tf_op jit(solution)/shard_map/ppermute | solution.py:24
  47.9 2.3 %collective-permute-start.11 = (f32[4,2,40,768]{3,2,1,0:T(8,128)S(1)}, f32[4,2,40,768]{3,2,1,0:T(8,128)}, u32[]{:S(2)}, u32[]{:S(2)}) collective-permute-start(f32[4,2,40,768]{3,2,1,0:T(8,128)S(1)} %add_bitcast_fusion.2), channel_id=1, source_target_pairs={{0,12},{1,13},{2,14},{3,15},{4,8},{5,9},{6,10},{7,11},{8,4},{9,5},... | collective-permute-start | bytes 2949128 | tf_op jit(solution)/shard_map/ppermute | solution.py:24
  50.2 13.0 %collective-permute-done = f32[2,4,2,40,768]{4,3,2,1,0:T(8,128)S(1)} collective-permute-done((f32[2,4,2,40,768]{4,3,2,1,0:T(8,128)S(1)}, f32[2,4,2,40,768]{4,3,2,1,0:T(8,128)S(1)}, u32[]{:S(2)}, u32[]{:S(2)}) %collective-permute-start) | collective-permute-done | bytes 1966112 | tf_op jit(solution)/shard_map/ppermute | solution.py:24
  63.2 14.1 %collective-permute-done.1 = f32[2,4,2,40,768]{4,3,2,1,0:T(8,128)S(1)} collective-permute-done((f32[2,4,2,40,768]{4,3,2,1,0:T(8,128)S(1)}, f32[2,4,2,40,768]{4,3,2,1,0:T(8,128)S(1)}, u32[]{:S(2)}, u32[]{:S(2)}) %collective-permute-start.1) | collective-permute-done | bytes 1966112 | tf_op jit(solution)/shard_map/ppermute | solution.py:24
  78.0 2.6 %collective-permute-start.12 = (f32[4,2,40,1024]{3,2,1,0:T(8,128)S(1)}, f32[4,2,40,1024]{3,2,1,0:T(8,128)S(1)}, u32[]{:S(2)}, u32[]{:S(2)}) collective-permute-start(f32[4,2,40,1024]{3,2,1,0:T(8,128)S(1)} %get-tuple-element.115), channel_id=1, source_target_pairs={{0,48},{1,49},{2,50},{3,51},{4,52},{5,53},{6,54},{7,55},{8,56},{9,... | collective-permute-start | bytes 3932168 | tf_op jit(solution)/shard_map/ppermute | solution.py:24
  80.8 2.8 %collective-permute-start.10 = (f32[4,2,40,768]{3,2,1,0:T(8,128)S(1)}, f32[4,2,40,768]{3,2,1,0:T(8,128)S(1)}, u32[]{:S(2)}, u32[]{:S(2)}) collective-permute-start(f32[4,2,40,768]{3,2,1,0:T(8,128)S(1)} %add_bitcast_fusion.3), channel_id=1, source_target_pairs={{0,3},{1,2},{2,1},{3,0},{4,7},{5,6},{6,5},{7,4},{8,11},{9,10},{10,... | collective-permute-start | bytes 2949128 | tf_op jit(solution)/shard_map/ppermute | solution.py:24
  84.4 3.1 %collective-permute-start.8 = (f32[4,2,40,768]{3,2,1,0:T(8,128)S(1)}, f32[4,2,40,768]{3,2,1,0:T(8,128)S(1)}, u32[]{:S(2)}, u32[]{:S(2)}) collective-permute-start(f32[4,2,40,768]{3,2,1,0:T(8,128)S(1)} %add_bitcast_fusion.4), channel_id=1, source_target_pairs={{0,12},{1,13},{2,14},{3,15},{4,8},{5,9},{6,10},{7,11},{8,4},{9,5},... | collective-permute-start | bytes 2949128 | tf_op jit(solution)/shard_map/ppermute | solution.py:24
  88.2 7.9 %collective-permute-done.10 = f32[4,2,40,768]{3,2,1,0:T(8,128)S(1)} collective-permute-done((f32[4,2,40,768]{3,2,1,0:T(8,128)S(1)}, f32[4,2,40,768]{3,2,1,0:T(8,128)S(1)}, u32[]{:S(2)}, u32[]{:S(2)}) %collective-permute-start.10) | collective-permute-done | bytes 983072 | tf_op jit(solution)/shard_map/ppermute | solution.py:24
  97.7 2.0 %collective-permute-done.13 = f32[8,128]{1,0:T(8,128)S(1)} collective-permute-done((f32[8,128]{1,0:T(8,128)S(1)}, f32[8,128]{1,0:T(8,128)S(1)}, u32[]{:S(2)}, u32[]{:S(2)}) %collective-permute-start.13) | collective-permute-done | bytes 4128 | tf_op jit(solution)/shard_map/ppermute | solution.py:24
  99.8 3.0 %collective-permute-start.14 = (f32[8,128]{1,0:T(8,128)S(1)}, f32[8,128]{1,0:T(8,128)S(1)}, u32[]{:S(2)}, u32[]{:S(2)}) collective-permute-start(f32[8,128]{1,0:T(8,128)S(1)} %add.259), channel_id=1, source_target_pairs={{0,12},{1,13},{2,14},{3,15},{4,8},{5,9},{6,10},{7,11},{8,4},{9,5},... | collective-permute-start | bytes 12296 | tf_op jit(solution)/shard_map/ppermute | solution.py:24
  102.8 1.7 bitcast_add_fusion.2
  105.1 4.8 %collective-permute-done.7 = f32[4,2,40,768]{3,2,1,0:T(8,128)S(1)} collective-permute-done((f32[4,2,40,768]{3,2,1,0:T(8,128)S(1)}, f32[4,2,40,768]{3,2,1,0:T(8,128)S(1)}, u32[]{:S(2)}, u32[]{:S(2)}) %collective-permute-start.7) | collective-permute-done | bytes 983072 | tf_op jit(solution)/shard_map/ppermute | solution.py:24
  116.9 1.7 collective-permute-done.21
  121.1 6.8 %collective-permute-done.18 = f32[2,2,40,768]{3,2,1,0:T(8,128)S(1)} collective-permute-done((f32[2,2,40,768]{3,2,1,0:T(8,128)S(1)}, f32[2,2,40,768]{3,2,1,0:T(8,128)S(1)}, u32[]{:S(2)}, u32[]{:S(2)}) %collective-permute-start.18) | collective-permute-done | bytes 491552 | tf_op jit(solution)/shard_map/ppermute | solution.py:24
  127.9 2.5 %collective-permute-start.22 = (f32[8,128]{1,0:T(8,128)S(1)}, f32[8,128]{1,0:T(8,128)S(1)}, u32[]{:S(2)}, u32[]{:S(2)}) collective-permute-start(f32[8,128]{1,0:T(8,128)S(1)} %add.277), channel_id=1, source_target_pairs={{0,48},{1,49},{2,50},{3,51},{4,52},{5,53},{6,54},{7,55},{8,56},{9,... | collective-permute-start | bytes 12296 | tf_op jit(solution)/shard_map/ppermute | solution.py:24
  130.4 3.1 %collective-permute-start.28 = (f32[2,40,1024]{2,1,0:T(8,128)S(1)}, f32[2,40,1024]{2,1,0:T(8,128)S(1)}, u32[]{:S(2)}, u32[]{:S(2)}) collective-permute-start(f32[2,40,1024]{2,1,0:T(8,128)S(1)} %fusion.4), channel_id=1, source_target_pairs={{0,12},{1,13},{2,14},{3,15},{4,8},{5,9},{6,10},{7,11},{8,4},{9,5},... | collective-permute-start | bytes 983048 | tf_op jit(solution)/shard_map/ppermute | solution.py:24
  133.6 2.8 %collective-permute-start.27 = (f32[2,40,768]{2,1,0:T(8,128)S(1)}, f32[2,40,768]{2,1,0:T(8,128)S(1)}, u32[]{:S(2)}, u32[]{:S(2)}) collective-permute-start(f32[2,40,768]{2,1,0:T(8,128)S(1)} %fusion.10), channel_id=1, source_target_pairs={{0,3},{1,2},{2,1},{3,0},{4,7},{5,6},{6,5},{7,4},{8,11},{9,10},{10,... | collective-permute-start | bytes 737288 | tf_op jit(solution)/shard_map/ppermute | solution.py:24
  136.4 6.7 %collective-permute-done.15 = f32[2,2,40,768]{3,2,1,0:T(8,128)S(1)} collective-permute-done((f32[2,2,40,768]{3,2,1,0:T(8,128)S(1)}, f32[2,2,40,768]{3,2,1,0:T(8,128)S(1)}, u32[]{:S(2)}, u32[]{:S(2)}) %collective-permute-start.15) | collective-permute-done | bytes 491552 | tf_op jit(solution)/shard_map/ppermute | solution.py:24
  143.2 2.7 %collective-permute-start.26 = (f32[2,40,768]{2,1,0:T(8,128)S(1)}, f32[2,40,768]{2,1,0:T(8,128)S(1)}, u32[]{:S(2)}, u32[]{:S(2)}) collective-permute-start(f32[2,40,768]{2,1,0:T(8,128)S(1)} %fusion.11), channel_id=1, source_target_pairs={{0,12},{1,13},{2,14},{3,15},{4,8},{5,9},{6,10},{7,11},{8,4},{9,5},... | collective-permute-start | bytes 737288 | tf_op jit(solution)/shard_map/ppermute | solution.py:24
  146.6 2.8 %collective-permute-start.24 = (f32[2,40,768]{2,1,0:T(8,128)S(1)}, f32[2,40,768]{2,1,0:T(8,128)S(1)}, u32[]{:S(2)}, u32[]{:S(2)}) collective-permute-start(f32[2,40,768]{2,1,0:T(8,128)S(1)} %fusion.14), channel_id=1, source_target_pairs={{0,3},{1,2},{2,1},{3,0},{4,7},{5,6},{6,5},{7,4},{8,11},{9,10},{10,... | collective-permute-start | bytes 737288 | tf_op jit(solution)/shard_map/ppermute | solution.py:24
  149.5 2.8 %collective-permute-start.23 = (f32[2,40,768]{2,1,0:T(8,128)S(1)}, f32[2,40,768]{2,1,0:T(8,128)S(1)}, u32[]{:S(2)}, u32[]{:S(2)}) collective-permute-start(f32[2,40,768]{2,1,0:T(8,128)S(1)} %fusion.15), channel_id=1, source_target_pairs={{0,12},{1,13},{2,14},{3,15},{4,8},{5,9},{6,10},{7,11},{8,4},{9,5},... | collective-permute-start | bytes 737288 | tf_op jit(solution)/shard_map/ppermute | solution.py:24
  154.9 2.0 %collective-permute-start.29 = (f32[2,40,768]{2,1,0:T(8,128)S(1)}, f32[2,40,768]{2,1,0:T(8,128)S(1)}, u32[]{:S(2)}, u32[]{:S(2)}) collective-permute-start(f32[2,40,768]{2,1,0:T(8,128)S(1)} %fusion.13), channel_id=1, source_target_pairs={{0,16},{1,17},{2,18},{3,19},{4,20},{5,21},{6,22},{7,23},{8,24},{9,... | collective-permute-start | bytes 737288 | tf_op jit(solution)/shard_map/ppermute | solution.py:24
  156.9 2.1 %collective-permute-done.23 = f32[2,40,768]{2,1,0:T(8,128)S(1)} collective-permute-done((f32[2,40,768]{2,1,0:T(8,128)S(1)}, f32[2,40,768]{2,1,0:T(8,128)S(1)}, u32[]{:S(2)}, u32[]{:S(2)}) %collective-permute-start.23) | collective-permute-done | bytes 245792 | tf_op jit(solution)/shard_map/ppermute | solution.py:24
  159.2 3.8 %collective-permute-done.30 = f32[2,40,768]{2,1,0:T(8,128)S(1)} collective-permute-done((f32[2,40,768]{2,1,0:T(8,128)S(1)}, f32[2,40,768]{2,1,0:T(8,128)S(1)}, u32[]{:S(2)}, u32[]{:S(2)}) %collective-permute-start.30) | collective-permute-done | bytes 245792 | tf_op jit(solution)/shard_map/ppermute | solution.py:24
  163.0 2.6 %collective-permute-done.29 = f32[2,40,768]{2,1,0:T(8,128)S(1)} collective-permute-done((f32[2,40,768]{2,1,0:T(8,128)S(1)}, f32[2,40,768]{2,1,0:T(8,128)S(1)}, u32[]{:S(2)}, u32[]{:S(2)}) %collective-permute-start.29) | collective-permute-done | bytes 245792 | tf_op jit(solution)/shard_map/ppermute | solution.py:24
  165.7 2.1 %collective-permute-start.34 = (f32[40,1024]{1,0:T(8,128)S(1)}, f32[40,1024]{1,0:T(8,128)S(1)}, u32[]{:S(2)}, u32[]{:S(2)}) collective-permute-start(f32[40,1024]{1,0:T(8,128)S(1)} %fusion.21), channel_id=1, source_target_pairs={{0,3},{1,2},{2,1},{3,0},{4,7},{5,6},{6,5},{7,4},{8,11},{9,10},{10,... | collective-permute-start | bytes 491528 | tf_op jit(solution)/shard_map/ppermute | solution.py:24
  169.3 1.9 %collective-permute-start.32 = (f32[40,768]{1,0:T(8,128)S(1)}, f32[40,768]{1,0:T(8,128)S(1)}, u32[]{:S(2)}, u32[]{:S(2)}) collective-permute-start(f32[40,768]{1,0:T(8,128)S(1)} %fusion.26), channel_id=1, source_target_pairs={{0,48},{1,49},{2,50},{3,51},{4,52},{5,53},{6,54},{7,55},{8,56},{9,... | collective-permute-start | bytes 368648 | tf_op jit(solution)/shard_map/ppermute | solution.py:24
  171.7 2.2 %collective-permute-done.33 = f32[40,768]{1,0:T(8,128)S(1)} collective-permute-done((f32[40,768]{1,0:T(8,128)S(1)}, f32[40,768]{1,0:T(8,128)S(1)}, u32[]{:S(2)}, u32[]{:S(2)}) %collective-permute-start.33) | collective-permute-done | bytes 122912 | tf_op jit(solution)/shard_map/ppermute | solution.py:24
  (87 shorter events, 32.0 us)
Async XLA Ops:
  15.4 61.9 %collective-permute-start.2 = (f32[2,4,4,40,1024]{4,3,2,1,0:T(8,128)S(1)}, f32[2,4,4,40,1024]{4,3,2,1,0:T(8,128)S(1)}, u32[]{:S(2)}, u32[]{:S(2)}) collective-permute-start(f32[2,4,4,40,1024]{4,3,2,1,0:T(8,128)S(1)} %get-tuple-element.70), channel_id=1, source_target_pairs={{0,16},{1,17},{2,18},{3,19},{4,20},{5,21},{6,22},{7,23},{8,24},{9,... | collective-permute-start | bytes 15728648 | tf_op jit(solution)/shard_map/ppermute | solution.py:24
  17.4 26.3 %collective-permute-start.3 = (f32[2,4,2,40,768]{4,3,2,1,0:T(8,128)S(1)}, f32[2,4,2,40,768]{4,3,2,1,0:T(8,128)S(1)}, u32[]{:S(2)}, u32[]{:S(2)}) collective-permute-start(f32[2,4,2,40,768]{4,3,2,1,0:T(8,128)S(1)} %get-tuple-element.72), channel_id=1, source_target_pairs={{0,1},{1,0},{2,3},{3,2},{4,5},{5,4},{6,7},{7,6},{8,9},{9,8},{10,11... | collective-permute-start | bytes 5898248 | tf_op jit(solution)/shard_map/ppermute | solution.py:24
  18.9 24.8 %collective-permute-start.4 = (f32[2,4,2,40,768]{4,3,2,1,0:T(8,128)S(1)}, f32[2,4,2,40,768]{4,3,2,1,0:T(8,128)}, u32[]{:S(2)}, u32[]{:S(2)}) collective-permute-start(f32[2,4,2,40,768]{4,3,2,1,0:T(8,128)S(1)} %get-tuple-element.73), channel_id=1, source_target_pairs={{0,4},{1,5},{2,6},{3,7},{4,0},{5,1},{6,2},{7,3},{8,12},{9,13},{10,... | collective-permute-start | bytes 5898248 | tf_op jit(solution)/shard_map/ppermute | solution.py:24
  20.5 21.6 %collective-permute-start.5 = (f32[8,128]{1,0:T(8,128)S(1)}, f32[8,128]{1,0:T(8,128)S(1)}, u32[]{:S(2)}, u32[]{:S(2)}) collective-permute-start(f32[8,128]{1,0:T(8,128)S(1)} %get-tuple-element.71), channel_id=1, source_target_pairs={{0,1},{1,0},{2,3},{3,2},{4,5},{5,4},{6,7},{7,6},{8,9},{9,8},{10,11... | collective-permute-start | bytes 12296 | tf_op jit(solution)/shard_map/ppermute | solution.py:24
  34.4 28.8 %collective-permute-start = (f32[2,4,2,40,768]{4,3,2,1,0:T(8,128)S(1)}, f32[2,4,2,40,768]{4,3,2,1,0:T(8,128)S(1)}, u32[]{:S(2)}, u32[]{:S(2)}) collective-permute-start(f32[2,4,2,40,768]{4,3,2,1,0:T(8,128)S(1)} %get-tuple-element.68), channel_id=1, source_target_pairs={{0,1},{1,0},{2,3},{3,2},{4,5},{5,4},{6,7},{7,6},{8,9},{9,8},{10,11... | collective-permute-start | bytes 5898248 | tf_op jit(solution)/shard_map/ppermute | solution.py:24
  42.1 35.2 %collective-permute-start.1 = (f32[2,4,2,40,768]{4,3,2,1,0:T(8,128)S(1)}, f32[2,4,2,40,768]{4,3,2,1,0:T(8,128)S(1)}, u32[]{:S(2)}, u32[]{:S(2)}) collective-permute-start(f32[2,4,2,40,768]{4,3,2,1,0:T(8,128)S(1)} %get-tuple-element.69), channel_id=1, source_target_pairs={{0,4},{1,5},{2,6},{3,7},{4,0},{5,1},{6,2},{7,3},{8,12},{9,13},{10,... | collective-permute-start | bytes 5898248 | tf_op jit(solution)/shard_map/ppermute | solution.py:24
  43.7 33.6 %collective-permute-start.6 = (f32[8,128]{1,0:T(8,128)S(1)}, f32[8,128]{1,0:T(8,128)S(1)}, u32[]{:S(2)}, u32[]{:S(2)}) collective-permute-start(f32[8,128]{1,0:T(8,128)S(1)} %add.243), channel_id=1, source_target_pairs={{0,3},{1,2},{2,1},{3,0},{4,7},{5,6},{6,5},{7,4},{8,11},{9,10},{10,... | collective-permute-start | bytes 12296 | tf_op jit(solution)/shard_map/ppermute | solution.py:24
  47.9 39.8 %collective-permute-start.11 = (f32[4,2,40,768]{3,2,1,0:T(8,128)S(1)}, f32[4,2,40,768]{3,2,1,0:T(8,128)}, u32[]{:S(2)}, u32[]{:S(2)}) collective-permute-start(f32[4,2,40,768]{3,2,1,0:T(8,128)S(1)} %add_bitcast_fusion.2), channel_id=1, source_target_pairs={{0,12},{1,13},{2,14},{3,15},{4,8},{5,9},{6,10},{7,11},{8,4},{9,5},... | collective-permute-start | bytes 2949128 | tf_op jit(solution)/shard_map/ppermute | solution.py:24
  78.0 21.7 %collective-permute-start.12 = (f32[4,2,40,1024]{3,2,1,0:T(8,128)S(1)}, f32[4,2,40,1024]{3,2,1,0:T(8,128)S(1)}, u32[]{:S(2)}, u32[]{:S(2)}) collective-permute-start(f32[4,2,40,1024]{3,2,1,0:T(8,128)S(1)} %get-tuple-element.115), channel_id=1, source_target_pairs={{0,48},{1,49},{2,50},{3,51},{4,52},{5,53},{6,54},{7,55},{8,56},{9,... | collective-permute-start | bytes 3932168 | tf_op jit(solution)/shard_map/ppermute | solution.py:24
  80.8 15.4 %collective-permute-start.10 = (f32[4,2,40,768]{3,2,1,0:T(8,128)S(1)}, f32[4,2,40,768]{3,2,1,0:T(8,128)S(1)}, u32[]{:S(2)}, u32[]{:S(2)}) collective-permute-start(f32[4,2,40,768]{3,2,1,0:T(8,128)S(1)} %add_bitcast_fusion.3), channel_id=1, source_target_pairs={{0,3},{1,2},{2,1},{3,0},{4,7},{5,6},{6,5},{7,4},{8,11},{9,10},{10,... | collective-permute-start | bytes 2949128 | tf_op jit(solution)/shard_map/ppermute | solution.py:24
  83.6 27.4 %collective-permute-start.9 = (f32[4,2,40,1024]{3,2,1,0:T(8,128)S(1)}, f32[4,2,40,1024]{3,2,1,0:T(8,128)S(1)}, u32[]{:S(2)}, u32[]{:S(2)}) collective-permute-start(f32[4,2,40,1024]{3,2,1,0:T(8,128)S(1)} %get-tuple-element.116), channel_id=1, source_target_pairs={{0,48},{1,49},{2,50},{3,51},{4,52},{5,53},{6,54},{7,55},{8,56},{9,... | collective-permute-start | bytes 3932168 | tf_op jit(solution)/shard_map/ppermute | solution.py:24
  84.4 20.7 %collective-permute-start.8 = (f32[4,2,40,768]{3,2,1,0:T(8,128)S(1)}, f32[4,2,40,768]{3,2,1,0:T(8,128)S(1)}, u32[]{:S(2)}, u32[]{:S(2)}) collective-permute-start(f32[4,2,40,768]{3,2,1,0:T(8,128)S(1)} %add_bitcast_fusion.4), channel_id=1, source_target_pairs={{0,12},{1,13},{2,14},{3,15},{4,8},{5,9},{6,10},{7,11},{8,4},{9,5},... | collective-permute-start | bytes 2949128 | tf_op jit(solution)/shard_map/ppermute | solution.py:24
  87.7 22.3 %collective-permute-start.7 = (f32[4,2,40,768]{3,2,1,0:T(8,128)S(1)}, f32[4,2,40,768]{3,2,1,0:T(8,128)S(1)}, u32[]{:S(2)}, u32[]{:S(2)}) collective-permute-start(f32[4,2,40,768]{3,2,1,0:T(8,128)S(1)} %add_bitcast_fusion.5), channel_id=1, source_target_pairs={{0,3},{1,2},{2,1},{3,0},{4,7},{5,6},{6,5},{7,4},{8,11},{9,10},{10,... | collective-permute-start | bytes 2949128 | tf_op jit(solution)/shard_map/ppermute | solution.py:24
  99.8 11.2 %collective-permute-start.14 = (f32[8,128]{1,0:T(8,128)S(1)}, f32[8,128]{1,0:T(8,128)S(1)}, u32[]{:S(2)}, u32[]{:S(2)}) collective-permute-start(f32[8,128]{1,0:T(8,128)S(1)} %add.259), channel_id=1, source_target_pairs={{0,12},{1,13},{2,14},{3,15},{4,8},{5,9},{6,10},{7,11},{8,4},{9,5},... | collective-permute-start | bytes 12296 | tf_op jit(solution)/shard_map/ppermute | solution.py:24
  104.5 15.6 %collective-permute-start.19 = (f32[2,2,40,768]{3,2,1,0:T(8,128)S(1)}, f32[2,2,40,768]{3,2,1,0:T(8,128)S(1)}, u32[]{:S(2)}, u32[]{:S(2)}) collective-permute-start(f32[2,2,40,768]{3,2,1,0:T(8,128)S(1)} %slice.303), channel_id=1, source_target_pairs={{0,1},{1,0},{2,3},{3,2},{4,5},{5,4},{6,7},{7,6},{8,9},{9,8},{10,11... | collective-permute-start | bytes 1474568 | tf_op jit(solution)/shard_map/ppermute | solution.py:24
  111.9 15.9 %collective-permute-start.20 = (f32[2,2,40,1024]{3,2,1,0:T(8,128)S(1)}, f32[2,2,40,1024]{3,2,1,0:T(8,128)S(1)}, u32[]{:S(2)}, u32[]{:S(2)}) collective-permute-start(f32[2,2,40,1024]{3,2,1,0:T(8,128)S(1)} %slice.304), channel_id=1, source_target_pairs={{0,4},{1,5},{2,6},{3,7},{4,0},{5,1},{6,2},{7,3},{8,12},{9,13},{10,... | collective-permute-start | bytes 1966088 | tf_op jit(solution)/shard_map/ppermute | solution.py:24
  113.9 14.0 %collective-permute-start.18 = (f32[2,2,40,768]{3,2,1,0:T(8,128)S(1)}, f32[2,2,40,768]{3,2,1,0:T(8,128)S(1)}, u32[]{:S(2)}, u32[]{:S(2)}) collective-permute-start(f32[2,2,40,768]{3,2,1,0:T(8,128)S(1)} %slice.302), channel_id=1, source_target_pairs={{0,4},{1,5},{2,6},{3,7},{4,0},{5,1},{6,2},{7,3},{8,12},{9,13},{10,... | collective-permute-start | bytes 1474568 | tf_op jit(solution)/shard_map/ppermute | solution.py:24
  115.4 30.5 %collective-permute-start.17 = (f32[2,2,40,1024]{3,2,1,0:T(8,128)S(1)}, f32[2,2,40,1024]{3,2,1,0:T(8,128)S(1)}, u32[]{:S(2)}, u32[]{:S(2)}) collective-permute-start(f32[2,2,40,1024]{3,2,1,0:T(8,128)S(1)} %slice.301), channel_id=1, source_target_pairs={{0,4},{1,5},{2,6},{3,7},{4,0},{5,1},{6,2},{7,3},{8,12},{9,13},{10,... | collective-permute-start | bytes 1966088 | tf_op jit(solution)/shard_map/ppermute | solution.py:24
  118.6 15.0 %collective-permute-start.16 = (f32[2,2,40,768]{3,2,1,0:T(8,128)S(1)}, f32[2,2,40,768]{3,2,1,0:T(8,128)S(1)}, u32[]{:S(2)}, u32[]{:S(2)}) collective-permute-start(f32[2,2,40,768]{3,2,1,0:T(8,128)S(1)} %slice.300), channel_id=1, source_target_pairs={{0,1},{1,0},{2,3},{3,2},{4,5},{5,4},{6,7},{7,6},{8,9},{9,8},{10,11... | collective-permute-start | bytes 1474568 | tf_op jit(solution)/shard_map/ppermute | solution.py:24
  120.1 23.1 %collective-permute-start.15 = (f32[2,2,40,768]{3,2,1,0:T(8,128)S(1)}, f32[2,2,40,768]{3,2,1,0:T(8,128)S(1)}, u32[]{:S(2)}, u32[]{:S(2)}) collective-permute-start(f32[2,2,40,768]{3,2,1,0:T(8,128)S(1)} %slice.299), channel_id=1, source_target_pairs={{0,4},{1,5},{2,6},{3,7},{4,0},{5,1},{6,2},{7,3},{8,12},{9,13},{10,... | collective-permute-start | bytes 1474568 | tf_op jit(solution)/shard_map/ppermute | solution.py:24
  127.9 18.0 %collective-permute-start.22 = (f32[8,128]{1,0:T(8,128)S(1)}, f32[8,128]{1,0:T(8,128)S(1)}, u32[]{:S(2)}, u32[]{:S(2)}) collective-permute-start(f32[8,128]{1,0:T(8,128)S(1)} %add.277), channel_id=1, source_target_pairs={{0,48},{1,49},{2,50},{3,51},{4,52},{5,53},{6,54},{7,55},{8,56},{9,... | collective-permute-start | bytes 12296 | tf_op jit(solution)/shard_map/ppermute | solution.py:24
  130.4 22.4 %collective-permute-start.28 = (f32[2,40,1024]{2,1,0:T(8,128)S(1)}, f32[2,40,1024]{2,1,0:T(8,128)S(1)}, u32[]{:S(2)}, u32[]{:S(2)}) collective-permute-start(f32[2,40,1024]{2,1,0:T(8,128)S(1)} %fusion.4), channel_id=1, source_target_pairs={{0,12},{1,13},{2,14},{3,15},{4,8},{5,9},{6,10},{7,11},{8,4},{9,5},... | collective-permute-start | bytes 983048 | tf_op jit(solution)/shard_map/ppermute | solution.py:24
  133.6 15.8 %collective-permute-start.27 = (f32[2,40,768]{2,1,0:T(8,128)S(1)}, f32[2,40,768]{2,1,0:T(8,128)S(1)}, u32[]{:S(2)}, u32[]{:S(2)}) collective-permute-start(f32[2,40,768]{2,1,0:T(8,128)S(1)} %fusion.10), channel_id=1, source_target_pairs={{0,3},{1,2},{2,1},{3,0},{4,7},{5,6},{6,5},{7,4},{8,11},{9,10},{10,... | collective-permute-start | bytes 737288 | tf_op jit(solution)/shard_map/ppermute | solution.py:24
  143.2 9.7 %collective-permute-start.26 = (f32[2,40,768]{2,1,0:T(8,128)S(1)}, f32[2,40,768]{2,1,0:T(8,128)S(1)}, u32[]{:S(2)}, u32[]{:S(2)}) collective-permute-start(f32[2,40,768]{2,1,0:T(8,128)S(1)} %fusion.11), channel_id=1, source_target_pairs={{0,12},{1,13},{2,14},{3,15},{4,8},{5,9},{6,10},{7,11},{8,4},{9,5},... | collective-permute-start | bytes 737288 | tf_op jit(solution)/shard_map/ppermute | solution.py:24
  146.0 13.1 %collective-permute-start.25 = (f32[2,40,1024]{2,1,0:T(8,128)S(1)}, f32[2,40,1024]{2,1,0:T(8,128)S(1)}, u32[]{:S(2)}, u32[]{:S(2)}) collective-permute-start(f32[2,40,1024]{2,1,0:T(8,128)S(1)} %fusion.5), channel_id=1, source_target_pairs={{0,12},{1,13},{2,14},{3,15},{4,8},{5,9},{6,10},{7,11},{8,4},{9,5},... | collective-permute-start | bytes 983048 | tf_op jit(solution)/shard_map/ppermute | solution.py:24
  146.6 8.3 %collective-permute-start.24 = (f32[2,40,768]{2,1,0:T(8,128)S(1)}, f32[2,40,768]{2,1,0:T(8,128)S(1)}, u32[]{:S(2)}, u32[]{:S(2)}) collective-permute-start(f32[2,40,768]{2,1,0:T(8,128)S(1)} %fusion.14), channel_id=1, source_target_pairs={{0,3},{1,2},{2,1},{3,0},{4,7},{5,6},{6,5},{7,4},{8,11},{9,10},{10,... | collective-permute-start | bytes 737288 | tf_op jit(solution)/shard_map/ppermute | solution.py:24
  149.5 9.6 %collective-permute-start.23 = (f32[2,40,768]{2,1,0:T(8,128)S(1)}, f32[2,40,768]{2,1,0:T(8,128)S(1)}, u32[]{:S(2)}, u32[]{:S(2)}) collective-permute-start(f32[2,40,768]{2,1,0:T(8,128)S(1)} %fusion.15), channel_id=1, source_target_pairs={{0,12},{1,13},{2,14},{3,15},{4,8},{5,9},{6,10},{7,11},{8,4},{9,5},... | collective-permute-start | bytes 737288 | tf_op jit(solution)/shard_map/ppermute | solution.py:24
  153.0 12.7 %collective-permute-start.31 = (f32[2,40,1024]{2,1,0:T(8,128)S(1)}, f32[2,40,1024]{2,1,0:T(8,128)S(1)}, u32[]{:S(2)}, u32[]{:S(2)}) collective-permute-start(f32[2,40,1024]{2,1,0:T(8,128)S(1)} %fusion.3), channel_id=1, source_target_pairs={{0,1},{1,0},{2,3},{3,2},{4,5},{5,4},{6,7},{7,6},{8,9},{9,8},{10,11... | collective-permute-start | bytes 983048 | tf_op jit(solution)/shard_map/ppermute | solution.py:24
  154.6 8.4 %collective-permute-start.30 = (f32[2,40,768]{2,1,0:T(8,128)S(1)}, f32[2,40,768]{2,1,0:T(8,128)S(1)}, u32[]{:S(2)}, u32[]{:S(2)}) collective-permute-start(f32[2,40,768]{2,1,0:T(8,128)S(1)} %fusion.9), channel_id=1, source_target_pairs={{0,16},{1,17},{2,18},{3,19},{4,20},{5,21},{6,22},{7,23},{8,24},{9,... | collective-permute-start | bytes 737288 | tf_op jit(solution)/shard_map/ppermute | solution.py:24
  154.9 10.8 %collective-permute-start.29 = (f32[2,40,768]{2,1,0:T(8,128)S(1)}, f32[2,40,768]{2,1,0:T(8,128)S(1)}, u32[]{:S(2)}, u32[]{:S(2)}) collective-permute-start(f32[2,40,768]{2,1,0:T(8,128)S(1)} %fusion.13), channel_id=1, source_target_pairs={{0,16},{1,17},{2,18},{3,19},{4,20},{5,21},{6,22},{7,23},{8,24},{9,... | collective-permute-start | bytes 737288 | tf_op jit(solution)/shard_map/ppermute | solution.py:24
  165.7 9.8 %collective-permute-start.34 = (f32[40,1024]{1,0:T(8,128)S(1)}, f32[40,1024]{1,0:T(8,128)S(1)}, u32[]{:S(2)}, u32[]{:S(2)}) collective-permute-start(f32[40,1024]{1,0:T(8,128)S(1)} %fusion.21), channel_id=1, source_target_pairs={{0,3},{1,2},{2,1},{3,0},{4,7},{5,6},{6,5},{7,4},{8,11},{9,10},{10,... | collective-permute-start | bytes 491528 | tf_op jit(solution)/shard_map/ppermute | solution.py:24
  167.8 6.2 %collective-permute-start.33 = (f32[40,768]{1,0:T(8,128)S(1)}, f32[40,768]{1,0:T(8,128)S(1)}, u32[]{:S(2)}, u32[]{:S(2)}) collective-permute-start(f32[40,768]{1,0:T(8,128)S(1)} %fusion.25), channel_id=1, source_target_pairs={{0,48},{1,49},{2,50},{3,51},{4,52},{5,53},{6,54},{7,55},{8,56},{9,... | collective-permute-start | bytes 368648 | tf_op jit(solution)/shard_map/ppermute | solution.py:24
  (6 other events, 24.1 us)

commit v3 on v2

v3 whole, which is shorter than its diff:
```python
import functools

import jax
import jax.numpy as jnp
from jax import lax
from jax.experimental import pallas as pl
from jax.experimental.pallas import tpu as pltpu
from jax.sharding import PartitionSpec as P

SLOTS, TOKENS, ROWS = 6, 192, 40
K = SLOTS * TOKENS
TILE = 16 * ROWS
STRIDE = {"x": 1, "y": 4, "z": 16}
COLUMNS = {"A": (0, 896), "B": (896, 896), "C": (1792, 768)}


def exchange(value, axis, turn):
    pairs = []
    for section in range(2):
        flip, stride = 1 if section == turn else 3, STRIDE[axis]
        for d in range(64):
            p = d // stride % 4
            pairs.append((section * 64 + d, section * 64 + d + ((p ^ flip) - p) * stride))
    return lax.ppermute(value, ("section", "dp"), pairs)


def products(half, groups, failed, counts, order, act, cot, *refs):
    outs, (acts, cots, total, sems) = list(refs[:-4]), refs[-4:]
    section, me = lax.axis_index("section"), lax.axis_index("dp")
    flips = (0, 3 - 2 * section, 1 + 2 * section, 2)
    xs, ys, zs = ([place ^ flip for flip in flips] for place in (me % 4, me // 4 % 4, me // 16))
    first = COLUMNS[groups[0]][0]
    fetch = [
        pltpu.make_async_copy(
            act.at[0, :, :, pl.ds(pl.multiple_of(zs[half + g] * TILE, 128), TILE)], acts.at[g], sems.at[g])
        for g in range(2)
    ]
    load = {}
    for n, group in enumerate(groups):
        column, columns = COLUMNS[group]
        load[group] = pltpu.make_async_copy(
            cot.at[0, :, :, pl.ds(column, columns)], cots.at[:, :, pl.ds(column - first, columns)], sems.at[2 + n])
    fetch[0].start()
    for copy in load.values():
        copy.start()
    fetch[1].start()
    alive = jnp.where(me == failed[0], 0, counts[0])
    live = [jnp.float32(0)] * SLOTS
    for position in range(SLOTS):
        for k in range(SLOTS):
            live[k] = jnp.where((order[0, position] == k) & (position < alive), jnp.float32(1), live[k])
    targets = {group: [outs.pop(0), outs.pop(0)] if group in "AB" else [outs.pop(0)] for group in groups}
    if half == 2 and "C" in groups:
        alive_rows = jnp.full((8, COLUMNS["C"][1]), alive.astype(jnp.float32))
        targets["C"][0][2 * TILE:, :] = alive_rows
        outs.pop(0)[...] = alive_rows
    for g in range(2):
        fetch[g].wait()
        rows = acts[g].reshape(K, TILE)
        for group in groups:
            column, columns = COLUMNS[group]
            span = slice(column - first, column - first + columns)
            if g == 0:
                load[group].wait()
                for k in range(SLOTS):
                    cots[k, :, span] = cots[k, :, span] * live[k].astype(jnp.bfloat16)
            total[:, :columns] = lax.dot_general(
                rows, cots[:, :, span].reshape(K, columns), (((0,), (0,)), ((), ())),
                preferred_element_type=jnp.float32)
            for i in range(4):
                for j in range(4):
                    start = ys[i] * 160 + xs[j] * ROWS if group == "B" else xs[i] * ROWS + ys[j] * 160
                    block = total[pl.ds(pl.multiple_of(start, 8), ROWS), :columns]
                    if group == "A":
                        targets["A"][i // 2][i % 2, j, g] = block
                    elif group == "B":
                        targets["B"][i // 2][i % 2, g, j] = block
                    else:
                        targets["C"][0][pl.ds(((g * 4 + i) * 4 + j) * ROWS, ROWS), :] = block


def partials(half, groups, activations, cotangents, failed, counts, order):
    f32 = lambda *shape: jax.ShapeDtypeStruct(shape, jnp.float32)
    shapes = []
    for group in groups:
        columns = COLUMNS[group][1]
        if group == "A":
            shapes += [f32(2, 4, 2, ROWS, columns)] * 2
        elif group == "B":
            shapes += [f32(2, 2, 4, ROWS, columns)] * 2
        elif half == 2:
            shapes += [f32(2 * TILE + 8, columns), f32(8, columns)]
        else:
            shapes += [f32(2 * TILE, columns)]
    return pl.pallas_call(
        functools.partial(products, half, groups),
        out_shape=shapes,
        in_specs=[pl.BlockSpec(memory_space=pltpu.SMEM)] * 3 + [pl.BlockSpec(memory_space=pltpu.HBM)] * 2,
        out_specs=[pl.BlockSpec(memory_space=pltpu.VMEM)] * len(shapes),
        scratch_shapes=[
            pltpu.VMEM((2, SLOTS, TOKENS, TILE), jnp.bfloat16),
            pltpu.VMEM((SLOTS, TOKENS, sum(COLUMNS[group][1] for group in groups)), jnp.bfloat16),
            pltpu.VMEM((TILE, max(COLUMNS[group][1] for group in groups)), jnp.float32),
            pltpu.SemaphoreType.DMA((5,)),
        ],
        compiler_params=pltpu.CompilerParams(vmem_limit_bytes=27 << 20),
        cost_estimate=pl.CostEstimate(flops=1024, bytes_accessed=1024, transcendentals=0),
    )(failed, counts, order, *(pltpu.with_memory_space_constraint(x, pltpu.HBM) for x in (activations, cotangents)))


def together(values):
    return list(lax.optimization_barrier(tuple(values)))


def shards(activations, cotangents, failed, counts, order):
    run = functools.partial(partials, failed=failed, counts=counts, order=order)
    *one, activations, cotangents = together([*run(2, "ABC", activations, cotangents), activations, cotangents])
    a_keep_far, a_send_far, b_keep_far, b_send_far, c_send, c_total = one
    a_keep_near, a_send_near, b_keep_near, b_send_near, c_keep = run(0, "ABC", activations, cotangents)

    def both(keep, got, total, rows):
        total = total + got[2 * rows:]
        return jnp.concatenate([keep[rows:] + got[rows:2 * rows], total], axis=0), keep[:rows] + got[:rows], total

    a_got_far, b_got_far = together([exchange(a_send_far, "x", 0), exchange(b_send_far, "y", 0)])
    a_got_near, b_got_near, c_got = together(
        [exchange(a_send_near, "x", 0), exchange(b_send_near, "y", 0), exchange(c_send, "z", 0)])
    a_late_far, b_late_far = together(
        [exchange(a_keep_far[1] + a_got_far[1], "x", 1), exchange(b_keep_far[1] + b_got_far[1], "y", 1)])
    c_out, c_stay, c_total = both(c_keep, c_got, c_total, TILE)
    a_late_near, b_late_near, c_late = together([
        exchange(a_keep_near[1] + a_got_near[1], "x", 1), exchange(b_keep_near[1] + b_got_near[1], "y", 1),
        exchange(c_out, "z", 1)])
    c_whole, c_total = c_stay + c_late[:TILE], c_total + c_late[TILE:]

    a_far = (a_keep_far[0] + a_got_far[0]) + a_late_far
    b_far = (b_keep_far[0] + b_got_far[0]) + b_late_far
    a_near = (a_keep_near[0] + a_got_near[0]) + a_late_near
    b_near = (b_keep_near[0] + b_got_near[0]) + b_late_near
    a_got_far, b_got = together([exchange(a_far[2:4], "y", 0), exchange(b_far, "z", 0)])
    a_got_near, c_got = together([
        exchange(a_near[2:4], "y", 0), exchange(jnp.concatenate([c_whole[320:], c_total], axis=0), "x", 0)])
    a_late = exchange(jnp.concatenate([a_far[1] + a_got_far[1], a_near[1] + a_got_near[1]], axis=0), "y", 1)
    b_late = exchange(b_near[1] + b_got[1], "z", 1)
    c_out, c_stay, c_total = both(c_whole[:320], c_got, c_total, 160)
    c_late = exchange(c_out, "x", 1)
    a_late, b_late, c_late = together([a_late, b_late, c_late])
    c_whole, c_total = c_stay + c_late[:160], c_total + c_late[160:]
    a_far, a_near = (a_far[0] + a_got_far[0]) + a_late[:2], (a_near[0] + a_got_near[0]) + a_late[2:]
    b_whole = (b_near[0] + b_got[0]) + b_late

    a_got, b_got = exchange(a_far, "z", 0), exchange(b_whole[2:4], "x", 0)
    c_got = exchange(jnp.concatenate([c_whole[80:], c_total], axis=0), "y", 0)
    a_got, b_got, c_got = together([a_got, b_got, c_got])
    a_late = exchange(a_near[1] + a_got[1], "z", 1)
    b_late = exchange(b_whole[1] + b_got[1], "x", 1)
    c_out, c_stay, c_total = both(c_whole[:80], c_got, c_total, 40)
    c_late = exchange(c_out, "y", 1)
    a_late, b_late, c_late = together([a_late, b_late, c_late])
    a = (a_near[0] + a_got[0]) + a_late
    b = (b_whole[0] + b_got[0]) + b_late
    c = c_stay + c_late[:40]
    total = (c_total + c_late[40:])[0, 0]
    return jnp.concatenate([a / total, b / total, c / total], axis=1)


def solution(mesh):
    in_specs = (
        P(("section", "dp"), None, None, None),
        P(("section", "dp"), None, None, None),
        P(),
        P("dp"),
        P("dp", None),
    )
    out_specs = P(("section", "dp"), None)
    return jax.shard_map(shards, mesh=mesh, in_specs=in_specs, out_specs=out_specs, check_vma=False)
```

time: 178 us -> 174 us (0.978)
  starting transfers between devices: 62.3 us -> 36.5 us
  waiting for transfers between devices: 77.3 us -> 98.2 us
  other arithmetic: 8.27 us -> 3.89 us
  Pallas kernels: 26.8 us -> 29.7 us
    ppermute x35 -> x23, starting transfers between devices: 62.3 us -> 36.5 us  [exchange(): return lax.ppermute(value, ('section', 'dp'), pairs)]
    ppermute x35 -> x23, waiting for transfers between devices: 77.3 us -> 98.2 us  [exchange(): return lax.ppermute(value, ('section', 'dp'), pairs)]
    add x31 -> x25, other arithmetic: 6.11 us -> 2.72 us  [the longest x2 0.49 us: shards(): c_whole, c_total = (c_stay + c_late[:TILE], c_total + c_late[TILE:])]
    pallas_call x2, Pallas kernels: 26.8 us -> 29.7 us  [partials(): pl.pallas_call(functools.partial(products, half, groups), out_shape=shape...]
  transfers between devices with their start and end apart: 35 -> 23, of which waited for: 16 -> 15; matrix products, arithmetic and copies ran while one was open for 4% -> 1% of each run, Pallas kernels for 8% -> 9%
where the time goes in v3:
time: 174 us; the launch traced here: 173 us
  waiting for transfers between devices  98.2 us (56%)
  starting transfers between devices  36.5 us (21%)
  Pallas kernels  29.7 us (17%)
  other arithmetic  3.89 us (2%)
  between operations  2.89 us (2%)
  local copies, waits for them, and re-layouts  1.94 us (1%)
    ppermute x23, waiting for transfers between devices, exchange(): return lax.ppermute(value, ('section', 'dp'), pairs)  98.2 us
    ppermute x23, starting transfers between devices, exchange(): return lax.ppermute(value, ('section', 'dp'), pairs)  36.5 us
    pallas_call x2, Pallas kernels, partials(): pl.pallas_call(functools.partial(products, half, groups), out_shape=shape...  29.7 us
  transfers between devices with their start and end apart: 23, of which 15 were waited for; matrix products, arithmetic and copies ran while one was open for 1% of the time, Pallas kernels for 9%

profile of v3, /device:TPU:0, one launch (start us, length us, event | category | flops | bytes accessed | tf_op | source)
XLA Modules:
  0.0 173.1 jit_solution(4937127422939656788)
XLA Ops:
  1.3 0.6 copy-done
  2.0 14.9 %shard_map.55 = (f32[2,4,2,40,896]{4,3,2,1,0:T(8,128)S(1)}, f32[2,4,2,40,896]{4,3,2,1,0:T(8,128)S(1)}, f32[2,2,4,40,896]{4,3,2,1,0:T(8,128)S(1)}, f32[2,2,4,40,8...) custom-call(s32[1]{0:T(128)S(6)} %copy.6.failed, s32[1]{0:T(128)S(6)} %copy.7.counts, ...), custom_call_target="tpu_custom_call" | custom-call | flops 1024 | bytes 1024 | tf_op jit(solution)/shard_map/pallas_call | solution.py:95
  16.8 1.7 collective-permute-start.8
  18.5 1.6 collective-permute-start.9
  20.1 1.9 %collective-permute-start.2 = (f32[1288,768]{1,0:T(8,128)S(1)}, f32[1288,768]{1,0:T(8,128)S(1)}, u32[]{:S(2)}, u32[]{:S(2)}) collective-permute-start(f32[1288,768]{1,0:T(8,128)S(1)} %get-tuple-element.58), channel_id=1, source_target_pairs={{0,16},{1,17},{2,18},{3,19},{4,20},{5,21},{6,22},{7,23},{8,24},{9,... | collective-permute-start | bytes 11870216 | tf_op jit(solution)/shard_map/ppermute | solution.py:24
  22.0 14.9 %shard_map.56 = (f32[2,4,2,40,896]{4,3,2,1,0:T(8,128)S(1)}, f32[2,4,2,40,896]{4,3,2,1,0:T(8,128)S(1)}, f32[2,2,4,40,896]{4,3,2,1,0:T(8,128)S(1)}, f32[2,2,4,40,896]{4,3,2,1,0:T(8,128)S(1)}, f32[1280,768]{1,0:T(8,128)S(1)}) custom-call(s32[1]{0:T(128)S(6)} %copy.6.failed, s32[1]{0:T(128)S(6)} %copy.7.counts, s32[1,6]{1,0:T(1,128)S(1)} %copy-done.1, ...), custom_call_target="tpu_custom_call" | custom-call | flops 1024 | bytes 1024 | tf_op jit(solution)/shard_map/pallas_call | solution.py:95
  37.9 7.1 %collective-permute-done.8 = f32[2,4,2,40,896]{4,3,2,1,0:T(8,128)S(1)} collective-permute-done((f32[2,4,2,40,896]{4,3,2,1,0:T(8,128)S(1)}, f32[2,4,2,40,896]{4,3,2,1,0:T(8,128)S(1)}, u32[]{:S(2)}, u32[]{:S(2)}) %collective-permute-start.8) | collective-permute-done | bytes 2293792 | tf_op jit(solution)/shard_map/ppermute | solution.py:24
  45.1 1.6 collective-permute-done.9
  46.8 3.1 %collective-permute-start.11 = (f32[2,4,40,896]{3,2,1,0:T(8,128)S(1)}, f32[2,4,40,896]{3,2,1,0:T(8,128)S(1)}, u32[]{:S(2)}, u32[]{:S(2)}) collective-permute-start(f32[2,4,40,896]{3,2,1,0:T(8,128)S(1)} %add_bitcast_fusion), channel_id=1, source_target_pairs={{0,12},{1,13},{2,14},{3,15},{4,8},{5,9},{6,10},{7,11},{8,4},{9,5},... | collective-permute-start | bytes 3440648 | tf_op jit(solution)/shard_map/ppermute | solution.py:24
  50.0 2.2 %collective-permute-start.10 = (f32[4,2,40,896]{3,2,1,0:T(8,128)S(1)}, f32[4,2,40,896]{3,2,1,0:T(8,128)S(1)}, u32[]{:S(2)}, u32[]{:S(2)}) collective-permute-start(f32[4,2,40,896]{3,2,1,0:T(8,128)S(1)} %add_bitcast_fusion.1), channel_id=1, source_target_pairs={{0,3},{1,2},{2,1},{3,0},{4,7},{5,6},{6,5},{7,4},{8,11},{9,10},{10,... | collective-permute-start | bytes 3440648 | tf_op jit(solution)/shard_map/ppermute | solution.py:24
  52.1 24.1 %collective-permute-done.11 = f32[2,4,40,896]{3,2,1,0:T(8,128)S(1)} collective-permute-done((f32[2,4,40,896]{3,2,1,0:T(8,128)S(1)}, f32[2,4,40,896]{3,2,1,0:T(8,128)S(1)}, u32[]{:S(2)}, u32[]{:S(2)}) %collective-permute-start.11) | collective-permute-done | bytes 1146912 | tf_op jit(solution)/shard_map/ppermute | solution.py:24
  76.2 3.2 %collective-permute-done.10 = f32[4,2,40,896]{3,2,1,0:T(8,128)S(1)} collective-permute-done((f32[4,2,40,896]{3,2,1,0:T(8,128)S(1)}, f32[4,2,40,896]{3,2,1,0:T(8,128)S(1)}, u32[]{:S(2)}, u32[]{:S(2)}) %collective-permute-start.10) | collective-permute-done | bytes 1146912 | tf_op jit(solution)/shard_map/ppermute | solution.py:24
  79.5 2.5 %collective-permute-done = f32[2,4,2,40,896]{4,3,2,1,0:T(8,128)S(1)} collective-permute-done((f32[2,4,2,40,896]{4,3,2,1,0:T(8,128)S(1)}, f32[2,4,2,40,896]{4,3,2,1,0:T(8,128)S(1)}, u32[]{:S(2)}, u32[]{:S(2)}) %collective-permute-start) | collective-permute-done | bytes 2293792 | tf_op jit(solution)/shard_map/ppermute | solution.py:24
  81.9 1.6 collective-permute-done.1
  84.0 4.1 %collective-permute-start.5 = (f32[648,768]{1,0:T(8,128)S(1)}, f32[648,768]{1,0:T(8,128)S(1)}, u32[]{:S(2)}, u32[]{:S(2)}) collective-permute-start(f32[648,768]{1,0:T(8,128)S(1)} %pad_maximum_fusion), channel_id=1, source_target_pairs={{0,48},{1,49},{2,50},{3,51},{4,52},{5,53},{6,54},{7,55},{8,56},{9,... | collective-permute-start | bytes 5971976 | tf_op jit(solution)/shard_map/ppermute | solution.py:24
  88.6 3.1 %collective-permute-start.4 = (f32[2,4,40,896]{3,2,1,0:T(8,128)S(1)}, f32[2,4,40,896]{3,2,1,0:T(8,128)S(1)}, u32[]{:S(2)}, u32[]{:S(2)}) collective-permute-start(f32[2,4,40,896]{3,2,1,0:T(8,128)S(1)} %add_bitcast_fusion.2), channel_id=1, source_target_pairs={{0,12},{1,13},{2,14},{3,15},{4,8},{5,9},{6,10},{7,11},{8,4},{9,5},... | collective-permute-start | bytes 3440648 | tf_op jit(solution)/shard_map/ppermute | solution.py:24
  91.8 2.4 %collective-permute-start.3 = (f32[4,2,40,896]{3,2,1,0:T(8,128)S(1)}, f32[4,2,40,896]{3,2,1,0:T(8,128)S(1)}, u32[]{:S(2)}, u32[]{:S(2)}) collective-permute-start(f32[4,2,40,896]{3,2,1,0:T(8,128)S(1)} %add_bitcast_fusion.3), channel_id=1, source_target_pairs={{0,3},{1,2},{2,1},{3,0},{4,7},{5,6},{6,5},{7,4},{8,11},{9,10},{10,... | collective-permute-start | bytes 3440648 | tf_op jit(solution)/shard_map/ppermute | solution.py:24
  94.7 15.8 %collective-permute-done.12 = f32[2,2,40,896]{3,2,1,0:T(8,128)S(1)} collective-permute-done((f32[2,2,40,896]{3,2,1,0:T(8,128)S(1)}, f32[2,2,40,896]{3,2,1,0:T(8,128)S(1)}, u32[]{:S(2)}, u32[]{:S(2)}) %collective-permute-start.12) | collective-permute-done | bytes 573472 | tf_op jit(solution)/shard_map/ppermute | solution.py:24
  110.5 6.2 %collective-permute-done.13 = f32[2,4,40,896]{3,2,1,0:T(8,128)S(1)} collective-permute-done((f32[2,4,40,896]{3,2,1,0:T(8,128)S(1)}, f32[2,4,40,896]{3,2,1,0:T(8,128)S(1)}, u32[]{:S(2)}, u32[]{:S(2)}) %collective-permute-start.13) | collective-permute-done | bytes 1146912 | tf_op jit(solution)/shard_map/ppermute | solution.py:24
  116.7 6.6 %collective-permute-done.5 = f32[648,768]{1,0:T(8,128)S(1)} collective-permute-done((f32[648,768]{1,0:T(8,128)S(1)}, f32[648,768]{1,0:T(8,128)S(1)}, u32[]{:S(2)}, u32[]{:S(2)}) %collective-permute-start.5) | collective-permute-done | bytes 1990688 | tf_op jit(solution)/shard_map/ppermute | solution.py:24
  124.8 1.5 collective-permute-start.6
  126.5 2.6 %collective-permute-start.15 = (f32[4,40,896]{2,1,0:T(8,128)S(1)}, f32[4,40,896]{2,1,0:T(8,128)S(1)}, u32[]{:S(2)}, u32[]{:S(2)}) collective-permute-start(f32[4,40,896]{2,1,0:T(8,128)S(1)} %fusion.2), channel_id=1, source_target_pairs={{0,48},{1,49},{2,50},{3,51},{4,52},{5,53},{6,54},{7,55},{8,56},{9,... | collective-permute-start | bytes 1720328 | tf_op jit(solution)/shard_map/ppermute | solution.py:24
  129.1 5.5 %collective-permute-done.6 = f32[2,2,40,896]{3,2,1,0:T(8,128)S(1)} collective-permute-done((f32[2,2,40,896]{3,2,1,0:T(8,128)S(1)}, f32[2,2,40,896]{3,2,1,0:T(8,128)S(1)}, u32[]{:S(2)}, u32[]{:S(2)}) %collective-permute-start.6) | collective-permute-done | bytes 573472 | tf_op jit(solution)/shard_map/ppermute | solution.py:24
  134.6 3.8 %collective-permute-done.7 = f32[328,768]{1,0:T(8,128)S(1)} collective-permute-done((f32[328,768]{1,0:T(8,128)S(1)}, f32[328,768]{1,0:T(8,128)S(1)}, u32[]{:S(2)}, u32[]{:S(2)}) %collective-permute-start.7) | collective-permute-done | bytes 1007648 | tf_op jit(solution)/shard_map/ppermute | solution.py:24
  138.5 3.1 %collective-permute-start.14 = (f32[4,40,896]{2,1,0:T(8,128)S(1)}, f32[4,40,896]{2,1,0:T(8,128)S(1)}, u32[]{:S(2)}, u32[]{:S(2)}) collective-permute-start(f32[4,40,896]{2,1,0:T(8,128)S(1)} %pad_maximum_fusion.2), channel_id=1, source_target_pairs={{0,12},{1,13},{2,14},{3,15},{4,8},{5,9},{6,10},{7,11},{8,4},{9,5},... | collective-permute-start | bytes 1720328 | tf_op jit(solution)/shard_map/ppermute | solution.py:24
  141.7 1.6 collective-permute-start.16
  143.3 10.4 %collective-permute-done.16 = f32[168,768]{1,0:T(8,128)S(1)} collective-permute-done((f32[168,768]{1,0:T(8,128)S(1)}, f32[168,768]{1,0:T(8,128)S(1)}, u32[]{:S(2)}, u32[]{:S(2)}) %collective-permute-start.16) | collective-permute-done | bytes 516128 | tf_op jit(solution)/shard_map/ppermute | solution.py:24
  154.4 6.9 %collective-permute-done.19 = f32[88,768]{1,0:T(8,128)S(1)} collective-permute-done((f32[88,768]{1,0:T(8,128)S(1)}, f32[88,768]{1,0:T(8,128)S(1)}, u32[]{:S(2)}, u32[]{:S(2)}) %collective-permute-start.19) | collective-permute-done | bytes 270368 | tf_op jit(solution)/shard_map/ppermute | solution.py:24
  161.4 2.4 %collective-permute-start.21 = (f32[40,896]{1,0:T(8,128)S(1)}, f32[40,896]{1,0:T(8,128)S(1)}, u32[]{:S(2)}, u32[]{:S(2)}) collective-permute-start(f32[40,896]{1,0:T(8,128)S(1)} %fusion.13), channel_id=1, source_target_pairs={{0,3},{1,2},{2,1},{3,0},{4,7},{5,6},{6,5},{7,4},{8,11},{9,10},{10,... | collective-permute-start | bytes 430088 | tf_op jit(solution)/shard_map/ppermute | solution.py:24
  163.9 3.0 %collective-permute-start.20 = (f32[40,896]{1,0:T(8,128)S(1)}, f32[40,896]{1,0:T(8,128)S(1)}, u32[]{:S(2)}, u32[]{:S(2)}) collective-permute-start(f32[40,896]{1,0:T(8,128)S(1)} %fusion.14), channel_id=1, source_target_pairs={{0,48},{1,49},{2,50},{3,51},{4,52},{5,53},{6,54},{7,55},{8,56},{9,... | collective-permute-start | bytes 430088 | tf_op jit(solution)/shard_map/ppermute | solution.py:24
  167.8 2.5 %collective-permute-done.20 = f32[40,896]{1,0:T(8,128)S(1)} collective-permute-done((f32[40,896]{1,0:T(8,128)S(1)}, f32[40,896]{1,0:T(8,128)S(1)}, u32[]{:S(2)}, u32[]{:S(2)}) %collective-permute-start.20) | collective-permute-done | bytes 143392 | tf_op jit(solution)/shard_map/ppermute | solution.py:24
  172.3 0.8 pad_maximum_fusion.4
  (61 shorter events, 7.1 us)
Async XLA Ops:
  1.3 0.7 copy-start
  2.0 20.0 %copy-start.1 = (s32[1,6]{1,0:T(1,128)S(1)}, s32[1,6]{1,0:T(1,128)}, u32[]{:S(2)}) copy-start(s32[1,6]{1,0:T(1,128)} %order.3) | copy-start | bytes 76
  16.8 28.2 %collective-permute-start.8 = (f32[2,4,2,40,896]{4,3,2,1,0:T(8,128)S(1)}, f32[2,4,2,40,896]{4,3,2,1,0:T(8,128)S(1)}, u32[]{:S(2)}, u32[]{:S(2)}) collective-permute-start(f32[2,4,2,40,896]{4,3,2,1,0:T(8,128)S(1)} %get-tuple-element.69), channel_id=1, source_target_pairs={{0,1},{1,0},{2,3},{3,2},{4,5},{5,4},{6,7},{7,6},{8,9},{9,8},{10,11... | collective-permute-start | bytes 6881288 | tf_op jit(solution)/shard_map/ppermute | solution.py:24
  18.5 28.1 %collective-permute-start.9 = (f32[2,2,4,40,896]{4,3,2,1,0:T(8,128)S(1)}, f32[2,2,4,40,896]{4,3,2,1,0:T(8,128)S(1)}, u32[]{:S(2)}, u32[]{:S(2)}) collective-permute-start(f32[2,2,4,40,896]{4,3,2,1,0:T(8,128)S(1)} %get-tuple-element.70), channel_id=1, source_target_pairs={{0,4},{1,5},{2,6},{3,7},{4,0},{5,1},{6,2},{7,3},{8,12},{9,13},{10,... | collective-permute-start | bytes 6881288 | tf_op jit(solution)/shard_map/ppermute | solution.py:24
  20.1 63.4 %collective-permute-start.2 = (f32[1288,768]{1,0:T(8,128)S(1)}, f32[1288,768]{1,0:T(8,128)S(1)}, u32[]{:S(2)}, u32[]{:S(2)}) collective-permute-start(f32[1288,768]{1,0:T(8,128)S(1)} %get-tuple-element.58), channel_id=1, source_target_pairs={{0,16},{1,17},{2,18},{3,19},{4,20},{5,21},{6,22},{7,23},{8,24},{9,... | collective-permute-start | bytes 11870216 | tf_op jit(solution)/shard_map/ppermute | solution.py:24
  36.9 45.1 %collective-permute-start = (f32[2,4,2,40,896]{4,3,2,1,0:T(8,128)S(1)}, f32[2,4,2,40,896]{4,3,2,1,0:T(8,128)S(1)}, u32[]{:S(2)}, u32[]{:S(2)}) collective-permute-start(f32[2,4,2,40,896]{4,3,2,1,0:T(8,128)S(1)} %get-tuple-element.56), channel_id=1, source_target_pairs={{0,1},{1,0},{2,3},{3,2},{4,5},{5,4},{6,7},{7,6},{8,9},{9,8},{10,11... | collective-permute-start | bytes 6881288 | tf_op jit(solution)/shard_map/ppermute | solution.py:24
  37.5 46.0 %collective-permute-start.1 = (f32[2,2,4,40,896]{4,3,2,1,0:T(8,128)S(1)}, f32[2,2,4,40,896]{4,3,2,1,0:T(8,128)S(1)}, u32[]{:S(2)}, u32[]{:S(2)}) collective-permute-start(f32[2,2,4,40,896]{4,3,2,1,0:T(8,128)S(1)} %get-tuple-element.57), channel_id=1, source_target_pairs={{0,4},{1,5},{2,6},{3,7},{4,0},{5,1},{6,2},{7,3},{8,12},{9,13},{10,... | collective-permute-start | bytes 6881288 | tf_op jit(solution)/shard_map/ppermute | solution.py:24
  46.8 29.5 %collective-permute-start.11 = (f32[2,4,40,896]{3,2,1,0:T(8,128)S(1)}, f32[2,4,40,896]{3,2,1,0:T(8,128)S(1)}, u32[]{:S(2)}, u32[]{:S(2)}) collective-permute-start(f32[2,4,40,896]{3,2,1,0:T(8,128)S(1)} %add_bitcast_fusion), channel_id=1, source_target_pairs={{0,12},{1,13},{2,14},{3,15},{4,8},{5,9},{6,10},{7,11},{8,4},{9,5},... | collective-permute-start | bytes 3440648 | tf_op jit(solution)/shard_map/ppermute | solution.py:24
  50.0 29.5 %collective-permute-start.10 = (f32[4,2,40,896]{3,2,1,0:T(8,128)S(1)}, f32[4,2,40,896]{3,2,1,0:T(8,128)S(1)}, u32[]{:S(2)}, u32[]{:S(2)}) collective-permute-start(f32[4,2,40,896]{3,2,1,0:T(8,128)S(1)} %add_bitcast_fusion.1), channel_id=1, source_target_pairs={{0,3},{1,2},{2,1},{3,0},{4,7},{5,6},{6,5},{7,4},{8,11},{9,10},{10,... | collective-permute-start | bytes 3440648 | tf_op jit(solution)/shard_map/ppermute | solution.py:24
  84.0 39.3 %collective-permute-start.5 = (f32[648,768]{1,0:T(8,128)S(1)}, f32[648,768]{1,0:T(8,128)S(1)}, u32[]{:S(2)}, u32[]{:S(2)}) collective-permute-start(f32[648,768]{1,0:T(8,128)S(1)} %pad_maximum_fusion), channel_id=1, source_target_pairs={{0,48},{1,49},{2,50},{3,51},{4,52},{5,53},{6,54},{7,55},{8,56},{9,... | collective-permute-start | bytes 5971976 | tf_op jit(solution)/shard_map/ppermute | solution.py:24
  88.4 28.3 %collective-permute-start.13 = (f32[2,4,40,896]{3,2,1,0:T(8,128)S(1)}, f32[2,4,40,896]{3,2,1,0:T(8,128)S(1)}, u32[]{:S(2)}, u32[]{:S(2)}) collective-permute-start(f32[2,4,40,896]{3,2,1,0:T(8,128)S(1)} %bitcast_add_fusion.1), channel_id=1, source_target_pairs={{0,16},{1,17},{2,18},{3,19},{4,20},{5,21},{6,22},{7,23},{8,24},{9,... | collective-permute-start | bytes 3440648 | tf_op jit(solution)/shard_map/ppermute | solution.py:24
  88.6 28.1 %collective-permute-start.4 = (f32[2,4,40,896]{3,2,1,0:T(8,128)S(1)}, f32[2,4,40,896]{3,2,1,0:T(8,128)S(1)}, u32[]{:S(2)}, u32[]{:S(2)}) collective-permute-start(f32[2,4,40,896]{3,2,1,0:T(8,128)S(1)} %add_bitcast_fusion.2), channel_id=1, source_target_pairs={{0,12},{1,13},{2,14},{3,15},{4,8},{5,9},{6,10},{7,11},{8,4},{9,5},... | collective-permute-start | bytes 3440648 | tf_op jit(solution)/shard_map/ppermute | solution.py:24
  91.8 24.9 %collective-permute-start.3 = (f32[4,2,40,896]{3,2,1,0:T(8,128)S(1)}, f32[4,2,40,896]{3,2,1,0:T(8,128)S(1)}, u32[]{:S(2)}, u32[]{:S(2)}) collective-permute-start(f32[4,2,40,896]{3,2,1,0:T(8,128)S(1)} %add_bitcast_fusion.3), channel_id=1, source_target_pairs={{0,3},{1,2},{2,1},{3,0},{4,7},{5,6},{6,5},{7,4},{8,11},{9,10},{10,... | collective-permute-start | bytes 3440648 | tf_op jit(solution)/shard_map/ppermute | solution.py:24
  94.5 16.0 %collective-permute-start.12 = (f32[2,2,40,896]{3,2,1,0:T(8,128)S(1)}, f32[2,2,40,896]{3,2,1,0:T(8,128)S(1)}, u32[]{:S(2)}, u32[]{:S(2)}) collective-permute-start(f32[2,2,40,896]{3,2,1,0:T(8,128)S(1)} %slice.270), channel_id=1, source_target_pairs={{0,4},{1,5},{2,6},{3,7},{4,0},{5,1},{6,2},{7,3},{8,12},{9,13},{10,... | collective-permute-start | bytes 1720328 | tf_op jit(solution)/shard_map/ppermute | solution.py:24
  124.0 14.4 %collective-permute-start.7 = (f32[328,768]{1,0:T(8,128)S(1)}, f32[328,768]{1,0:T(8,128)S(1)}, u32[]{:S(2)}, u32[]{:S(2)}) collective-permute-start(f32[328,768]{1,0:T(8,128)S(1)} %pad_maximum_fusion.1), channel_id=1, source_target_pairs={{0,1},{1,0},{2,3},{3,2},{4,5},{5,4},{6,7},{7,6},{8,9},{9,8},{10,11... | collective-permute-start | bytes 3022856 | tf_op jit(solution)/shard_map/ppermute | solution.py:24
  124.8 9.8 %collective-permute-start.6 = (f32[2,2,40,896]{3,2,1,0:T(8,128)S(1)}, f32[2,2,40,896]{3,2,1,0:T(8,128)S(1)}, u32[]{:S(2)}, u32[]{:S(2)}) collective-permute-start(f32[2,2,40,896]{3,2,1,0:T(8,128)S(1)} %slice.267), channel_id=1, source_target_pairs={{0,4},{1,5},{2,6},{3,7},{4,0},{5,1},{6,2},{7,3},{8,12},{9,13},{10,... | collective-permute-start | bytes 1720328 | tf_op jit(solution)/shard_map/ppermute | solution.py:24
  126.5 16.8 %collective-permute-start.15 = (f32[4,40,896]{2,1,0:T(8,128)S(1)}, f32[4,40,896]{2,1,0:T(8,128)S(1)}, u32[]{:S(2)}, u32[]{:S(2)}) collective-permute-start(f32[4,40,896]{2,1,0:T(8,128)S(1)} %fusion.2), channel_id=1, source_target_pairs={{0,48},{1,49},{2,50},{3,51},{4,52},{5,53},{6,54},{7,55},{8,56},{9,... | collective-permute-start | bytes 1720328 | tf_op jit(solution)/shard_map/ppermute | solution.py:24
  138.5 15.2 %collective-permute-start.14 = (f32[4,40,896]{2,1,0:T(8,128)S(1)}, f32[4,40,896]{2,1,0:T(8,128)S(1)}, u32[]{:S(2)}, u32[]{:S(2)}) collective-permute-start(f32[4,40,896]{2,1,0:T(8,128)S(1)} %pad_maximum_fusion.2), channel_id=1, source_target_pairs={{0,12},{1,13},{2,14},{3,15},{4,8},{5,9},{6,10},{7,11},{8,4},{9,5},... | collective-permute-start | bytes 1720328 | tf_op jit(solution)/shard_map/ppermute | solution.py:24
  141.7 12.0 %collective-permute-start.16 = (f32[168,768]{1,0:T(8,128)S(1)}, f32[168,768]{1,0:T(8,128)S(1)}, u32[]{:S(2)}, u32[]{:S(2)}) collective-permute-start(f32[168,768]{1,0:T(8,128)S(1)} %pad_maximum_fusion.3), channel_id=1, source_target_pairs={{0,3},{1,2},{2,1},{3,0},{4,7},{5,6},{6,5},{7,4},{8,11},{9,10},{10,... | collective-permute-start | bytes 1548296 | tf_op jit(solution)/shard_map/ppermute | solution.py:24
  154.1 7.2 %collective-permute-start.18 = (f32[2,40,896]{2,1,0:T(8,128)S(1)}, f32[2,40,896]{2,1,0:T(8,128)S(1)}, u32[]{:S(2)}, u32[]{:S(2)}) collective-permute-start(f32[2,40,896]{2,1,0:T(8,128)S(1)} %slice.277), channel_id=1, source_target_pairs={{0,1},{1,0},{2,3},{3,2},{4,5},{5,4},{6,7},{7,6},{8,9},{9,8},{10,11... | collective-permute-start | bytes 860168 | tf_op jit(solution)/shard_map/ppermute | solution.py:24
  154.2 7.1 %collective-permute-start.17 = (f32[2,40,896]{2,1,0:T(8,128)S(1)}, f32[2,40,896]{2,1,0:T(8,128)S(1)}, u32[]{:S(2)}, u32[]{:S(2)}) collective-permute-start(f32[2,40,896]{2,1,0:T(8,128)S(1)} %get-tuple-element.89), channel_id=1, source_target_pairs={{0,16},{1,17},{2,18},{3,19},{4,20},{5,21},{6,22},{7,23},{8,24},{9,... | collective-permute-start | bytes 860168 | tf_op jit(solution)/shard_map/ppermute | solution.py:24
  154.3 7.0 %collective-permute-start.19 = (f32[88,768]{1,0:T(8,128)S(1)}, f32[88,768]{1,0:T(8,128)S(1)}, u32[]{:S(2)}, u32[]{:S(2)}) collective-permute-start(f32[88,768]{1,0:T(8,128)S(1)} %pad_maximum_fusion.5), channel_id=1, source_target_pairs={{0,4},{1,5},{2,6},{3,7},{4,0},{5,1},{6,2},{7,3},{8,12},{9,13},{10,... | collective-permute-start | bytes 811016 | tf_op jit(solution)/shard_map/ppermute | solution.py:24
  161.4 6.4 %collective-permute-start.21 = (f32[40,896]{1,0:T(8,128)S(1)}, f32[40,896]{1,0:T(8,128)S(1)}, u32[]{:S(2)}, u32[]{:S(2)}) collective-permute-start(f32[40,896]{1,0:T(8,128)S(1)} %fusion.13), channel_id=1, source_target_pairs={{0,3},{1,2},{2,1},{3,0},{4,7},{5,6},{6,5},{7,4},{8,11},{9,10},{10,... | collective-permute-start | bytes 430088 | tf_op jit(solution)/shard_map/ppermute | solution.py:24
  163.8 6.5 %collective-permute-start.22 = (f32[48,768]{1,0:T(8,128)S(1)}, f32[48,768]{1,0:T(8,128)S(1)}, u32[]{:S(2)}, u32[]{:S(2)}) collective-permute-start(f32[48,768]{1,0:T(8,128)S(1)} %pad_maximum_fusion.6), channel_id=1, source_target_pairs={{0,12},{1,13},{2,14},{3,15},{4,8},{5,9},{6,10},{7,11},{8,4},{9,5},... | collective-permute-start | bytes 442376 | tf_op jit(solution)/shard_map/ppermute | solution.py:24
  163.9 6.4 %collective-permute-start.20 = (f32[40,896]{1,0:T(8,128)S(1)}, f32[40,896]{1,0:T(8,128)S(1)}, u32[]{:S(2)}, u32[]{:S(2)}) collective-permute-start(f32[40,896]{1,0:T(8,128)S(1)} %fusion.14), channel_id=1, source_target_pairs={{0,48},{1,49},{2,50},{3,51},{4,52},{5,53},{6,54},{7,55},{8,56},{9,... | collective-permute-start | bytes 430088 | tf_op jit(solution)/shard_map/ppermute | solution.py:24

commit v4 on v2

v4 whole, which is shorter than its diff:
```python
import functools

import jax
import jax.numpy as jnp
from jax import lax
from jax.experimental import pallas as pl
from jax.experimental.pallas import tpu as pltpu
from jax.sharding import PartitionSpec as P

SLOTS, TOKENS, ROWS = 6, 192, 40
K = SLOTS * TOKENS
TILE = 16 * ROWS
STRIDE = {"x": 1, "y": 4, "z": 16}
COLUMNS = {"A": (0, 896), "B": (896, 896), "C": (1792, 768)}


def exchange(value, axis, turn):
    pairs = []
    for section in range(2):
        flip, stride = 1 if section == turn else 3, STRIDE[axis]
        for d in range(64):
            p = d // stride % 4
            pairs.append((section * 64 + d, section * 64 + d + ((p ^ flip) - p) * stride))
    return lax.ppermute(value, ("section", "dp"), pairs)


def products(half, failed, counts, order, act, cot, *refs):
    outs, (acts, cots, total, sems) = refs[:-4], refs[-4:]
    section, me = lax.axis_index("section"), lax.axis_index("dp")
    flips = (0, 3 - 2 * section, 1 + 2 * section, 2)
    xs, ys, zs = ([place ^ flip for flip in flips] for place in (me % 4, me // 4 % 4, me // 16))
    fetch = [
        pltpu.make_async_copy(
            act.at[0, :, :, pl.ds(pl.multiple_of(zs[half + g] * TILE, 128), TILE)], acts.at[g], sems.at[g])
        for g in range(2)
    ]
    load = {}
    for n, pack in enumerate(("AB", "C")):
        span = pl.ds(COLUMNS[pack[0]][0], sum(COLUMNS[pack[-1]]) - COLUMNS[pack[0]][0])
        load[pack] = pltpu.make_async_copy(cot.at[0, :, :, span], cots.at[:, :, span], sems.at[2 + n])
    fetch[0].start()
    for copy in load.values():
        copy.start()
    fetch[1].start()
    alive = jnp.where(me == failed[0], 0, counts[0])
    live = [jnp.float32(0)] * SLOTS
    for position in range(SLOTS):
        for k in range(SLOTS):
            live[k] = jnp.where((order[0, position] == k) & (position < alive), jnp.float32(1), live[k])
    if half == 2:
        alive_rows = jnp.full((8, COLUMNS["C"][1]), alive.astype(jnp.float32))
        outs[4][2 * TILE:, :] = alive_rows
        outs[5][...] = alive_rows
    for g in range(2):
        fetch[g].wait()
        rows = acts[g].reshape(K, TILE)
        for pack in ("AB", "C"):
            first, last = COLUMNS[pack[0]][0], sum(COLUMNS[pack[-1]])
            if g == 0:
                load[pack].wait()
                for k in range(SLOTS):
                    cots[k, :, first:last] = cots[k, :, first:last] * live[k].astype(jnp.bfloat16)
            total[:, :last - first] = lax.dot_general(
                rows, cots[:, :, first:last].reshape(K, last - first), (((0,), (0,)), ((), ())),
                preferred_element_type=jnp.float32)
            for group in pack:
                column, columns = COLUMNS[group]
                for i in range(4):
                    for j in range(4):
                        start = ys[i] * 160 + xs[j] * ROWS if group == "B" else xs[i] * ROWS + ys[j] * 160
                        block = total[pl.ds(pl.multiple_of(start, 8), ROWS), column - first:column - first + columns]
                        if group == "A":
                            outs[i // 2][i % 2, j, g] = block
                        elif group == "B":
                            outs[2 + i // 2][i % 2, g, j] = block
                        else:
                            outs[4][pl.ds(((g * 4 + i) * 4 + j) * ROWS, ROWS), :] = block


def partials(half, activations, cotangents, failed, counts, order):
    a, b, c = (COLUMNS[group][1] for group in "ABC")
    shapes = [(2, 4, 2, ROWS, a)] * 2 + [(2, 2, 4, ROWS, b)] * 2
    shapes += [(2 * TILE + 8, c), (8, c)] if half == 2 else [(2 * TILE, c)]
    return pl.pallas_call(
        functools.partial(products, half),
        out_shape=[jax.ShapeDtypeStruct(shape, jnp.float32) for shape in shapes],
        in_specs=[pl.BlockSpec(memory_space=pltpu.SMEM)] * 3 + [pl.BlockSpec(memory_space=pltpu.HBM)] * 2,
        out_specs=[pl.BlockSpec(memory_space=pltpu.VMEM)] * len(shapes),
        scratch_shapes=[
            pltpu.VMEM((2, SLOTS, TOKENS, TILE), jnp.bfloat16),
            pltpu.VMEM((SLOTS, TOKENS, a + b + c), jnp.bfloat16),
            pltpu.VMEM((TILE, max(a + b, c)), jnp.float32),
            pltpu.SemaphoreType.DMA((4,)),
        ],
        compiler_params=pltpu.CompilerParams(vmem_limit_bytes=28 << 20),
        cost_estimate=pl.CostEstimate(flops=1024, bytes_accessed=1024, transcendentals=0),
    )(failed, counts, order, *(pltpu.with_memory_space_constraint(x, pltpu.HBM) for x in (activations, cotangents)))


def together(values):
    return list(lax.optimization_barrier(tuple(values)))


def shards(activations, cotangents, failed, counts, order):
    run = functools.partial(partials, failed=failed, counts=counts, order=order)
    *one, activations, cotangents = together([*run(2, activations, cotangents), activations, cotangents])
    a_keep_far, a_send_far, b_keep_far, b_send_far, c_send, c_total = one
    a_keep_near, a_send_near, b_keep_near, b_send_near, c_keep = run(0, activations, cotangents)
    taken = None

    def take(got):
        nonlocal taken
        taken = got if taken is None else together([got, taken])[0]
        return taken

    def both(keep, got, total, rows):
        total = total + got[2 * rows:]
        return jnp.concatenate([keep[rows:] + got[rows:2 * rows], total], axis=0), keep[:rows] + got[:rows], total

    a1f, b1f, c1 = exchange(a_send_far, "x", 0), exchange(b_send_far, "y", 0), exchange(c_send, "z", 0)
    a1n, b1n = exchange(a_send_near, "x", 0), exchange(b_send_near, "y", 0)
    a1f = take(a1f)
    a2f = exchange(a_keep_far[1] + a1f[1], "x", 1)
    b1f = take(b1f)
    b2f = exchange(b_keep_far[1] + b1f[1], "y", 1)
    c1 = take(c1)
    c_out, c_stay, c_total = both(c_keep, c1, c_total, TILE)
    c2 = exchange(c_out, "z", 1)
    a1n = take(a1n)
    a2n = exchange(a_keep_near[1] + a1n[1], "x", 1)
    b1n = take(b1n)
    b2n = exchange(b_keep_near[1] + b1n[1], "y", 1)
    a2f = take(a2f)
    a_far = (a_keep_far[0] + a1f[0]) + a2f
    a3f = exchange(a_far[2:4], "y", 0)
    b2f = take(b2f)
    b_far = (b_keep_far[0] + b1f[0]) + b2f
    b3 = exchange(b_far, "z", 0)
    c2 = take(c2)
    c_whole, c_total = c_stay + c2[:TILE], c_total + c2[TILE:]
    c3 = exchange(jnp.concatenate([c_whole[320:], c_total], axis=0), "x", 0)
    a2n = take(a2n)
    a_near = (a_keep_near[0] + a1n[0]) + a2n
    a3n = exchange(a_near[2:4], "y", 0)
    b2n = take(b2n)
    b_near = (b_keep_near[0] + b1n[0]) + b2n
    a3f = take(a3f)
    b3 = take(b3)
    b4 = exchange(b_near[1] + b3[1], "z", 1)
    c3 = take(c3)
    c_out, c_stay, c_total = both(c_whole[:320], c3, c_total, 160)
    c4 = exchange(c_out, "x", 1)
    a3n = take(a3n)
    a4 = exchange(jnp.concatenate([a_far[1] + a3f[1], a_near[1] + a3n[1]], axis=0), "y", 1)
    b4 = take(b4)
    b_whole = (b_near[0] + b3[0]) + b4
    b5 = exchange(b_whole[2:4], "x", 0)
    c4 = take(c4)
    c_whole, c_total = c_stay + c4[:160], c_total + c4[160:]
    c5 = exchange(jnp.concatenate([c_whole[80:], c_total], axis=0), "y", 0)
    a4 = take(a4)
    a_far, a_near = (a_far[0] + a3f[0]) + a4[:2], (a_near[0] + a3n[0]) + a4[2:]
    a5 = exchange(a_far, "z", 0)
    b5 = take(b5)
    b6 = exchange(b_whole[1] + b5[1], "x", 1)
    c5 = take(c5)
    c_out, c_stay, c_total = both(c_whole[:80], c5, c_total, 40)
    c6 = exchange(c_out, "y", 1)
    a5 = take(a5)
    a6 = exchange(a_near[1] + a5[1], "z", 1)
    b6, c6, a6 = together([b6, c6, a6])
    a = (a_near[0] + a5[0]) + a6
    b = (b_whole[0] + b5[0]) + b6
    c = c_stay + c6[:40]
    total = (c_total + c6[40:])[0, 0]
    return jnp.concatenate([a / total, b / total, c / total], axis=1)


def solution(mesh):
    in_specs = (
        P(("section", "dp"), None, None, None),
        P(("section", "dp"), None, None, None),
        P(),
        P("dp"),
        P("dp", None),
    )
    out_specs = P(("section", "dp"), None)
    return jax.shard_map(shards, mesh=mesh, in_specs=in_specs, out_specs=out_specs, check_vma=False)
```

time: 178 us -> 163 us (0.916)
  starting transfers between devices: 62.3 us -> 39.4 us
  waiting for transfers between devices: 77.3 us -> 87.3 us
  other arithmetic: 8.27 us -> 3.8 us
    ppermute x35 -> x23, starting transfers between devices: 62.3 us -> 39.4 us  [exchange(): return lax.ppermute(value, ('section', 'dp'), pairs)]
    ppermute x35 -> x23, waiting for transfers between devices: 77.3 us -> 87.3 us  [exchange(): return lax.ppermute(value, ('section', 'dp'), pairs)]
    add x31 -> x24, other arithmetic: 6.11 us -> 2.63 us  [the longest x3 0.49 us: both(): keep[rows:] + got[rows:2 * rows]]
  transfers between devices with their start and end apart: 35 -> 23, of which waited for: 16 -> 10; matrix products, arithmetic and copies ran while one was open for 4% -> 2% of each run, Pallas kernels for 8% -> 9%
where the time goes in v4:
time: 163 us
  waiting for transfers between devices  87.3 us (54%)
  starting transfers between devices  39.4 us (24%)
  Pallas kernels  27.9 us (17%)
  other arithmetic  3.8 us (2%)
  between operations  2.92 us (2%)
  local copies, waits for them, and re-layouts  1.94 us (1%)
    ppermute x23, waiting for transfers between devices, exchange(): return lax.ppermute(value, ('section', 'dp'), pairs)  87.3 us
    ppermute x23, starting transfers between devices, exchange(): return lax.ppermute(value, ('section', 'dp'), pairs)  39.4 us
    pallas_call x2, Pallas kernels, partials(): pl.pallas_call(functools.partial(products, half), out_shape=[jax.ShapeDty...  27.9 us
  transfers between devices with their start and end apart: 23, of which 10 were waited for; matrix products, arithmetic and copies ran while one was open for 2% of the time, Pallas kernels for 9%

profile of v4, /device:TPU:0, one launch (start us, length us, event | category | flops | bytes accessed | tf_op | source)
XLA Modules:
  0.0 163.3 jit_solution(14166309483569824768)
XLA Ops:
  1.3 0.6 copy-done
  2.0 14.0 %shard_map.55 = (f32[2,4,2,40,896]{4,3,2,1,0:T(8,128)S(1)}, f32[2,4,2,40,896]{4,3,2,1,0:T(8,128)S(1)}, f32[2,2,4,40,896]{4,3,2,1,0:T(8,128)S(1)}, f32[2,2,4,40,8...) custom-call(s32[1]{0:T(128)S(6)} %copy.6.failed, s32[1]{0:T(128)S(6)} %copy.7.counts, ...), custom_call_target="tpu_custom_call" | custom-call | flops 1024 | bytes 1024 | tf_op jit(solution)/shard_map/pallas_call | solution.py:84
  15.9 2.1 %collective-permute-start.1 = (f32[1288,768]{1,0:T(8,128)S(1)}, f32[1288,768]{1,0:T(8,128)S(1)}, u32[]{:S(2)}, u32[]{:S(2)}) collective-permute-start(f32[1288,768]{1,0:T(8,128)S(1)} %get-tuple-element.56), channel_id=1, source_target_pairs={{0,16},{1,17},{2,18},{3,19},{4,20},{5,21},{6,22},{7,23},{8,24},{9,... | collective-permute-start | bytes 11870216 | tf_op jit(solution)/shard_map/ppermute | solution.py:24
  18.0 1.6 collective-permute-start.2
  19.6 1.5 collective-permute-start.3
  21.1 14.0 %shard_map.56 = (f32[2,4,2,40,896]{4,3,2,1,0:T(8,128)S(1)}, f32[2,4,2,40,896]{4,3,2,1,0:T(8,128)S(1)}, f32[2,2,4,40,896]{4,3,2,1,0:T(8,128)S(1)}, f32[2,2,4,40,896]{4,3,2,1,0:T(8,128)S(1)}, f32[1280,768]{1,0:T(8,128)S(1)}) custom-call(s32[1]{0:T(128)S(6)} %copy.6.failed, s32[1]{0:T(128)S(6)} %copy.7.counts, s32[1,6]{1,0:T(1,128)S(1)} %copy-done.1, ...), custom_call_target="tpu_custom_call" | custom-call | flops 1024 | bytes 1024 | tf_op jit(solution)/shard_map/pallas_call | solution.py:84
  35.0 0.6 collective-permute-start
  36.1 10.0 %collective-permute-done.2 = f32[2,2,4,40,896]{4,3,2,1,0:T(8,128)S(1)} collective-permute-done((f32[2,2,4,40,896]{4,3,2,1,0:T(8,128)S(1)}, f32[2,2,4,40,896]{4,3,2,1,0:T(8,128)S(1)}, u32[]{:S(2)}, u32[]{:S(2)}) %collective-permute-start.2) | collective-permute-done | bytes 2293792 | tf_op jit(solution)/shard_map/ppermute | solution.py:24
  46.1 1.6 collective-permute-done.3
  47.8 2.3 %collective-permute-start.6 = (f32[2,4,40,896]{3,2,1,0:T(8,128)S(1)}, f32[2,4,40,896]{3,2,1,0:T(8,128)S(1)}, u32[]{:S(2)}, u32[]{:S(2)}) collective-permute-start(f32[2,4,40,896]{3,2,1,0:T(8,128)S(1)} %add_bitcast_fusion.1), channel_id=1, source_target_pairs={{0,12},{1,13},{2,14},{3,15},{4,8},{5,9},{6,10},{7,11},{8,4},{9,5},... | collective-permute-start | bytes 3440648 | tf_op jit(solution)/shard_map/ppermute | solution.py:24
  50.2 2.8 %collective-permute-start.7 = (f32[4,2,40,896]{3,2,1,0:T(8,128)S(1)}, f32[4,2,40,896]{3,2,1,0:T(8,128)S(1)}, u32[]{:S(2)}, u32[]{:S(2)}) collective-permute-start(f32[4,2,40,896]{3,2,1,0:T(8,128)S(1)} %fusion.2), channel_id=1, source_target_pairs={{0,3},{1,2},{2,1},{3,0},{4,7},{5,6},{6,5},{7,4},{8,11},{9,10},{10,... | collective-permute-start | bytes 3440648 | tf_op jit(solution)/shard_map/ppermute | solution.py:24
  53.1 8.9 %collective-permute-done.1 = f32[1288,768]{1,0:T(8,128)S(1)} collective-permute-done((f32[1288,768]{1,0:T(8,128)S(1)}, f32[1288,768]{1,0:T(8,128)S(1)}, u32[]{:S(2)}, u32[]{:S(2)}) %collective-permute-start.1) | collective-permute-done | bytes 3956768 | tf_op jit(solution)/shard_map/ppermute | solution.py:24
  62.5 4.2 %collective-permute-start.5 = (f32[648,768]{1,0:T(8,128)S(1)}, f32[648,768]{1,0:T(8,128)S(1)}, u32[]{:S(2)}, u32[]{:S(2)}) collective-permute-start(f32[648,768]{1,0:T(8,128)S(1)} %pad_maximum_fusion), channel_id=1, source_target_pairs={{0,48},{1,49},{2,50},{3,51},{4,52},{5,53},{6,54},{7,55},{8,56},{9,... | collective-permute-start | bytes 5971976 | tf_op jit(solution)/shard_map/ppermute | solution.py:24
  66.7 17.9 %collective-permute-done = f32[2,4,2,40,896]{4,3,2,1,0:T(8,128)S(1)} collective-permute-done((f32[2,4,2,40,896]{4,3,2,1,0:T(8,128)S(1)}, f32[2,4,2,40,896]{4,3,2,1,0:T(8,128)S(1)}, u32[]{:S(2)}, u32[]{:S(2)}) %collective-permute-start) | collective-permute-done | bytes 2293792 | tf_op jit(solution)/shard_map/ppermute | solution.py:24
  85.1 2.3 %collective-permute-start.13 = (f32[2,4,40,896]{3,2,1,0:T(8,128)S(1)}, f32[2,4,40,896]{3,2,1,0:T(8,128)S(1)}, u32[]{:S(2)}, u32[]{:S(2)}) collective-permute-start(f32[2,4,40,896]{3,2,1,0:T(8,128)S(1)} %add_bitcast_fusion), channel_id=1, source_target_pairs={{0,12},{1,13},{2,14},{3,15},{4,8},{5,9},{6,10},{7,11},{8,4},{9,5},... | collective-permute-start | bytes 3440648 | tf_op jit(solution)/shard_map/ppermute | solution.py:24
  87.5 2.8 %collective-permute-start.4 = (f32[4,2,40,896]{3,2,1,0:T(8,128)S(1)}, f32[4,2,40,896]{3,2,1,0:T(8,128)S(1)}, u32[]{:S(2)}, u32[]{:S(2)}) collective-permute-start(f32[4,2,40,896]{3,2,1,0:T(8,128)S(1)} %add_bitcast_fusion.2), channel_id=1, source_target_pairs={{0,3},{1,2},{2,1},{3,0},{4,7},{5,6},{6,5},{7,4},{8,11},{9,10},{10,... | collective-permute-start | bytes 3440648 | tf_op jit(solution)/shard_map/ppermute | solution.py:24
  90.6 0.8 collective-permute-start.12
  92.0 1.1 collective-permute-start.10
  93.1 21.4 %collective-permute-done.4 = f32[4,2,40,896]{3,2,1,0:T(8,128)S(1)} collective-permute-done((f32[4,2,40,896]{3,2,1,0:T(8,128)S(1)}, f32[4,2,40,896]{3,2,1,0:T(8,128)S(1)}, u32[]{:S(2)}, u32[]{:S(2)}) %collective-permute-start.4) | collective-permute-done | bytes 1146912 | tf_op jit(solution)/shard_map/ppermute | solution.py:24
  114.7 5.2 %collective-permute-start.16 = (f32[4,40,896]{2,1,0:T(8,128)S(1)}, f32[4,40,896]{2,1,0:T(8,128)S(1)}, u32[]{:S(2)}, u32[]{:S(2)}) collective-permute-start(f32[4,40,896]{2,1,0:T(8,128)S(1)} %fusion.5), channel_id=1, source_target_pairs={{0,48},{1,49},{2,50},{3,51},{4,52},{5,53},{6,54},{7,55},{8,56},{9,... | collective-permute-start | bytes 1720328 | tf_op jit(solution)/shard_map/ppermute | solution.py:24
  120.9 3.0 %collective-permute-start.15 = (f32[168,768]{1,0:T(8,128)S(1)}, f32[168,768]{1,0:T(8,128)S(1)}, u32[]{:S(2)}, u32[]{:S(2)}) collective-permute-start(f32[168,768]{1,0:T(8,128)S(1)} %pad_maximum_fusion.3), channel_id=1, source_target_pairs={{0,3},{1,2},{2,1},{3,0},{4,7},{5,6},{6,5},{7,4},{8,11},{9,10},{10,... | collective-permute-start | bytes 1548296 | tf_op jit(solution)/shard_map/ppermute | solution.py:24
  123.9 6.6 %collective-permute-done.9 = f32[2,2,40,896]{3,2,1,0:T(8,128)S(1)} collective-permute-done((f32[2,2,40,896]{3,2,1,0:T(8,128)S(1)}, f32[2,2,40,896]{3,2,1,0:T(8,128)S(1)}, u32[]{:S(2)}, u32[]{:S(2)}) %collective-permute-start.9) | collective-permute-done | bytes 573472 | tf_op jit(solution)/shard_map/ppermute | solution.py:24
  130.7 1.7 %collective-permute-start.19 = (f32[2,40,896]{2,1,0:T(8,128)S(1)}, f32[2,40,896]{2,1,0:T(8,128)S(1)}, u32[]{:S(2)}, u32[]{:S(2)}) collective-permute-start(f32[2,40,896]{2,1,0:T(8,128)S(1)} %slice.281), channel_id=1, source_target_pairs={{0,1},{1,0},{2,3},{3,2},{4,5},{5,4},{6,7},{7,6},{8,9},{9,8},{10,11... | collective-permute-start | bytes 860168 | tf_op jit(solution)/shard_map/ppermute | solution.py:24
  132.6 1.8 %collective-permute-done.15 = f32[168,768]{1,0:T(8,128)S(1)} collective-permute-done((f32[168,768]{1,0:T(8,128)S(1)}, f32[168,768]{1,0:T(8,128)S(1)}, u32[]{:S(2)}, u32[]{:S(2)}) %collective-permute-start.15) | collective-permute-done | bytes 516128 | tf_op jit(solution)/shard_map/ppermute | solution.py:24
  134.5 1.2 collective-permute-start.18
  135.8 7.7 %collective-permute-done.14 = f32[4,40,896]{2,1,0:T(8,128)S(1)} collective-permute-done((f32[4,40,896]{2,1,0:T(8,128)S(1)}, f32[4,40,896]{2,1,0:T(8,128)S(1)}, u32[]{:S(2)}, u32[]{:S(2)}) %collective-permute-start.14) | collective-permute-done | bytes 573472 | tf_op jit(solution)/shard_map/ppermute | solution.py:24
  143.5 3.7 %collective-permute-start.20 = (f32[40,896]{1,0:T(8,128)S(1)}, f32[40,896]{1,0:T(8,128)S(1)}, u32[]{:S(2)}, u32[]{:S(2)}) collective-permute-start(f32[40,896]{1,0:T(8,128)S(1)} %fusion.17), channel_id=1, source_target_pairs={{0,3},{1,2},{2,1},{3,0},{4,7},{5,6},{6,5},{7,4},{8,11},{9,10},{10,... | collective-permute-start | bytes 430088 | tf_op jit(solution)/shard_map/ppermute | solution.py:24
  147.5 1.0 collective-permute-start.21
  148.5 5.5 %collective-permute-done.17 = f32[2,40,896]{2,1,0:T(8,128)S(1)} collective-permute-done((f32[2,40,896]{2,1,0:T(8,128)S(1)}, f32[2,40,896]{2,1,0:T(8,128)S(1)}, u32[]{:S(2)}, u32[]{:S(2)}) %collective-permute-start.17) | collective-permute-done | bytes 286752 | tf_op jit(solution)/shard_map/ppermute | solution.py:24
  154.7 5.8 %collective-permute-done.22 = f32[40,896]{1,0:T(8,128)S(1)} collective-permute-done((f32[40,896]{1,0:T(8,128)S(1)}, f32[40,896]{1,0:T(8,128)S(1)}, u32[]{:S(2)}, u32[]{:S(2)}) %collective-permute-start.22) | collective-permute-done | bytes 143392 | tf_op jit(solution)/shard_map/ppermute | solution.py:24
  160.4 0.6 slice.286
  162.5 0.8 pad_maximum_fusion.4
  (61 shorter events, 5.2 us)
Async XLA Ops:
  1.3 0.7 copy-start
  2.0 19.1 %copy-start.1 = (s32[1,6]{1,0:T(1,128)S(1)}, s32[1,6]{1,0:T(1,128)}, u32[]{:S(2)}) copy-start(s32[1,6]{1,0:T(1,128)} %order.3) | copy-start | bytes 76
  15.9 46.0 %collective-permute-start.1 = (f32[1288,768]{1,0:T(8,128)S(1)}, f32[1288,768]{1,0:T(8,128)S(1)}, u32[]{:S(2)}, u32[]{:S(2)}) collective-permute-start(f32[1288,768]{1,0:T(8,128)S(1)} %get-tuple-element.56), channel_id=1, source_target_pairs={{0,16},{1,17},{2,18},{3,19},{4,20},{5,21},{6,22},{7,23},{8,24},{9,... | collective-permute-start | bytes 11870216 | tf_op jit(solution)/shard_map/ppermute | solution.py:24
  18.0 28.1 %collective-permute-start.2 = (f32[2,2,4,40,896]{4,3,2,1,0:T(8,128)S(1)}, f32[2,2,4,40,896]{4,3,2,1,0:T(8,128)S(1)}, u32[]{:S(2)}, u32[]{:S(2)}) collective-permute-start(f32[2,2,4,40,896]{4,3,2,1,0:T(8,128)S(1)} %get-tuple-element.57), channel_id=1, source_target_pairs={{0,4},{1,5},{2,6},{3,7},{4,0},{5,1},{6,2},{7,3},{8,12},{9,13},{10,... | collective-permute-start | bytes 6881288 | tf_op jit(solution)/shard_map/ppermute | solution.py:24
  19.6 28.1 %collective-permute-start.3 = (f32[2,4,2,40,896]{4,3,2,1,0:T(8,128)S(1)}, f32[2,4,2,40,896]{4,3,2,1,0:T(8,128)S(1)}, u32[]{:S(2)}, u32[]{:S(2)}) collective-permute-start(f32[2,4,2,40,896]{4,3,2,1,0:T(8,128)S(1)} %get-tuple-element.58), channel_id=1, source_target_pairs={{0,1},{1,0},{2,3},{3,2},{4,5},{5,4},{6,7},{7,6},{8,9},{9,8},{10,11... | collective-permute-start | bytes 6881288 | tf_op jit(solution)/shard_map/ppermute | solution.py:24
  35.0 49.5 %collective-permute-start = (f32[2,4,2,40,896]{4,3,2,1,0:T(8,128)S(1)}, f32[2,4,2,40,896]{4,3,2,1,0:T(8,128)S(1)}, u32[]{:S(2)}, u32[]{:S(2)}) collective-permute-start(f32[2,4,2,40,896]{4,3,2,1,0:T(8,128)S(1)} %get-tuple-element.55), channel_id=1, source_target_pairs={{0,1},{1,0},{2,3},{3,2},{4,5},{5,4},{6,7},{7,6},{8,9},{9,8},{10,11... | collective-permute-start | bytes 6881288 | tf_op jit(solution)/shard_map/ppermute | solution.py:24
  35.7 48.9 %collective-permute-start.8 = (f32[2,2,4,40,896]{4,3,2,1,0:T(8,128)S(1)}, f32[2,2,4,40,896]{4,3,2,1,0:T(8,128)S(1)}, u32[]{:S(2)}, u32[]{:S(2)}) collective-permute-start(f32[2,2,4,40,896]{4,3,2,1,0:T(8,128)S(1)} %get-tuple-element.66), channel_id=1, source_target_pairs={{0,4},{1,5},{2,6},{3,7},{4,0},{5,1},{6,2},{7,3},{8,12},{9,13},{10,... | collective-permute-start | bytes 6881288 | tf_op jit(solution)/shard_map/ppermute | solution.py:24
  47.8 36.8 %collective-permute-start.6 = (f32[2,4,40,896]{3,2,1,0:T(8,128)S(1)}, f32[2,4,40,896]{3,2,1,0:T(8,128)S(1)}, u32[]{:S(2)}, u32[]{:S(2)}) collective-permute-start(f32[2,4,40,896]{3,2,1,0:T(8,128)S(1)} %add_bitcast_fusion.1), channel_id=1, source_target_pairs={{0,12},{1,13},{2,14},{3,15},{4,8},{5,9},{6,10},{7,11},{8,4},{9,5},... | collective-permute-start | bytes 3440648 | tf_op jit(solution)/shard_map/ppermute | solution.py:24
  50.2 34.4 %collective-permute-start.7 = (f32[4,2,40,896]{3,2,1,0:T(8,128)S(1)}, f32[4,2,40,896]{3,2,1,0:T(8,128)S(1)}, u32[]{:S(2)}, u32[]{:S(2)}) collective-permute-start(f32[4,2,40,896]{3,2,1,0:T(8,128)S(1)} %fusion.2), channel_id=1, source_target_pairs={{0,3},{1,2},{2,1},{3,0},{4,7},{5,6},{6,5},{7,4},{8,11},{9,10},{10,... | collective-permute-start | bytes 3440648 | tf_op jit(solution)/shard_map/ppermute | solution.py:24
  62.5 28.8 %collective-permute-start.5 = (f32[648,768]{1,0:T(8,128)S(1)}, f32[648,768]{1,0:T(8,128)S(1)}, u32[]{:S(2)}, u32[]{:S(2)}) collective-permute-start(f32[648,768]{1,0:T(8,128)S(1)} %pad_maximum_fusion), channel_id=1, source_target_pairs={{0,48},{1,49},{2,50},{3,51},{4,52},{5,53},{6,54},{7,55},{8,56},{9,... | collective-permute-start | bytes 5971976 | tf_op jit(solution)/shard_map/ppermute | solution.py:24
  84.8 29.7 %collective-permute-start.11 = (f32[2,4,40,896]{3,2,1,0:T(8,128)S(1)}, f32[2,4,40,896]{3,2,1,0:T(8,128)S(1)}, u32[]{:S(2)}, u32[]{:S(2)}) collective-permute-start(f32[2,4,40,896]{3,2,1,0:T(8,128)S(1)} %bitcast_add_fusion.1), channel_id=1, source_target_pairs={{0,16},{1,17},{2,18},{3,19},{4,20},{5,21},{6,22},{7,23},{8,24},{9,... | collective-permute-start | bytes 3440648 | tf_op jit(solution)/shard_map/ppermute | solution.py:24
  85.1 29.4 %collective-permute-start.13 = (f32[2,4,40,896]{3,2,1,0:T(8,128)S(1)}, f32[2,4,40,896]{3,2,1,0:T(8,128)S(1)}, u32[]{:S(2)}, u32[]{:S(2)}) collective-permute-start(f32[2,4,40,896]{3,2,1,0:T(8,128)S(1)} %add_bitcast_fusion), channel_id=1, source_target_pairs={{0,12},{1,13},{2,14},{3,15},{4,8},{5,9},{6,10},{7,11},{8,4},{9,5},... | collective-permute-start | bytes 3440648 | tf_op jit(solution)/shard_map/ppermute | solution.py:24
  87.5 27.0 %collective-permute-start.4 = (f32[4,2,40,896]{3,2,1,0:T(8,128)S(1)}, f32[4,2,40,896]{3,2,1,0:T(8,128)S(1)}, u32[]{:S(2)}, u32[]{:S(2)}) collective-permute-start(f32[4,2,40,896]{3,2,1,0:T(8,128)S(1)} %add_bitcast_fusion.2), channel_id=1, source_target_pairs={{0,3},{1,2},{2,1},{3,0},{4,7},{5,6},{6,5},{7,4},{8,11},{9,10},{10,... | collective-permute-start | bytes 3440648 | tf_op jit(solution)/shard_map/ppermute | solution.py:24
  90.6 23.9 %collective-permute-start.12 = (f32[2,2,40,896]{3,2,1,0:T(8,128)S(1)}, f32[2,2,40,896]{3,2,1,0:T(8,128)S(1)}, u32[]{:S(2)}, u32[]{:S(2)}) collective-permute-start(f32[2,2,40,896]{3,2,1,0:T(8,128)S(1)} %slice.271), channel_id=1, source_target_pairs={{0,4},{1,5},{2,6},{3,7},{4,0},{5,1},{6,2},{7,3},{8,12},{9,13},{10,... | collective-permute-start | bytes 1720328 | tf_op jit(solution)/shard_map/ppermute | solution.py:24
  92.0 28.8 %collective-permute-start.10 = (f32[328,768]{1,0:T(8,128)S(1)}, f32[328,768]{1,0:T(8,128)S(1)}, u32[]{:S(2)}, u32[]{:S(2)}) collective-permute-start(f32[328,768]{1,0:T(8,128)S(1)} %pad_maximum_fusion.1), channel_id=1, source_target_pairs={{0,1},{1,0},{2,3},{3,2},{4,5},{5,4},{6,7},{7,6},{8,9},{9,8},{10,11... | collective-permute-start | bytes 3022856 | tf_op jit(solution)/shard_map/ppermute | solution.py:24
  114.7 15.8 %collective-permute-start.16 = (f32[4,40,896]{2,1,0:T(8,128)S(1)}, f32[4,40,896]{2,1,0:T(8,128)S(1)}, u32[]{:S(2)}, u32[]{:S(2)}) collective-permute-start(f32[4,40,896]{2,1,0:T(8,128)S(1)} %fusion.5), channel_id=1, source_target_pairs={{0,48},{1,49},{2,50},{3,51},{4,52},{5,53},{6,54},{7,55},{8,56},{9,... | collective-permute-start | bytes 1720328 | tf_op jit(solution)/shard_map/ppermute | solution.py:24
  120.2 10.4 %collective-permute-start.9 = (f32[2,2,40,896]{3,2,1,0:T(8,128)S(1)}, f32[2,2,40,896]{3,2,1,0:T(8,128)S(1)}, u32[]{:S(2)}, u32[]{:S(2)}) collective-permute-start(f32[2,2,40,896]{3,2,1,0:T(8,128)S(1)} %slice.268), channel_id=1, source_target_pairs={{0,4},{1,5},{2,6},{3,7},{4,0},{5,1},{6,2},{7,3},{8,12},{9,13},{10,... | collective-permute-start | bytes 1720328 | tf_op jit(solution)/shard_map/ppermute | solution.py:24
  120.9 13.5 %collective-permute-start.15 = (f32[168,768]{1,0:T(8,128)S(1)}, f32[168,768]{1,0:T(8,128)S(1)}, u32[]{:S(2)}, u32[]{:S(2)}) collective-permute-start(f32[168,768]{1,0:T(8,128)S(1)} %pad_maximum_fusion.3), channel_id=1, source_target_pairs={{0,3},{1,2},{2,1},{3,0},{4,7},{5,6},{6,5},{7,4},{8,11},{9,10},{10,... | collective-permute-start | bytes 1548296 | tf_op jit(solution)/shard_map/ppermute | solution.py:24
  130.7 12.8 %collective-permute-start.19 = (f32[2,40,896]{2,1,0:T(8,128)S(1)}, f32[2,40,896]{2,1,0:T(8,128)S(1)}, u32[]{:S(2)}, u32[]{:S(2)}) collective-permute-start(f32[2,40,896]{2,1,0:T(8,128)S(1)} %slice.281), channel_id=1, source_target_pairs={{0,1},{1,0},{2,3},{3,2},{4,5},{5,4},{6,7},{7,6},{8,9},{9,8},{10,11... | collective-permute-start | bytes 860168 | tf_op jit(solution)/shard_map/ppermute | solution.py:24
  132.5 11.0 %collective-permute-start.14 = (f32[4,40,896]{2,1,0:T(8,128)S(1)}, f32[4,40,896]{2,1,0:T(8,128)S(1)}, u32[]{:S(2)}, u32[]{:S(2)}) collective-permute-start(f32[4,40,896]{2,1,0:T(8,128)S(1)} %pad_maximum_fusion.2), channel_id=1, source_target_pairs={{0,12},{1,13},{2,14},{3,15},{4,8},{5,9},{6,10},{7,11},{8,4},{9,5},... | collective-permute-start | bytes 1720328 | tf_op jit(solution)/shard_map/ppermute | solution.py:24
  134.5 12.9 %collective-permute-start.18 = (f32[88,768]{1,0:T(8,128)S(1)}, f32[88,768]{1,0:T(8,128)S(1)}, u32[]{:S(2)}, u32[]{:S(2)}) collective-permute-start(f32[88,768]{1,0:T(8,128)S(1)} %pad_maximum_fusion.5), channel_id=1, source_target_pairs={{0,4},{1,5},{2,6},{3,7},{4,0},{5,1},{6,2},{7,3},{8,12},{9,13},{10,... | collective-permute-start | bytes 811016 | tf_op jit(solution)/shard_map/ppermute | solution.py:24
  143.5 11.1 %collective-permute-start.20 = (f32[40,896]{1,0:T(8,128)S(1)}, f32[40,896]{1,0:T(8,128)S(1)}, u32[]{:S(2)}, u32[]{:S(2)}) collective-permute-start(f32[40,896]{1,0:T(8,128)S(1)} %fusion.17), channel_id=1, source_target_pairs={{0,3},{1,2},{2,1},{3,0},{4,7},{5,6},{6,5},{7,4},{8,11},{9,10},{10,... | collective-permute-start | bytes 430088 | tf_op jit(solution)/shard_map/ppermute | solution.py:24
  147.3 6.7 %collective-permute-start.17 = (f32[2,40,896]{2,1,0:T(8,128)S(1)}, f32[2,40,896]{2,1,0:T(8,128)S(1)}, u32[]{:S(2)}, u32[]{:S(2)}) collective-permute-start(f32[2,40,896]{2,1,0:T(8,128)S(1)} %get-tuple-element.87), channel_id=1, source_target_pairs={{0,16},{1,17},{2,18},{3,19},{4,20},{5,21},{6,22},{7,23},{8,24},{9,... | collective-permute-start | bytes 860168 | tf_op jit(solution)/shard_map/ppermute | solution.py:24
  147.5 7.2 %collective-permute-start.21 = (f32[48,768]{1,0:T(8,128)S(1)}, f32[48,768]{1,0:T(8,128)S(1)}, u32[]{:S(2)}, u32[]{:S(2)}) collective-permute-start(f32[48,768]{1,0:T(8,128)S(1)} %pad_maximum_fusion.6), channel_id=1, source_target_pairs={{0,12},{1,13},{2,14},{3,15},{4,8},{5,9},{6,10},{7,11},{8,4},{9,5},... | collective-permute-start | bytes 442376 | tf_op jit(solution)/shard_map/ppermute | solution.py:24
  154.1 6.4 %collective-permute-start.22 = (f32[40,896]{1,0:T(8,128)S(1)}, f32[40,896]{1,0:T(8,128)S(1)}, u32[]{:S(2)}, u32[]{:S(2)}) collective-permute-start(f32[40,896]{1,0:T(8,128)S(1)} %fusion.16), channel_id=1, source_target_pairs={{0,48},{1,49},{2,50},{3,51},{4,52},{5,53},{6,54},{7,55},{8,56},{9,... | collective-permute-start | bytes 430088 | tf_op jit(solution)/shard_map/ppermute | solution.py:24

commit v5 on v4

v5 whole, which is shorter than its diff:
```python
import functools

import jax
import jax.numpy as jnp
from jax import lax
from jax.experimental import pallas as pl
from jax.experimental.pallas import tpu as pltpu
from jax.sharding import PartitionSpec as P

SLOTS, TOKENS, ROWS = 6, 192, 40
K = SLOTS * TOKENS
TILE = 16 * ROWS
STRIDE = {"x": 1, "y": 4, "z": 16}
COLUMNS = {"A": (0, 896), "B": (896, 896), "C": (1792, 768)}


def exchange(value, axis, turn):
    pairs = []
    for section in range(2):
        flip, stride = 1 if section == turn else 3, STRIDE[axis]
        for d in range(64):
            p = d // stride % 4
            pairs.append((section * 64 + d, section * 64 + d + ((p ^ flip) - p) * stride))
    return lax.ppermute(value, ("section", "dp"), pairs)


def masked(failed, counts, order, cots):
    me = lax.axis_index("dp")
    alive = jnp.where(me == failed[0], 0, counts[0])
    for k in range(SLOTS):
        live = jnp.float32(0)
        for position in range(SLOTS):
            live = jnp.where((order[0, position] == k) & (position < alive), jnp.float32(1), live)
        cots[k] = cots[k] * live.astype(jnp.bfloat16)
    return alive.astype(jnp.float32)


def product(rows, cots):
    return lax.dot_general(
        rows.reshape(K, TILE), cots[...].reshape(K, cots.shape[2]), (((0,), (0,)), ((), ())),
        preferred_element_type=jnp.float32)


def whole_products(failed, counts, order, act, cot, out, acts, cots, total, sems):
    column, columns = COLUMNS["C"]
    load = pltpu.make_async_copy(cot.at[0, :, :, pl.ds(column, columns)], cots, sems.at[0])
    fetch = [
        pltpu.make_async_copy(act.at[0, :, :, pl.ds(g * TILE, TILE)], acts.at[g], sems.at[1 + g]) for g in range(4)
    ]
    store = [pltpu.make_async_copy(total.at[g], out.at[pl.ds(g * TILE, TILE), :], sems.at[5 + g]) for g in range(4)]
    load.start()
    for copy in fetch:
        copy.start()
    load.wait()
    masked(failed, counts, order, cots)
    for g in range(4):
        fetch[g].wait()
        total[g] = product(acts[g], cots)
        store[g].start()
    for copy in store:
        copy.wait()


def products(half, failed, counts, order, act, cot, *refs):
    (a_keep, a_send, b_keep, b_send), (acts, cots, total, sems) = refs[:4], refs[-4:]
    section, me = lax.axis_index("section"), lax.axis_index("dp")
    flips = (0, 3 - 2 * section, 1 + 2 * section, 2)
    xs, ys, zs = ([place ^ flip for flip in flips] for place in (me % 4, me // 4 % 4, me // 16))
    width = COLUMNS["B"][0]
    load = pltpu.make_async_copy(cot.at[0, :, :, pl.ds(0, 2 * width)], cots, sems.at[0])
    fetch = [
        pltpu.make_async_copy(
            act.at[0, :, :, pl.ds(pl.multiple_of(zs[half + g] * TILE, 128), TILE)], acts.at[g], sems.at[1 + g])
        for g in range(2)
    ]
    load.start()
    for copy in fetch:
        copy.start()
    load.wait()
    alive = masked(failed, counts, order, cots)
    if half == 2:
        alive_rows = jnp.full((8, width), alive)
        b_send[TILE:, :] = alive_rows
        refs[4][...] = alive_rows
    for g in range(2):
        fetch[g].wait()
        total[...] = product(acts[g], cots)
        for i in range(4):
            for j in range(4):
                rows = pl.ds(pl.multiple_of(xs[i] * ROWS + ys[j] * 160, 8), ROWS)
                (a_keep if i < 2 else a_send)[i % 2, j, g] = total[rows, :width]
                rows = pl.ds(pl.multiple_of(ys[i] * 160 + xs[j] * ROWS, 8), ROWS)
                (b_keep if i < 2 else b_send)[pl.ds(((i % 2 * 2 + g) * 4 + j) * ROWS, ROWS), :] = total[rows, width:]


def call(kernel, shapes, out_space, scratch, limit, activations, cotangents, failed, counts, order):
    return pl.pallas_call(
        kernel,
        out_shape=[pltpu.HBM(shape, jnp.float32) if out_space == pltpu.HBM else jax.ShapeDtypeStruct(shape, jnp.float32) for shape in shapes],
        in_specs=[pl.BlockSpec(memory_space=pltpu.SMEM)] * 3 + [pl.BlockSpec(memory_space=pltpu.HBM)] * 2,
        out_specs=[pl.BlockSpec(memory_space=out_space)] * len(shapes),
        scratch_shapes=scratch,
        compiler_params=pltpu.CompilerParams(vmem_limit_bytes=limit << 20),
        cost_estimate=pl.CostEstimate(flops=1024, bytes_accessed=1024, transcendentals=0),
    )(failed, counts, order, *(pltpu.with_memory_space_constraint(x, pltpu.HBM) for x in (activations, cotangents)))


def partials(half, *args):
    width = COLUMNS["B"][0]
    shapes = [(2, 4, 2, ROWS, width)] * 2 + [(TILE, width), (TILE + 8, width) if half == 2 else (TILE, width)]
    shapes += [(8, width)] if half == 2 else []
    scratch = [
        pltpu.VMEM((2, SLOTS, TOKENS, TILE), jnp.bfloat16),
        pltpu.VMEM((SLOTS, TOKENS, 2 * width), jnp.bfloat16),
        pltpu.VMEM((TILE, 2 * width), jnp.float32),
        pltpu.SemaphoreType.DMA((3,)),
    ]
    return call(functools.partial(products, half), shapes, pltpu.VMEM, scratch, 22, *args)


def whole_partial(*args):
    columns = COLUMNS["C"][1]
    scratch = [
        pltpu.VMEM((4, SLOTS, TOKENS, TILE), jnp.bfloat16),
        pltpu.VMEM((SLOTS, TOKENS, columns), jnp.bfloat16),
        pltpu.VMEM((4, TILE, columns), jnp.float32),
        pltpu.SemaphoreType.DMA((9,)),
    ]
    return call(whole_products, [(4 * TILE, columns)], pltpu.HBM, scratch, 22, *args)[0]


def together(values):
    return list(lax.optimization_barrier(tuple(values)))


def shards(activations, cotangents, failed, counts, order):
    c = whole_partial(activations, cotangents, failed, counts, order)
    c, activations, cotangents = together([c, activations, cotangents])
    c = lax.psum_scatter(
        c, "dp", scatter_dimension=0, tiled=True, axis_index_groups=[[d + 16 * z for z in range(4)] for d in range(16)])
    c = lax.psum_scatter(
        c, "dp", scatter_dimension=0, tiled=True, axis_index_groups=[[d + 16 * z for d in range(16)] for z in range(4)])
    *one, activations, cotangents = together(
        [*partials(2, activations, cotangents, failed, counts, order), activations, cotangents])
    a_keep_far, a_send_far, b_keep_far, b_send_far, total = one
    a_keep_near, a_send_near, b_keep_near, b_send_near = partials(0, activations, cotangents, failed, counts, order)
    taken = None

    def take(got):
        nonlocal taken
        taken = got if taken is None else together([got, taken])[0]
        return taken

    def under(rows, total):
        return jnp.concatenate([rows, total], axis=0)

    a1f, b1f = exchange(a_send_far, "x", 0), exchange(b_send_far, "y", 0)
    a1n, b1n = exchange(a_send_near, "x", 0), exchange(b_send_near, "y", 0)
    a1f = take(a1f)
    a2f = exchange(a_keep_far[1] + a1f[1], "x", 1)
    b1f = take(b1f)
    total = total + b1f[640:]
    b2f = exchange(under(b_keep_far[320:] + b1f[320:640], total), "y", 1)
    a1n = take(a1n)
    a2n = exchange(a_keep_near[1] + a1n[1], "x", 1)
    b1n = take(b1n)
    b2n = exchange(b_keep_near[320:] + b1n[320:], "y", 1)
    a2f = take(a2f)
    a_far = (a_keep_far[0] + a1f[0]) + a2f
    a3f = exchange(a_far[2:4], "y", 0)
    b2f = take(b2f)
    total = total + b2f[320:]
    b3 = exchange(under((b_keep_far[:320] + b1f[:320]) + b2f[:320], total), "z", 0)
    a2n = take(a2n)
    a_near = (a_keep_near[0] + a1n[0]) + a2n
    a3n = exchange(a_near[2:4], "y", 0)
    b2n = take(b2n)
    b_near = (b_keep_near[:320] + b1n[:320]) + b2n
    b3 = take(b3)
    total = total + b3[320:]
    b4 = exchange(under(b_near[160:] + b3[160:320], total), "z", 1)
    a3f = take(a3f)
    a3n = take(a3n)
    a4 = exchange(jnp.concatenate([a_far[1] + a3f[1], a_near[1] + a3n[1]], axis=0), "y", 1)
    b4 = take(b4)
    total = total + b4[160:]
    b_whole = (b_near[:160] + b3[:160]) + b4[:160]
    b5 = exchange(under(b_whole[80:], total), "x", 0)
    a4 = take(a4)
    a_far, a_near = (a_far[0] + a3f[0]) + a4[:2], (a_near[0] + a3n[0]) + a4[2:]
    a5 = exchange(a_far, "z", 0)
    b5 = take(b5)
    total = total + b5[80:]
    b6 = exchange(under(b_whole[40:80] + b5[40:80], total), "x", 1)
    a5 = take(a5)
    a6 = exchange(a_near[1] + a5[1], "z", 1)
    b6, a6, c = together([b6, a6, c])
    a = (a_near[0] + a5[0]) + a6
    b = (b_whole[:40] + b5[:40]) + b6[:40]
    total = (total + b6[40:])[0, 0]
    return jnp.concatenate([a / total, b / total, c / total], axis=1)


def solution(mesh):
    in_specs = (
        P(("section", "dp"), None, None, None),
        P(("section", "dp"), None, None, None),
        P(),
        P("dp"),
        P("dp", None),
    )
    out_specs = P(("section", "dp"), None)
    return jax.shard_map(shards, mesh=mesh, in_specs=in_specs, out_specs=out_specs, check_vma=False)
```

time: 163 us -> 216 us (1.33)
  waiting for transfers between devices: 87.3 us -> 121 us
  between operations: 2.92 us -> 16.3 us
  starting transfers between devices: 39.4 us -> 26.8 us
  other arithmetic: 3.8 us -> 11.6 us
  Pallas kernels: 27.9 us -> 33.2 us
  local copies, waits for them, and re-layouts: 1.94 us -> 7.09 us
    optimization_barrier x0 -> x1, waiting for transfers between devices: none -> 33.3 us  [together(): return list(lax.optimization_barrier(tuple(values)))]
    ppermute x23 -> x17, starting transfers between devices: 39.4 us -> 26.8 us  [exchange(): return lax.ppermute(value, ('section', 'dp'), pairs)]
    pallas_call x2 -> x3, Pallas kernels: 27.9 us -> 33.2 us  [call(): pl.pallas_call(kernel, out_shape=[pltpu.HBM(shape, jnp.float32) if out_sp...]
    add x17 -> x12, other arithmetic: 1.84 us -> 5.46 us  [the longest x1 1.76 us: shards(): b_near = b_keep_near[:320] + b1n[:320] + b2n]
    unnamed x4 -> x14, local copies, waits for them, and re-layouts: 0.65 us -> 4.2 us
    ppermute x23 -> x17, waiting for transfers between devices: 87.3 us -> 87.3 us  [exchange(): return lax.ppermute(value, ('section', 'dp'), pairs)]
  transfers between devices with their start and end apart: 23 -> 19, of which waited for: 10 -> 10; matrix products, arithmetic and copies ran while one was open for 2% -> 6% of each run, Pallas kernels for 9% -> 10%
where the time goes in v5:
time: 216 us
  waiting for transfers between devices  121 us (56%)
  Pallas kernels  33.2 us (15%)
  starting transfers between devices  26.8 us (12%)
  between operations  16.3 us (8%)
  other arithmetic  11.6 us (5%)
  local copies, waits for them, and re-layouts  7.09 us (3%)
    ppermute x17, waiting for transfers between devices, exchange(): return lax.ppermute(value, ('section', 'dp'), pairs)  87.3 us
    optimization_barrier x1, waiting for transfers between devices, together(): return list(lax.optimization_barrier(tuple(values)))  33.3 us
    pallas_call x3, Pallas kernels, call(): pl.pallas_call(kernel, out_shape=[pltpu.HBM(shape, jnp.float32) if out_sp...  33.2 us
    ppermute x17, starting transfers between devices, exchange(): return lax.ppermute(value, ('section', 'dp'), pairs)  26.8 us
  transfers between devices with their start and end apart: 19, of which 10 were waited for; matrix products, arithmetic and copies ran while one was open for 6% of the time, Pallas kernels for 10%

profile of v5, /device:TPU:0, one launch (start us, length us, event | category | flops | bytes accessed | tf_op | source)
XLA Modules:
  0.0 215.7 jit_solution(11298051643955647496)
XLA Ops:
  8.5 11.4 %shard_map.55 = f32[2560,768]{1,0:T(8,128)} custom-call(s32[1]{0:T(128)S(6)} %copy.6.failed, s32[1]{0:T(128)S(6)} %copy.7.counts, s32[1,6]{1,0:T(1,128)S(1)} %copy-done, bf16[1,6,192,2560]{3,2,1,0:T(8,128)(2,1)} %act.3, bf16[1,6,192,2560]{3,2,1,0:T(8,128)(2,1)} %cot.3), custom_call_target="tpu_custom_call" | custom-call | flops 1024 | bytes 1024 | tf_op jit(solution)/shard_map/pallas_call | solution.py:97
  20.5 10.9 %shard_map.56 = (f32[2,4,2,40,896]{4,3,2,1,0:T(8,128)S(1)}, f32[2,4,2,40,896]{4,3,2,1,0:T(8,128)S(1)}, f32[640,896]{1,0:T(8,128)S(1)}, f32[648,896]{1,0:T(8,128)S(1)}, f32[8,896]{1,0:T(8,128)S(1)}) custom-call(s32[1]{0:T(128)S(6)} %copy.6.failed, s32[1]{0:T(128)S(6)} %copy.7.counts, s32[1,6]{1,0:T(1,128)S(1)} %copy-done.1, bf16[1,6,192,2560]{3,2,1,0:T(8,128)(2,1)} %act.3, ...), custom_call_target="tpu_custom_call" | custom-call | flops 1024 | bytes 1024 | tf_op jit(solution)/shard_map/pallas_call | solution.py:97
  31.5 1.7 collective-permute-start.1
  33.2 1.5 collective-permute-start.2
  34.7 10.9 %shard_map.57 = (f32[2,4,2,40,896]{4,3,2,1,0:T(8,128)S(1)}, f32[2,4,2,40,896]{4,3,2,1,0:T(8,128)S(1)}, f32[640,896]{1,0:T(8,128)S(1)}, f32[640,896]{1,0:T(8,128)S(1)}) custom-call(s32[1]{0:T(128)S(6)} %copy.6.failed, s32[1]{0:T(128)S(6)} %copy.7.counts, s32[1,6]{1,0:T(1,128)S(1)} %copy-done.1, bf16[1,6,192,2560]{3,2,1,0:T(8,128)(2,1)} %act.3, ...), custom_call_target="tpu_custom_call" | custom-call | flops 1024 | bytes 1024 | tf_op jit(solution)/shard_map/pallas_call | solution.py:97
  46.7 14.7 %collective-permute-done.2 = f32[2,4,2,40,896]{4,3,2,1,0:T(8,128)S(1)} collective-permute-done((f32[2,4,2,40,896]{4,3,2,1,0:T(8,128)S(1)}, f32[2,4,2,40,896]{4,3,2,1,0:T(8,128)S(1)}, u32[]{:S(2)}, u32[]{:S(2)}) %collective-permute-start.2) | collective-permute-done | bytes 2293792 | tf_op jit(solution)/shard_map/ppermute | solution.py:24
  61.6 2.3 %collective-permute-start.4 = (f32[328,896]{1,0:T(8,128)S(1)}, f32[328,896]{1,0:T(8,128)S(1)}, u32[]{:S(2)}, u32[]{:S(2)}) collective-permute-start(f32[328,896]{1,0:T(8,128)S(1)} %pad_maximum_fusion), channel_id=1, source_target_pairs={{0,12},{1,13},{2,14},{3,15},{4,8},{5,9},{6,10},{7,11},{8,4},{9,5},... | collective-permute-start | bytes 3526664 | tf_op jit(solution)/shard_map/ppermute | solution.py:24
  64.0 2.8 %collective-permute-start.5 = (f32[4,2,40,896]{3,2,1,0:T(8,128)S(1)}, f32[4,2,40,896]{3,2,1,0:T(8,128)S(1)}, u32[]{:S(2)}, u32[]{:S(2)}) collective-permute-start(f32[4,2,40,896]{3,2,1,0:T(8,128)S(1)} %fusion.2), channel_id=1, source_target_pairs={{0,3},{1,2},{2,1},{3,0},{4,7},{5,6},{6,5},{7,4},{8,11},{9,10},{10,... | collective-permute-start | bytes 3440648 | tf_op jit(solution)/shard_map/ppermute | solution.py:24
  66.8 31.4 %collective-permute-done = f32[2,4,2,40,896]{4,3,2,1,0:T(8,128)S(1)} collective-permute-done((f32[2,4,2,40,896]{4,3,2,1,0:T(8,128)S(1)}, f32[2,4,2,40,896]{4,3,2,1,0:T(8,128)S(1)}, u32[]{:S(2)}, u32[]{:S(2)}) %collective-permute-start) | collective-permute-done | bytes 2293792 | tf_op jit(solution)/shard_map/ppermute | solution.py:24
  98.4 2.8 %collective-permute-start.3 = (f32[4,2,40,896]{3,2,1,0:T(8,128)S(1)}, f32[4,2,40,896]{3,2,1,0:T(8,128)S(1)}, u32[]{:S(2)}, u32[]{:S(2)}) collective-permute-start(f32[4,2,40,896]{3,2,1,0:T(8,128)S(1)} %add_bitcast_fusion), channel_id=1, source_target_pairs={{0,3},{1,2},{2,1},{3,0},{4,7},{5,6},{6,5},{7,4},{8,11},{9,10},{10,... | collective-permute-start | bytes 3440648 | tf_op jit(solution)/shard_map/ppermute | solution.py:24
  101.4 1.3 copy-done.4
  102.7 2.2 %collective-permute-start.10 = (f32[320,896]{1,0:T(8,128)S(1)}, f32[320,896]{1,0:T(8,128)}, u32[]{:S(2)}, u32[]{:S(2)}) collective-permute-start(f32[320,896]{1,0:T(8,128)S(1)} %slice_add_fusion.2), channel_id=1, source_target_pairs={{0,12},{1,13},{2,14},{3,15},{4,8},{5,9},{6,10},{7,11},{8,4},{9,5},... | collective-permute-start | bytes 3440648 | tf_op jit(solution)/shard_map/ppermute | solution.py:24
  105.1 1.1 pad_maximum_fusion.1
  106.2 1.9 collective-permute-start.9
  108.3 0.9 slice.208
  109.9 5.6 %collective-permute-done.3 = f32[4,2,40,896]{3,2,1,0:T(8,128)S(1)} collective-permute-done((f32[4,2,40,896]{3,2,1,0:T(8,128)S(1)}, f32[4,2,40,896]{3,2,1,0:T(8,128)S(1)}, u32[]{:S(2)}, u32[]{:S(2)}) %collective-permute-start.3) | collective-permute-done | bytes 1146912 | tf_op jit(solution)/shard_map/ppermute | solution.py:24
  115.7 1.0 copy-done.2
  116.7 0.9 slice.206
  118.0 10.1 %collective-permute-done.10 = f32[320,896]{1,0:T(8,128)} collective-permute-done((f32[320,896]{1,0:T(8,128)S(1)}, f32[320,896]{1,0:T(8,128)}, u32[]{:S(2)}, u32[]{:S(2)}) %collective-permute-start.10) | collective-permute-done | bytes 1146912 | tf_op jit(solution)/shard_map/ppermute | solution.py:24
  128.1 1.8 add_add_fusion
  130.6 1.2 slice_add_fusion.6
  131.9 7.1 %collective-permute-start.12 = (f32[168,896]{1,0:T(8,128)S(1)}, f32[168,896]{1,0:T(8,128)S(1)}, u32[]{:S(2)}, u32[]{:S(2)}) collective-permute-start(f32[168,896]{1,0:T(8,128)S(1)} %pad_maximum_fusion.2), channel_id=1, source_target_pairs={{0,48},{1,49},{2,50},{3,51},{4,52},{5,53},{6,54},{7,55},{8,56},{9,... | collective-permute-start | bytes 1806344 | tf_op jit(solution)/shard_map/ppermute | solution.py:24
  139.0 1.2 fusion.6
  140.3 2.0 collective-permute-start.11
  142.3 4.7 %collective-permute-done.12 = f32[168,896]{1,0:T(8,128)S(1)} collective-permute-done((f32[168,896]{1,0:T(8,128)S(1)}, f32[168,896]{1,0:T(8,128)S(1)}, u32[]{:S(2)}, u32[]{:S(2)}) %collective-permute-start.12) | collective-permute-done | bytes 602144 | tf_op jit(solution)/shard_map/ppermute | solution.py:24
  147.0 5.6 %collective-permute-done.11 = f32[4,40,896]{2,1,0:T(8,128)S(1)} collective-permute-done((f32[4,40,896]{2,1,0:T(8,128)S(1)}, f32[4,40,896]{2,1,0:T(8,128)S(1)}, u32[]{:S(2)}, u32[]{:S(2)}) %collective-permute-start.11) | collective-permute-done | bytes 573472 | tf_op jit(solution)/shard_map/ppermute | solution.py:24
  152.7 1.2 fusion.3
  154.0 1.1 fusion.5
  155.2 8.6 %collective-permute-done.14 = f32[88,896]{1,0:T(8,128)S(1)} collective-permute-done((f32[88,896]{1,0:T(8,128)S(1)}, f32[88,896]{1,0:T(8,128)S(1)}, u32[]{:S(2)}, u32[]{:S(2)}) %collective-permute-start.14) | collective-permute-done | bytes 315424 | tf_op jit(solution)/shard_map/ppermute | solution.py:24
  165.3 5.7 %collective-permute-done.16 = f32[40,896]{1,0:T(8,128)S(1)} collective-permute-done((f32[40,896]{1,0:T(8,128)S(1)}, f32[40,896]{1,0:T(8,128)S(1)}, u32[]{:S(2)}, u32[]{:S(2)}) %collective-permute-start.16) | collective-permute-done | bytes 143392 | tf_op jit(solution)/shard_map/ppermute | solution.py:24
  171.8 33.3 %reduce-scatter.7.cloned.1.call-done = f32[40,768]{1,0:T(8,128)} async-done(((f32[640,768]{1,0:T(8,128)}), f32[40,768]{1,0:T(8,128)}) %reduce-scatter.7.cloned.1.call-update) | async-done | bytes 122896 | tf_op jit(solution)/shard_map/optimization_barrier | solution.py:133
  207.0 0.9 fusion.11
  (59 shorter events, 9.4 us)
Async XLA Ops:
  6.5 121.5 %reduce-scatter.5.cloned.1.call-start = ((), (), s32[]{:S(2)}) async-start(), calls=%async_computation.2 | async-start | bytes 9830400 | tf_op jit(solution)/shard_map/reduce_scatter | solution.py:139
  7.8 0.7 copy-start
  19.9 0.7 copy-start.1
  19.9 185.2 %reduce-scatter.7.cloned.1.call-start = ((), (), s32[]{:S(2)}) async-start(), calls=%async_computation.3 | async-start | bytes 2088960
  31.5 29.9 %collective-permute-start.1 = (f32[648,896]{1,0:T(8,128)S(1)}, f32[648,896]{1,0:T(8,128)S(1)}, u32[]{:S(2)}, u32[]{:S(2)}) collective-permute-start(f32[648,896]{1,0:T(8,128)S(1)} %get-tuple-element.52), channel_id=1, source_target_pairs={{0,4},{1,5},{2,6},{3,7},{4,0},{5,1},{6,2},{7,3},{8,12},{9,13},{10,... | collective-permute-start | bytes 6967304 | tf_op jit(solution)/shard_map/ppermute | solution.py:24
  33.2 28.1 %collective-permute-start.2 = (f32[2,4,2,40,896]{4,3,2,1,0:T(8,128)S(1)}, f32[2,4,2,40,896]{4,3,2,1,0:T(8,128)S(1)}, u32[]{:S(2)}, u32[]{:S(2)}) collective-permute-start(f32[2,4,2,40,896]{4,3,2,1,0:T(8,128)S(1)} %get-tuple-element.53), channel_id=1, source_target_pairs={{0,1},{1,0},{2,3},{3,2},{4,5},{5,4},{6,7},{7,6},{8,9},{9,8},{10,11... | collective-permute-start | bytes 6881288 | tf_op jit(solution)/shard_map/ppermute | solution.py:24
  45.6 52.6 %collective-permute-start = (f32[2,4,2,40,896]{4,3,2,1,0:T(8,128)S(1)}, f32[2,4,2,40,896]{4,3,2,1,0:T(8,128)S(1)}, u32[]{:S(2)}, u32[]{:S(2)}) collective-permute-start(f32[2,4,2,40,896]{4,3,2,1,0:T(8,128)S(1)} %get-tuple-element.51), channel_id=1, source_target_pairs={{0,1},{1,0},{2,3},{3,2},{4,5},{5,4},{6,7},{7,6},{8,9},{9,8},{10,11... | collective-permute-start | bytes 6881288 | tf_op jit(solution)/shard_map/ppermute | solution.py:24
  46.3 55.0 %collective-permute-start.6 = (f32[640,896]{1,0:T(8,128)S(1)}, f32[640,896]{1,0:T(8,128)S(1)}, u32[]{:S(2)}, u32[]{:S(2)}) collective-permute-start(f32[640,896]{1,0:T(8,128)S(1)} %get-tuple-element.59), channel_id=1, source_target_pairs={{0,4},{1,5},{2,6},{3,7},{4,0},{5,1},{6,2},{7,3},{8,12},{9,13},{10,... | collective-permute-start | bytes 6881288 | tf_op jit(solution)/shard_map/ppermute | solution.py:24
  61.6 43.3 %collective-permute-start.4 = (f32[328,896]{1,0:T(8,128)S(1)}, f32[328,896]{1,0:T(8,128)S(1)}, u32[]{:S(2)}, u32[]{:S(2)}) collective-permute-start(f32[328,896]{1,0:T(8,128)S(1)} %pad_maximum_fusion), channel_id=1, source_target_pairs={{0,12},{1,13},{2,14},{3,15},{4,8},{5,9},{6,10},{7,11},{8,4},{9,5},... | collective-permute-start | bytes 3526664 | tf_op jit(solution)/shard_map/ppermute | solution.py:24
  64.0 40.9 %collective-permute-start.5 = (f32[4,2,40,896]{3,2,1,0:T(8,128)S(1)}, f32[4,2,40,896]{3,2,1,0:T(8,128)S(1)}, u32[]{:S(2)}, u32[]{:S(2)}) collective-permute-start(f32[4,2,40,896]{3,2,1,0:T(8,128)S(1)} %fusion.2), channel_id=1, source_target_pairs={{0,3},{1,2},{2,1},{3,0},{4,7},{5,6},{6,5},{7,4},{8,11},{9,10},{10,... | collective-permute-start | bytes 3440648 | tf_op jit(solution)/shard_map/ppermute | solution.py:24
  98.4 17.1 %collective-permute-start.3 = (f32[4,2,40,896]{3,2,1,0:T(8,128)S(1)}, f32[4,2,40,896]{3,2,1,0:T(8,128)S(1)}, u32[]{:S(2)}, u32[]{:S(2)}) collective-permute-start(f32[4,2,40,896]{3,2,1,0:T(8,128)S(1)} %add_bitcast_fusion), channel_id=1, source_target_pairs={{0,3},{1,2},{2,1},{3,0},{4,7},{5,6},{6,5},{7,4},{8,11},{9,10},{10,... | collective-permute-start | bytes 3440648 | tf_op jit(solution)/shard_map/ppermute | solution.py:24
  101.2 1.5 copy-start.4
  102.7 25.4 %collective-permute-start.10 = (f32[320,896]{1,0:T(8,128)S(1)}, f32[320,896]{1,0:T(8,128)}, u32[]{:S(2)}, u32[]{:S(2)}) collective-permute-start(f32[320,896]{1,0:T(8,128)S(1)} %slice_add_fusion.2), channel_id=1, source_target_pairs={{0,12},{1,13},{2,14},{3,15},{4,8},{5,9},{6,10},{7,11},{8,4},{9,5},... | collective-permute-start | bytes 3440648 | tf_op jit(solution)/shard_map/ppermute | solution.py:24
  106.2 23.6 %collective-permute-start.9 = (f32[328,896]{1,0:T(8,128)}, f32[328,896]{1,0:T(8,128)}, u32[]{:S(2)}, u32[]{:S(2)}) collective-permute-start(f32[328,896]{1,0:T(8,128)} %pad_maximum_fusion.1), channel_id=1, source_target_pairs={{0,16},{1,17},{2,18},{3,19},{4,20},{5,21},{6,22},{7,23},{8,24},{9,... | collective-permute-start | bytes 3526664 | tf_op jit(solution)/shard_map/ppermute | solution.py:24
  109.2 20.7 %collective-permute-start.8 = (f32[2,2,40,896]{3,2,1,0:T(8,128)}, f32[2,2,40,896]{3,2,1,0:T(8,128)}, u32[]{:S(2)}, u32[]{:S(2)}) collective-permute-start(f32[2,2,40,896]{3,2,1,0:T(8,128)} %slice.208), channel_id=1, source_target_pairs={{0,4},{1,5},{2,6},{3,7},{4,0},{5,1},{6,2},{7,3},{8,12},{9,13},{10,... | collective-permute-start | bytes 1720328 | tf_op jit(solution)/shard_map/ppermute | solution.py:24
  115.7 1.0 copy-start.2
  117.6 12.3 %collective-permute-start.7 = (f32[2,2,40,896]{3,2,1,0:T(8,128)}, f32[2,2,40,896]{3,2,1,0:T(8,128)}, u32[]{:S(2)}, u32[]{:S(2)}) collective-permute-start(f32[2,2,40,896]{3,2,1,0:T(8,128)} %slice.206), channel_id=1, source_target_pairs={{0,4},{1,5},{2,6},{3,7},{4,0},{5,1},{6,2},{7,3},{8,12},{9,13},{10,... | collective-permute-start | bytes 1720328 | tf_op jit(solution)/shard_map/ppermute | solution.py:24
  130.6 8.4 %copy-start.3 = (f32[4,2,40,896]{3,2,1,0:T(8,128)S(1)}, f32[4,2,40,896]{3,2,1,0:T(8,128)}, u32[]{:S(2)}) copy-start(f32[4,2,40,896]{3,2,1,0:T(8,128)} %copy-done.2) | copy-start | bytes 3440644
  131.9 15.1 %collective-permute-start.12 = (f32[168,896]{1,0:T(8,128)S(1)}, f32[168,896]{1,0:T(8,128)S(1)}, u32[]{:S(2)}, u32[]{:S(2)}) collective-permute-start(f32[168,896]{1,0:T(8,128)S(1)} %pad_maximum_fusion.2), channel_id=1, source_target_pairs={{0,48},{1,49},{2,50},{3,51},{4,52},{5,53},{6,54},{7,55},{8,56},{9,... | collective-permute-start | bytes 1806344 | tf_op jit(solution)/shard_map/ppermute | solution.py:24
  140.3 12.4 %collective-permute-start.11 = (f32[4,40,896]{2,1,0:T(8,128)S(1)}, f32[4,40,896]{2,1,0:T(8,128)S(1)}, u32[]{:S(2)}, u32[]{:S(2)}) collective-permute-start(f32[4,40,896]{2,1,0:T(8,128)S(1)} %pad_maximum_fusion.3), channel_id=1, source_target_pairs={{0,12},{1,13},{2,14},{3,15},{4,8},{5,9},{6,10},{7,11},{8,4},{9,5},... | collective-permute-start | bytes 1720328 | tf_op jit(solution)/shard_map/ppermute | solution.py:24
  153.9 9.9 %collective-permute-start.14 = (f32[88,896]{1,0:T(8,128)S(1)}, f32[88,896]{1,0:T(8,128)S(1)}, u32[]{:S(2)}, u32[]{:S(2)}) collective-permute-start(f32[88,896]{1,0:T(8,128)S(1)} %pad_maximum_fusion.5), channel_id=1, source_target_pairs={{0,1},{1,0},{2,3},{3,2},{4,5},{5,4},{6,7},{7,6},{8,9},{9,8},{10,11... | collective-permute-start | bytes 946184 | tf_op jit(solution)/shard_map/ppermute | solution.py:24
  155.2 8.7 %collective-permute-start.13 = (f32[2,40,896]{2,1,0:T(8,128)S(1)}, f32[2,40,896]{2,1,0:T(8,128)S(1)}, u32[]{:S(2)}, u32[]{:S(2)}) collective-permute-start(f32[2,40,896]{2,1,0:T(8,128)S(1)} %get-tuple-element.77), channel_id=1, source_target_pairs={{0,16},{1,17},{2,18},{3,19},{4,20},{5,21},{6,22},{7,23},{8,24},{9,... | collective-permute-start | bytes 860168 | tf_op jit(solution)/shard_map/ppermute | solution.py:24
  163.8 0.7 copy-start.5
  164.6 7.2 %collective-permute-start.15 = (f32[48,896]{1,0:T(8,128)S(1)}, f32[48,896]{1,0:T(8,128)S(1)}, u32[]{:S(2)}, u32[]{:S(2)}) collective-permute-start(f32[48,896]{1,0:T(8,128)S(1)} %pad_maximum_fusion.6), channel_id=1, source_target_pairs={{0,3},{1,2},{2,1},{3,0},{4,7},{5,6},{6,5},{7,4},{8,11},{9,10},{10,... | collective-permute-start | bytes 516104 | tf_op jit(solution)/shard_map/ppermute | solution.py:24
  164.6 6.4 %collective-permute-start.16 = (f32[40,896]{1,0:T(8,128)S(1)}, f32[40,896]{1,0:T(8,128)S(1)}, u32[]{:S(2)}, u32[]{:S(2)}) collective-permute-start(f32[40,896]{1,0:T(8,128)S(1)} %fusion.12), channel_id=1, source_target_pairs={{0,48},{1,49},{2,50},{3,51},{4,52},{5,53},{6,54},{7,55},{8,56},{9,... | collective-permute-start | bytes 430088 | tf_op jit(solution)/shard_map/ppermute | solution.py:24
  205.1 2.9 %copy-start.6 = (f32[40,768]{1,0:T(8,128)S(1)}, f32[40,768]{1,0:T(8,128)}, u32[]{:S(2)}) copy-start(f32[40,768]{1,0:T(8,128)} %reduce-scatter.7.cloned.1.call-done) | copy-start | bytes 368644
Sparse Core Ops, SparseCore 0:
  20.0 79.4 reduce-scatter.4
  128.2 76.8 reduce-scatter.6

commit v6 on v4

--- a/solution.py
+++ b/solution.py
@@ -130,13 +130,12 @@
     a2n = exchange(a_keep_near[1] + a1n[1], "x", 1)
     b1n = take(b1n)
     b2n = exchange(b_keep_near[1] + b1n[1], "y", 1)
-    a2f = take(a2f)
+    a2f, b2f, c2, _ = together([a2f, b2f, c2, taken])
+    taken = c2
     a_far = (a_keep_far[0] + a1f[0]) + a2f
     a3f = exchange(a_far[2:4], "y", 0)
-    b2f = take(b2f)
     b_far = (b_keep_far[0] + b1f[0]) + b2f
     b3 = exchange(b_far, "z", 0)
-    c2 = take(c2)
     c_whole, c_total = c_stay + c2[:TILE], c_total + c2[TILE:]
     c3 = exchange(jnp.concatenate([c_whole[320:], c_total], axis=0), "x", 0)
     a2n = take(a2n)
@@ -144,12 +143,12 @@
     a3n = exchange(a_near[2:4], "y", 0)
     b2n = take(b2n)
     b_near = (b_keep_near[0] + b1n[0]) + b2n
-    a3f = take(a3f)
     b3 = take(b3)
     b4 = exchange(b_near[1] + b3[1], "z", 1)
     c3 = take(c3)
     c_out, c_stay, c_total = both(c_whole[:320], c3, c_total, 160)
     c4 = exchange(c_out, "x", 1)
+    a3f = take(a3f)
     a3n = take(a3n)
     a4 = exchange(jnp.concatenate([a_far[1] + a3f[1], a_near[1] + a3n[1]], axis=0), "y", 1)
     b4 = take(b4)

time: 163 us -> 146 us (0.90); the launches traced: 163 us -> 144 us
  waiting for transfers between devices: 87.3 us -> 69.1 us
    ppermute x23, waiting for transfers between devices: 87.3 us -> 69.1 us  [exchange(): return lax.ppermute(value, ('section', 'dp'), pairs)]
  transfers between devices with their start and end apart: 23 -> 23, of which waited for: 10 -> 19; matrix products, arithmetic and copies ran while one was open for 2% -> 3% of each run, Pallas kernels for 9% -> 10%
where the time goes in v6:
time: 146 us; the launch traced here: 144 us
  waiting for transfers between devices  69.1 us (47%)
  starting transfers between devices  38.7 us (27%)
  Pallas kernels  27.9 us (19%)
  other arithmetic  3.84 us (3%)
  between operations  2.86 us (2%)
  local copies, waits for them, and re-layouts  1.93 us (1%)
    ppermute x23, waiting for transfers between devices, exchange(): return lax.ppermute(value, ('section', 'dp'), pairs)  69.1 us
    ppermute x23, starting transfers between devices, exchange(): return lax.ppermute(value, ('section', 'dp'), pairs)  38.7 us
    pallas_call x2, Pallas kernels, partials(): pl.pallas_call(functools.partial(products, half), out_shape=[jax.ShapeDty...  27.9 us
  transfers between devices with their start and end apart: 23, of which 19 were waited for; matrix products, arithmetic and copies ran while one was open for 3% of the time, Pallas kernels for 10%

profile of v6, /device:TPU:0, one launch (start us, length us, event | category | flops | bytes accessed | tf_op | source)
XLA Modules:
  0.0 144.4 jit_solution(7523686428619795683)
XLA Ops:
  2.0 14.0 %shard_map.55 = (f32[2,4,2,40,896]{4,3,2,1,0:T(8,128)S(1)}, f32[2,4,2,40,896]{4,3,2,1,0:T(8,128)S(1)}, f32[2,2,4,40,896]{4,3,2,1,0:T(8,128)S(1)}, f32[2,2,4,40,8...) custom-call(s32[1]{0:T(128)S(6)} %copy.6.failed, s32[1]{0:T(128)S(6)} %copy.7.counts, ...), custom_call_target="tpu_custom_call" | custom-call | flops 1024 | bytes 1024 | tf_op jit(solution)/shard_map/pallas_call | solution.py:84
  15.9 2.1 %collective-permute-start.1 = (f32[1288,768]{1,0:T(8,128)S(1)}, f32[1288,768]{1,0:T(8,128)S(1)}, u32[]{:S(2)}, u32[]{:S(2)}) collective-permute-start(f32[1288,768]{1,0:T(8,128)S(1)} %get-tuple-element.56), channel_id=1, source_target_pairs={{0,16},{1,17},{2,18},{3,19},{4,20},{5,21},{6,22},{7,23},{8,24},{9,... | collective-permute-start | bytes 11870216 | tf_op jit(solution)/shard_map/ppermute | solution.py:24
  18.0 1.5 %collective-permute-start.3 = (f32[2,4,2,40,896]{4,3,2,1,0:T(8,128)S(1)}, f32[2,4,2,40,896]{4,3,2,1,0:T(8,128)S(1)}, u32[]{:S(2)}, u32[]{:S(2)}) collective-permute-start(f32[2,4,2,40,896]{4,3,2,1,0:T(8,128)S(1)} %get-tuple-element.58), channel_id=1, source_target_pairs={{0,1},{1,0},{2,3},{3,2},{4,5},{5,4},{6,7},{7,6},{8,9},{9,8},{10,11... | collective-permute-start | bytes 6881288 | tf_op jit(solution)/shard_map/ppermute | solution.py:24
  19.5 1.6 %collective-permute-start.2 = (f32[2,2,4,40,896]{4,3,2,1,0:T(8,128)S(1)}, f32[2,2,4,40,896]{4,3,2,1,0:T(8,128)S(1)}, u32[]{:S(2)}, u32[]{:S(2)}) collective-permute-start(f32[2,2,4,40,896]{4,3,2,1,0:T(8,128)S(1)} %get-tuple-element.57), channel_id=1, source_target_pairs={{0,4},{1,5},{2,6},{3,7},{4,0},{5,1},{6,2},{7,3},{8,12},{9,13},{10,... | collective-permute-start | bytes 6881288 | tf_op jit(solution)/shard_map/ppermute | solution.py:24
  21.1 14.0 %shard_map.56 = (f32[2,4,2,40,896]{4,3,2,1,0:T(8,128)S(1)}, f32[2,4,2,40,896]{4,3,2,1,0:T(8,128)S(1)}, f32[2,2,4,40,896]{4,3,2,1,0:T(8,128)S(1)}, f32[2,2,4,40,896]{4,3,2,1,0:T(8,128)S(1)}, f32[1280,768]{1,0:T(8,128)S(1)}) custom-call(s32[1]{0:T(128)S(6)} %copy.6.failed, s32[1]{0:T(128)S(6)} %copy.7.counts, s32[1,6]{1,0:T(1,128)S(1)} %copy-done.1, ...), custom_call_target="tpu_custom_call" | custom-call | flops 1024 | bytes 1024 | tf_op jit(solution)/shard_map/pallas_call | solution.py:84
  36.1 10.0 %collective-permute-done.3 = f32[2,4,2,40,896]{4,3,2,1,0:T(8,128)S(1)} collective-permute-done((f32[2,4,2,40,896]{4,3,2,1,0:T(8,128)S(1)}, f32[2,4,2,40,896]{4,3,2,1,0:T(8,128)S(1)}, u32[]{:S(2)}, u32[]{:S(2)}) %collective-permute-start.3) | collective-permute-done | bytes 2293792 | tf_op jit(solution)/shard_map/ppermute | solution.py:24
  46.1 1.5 %collective-permute-done.2 = f32[2,2,4,40,896]{4,3,2,1,0:T(8,128)S(1)} collective-permute-done((f32[2,2,4,40,896]{4,3,2,1,0:T(8,128)S(1)}, f32[2,2,4,40,896]{4,3,2,1,0:T(8,128)S(1)}, u32[]{:S(2)}, u32[]{:S(2)}) %collective-permute-start.2) | collective-permute-done | bytes 2293792 | tf_op jit(solution)/shard_map/ppermute | solution.py:24
  47.6 14.3 %collective-permute-done.1 = f32[1288,768]{1,0:T(8,128)S(1)} collective-permute-done((f32[1288,768]{1,0:T(8,128)S(1)}, f32[1288,768]{1,0:T(8,128)S(1)}, u32[]{:S(2)}, u32[]{:S(2)}) %collective-permute-start.1) | collective-permute-done | bytes 3956768 | tf_op jit(solution)/shard_map/ppermute | solution.py:24
  62.5 4.2 %collective-permute-start.7 = (f32[648,768]{1,0:T(8,128)S(1)}, f32[648,768]{1,0:T(8,128)S(1)}, u32[]{:S(2)}, u32[]{:S(2)}) collective-permute-start(f32[648,768]{1,0:T(8,128)S(1)} %pad_maximum_fusion), channel_id=1, source_target_pairs={{0,48},{1,49},{2,50},{3,51},{4,52},{5,53},{6,54},{7,55},{8,56},{9,... | collective-permute-start | bytes 5971976 | tf_op jit(solution)/shard_map/ppermute | solution.py:24
  66.8 3.1 %collective-permute-start.6 = (f32[2,4,40,896]{3,2,1,0:T(8,128)S(1)}, f32[2,4,40,896]{3,2,1,0:T(8,128)S(1)}, u32[]{:S(2)}, u32[]{:S(2)}) collective-permute-start(f32[2,4,40,896]{3,2,1,0:T(8,128)S(1)} %add_bitcast_fusion.1), channel_id=1, source_target_pairs={{0,12},{1,13},{2,14},{3,15},{4,8},{5,9},{6,10},{7,11},{8,4},{9,5},... | collective-permute-start | bytes 3440648 | tf_op jit(solution)/shard_map/ppermute | solution.py:24
  70.0 2.8 %collective-permute-start.5 = (f32[4,2,40,896]{3,2,1,0:T(8,128)S(1)}, f32[4,2,40,896]{3,2,1,0:T(8,128)S(1)}, u32[]{:S(2)}, u32[]{:S(2)}) collective-permute-start(f32[4,2,40,896]{3,2,1,0:T(8,128)S(1)} %fusion.2), channel_id=1, source_target_pairs={{0,3},{1,2},{2,1},{3,0},{4,7},{5,6},{6,5},{7,4},{8,11},{9,10},{10,... | collective-permute-start | bytes 3440648 | tf_op jit(solution)/shard_map/ppermute | solution.py:24
  73.4 4.5 %collective-permute-done.8 = f32[2,2,4,40,896]{4,3,2,1,0:T(8,128)S(1)} collective-permute-done((f32[2,2,4,40,896]{4,3,2,1,0:T(8,128)S(1)}, f32[2,2,4,40,896]{4,3,2,1,0:T(8,128)S(1)}, u32[]{:S(2)}, u32[]{:S(2)}) %collective-permute-start.8) | collective-permute-done | bytes 2293792 | tf_op jit(solution)/shard_map/ppermute | solution.py:24
  78.0 1.5 %collective-permute-start.4 = (f32[4,2,40,896]{3,2,1,0:T(8,128)S(1)}, f32[4,2,40,896]{3,2,1,0:T(8,128)S(1)}, u32[]{:S(2)}, u32[]{:S(2)}) collective-permute-start(f32[4,2,40,896]{3,2,1,0:T(8,128)S(1)} %add_bitcast_fusion.2), channel_id=1, source_target_pairs={{0,3},{1,2},{2,1},{3,0},{4,7},{5,6},{6,5},{7,4},{8,11},{9,10},{10,... | collective-permute-start | bytes 3440648 | tf_op jit(solution)/shard_map/ppermute | solution.py:24
  79.7 3.1 %collective-permute-start.13 = (f32[2,4,40,896]{3,2,1,0:T(8,128)S(1)}, f32[2,4,40,896]{3,2,1,0:T(8,128)S(1)}, u32[]{:S(2)}, u32[]{:S(2)}) collective-permute-start(f32[2,4,40,896]{3,2,1,0:T(8,128)S(1)} %add_bitcast_fusion), channel_id=1, source_target_pairs={{0,12},{1,13},{2,14},{3,15},{4,8},{5,9},{6,10},{7,11},{8,4},{9,5},... | collective-permute-start | bytes 3440648 | tf_op jit(solution)/shard_map/ppermute | solution.py:24
  82.8 4.7 %collective-permute-done.6 = f32[2,4,40,896]{3,2,1,0:T(8,128)S(1)} collective-permute-done((f32[2,4,40,896]{3,2,1,0:T(8,128)S(1)}, f32[2,4,40,896]{3,2,1,0:T(8,128)S(1)}, u32[]{:S(2)}, u32[]{:S(2)}) %collective-permute-start.6) | collective-permute-done | bytes 1146912 | tf_op jit(solution)/shard_map/ppermute | solution.py:24
  87.5 2.1 %collective-permute-done.7 = f32[648,768]{1,0:T(8,128)S(1)} collective-permute-done((f32[648,768]{1,0:T(8,128)S(1)}, f32[648,768]{1,0:T(8,128)S(1)}, u32[]{:S(2)}, u32[]{:S(2)}) %collective-permute-start.7) | collective-permute-done | bytes 1990688 | tf_op jit(solution)/shard_map/ppermute | solution.py:24
  90.5 1.6 %collective-permute-start.11 = (f32[328,768]{1,0:T(8,128)S(1)}, f32[328,768]{1,0:T(8,128)S(1)}, u32[]{:S(2)}, u32[]{:S(2)}) collective-permute-start(f32[328,768]{1,0:T(8,128)S(1)} %pad_maximum_fusion.1), channel_id=1, source_target_pairs={{0,1},{1,0},{2,3},{3,2},{4,5},{5,4},{6,7},{7,6},{8,9},{9,8},{10,11... | collective-permute-start | bytes 3022856 | tf_op jit(solution)/shard_map/ppermute | solution.py:24
  92.3 1.7 %collective-permute-start.10 = (f32[2,2,40,896]{3,2,1,0:T(8,128)S(1)}, f32[2,2,40,896]{3,2,1,0:T(8,128)S(1)}, u32[]{:S(2)}, u32[]{:S(2)}) collective-permute-start(f32[2,2,40,896]{3,2,1,0:T(8,128)S(1)} %slice.270), channel_id=1, source_target_pairs={{0,4},{1,5},{2,6},{3,7},{4,0},{5,1},{6,2},{7,3},{8,12},{9,13},{10,... | collective-permute-start | bytes 1720328 | tf_op jit(solution)/shard_map/ppermute | solution.py:24
  94.0 9.7 %collective-permute-done.4 = f32[4,2,40,896]{3,2,1,0:T(8,128)S(1)} collective-permute-done((f32[4,2,40,896]{3,2,1,0:T(8,128)S(1)}, f32[4,2,40,896]{3,2,1,0:T(8,128)S(1)}, u32[]{:S(2)}, u32[]{:S(2)}) %collective-permute-start.4) | collective-permute-done | bytes 1146912 | tf_op jit(solution)/shard_map/ppermute | solution.py:24
  104.3 1.4 collective-permute-done.12
  106.2 3.0 %collective-permute-start.16 = (f32[4,40,896]{2,1,0:T(8,128)S(1)}, f32[4,40,896]{2,1,0:T(8,128)S(1)}, u32[]{:S(2)}, u32[]{:S(2)}) collective-permute-start(f32[4,40,896]{2,1,0:T(8,128)S(1)} %fusion.5), channel_id=1, source_target_pairs={{0,48},{1,49},{2,50},{3,51},{4,52},{5,53},{6,54},{7,55},{8,56},{9,... | collective-permute-start | bytes 1720328 | tf_op jit(solution)/shard_map/ppermute | solution.py:24
  109.2 2.8 %collective-permute-start.15 = (f32[168,768]{1,0:T(8,128)S(1)}, f32[168,768]{1,0:T(8,128)S(1)}, u32[]{:S(2)}, u32[]{:S(2)}) collective-permute-start(f32[168,768]{1,0:T(8,128)S(1)} %pad_maximum_fusion.3), channel_id=1, source_target_pairs={{0,3},{1,2},{2,1},{3,0},{4,7},{5,6},{6,5},{7,4},{8,11},{9,10},{10,... | collective-permute-start | bytes 1548296 | tf_op jit(solution)/shard_map/ppermute | solution.py:24
  112.1 1.8 %collective-permute-done.9 = f32[2,2,40,896]{3,2,1,0:T(8,128)S(1)} collective-permute-done((f32[2,2,40,896]{3,2,1,0:T(8,128)S(1)}, f32[2,2,40,896]{3,2,1,0:T(8,128)S(1)}, u32[]{:S(2)}, u32[]{:S(2)}) %collective-permute-start.9) | collective-permute-done | bytes 573472 | tf_op jit(solution)/shard_map/ppermute | solution.py:24
  114.0 1.3 collective-permute-start.14
  115.3 1.9 %collective-permute-done.16 = f32[4,40,896]{2,1,0:T(8,128)S(1)} collective-permute-done((f32[4,40,896]{2,1,0:T(8,128)S(1)}, f32[4,40,896]{2,1,0:T(8,128)S(1)}, u32[]{:S(2)}, u32[]{:S(2)}) %collective-permute-start.16) | collective-permute-done | bytes 573472 | tf_op jit(solution)/shard_map/ppermute | solution.py:24
  117.2 2.4 %collective-permute-done.15 = f32[168,768]{1,0:T(8,128)S(1)} collective-permute-done((f32[168,768]{1,0:T(8,128)S(1)}, f32[168,768]{1,0:T(8,128)S(1)}, u32[]{:S(2)}, u32[]{:S(2)}) %collective-permute-start.15) | collective-permute-done | bytes 516128 | tf_op jit(solution)/shard_map/ppermute | solution.py:24
  120.3 4.7 %collective-permute-done.14 = f32[4,40,896]{2,1,0:T(8,128)S(1)} collective-permute-done((f32[4,40,896]{2,1,0:T(8,128)S(1)}, f32[4,40,896]{2,1,0:T(8,128)S(1)}, u32[]{:S(2)}, u32[]{:S(2)}) %collective-permute-start.14) | collective-permute-done | bytes 573472 | tf_op jit(solution)/shard_map/ppermute | solution.py:24
  125.2 1.4 collective-permute-done.19
  126.6 4.9 %collective-permute-done.18 = f32[88,768]{1,0:T(8,128)S(1)} collective-permute-done((f32[88,768]{1,0:T(8,128)S(1)}, f32[88,768]{1,0:T(8,128)S(1)}, u32[]{:S(2)}, u32[]{:S(2)}) %collective-permute-start.18) | collective-permute-done | bytes 270368 | tf_op jit(solution)/shard_map/ppermute | solution.py:24
  131.9 1.3 collective-permute-start.21
  133.6 4.9 %collective-permute-start.20 = (f32[40,896]{1,0:T(8,128)S(1)}, f32[40,896]{1,0:T(8,128)S(1)}, u32[]{:S(2)}, u32[]{:S(2)}) collective-permute-start(f32[40,896]{1,0:T(8,128)S(1)} %fusion.17), channel_id=1, source_target_pairs={{0,3},{1,2},{2,1},{3,0},{4,7},{5,6},{6,5},{7,4},{8,11},{9,10},{10,... | collective-permute-start | bytes 430088 | tf_op jit(solution)/shard_map/ppermute | solution.py:24
  139.5 2.0 %collective-permute-done.20 = f32[40,896]{1,0:T(8,128)S(1)} collective-permute-done((f32[40,896]{1,0:T(8,128)S(1)}, f32[40,896]{1,0:T(8,128)S(1)}, u32[]{:S(2)}, u32[]{:S(2)}) %collective-permute-start.20) | collective-permute-done | bytes 143392 | tf_op jit(solution)/shard_map/ppermute | solution.py:24
  (61 shorter events, 9.9 us)
Async XLA Ops:
  1.3 0.7 copy-start
  2.0 19.1 %copy-start.1 = (s32[1,6]{1,0:T(1,128)S(1)}, s32[1,6]{1,0:T(1,128)}, u32[]{:S(2)}) copy-start(s32[1,6]{1,0:T(1,128)} %order.3) | copy-start | bytes 76
  15.9 46.0 %collective-permute-start.1 = (f32[1288,768]{1,0:T(8,128)S(1)}, f32[1288,768]{1,0:T(8,128)S(1)}, u32[]{:S(2)}, u32[]{:S(2)}) collective-permute-start(f32[1288,768]{1,0:T(8,128)S(1)} %get-tuple-element.56), channel_id=1, source_target_pairs={{0,16},{1,17},{2,18},{3,19},{4,20},{5,21},{6,22},{7,23},{8,24},{9,... | collective-permute-start | bytes 11870216 | tf_op jit(solution)/shard_map/ppermute | solution.py:24
  18.0 28.1 %collective-permute-start.3 = (f32[2,4,2,40,896]{4,3,2,1,0:T(8,128)S(1)}, f32[2,4,2,40,896]{4,3,2,1,0:T(8,128)S(1)}, u32[]{:S(2)}, u32[]{:S(2)}) collective-permute-start(f32[2,4,2,40,896]{4,3,2,1,0:T(8,128)S(1)} %get-tuple-element.58), channel_id=1, source_target_pairs={{0,1},{1,0},{2,3},{3,2},{4,5},{5,4},{6,7},{7,6},{8,9},{9,8},{10,11... | collective-permute-start | bytes 6881288 | tf_op jit(solution)/shard_map/ppermute | solution.py:24
  19.5 28.1 %collective-permute-start.2 = (f32[2,2,4,40,896]{4,3,2,1,0:T(8,128)S(1)}, f32[2,2,4,40,896]{4,3,2,1,0:T(8,128)S(1)}, u32[]{:S(2)}, u32[]{:S(2)}) collective-permute-start(f32[2,2,4,40,896]{4,3,2,1,0:T(8,128)S(1)} %get-tuple-element.57), channel_id=1, source_target_pairs={{0,4},{1,5},{2,6},{3,7},{4,0},{5,1},{6,2},{7,3},{8,12},{9,13},{10,... | collective-permute-start | bytes 6881288 | tf_op jit(solution)/shard_map/ppermute | solution.py:24
  35.0 38.4 %collective-permute-start = (f32[2,4,2,40,896]{4,3,2,1,0:T(8,128)S(1)}, f32[2,4,2,40,896]{4,3,2,1,0:T(8,128)S(1)}, u32[]{:S(2)}, u32[]{:S(2)}) collective-permute-start(f32[2,4,2,40,896]{4,3,2,1,0:T(8,128)S(1)} %get-tuple-element.55), channel_id=1, source_target_pairs={{0,1},{1,0},{2,3},{3,2},{4,5},{5,4},{6,7},{7,6},{8,9},{9,8},{10,11... | collective-permute-start | bytes 6881288 | tf_op jit(solution)/shard_map/ppermute | solution.py:24
  35.7 42.2 %collective-permute-start.8 = (f32[2,2,4,40,896]{4,3,2,1,0:T(8,128)S(1)}, f32[2,2,4,40,896]{4,3,2,1,0:T(8,128)S(1)}, u32[]{:S(2)}, u32[]{:S(2)}) collective-permute-start(f32[2,2,4,40,896]{4,3,2,1,0:T(8,128)S(1)} %get-tuple-element.66), channel_id=1, source_target_pairs={{0,4},{1,5},{2,6},{3,7},{4,0},{5,1},{6,2},{7,3},{8,12},{9,13},{10,... | collective-permute-start | bytes 6881288 | tf_op jit(solution)/shard_map/ppermute | solution.py:24
  62.5 27.1 %collective-permute-start.7 = (f32[648,768]{1,0:T(8,128)S(1)}, f32[648,768]{1,0:T(8,128)S(1)}, u32[]{:S(2)}, u32[]{:S(2)}) collective-permute-start(f32[648,768]{1,0:T(8,128)S(1)} %pad_maximum_fusion), channel_id=1, source_target_pairs={{0,48},{1,49},{2,50},{3,51},{4,52},{5,53},{6,54},{7,55},{8,56},{9,... | collective-permute-start | bytes 5971976 | tf_op jit(solution)/shard_map/ppermute | solution.py:24
  66.8 20.7 %collective-permute-start.6 = (f32[2,4,40,896]{3,2,1,0:T(8,128)S(1)}, f32[2,4,40,896]{3,2,1,0:T(8,128)S(1)}, u32[]{:S(2)}, u32[]{:S(2)}) collective-permute-start(f32[2,4,40,896]{3,2,1,0:T(8,128)S(1)} %add_bitcast_fusion.1), channel_id=1, source_target_pairs={{0,12},{1,13},{2,14},{3,15},{4,8},{5,9},{6,10},{7,11},{8,4},{9,5},... | collective-permute-start | bytes 3440648 | tf_op jit(solution)/shard_map/ppermute | solution.py:24
  70.0 17.4 %collective-permute-start.5 = (f32[4,2,40,896]{3,2,1,0:T(8,128)S(1)}, f32[4,2,40,896]{3,2,1,0:T(8,128)S(1)}, u32[]{:S(2)}, u32[]{:S(2)}) collective-permute-start(f32[4,2,40,896]{3,2,1,0:T(8,128)S(1)} %fusion.2), channel_id=1, source_target_pairs={{0,3},{1,2},{2,1},{3,0},{4,7},{5,6},{6,5},{7,4},{8,11},{9,10},{10,... | collective-permute-start | bytes 3440648 | tf_op jit(solution)/shard_map/ppermute | solution.py:24
  78.0 25.6 %collective-permute-start.4 = (f32[4,2,40,896]{3,2,1,0:T(8,128)S(1)}, f32[4,2,40,896]{3,2,1,0:T(8,128)S(1)}, u32[]{:S(2)}, u32[]{:S(2)}) collective-permute-start(f32[4,2,40,896]{3,2,1,0:T(8,128)S(1)} %add_bitcast_fusion.2), channel_id=1, source_target_pairs={{0,3},{1,2},{2,1},{3,0},{4,7},{5,6},{6,5},{7,4},{8,11},{9,10},{10,... | collective-permute-start | bytes 3440648 | tf_op jit(solution)/shard_map/ppermute | solution.py:24
  79.7 24.0 %collective-permute-start.13 = (f32[2,4,40,896]{3,2,1,0:T(8,128)S(1)}, f32[2,4,40,896]{3,2,1,0:T(8,128)S(1)}, u32[]{:S(2)}, u32[]{:S(2)}) collective-permute-start(f32[2,4,40,896]{3,2,1,0:T(8,128)S(1)} %add_bitcast_fusion), channel_id=1, source_target_pairs={{0,12},{1,13},{2,14},{3,15},{4,8},{5,9},{6,10},{7,11},{8,4},{9,5},... | collective-permute-start | bytes 3440648 | tf_op jit(solution)/shard_map/ppermute | solution.py:24
  89.8 15.9 %collective-permute-start.12 = (f32[2,4,40,896]{3,2,1,0:T(8,128)S(1)}, f32[2,4,40,896]{3,2,1,0:T(8,128)S(1)}, u32[]{:S(2)}, u32[]{:S(2)}) collective-permute-start(f32[2,4,40,896]{3,2,1,0:T(8,128)S(1)} %bitcast_add_fusion.1), channel_id=1, source_target_pairs={{0,16},{1,17},{2,18},{3,19},{4,20},{5,21},{6,22},{7,23},{8,24},{9,... | collective-permute-start | bytes 3440648 | tf_op jit(solution)/shard_map/ppermute | solution.py:24
  90.5 15.6 %collective-permute-start.11 = (f32[328,768]{1,0:T(8,128)S(1)}, f32[328,768]{1,0:T(8,128)S(1)}, u32[]{:S(2)}, u32[]{:S(2)}) collective-permute-start(f32[328,768]{1,0:T(8,128)S(1)} %pad_maximum_fusion.1), channel_id=1, source_target_pairs={{0,1},{1,0},{2,3},{3,2},{4,5},{5,4},{6,7},{7,6},{8,9},{9,8},{10,11... | collective-permute-start | bytes 3022856 | tf_op jit(solution)/shard_map/ppermute | solution.py:24
  92.3 19.7 %collective-permute-start.10 = (f32[2,2,40,896]{3,2,1,0:T(8,128)S(1)}, f32[2,2,40,896]{3,2,1,0:T(8,128)S(1)}, u32[]{:S(2)}, u32[]{:S(2)}) collective-permute-start(f32[2,2,40,896]{3,2,1,0:T(8,128)S(1)} %slice.270), channel_id=1, source_target_pairs={{0,4},{1,5},{2,6},{3,7},{4,0},{5,1},{6,2},{7,3},{8,12},{9,13},{10,... | collective-permute-start | bytes 1720328 | tf_op jit(solution)/shard_map/ppermute | solution.py:24
  103.9 10.0 %collective-permute-start.9 = (f32[2,2,40,896]{3,2,1,0:T(8,128)S(1)}, f32[2,2,40,896]{3,2,1,0:T(8,128)S(1)}, u32[]{:S(2)}, u32[]{:S(2)}) collective-permute-start(f32[2,2,40,896]{3,2,1,0:T(8,128)S(1)} %slice.268), channel_id=1, source_target_pairs={{0,4},{1,5},{2,6},{3,7},{4,0},{5,1},{6,2},{7,3},{8,12},{9,13},{10,... | collective-permute-start | bytes 1720328 | tf_op jit(solution)/shard_map/ppermute | solution.py:24
  106.2 11.0 %collective-permute-start.16 = (f32[4,40,896]{2,1,0:T(8,128)S(1)}, f32[4,40,896]{2,1,0:T(8,128)S(1)}, u32[]{:S(2)}, u32[]{:S(2)}) collective-permute-start(f32[4,40,896]{2,1,0:T(8,128)S(1)} %fusion.5), channel_id=1, source_target_pairs={{0,48},{1,49},{2,50},{3,51},{4,52},{5,53},{6,54},{7,55},{8,56},{9,... | collective-permute-start | bytes 1720328 | tf_op jit(solution)/shard_map/ppermute | solution.py:24
  109.2 10.4 %collective-permute-start.15 = (f32[168,768]{1,0:T(8,128)S(1)}, f32[168,768]{1,0:T(8,128)S(1)}, u32[]{:S(2)}, u32[]{:S(2)}) collective-permute-start(f32[168,768]{1,0:T(8,128)S(1)} %pad_maximum_fusion.3), channel_id=1, source_target_pairs={{0,3},{1,2},{2,1},{3,0},{4,7},{5,6},{6,5},{7,4},{8,11},{9,10},{10,... | collective-permute-start | bytes 1548296 | tf_op jit(solution)/shard_map/ppermute | solution.py:24
  114.0 11.0 %collective-permute-start.14 = (f32[4,40,896]{2,1,0:T(8,128)S(1)}, f32[4,40,896]{2,1,0:T(8,128)S(1)}, u32[]{:S(2)}, u32[]{:S(2)}) collective-permute-start(f32[4,40,896]{2,1,0:T(8,128)S(1)} %pad_maximum_fusion.2), channel_id=1, source_target_pairs={{0,12},{1,13},{2,14},{3,15},{4,8},{5,9},{6,10},{7,11},{8,4},{9,5},... | collective-permute-start | bytes 1720328 | tf_op jit(solution)/shard_map/ppermute | solution.py:24
  119.9 6.7 %collective-permute-start.19 = (f32[2,40,896]{2,1,0:T(8,128)S(1)}, f32[2,40,896]{2,1,0:T(8,128)S(1)}, u32[]{:S(2)}, u32[]{:S(2)}) collective-permute-start(f32[2,40,896]{2,1,0:T(8,128)S(1)} %slice.281), channel_id=1, source_target_pairs={{0,1},{1,0},{2,3},{3,2},{4,5},{5,4},{6,7},{7,6},{8,9},{9,8},{10,11... | collective-permute-start | bytes 860168 | tf_op jit(solution)/shard_map/ppermute | solution.py:24
  125.0 6.5 %collective-permute-start.18 = (f32[88,768]{1,0:T(8,128)S(1)}, f32[88,768]{1,0:T(8,128)S(1)}, u32[]{:S(2)}, u32[]{:S(2)}) collective-permute-start(f32[88,768]{1,0:T(8,128)S(1)} %pad_maximum_fusion.5), channel_id=1, source_target_pairs={{0,4},{1,5},{2,6},{3,7},{4,0},{5,1},{6,2},{7,3},{8,12},{9,13},{10,... | collective-permute-start | bytes 811016 | tf_op jit(solution)/shard_map/ppermute | solution.py:24
  125.1 6.7 %collective-permute-start.17 = (f32[2,40,896]{2,1,0:T(8,128)S(1)}, f32[2,40,896]{2,1,0:T(8,128)S(1)}, u32[]{:S(2)}, u32[]{:S(2)}) collective-permute-start(f32[2,40,896]{2,1,0:T(8,128)S(1)} %get-tuple-element.87), channel_id=1, source_target_pairs={{0,16},{1,17},{2,18},{3,19},{4,20},{5,21},{6,22},{7,23},{8,24},{9,... | collective-permute-start | bytes 860168 | tf_op jit(solution)/shard_map/ppermute | solution.py:24
  131.9 9.7 %collective-permute-start.21 = (f32[48,768]{1,0:T(8,128)S(1)}, f32[48,768]{1,0:T(8,128)S(1)}, u32[]{:S(2)}, u32[]{:S(2)}) collective-permute-start(f32[48,768]{1,0:T(8,128)S(1)} %pad_maximum_fusion.6), channel_id=1, source_target_pairs={{0,12},{1,13},{2,14},{3,15},{4,8},{5,9},{6,10},{7,11},{8,4},{9,5},... | collective-permute-start | bytes 442376 | tf_op jit(solution)/shard_map/ppermute | solution.py:24
  133.2 6.4 %collective-permute-start.22 = (f32[40,896]{1,0:T(8,128)S(1)}, f32[40,896]{1,0:T(8,128)S(1)}, u32[]{:S(2)}, u32[]{:S(2)}) collective-permute-start(f32[40,896]{1,0:T(8,128)S(1)} %fusion.16), channel_id=1, source_target_pairs={{0,48},{1,49},{2,50},{3,51},{4,52},{5,53},{6,54},{7,55},{8,56},{9,... | collective-permute-start | bytes 430088 | tf_op jit(solution)/shard_map/ppermute | solution.py:24
  133.6 8.0 %collective-permute-start.20 = (f32[40,896]{1,0:T(8,128)S(1)}, f32[40,896]{1,0:T(8,128)S(1)}, u32[]{:S(2)}, u32[]{:S(2)}) collective-permute-start(f32[40,896]{1,0:T(8,128)S(1)} %fusion.17), channel_id=1, source_target_pairs={{0,3},{1,2},{2,1},{3,0},{4,7},{5,6},{6,5},{7,4},{8,11},{9,10},{10,... | collective-permute-start | bytes 430088 | tf_op jit(solution)/shard_map/ppermute | solution.py:24

commit v7 on v6

--- a/solution.py
+++ b/solution.py
@@ -25,7 +25,7 @@
 
 
 def products(half, failed, counts, order, act, cot, *refs):
-    outs, (acts, cots, total, sems) = refs[:-4], refs[-4:]
+    outs, (acts, cots, total, asked, sems) = refs[:-5], refs[-5:]
     section, me = lax.axis_index("section"), lax.axis_index("dp")
     flips = (0, 3 - 2 * section, 1 + 2 * section, 2)
     xs, ys, zs = ([place ^ flip for flip in flips] for place in (me % 4, me // 4 % 4, me // 16))
@@ -35,18 +35,19 @@
         for g in range(2)
     ]
     load = {}
-    for n, pack in enumerate(("AB", "C")):
+    for n, pack in enumerate(("C", "AB")):
         span = pl.ds(COLUMNS[pack[0]][0], sum(COLUMNS[pack[-1]]) - COLUMNS[pack[0]][0])
         load[pack] = pltpu.make_async_copy(cot.at[0, :, :, span], cots.at[:, :, span], sems.at[2 + n])
+    ask = pltpu.make_async_copy(order, asked, sems.at[4])
+    ask.start()
+    load["C"].start()
     fetch[0].start()
-    for copy in load.values():
-        copy.start()
-    fetch[1].start()
+    ask.wait()
     alive = jnp.where(me == failed[0], 0, counts[0])
     live = [jnp.float32(0)] * SLOTS
     for position in range(SLOTS):
         for k in range(SLOTS):
-            live[k] = jnp.where((order[0, position] == k) & (position < alive), jnp.float32(1), live[k])
+            live[k] = jnp.where((asked[0, position] == k) & (position < alive), jnp.float32(1), live[k])
     if half == 2:
         alive_rows = jnp.full((8, COLUMNS["C"][1]), alive.astype(jnp.float32))
         outs[4][2 * TILE:, :] = alive_rows
@@ -54,10 +55,13 @@
     for g in range(2):
         fetch[g].wait()
         rows = acts[g].reshape(K, TILE)
-        for pack in ("AB", "C"):
+        for pack in ("C", "AB"):
             first, last = COLUMNS[pack[0]][0], sum(COLUMNS[pack[-1]])
             if g == 0:
                 load[pack].wait()
+                if pack == "C":
+                    load["AB"].start()
+                    fetch[1].start()
                 for k in range(SLOTS):
                     cots[k, :, first:last] = cots[k, :, first:last] * live[k].astype(jnp.bfloat16)
             total[:, :last - first] = lax.dot_general(
@@ -84,17 +88,18 @@
     return pl.pallas_call(
         functools.partial(products, half),
         out_shape=[jax.ShapeDtypeStruct(shape, jnp.float32) for shape in shapes],
-        in_specs=[pl.BlockSpec(memory_space=pltpu.SMEM)] * 3 + [pl.BlockSpec(memory_space=pltpu.HBM)] * 2,
+        in_specs=[pl.BlockSpec(memory_space=pltpu.SMEM)] * 2 + [pl.BlockSpec(memory_space=pltpu.HBM)] * 3,
         out_specs=[pl.BlockSpec(memory_space=pltpu.VMEM)] * len(shapes),
         scratch_shapes=[
             pltpu.VMEM((2, SLOTS, TOKENS, TILE), jnp.bfloat16),
             pltpu.VMEM((SLOTS, TOKENS, a + b + c), jnp.bfloat16),
             pltpu.VMEM((TILE, max(a + b, c)), jnp.float32),
-            pltpu.SemaphoreType.DMA((4,)),
+            pltpu.SMEM((1, SLOTS), jnp.int32),
+            pltpu.SemaphoreType.DMA((5,)),
         ],
         compiler_params=pltpu.CompilerParams(vmem_limit_bytes=28 << 20),
         cost_estimate=pl.CostEstimate(flops=1024, bytes_accessed=1024, transcendentals=0),
-    )(failed, counts, order, *(pltpu.with_memory_space_constraint(x, pltpu.HBM) for x in (activations, cotangents)))
+    )(failed, counts, *(pltpu.with_memory_space_constraint(x, pltpu.HBM) for x in (order, activations, cotangents)))
 
 
 def together(values):
@@ -165,14 +170,16 @@
     c5 = take(c5)
     c_out, c_stay, c_total = both(c_whole[:80], c5, c_total, 40)
     c6 = exchange(c_out, "y", 1)
-    a5 = take(a5)
+    a5 = together([take(a5), b6])[0]
     a6 = exchange(a_near[1] + a5[1], "z", 1)
     b6, c6, a6 = together([b6, c6, a6])
     a = (a_near[0] + a5[0]) + a6
     b = (b_whole[0] + b5[0]) + b6
     c = c_stay + c6[:40]
-    total = (c_total + c6[40:])[0, 0]
-    return jnp.concatenate([a / total, b / total, c / total], axis=1)
+    total = c_total + c6[40:]
+    total = jnp.concatenate([total, total, total, total[:, :256]], axis=1)
+    gradient = jnp.concatenate([a, b, c], axis=1)
+    return (gradient.reshape(5, 8, 2560) / total).reshape(40, 2560)
 
 
 def solution(mesh):

time: 146 us -> 146 us (level)
  waiting for transfers between devices: 69.1 us -> 75.6 us
  Pallas kernels: 27.9 us -> 25.9 us
  local copies, waits for them, and re-layouts: 1.93 us -> 0.18 us
    ppermute x23, waiting for transfers between devices: 69.1 us -> 75.6 us  [exchange(): return lax.ppermute(value, ('section', 'dp'), pairs)]
    pallas_call x2, Pallas kernels: 27.9 us -> 25.9 us  [partials(): pl.pallas_call(functools.partial(products, half), out_shape=[jax.ShapeDty...]
  transfers between devices with their start and end apart: 23 -> 23, of which waited for: 19 -> 19; matrix products, arithmetic and copies ran while one was open for 3% -> 2% of each run, Pallas kernels for 10% -> 9%
where the time goes in v7:
time: 146 us
  waiting for transfers between devices  75.6 us (52%)
  starting transfers between devices  38.5 us (26%)
  Pallas kernels  25.9 us (18%)
  other arithmetic  4.03 us (3%)
  between operations  1.53 us (1%)
    ppermute x23, waiting for transfers between devices, exchange(): return lax.ppermute(value, ('section', 'dp'), pairs)  75.6 us
    ppermute x23, starting transfers between devices, exchange(): return lax.ppermute(value, ('section', 'dp'), pairs)  38.5 us
    pallas_call x2, Pallas kernels, partials(): pl.pallas_call(functools.partial(products, half), out_shape=[jax.ShapeDty...  25.9 us
  transfers between devices with their start and end apart: 23, of which 19 were waited for; matrix products, arithmetic and copies ran while one was open for 2% of the time, Pallas kernels for 9%

profile of v7, /device:TPU:0, one launch (start us, length us, event | category | flops | bytes accessed | tf_op | source)
XLA Modules:
  0.0 145.7 jit_solution(16881745005223761826)
XLA Ops:
  1.3 12.9 %shard_map.55 = (f32[2,4,2,40,896]{4,3,2,1,0:T(8,128)S(1)}, f32[2,4,2,40,896]{4,3,2,1,0:T(8,128)S(1)}, f32[2,2,4,40,896]{4,3,2,1,0:T(8,128)S(1)}, f32[2,2,4,40,8...) custom-call(s32[1]{0:T(128)S(6)} %copy.6.failed, s32[1]{0:T(128)S(6)} %copy.7.counts, ...), custom_call_target="tpu_custom_call" | custom-call | flops 1024 | bytes 1024 | tf_op jit(solution)/shard_map/pallas_call | solution.py:88
  14.2 2.1 %collective-permute-start.1 = (f32[1288,768]{1,0:T(8,128)S(1)}, f32[1288,768]{1,0:T(8,128)S(1)}, u32[]{:S(2)}, u32[]{:S(2)}) collective-permute-start(f32[1288,768]{1,0:T(8,128)S(1)} %get-tuple-element.57), channel_id=1, source_target_pairs={{0,16},{1,17},{2,18},{3,19},{4,20},{5,21},{6,22},{7,23},{8,24},{9,... | collective-permute-start | bytes 11870216 | tf_op jit(solution)/shard_map/ppermute | solution.py:24
  17.8 1.6 %collective-permute-start.2 = (f32[2,2,4,40,896]{4,3,2,1,0:T(8,128)S(1)}, f32[2,2,4,40,896]{4,3,2,1,0:T(8,128)S(1)}, u32[]{:S(2)}, u32[]{:S(2)}) collective-permute-start(f32[2,2,4,40,896]{4,3,2,1,0:T(8,128)S(1)} %get-tuple-element.58), channel_id=1, source_target_pairs={{0,4},{1,5},{2,6},{3,7},{4,0},{5,1},{6,2},{7,3},{8,12},{9,13},{10,... | collective-permute-start | bytes 6881288 | tf_op jit(solution)/shard_map/ppermute | solution.py:24
  19.4 12.9 %shard_map.56 = (f32[2,4,2,40,896]{4,3,2,1,0:T(8,128)S(1)}, f32[2,4,2,40,896]{4,3,2,1,0:T(8,128)S(1)}, f32[2,2,4,40,896]{4,3,2,1,0:T(8,128)S(1)}, f32[2,2,4,40,896]{4,3,2,1,0:T(8,128)S(1)}, f32[1280,768]{1,0:T(8,128)S(1)}) custom-call(s32[1]{0:T(128)S(6)} %copy.6.failed, s32[1]{0:T(128)S(6)} %copy.7.counts, s32[1,6]{1,0:T(1,128)} %order.3, ...), custom_call_target="tpu_custom_call" | custom-call | flops 1024 | bytes 1024 | tf_op jit(solution)/shard_map/pallas_call | solution.py:88
  33.4 11.1 %collective-permute-done.3 = f32[2,4,2,40,896]{4,3,2,1,0:T(8,128)S(1)} collective-permute-done((f32[2,4,2,40,896]{4,3,2,1,0:T(8,128)S(1)}, f32[2,4,2,40,896]{4,3,2,1,0:T(8,128)S(1)}, u32[]{:S(2)}, u32[]{:S(2)}) %collective-permute-start.3) | collective-permute-done | bytes 2293792 | tf_op jit(solution)/shard_map/ppermute | solution.py:24
  44.5 1.5 %collective-permute-done.2 = f32[2,2,4,40,896]{4,3,2,1,0:T(8,128)S(1)} collective-permute-done((f32[2,2,4,40,896]{4,3,2,1,0:T(8,128)S(1)}, f32[2,2,4,40,896]{4,3,2,1,0:T(8,128)S(1)}, u32[]{:S(2)}, u32[]{:S(2)}) %collective-permute-start.2) | collective-permute-done | bytes 2293792 | tf_op jit(solution)/shard_map/ppermute | solution.py:24
  46.0 14.3 %collective-permute-done.1 = f32[1288,768]{1,0:T(8,128)S(1)} collective-permute-done((f32[1288,768]{1,0:T(8,128)S(1)}, f32[1288,768]{1,0:T(8,128)S(1)}, u32[]{:S(2)}, u32[]{:S(2)}) %collective-permute-start.1) | collective-permute-done | bytes 3956768 | tf_op jit(solution)/shard_map/ppermute | solution.py:24
  60.8 4.3 %collective-permute-start.7 = (f32[648,768]{1,0:T(8,128)S(1)}, f32[648,768]{1,0:T(8,128)S(1)}, u32[]{:S(2)}, u32[]{:S(2)}) collective-permute-start(f32[648,768]{1,0:T(8,128)S(1)} %pad_maximum_fusion), channel_id=1, source_target_pairs={{0,48},{1,49},{2,50},{3,51},{4,52},{5,53},{6,54},{7,55},{8,56},{9,... | collective-permute-start | bytes 5971976 | tf_op jit(solution)/shard_map/ppermute | solution.py:24
  65.2 3.1 %collective-permute-start.6 = (f32[2,4,40,896]{3,2,1,0:T(8,128)S(1)}, f32[2,4,40,896]{3,2,1,0:T(8,128)S(1)}, u32[]{:S(2)}, u32[]{:S(2)}) collective-permute-start(f32[2,4,40,896]{3,2,1,0:T(8,128)S(1)} %add_bitcast_fusion.1), channel_id=1, source_target_pairs={{0,12},{1,13},{2,14},{3,15},{4,8},{5,9},{6,10},{7,11},{8,4},{9,5},... | collective-permute-start | bytes 3440648 | tf_op jit(solution)/shard_map/ppermute | solution.py:24
  68.4 2.8 %collective-permute-start.5 = (f32[4,2,40,896]{3,2,1,0:T(8,128)S(1)}, f32[4,2,40,896]{3,2,1,0:T(8,128)S(1)}, u32[]{:S(2)}, u32[]{:S(2)}) collective-permute-start(f32[4,2,40,896]{3,2,1,0:T(8,128)S(1)} %fusion.2), channel_id=1, source_target_pairs={{0,3},{1,2},{2,1},{3,0},{4,7},{5,6},{6,5},{7,4},{8,11},{9,10},{10,... | collective-permute-start | bytes 3440648 | tf_op jit(solution)/shard_map/ppermute | solution.py:24
  71.8 4.5 %collective-permute-done.8 = f32[2,2,4,40,896]{4,3,2,1,0:T(8,128)S(1)} collective-permute-done((f32[2,2,4,40,896]{4,3,2,1,0:T(8,128)S(1)}, f32[2,2,4,40,896]{4,3,2,1,0:T(8,128)S(1)}, u32[]{:S(2)}, u32[]{:S(2)}) %collective-permute-start.8) | collective-permute-done | bytes 2293792 | tf_op jit(solution)/shard_map/ppermute | solution.py:24
  76.4 1.5 %collective-permute-start.4 = (f32[4,2,40,896]{3,2,1,0:T(8,128)S(1)}, f32[4,2,40,896]{3,2,1,0:T(8,128)S(1)}, u32[]{:S(2)}, u32[]{:S(2)}) collective-permute-start(f32[4,2,40,896]{3,2,1,0:T(8,128)S(1)} %add_bitcast_fusion.2), channel_id=1, source_target_pairs={{0,3},{1,2},{2,1},{3,0},{4,7},{5,6},{6,5},{7,4},{8,11},{9,10},{10,... | collective-permute-start | bytes 3440648 | tf_op jit(solution)/shard_map/ppermute | solution.py:24
  78.0 3.1 %collective-permute-start.13 = (f32[2,4,40,896]{3,2,1,0:T(8,128)S(1)}, f32[2,4,40,896]{3,2,1,0:T(8,128)S(1)}, u32[]{:S(2)}, u32[]{:S(2)}) collective-permute-start(f32[2,4,40,896]{3,2,1,0:T(8,128)S(1)} %add_bitcast_fusion), channel_id=1, source_target_pairs={{0,12},{1,13},{2,14},{3,15},{4,8},{5,9},{6,10},{7,11},{8,4},{9,5},... | collective-permute-start | bytes 3440648 | tf_op jit(solution)/shard_map/ppermute | solution.py:24
  81.1 4.7 %collective-permute-done.6 = f32[2,4,40,896]{3,2,1,0:T(8,128)S(1)} collective-permute-done((f32[2,4,40,896]{3,2,1,0:T(8,128)S(1)}, f32[2,4,40,896]{3,2,1,0:T(8,128)S(1)}, u32[]{:S(2)}, u32[]{:S(2)}) %collective-permute-start.6) | collective-permute-done | bytes 1146912 | tf_op jit(solution)/shard_map/ppermute | solution.py:24
  85.8 2.2 %collective-permute-done.7 = f32[648,768]{1,0:T(8,128)S(1)} collective-permute-done((f32[648,768]{1,0:T(8,128)S(1)}, f32[648,768]{1,0:T(8,128)S(1)}, u32[]{:S(2)}, u32[]{:S(2)}) %collective-permute-start.7) | collective-permute-done | bytes 1990688 | tf_op jit(solution)/shard_map/ppermute | solution.py:24
  88.9 1.8 %collective-permute-start.11 = (f32[328,768]{1,0:T(8,128)S(1)}, f32[328,768]{1,0:T(8,128)S(1)}, u32[]{:S(2)}, u32[]{:S(2)}) collective-permute-start(f32[328,768]{1,0:T(8,128)S(1)} %pad_maximum_fusion.1), channel_id=1, source_target_pairs={{0,1},{1,0},{2,3},{3,2},{4,5},{5,4},{6,7},{7,6},{8,9},{9,8},{10,11... | collective-permute-start | bytes 3022856 | tf_op jit(solution)/shard_map/ppermute | solution.py:24
  90.9 1.7 %collective-permute-start.10 = (f32[2,2,40,896]{3,2,1,0:T(8,128)S(1)}, f32[2,2,40,896]{3,2,1,0:T(8,128)S(1)}, u32[]{:S(2)}, u32[]{:S(2)}) collective-permute-start(f32[2,2,40,896]{3,2,1,0:T(8,128)S(1)} %slice.270), channel_id=1, source_target_pairs={{0,4},{1,5},{2,6},{3,7},{4,0},{5,1},{6,2},{7,3},{8,12},{9,13},{10,... | collective-permute-start | bytes 1720328 | tf_op jit(solution)/shard_map/ppermute | solution.py:24
  92.6 9.3 %collective-permute-done.4 = f32[4,2,40,896]{3,2,1,0:T(8,128)S(1)} collective-permute-done((f32[4,2,40,896]{3,2,1,0:T(8,128)S(1)}, f32[4,2,40,896]{3,2,1,0:T(8,128)S(1)}, u32[]{:S(2)}, u32[]{:S(2)}) %collective-permute-start.4) | collective-permute-done | bytes 1146912 | tf_op jit(solution)/shard_map/ppermute | solution.py:24
  102.5 1.6 %collective-permute-done.12 = f32[2,4,40,896]{3,2,1,0:T(8,128)S(1)} collective-permute-done((f32[2,4,40,896]{3,2,1,0:T(8,128)S(1)}, f32[2,4,40,896]{3,2,1,0:T(8,128)S(1)}, u32[]{:S(2)}, u32[]{:S(2)}) %collective-permute-start.12) | collective-permute-done | bytes 1146912 | tf_op jit(solution)/shard_map/ppermute | solution.py:24
  104.5 3.0 %collective-permute-start.16 = (f32[4,40,896]{2,1,0:T(8,128)S(1)}, f32[4,40,896]{2,1,0:T(8,128)S(1)}, u32[]{:S(2)}, u32[]{:S(2)}) collective-permute-start(f32[4,40,896]{2,1,0:T(8,128)S(1)} %fusion.5), channel_id=1, source_target_pairs={{0,48},{1,49},{2,50},{3,51},{4,52},{5,53},{6,54},{7,55},{8,56},{9,... | collective-permute-start | bytes 1720328 | tf_op jit(solution)/shard_map/ppermute | solution.py:24
  107.6 2.8 %collective-permute-start.15 = (f32[168,768]{1,0:T(8,128)S(1)}, f32[168,768]{1,0:T(8,128)S(1)}, u32[]{:S(2)}, u32[]{:S(2)}) collective-permute-start(f32[168,768]{1,0:T(8,128)S(1)} %pad_maximum_fusion.3), channel_id=1, source_target_pairs={{0,3},{1,2},{2,1},{3,0},{4,7},{5,6},{6,5},{7,4},{8,11},{9,10},{10,... | collective-permute-start | bytes 1548296 | tf_op jit(solution)/shard_map/ppermute | solution.py:24
  110.5 1.5 %collective-permute-done.9 = f32[2,2,40,896]{3,2,1,0:T(8,128)S(1)} collective-permute-done((f32[2,2,40,896]{3,2,1,0:T(8,128)S(1)}, f32[2,2,40,896]{3,2,1,0:T(8,128)S(1)}, u32[]{:S(2)}, u32[]{:S(2)}) %collective-permute-start.9) | collective-permute-done | bytes 573472 | tf_op jit(solution)/shard_map/ppermute | solution.py:24
  112.1 1.6 %collective-permute-start.14 = (f32[4,40,896]{2,1,0:T(8,128)S(1)}, f32[4,40,896]{2,1,0:T(8,128)S(1)}, u32[]{:S(2)}, u32[]{:S(2)}) collective-permute-start(f32[4,40,896]{2,1,0:T(8,128)S(1)} %pad_maximum_fusion.2), channel_id=1, source_target_pairs={{0,12},{1,13},{2,14},{3,15},{4,8},{5,9},{6,10},{7,11},{8,4},{9,5},... | collective-permute-start | bytes 1720328 | tf_op jit(solution)/shard_map/ppermute | solution.py:24
  113.7 1.8 %collective-permute-done.16 = f32[4,40,896]{2,1,0:T(8,128)S(1)} collective-permute-done((f32[4,40,896]{2,1,0:T(8,128)S(1)}, f32[4,40,896]{2,1,0:T(8,128)S(1)}, u32[]{:S(2)}, u32[]{:S(2)}) %collective-permute-start.16) | collective-permute-done | bytes 573472 | tf_op jit(solution)/shard_map/ppermute | solution.py:24
  115.5 2.5 %collective-permute-done.15 = f32[168,768]{1,0:T(8,128)S(1)} collective-permute-done((f32[168,768]{1,0:T(8,128)S(1)}, f32[168,768]{1,0:T(8,128)S(1)}, u32[]{:S(2)}, u32[]{:S(2)}) %collective-permute-start.15) | collective-permute-done | bytes 516128 | tf_op jit(solution)/shard_map/ppermute | solution.py:24
  118.6 4.4 %collective-permute-done.14 = f32[4,40,896]{2,1,0:T(8,128)S(1)} collective-permute-done((f32[4,40,896]{2,1,0:T(8,128)S(1)}, f32[4,40,896]{2,1,0:T(8,128)S(1)}, u32[]{:S(2)}, u32[]{:S(2)}) %collective-permute-start.14) | collective-permute-done | bytes 573472 | tf_op jit(solution)/shard_map/ppermute | solution.py:24
  123.3 1.7 %collective-permute-done.19 = f32[2,40,896]{2,1,0:T(8,128)S(1)} collective-permute-done((f32[2,40,896]{2,1,0:T(8,128)S(1)}, f32[2,40,896]{2,1,0:T(8,128)S(1)}, u32[]{:S(2)}, u32[]{:S(2)}) %collective-permute-start.19) | collective-permute-done | bytes 286752 | tf_op jit(solution)/shard_map/ppermute | solution.py:24
  125.0 4.5 %collective-permute-done.18 = f32[88,768]{1,0:T(8,128)S(1)} collective-permute-done((f32[88,768]{1,0:T(8,128)S(1)}, f32[88,768]{1,0:T(8,128)S(1)}, u32[]{:S(2)}, u32[]{:S(2)}) %collective-permute-start.18) | collective-permute-done | bytes 270368 | tf_op jit(solution)/shard_map/ppermute | solution.py:24
  129.5 5.8 %collective-permute-start.20 = (f32[40,896]{1,0:T(8,128)S(1)}, f32[40,896]{1,0:T(8,128)S(1)}, u32[]{:S(2)}, u32[]{:S(2)}) collective-permute-start(f32[40,896]{1,0:T(8,128)S(1)} %fusion.16), channel_id=1, source_target_pairs={{0,3},{1,2},{2,1},{3,0},{4,7},{5,6},{6,5},{7,4},{8,11},{9,10},{10,... | collective-permute-start | bytes 430088 | tf_op jit(solution)/shard_map/ppermute | solution.py:24
  135.5 2.9 %collective-permute-done.20 = f32[40,896]{1,0:T(8,128)S(1)} collective-permute-done((f32[40,896]{1,0:T(8,128)S(1)}, f32[40,896]{1,0:T(8,128)S(1)}, u32[]{:S(2)}, u32[]{:S(2)}) %collective-permute-start.20) | collective-permute-done | bytes 143392 | tf_op jit(solution)/shard_map/ppermute | solution.py:24
  138.5 3.3 %collective-permute-done.21 = f32[48,768]{1,0:T(8,128)S(1)} collective-permute-done((f32[48,768]{1,0:T(8,128)S(1)}, f32[48,768]{1,0:T(8,128)S(1)}, u32[]{:S(2)}, u32[]{:S(2)}) %collective-permute-start.21) | collective-permute-done | bytes 147488 | tf_op jit(solution)/shard_map/ppermute | solution.py:24
  141.8 3.0 %collective-permute-done.22 = f32[40,896]{1,0:T(8,128)S(1)} collective-permute-done((f32[40,896]{1,0:T(8,128)S(1)}, f32[40,896]{1,0:T(8,128)S(1)}, u32[]{:S(2)}, u32[]{:S(2)}) %collective-permute-start.22) | collective-permute-done | bytes 143392 | tf_op jit(solution)/shard_map/ppermute | solution.py:24
  (58 shorter events, 8.4 us)
Async XLA Ops:
  14.2 46.0 %collective-permute-start.1 = (f32[1288,768]{1,0:T(8,128)S(1)}, f32[1288,768]{1,0:T(8,128)S(1)}, u32[]{:S(2)}, u32[]{:S(2)}) collective-permute-start(f32[1288,768]{1,0:T(8,128)S(1)} %get-tuple-element.57), channel_id=1, source_target_pairs={{0,16},{1,17},{2,18},{3,19},{4,20},{5,21},{6,22},{7,23},{8,24},{9,... | collective-permute-start | bytes 11870216 | tf_op jit(solution)/shard_map/ppermute | solution.py:24
  16.3 28.1 %collective-permute-start.3 = (f32[2,4,2,40,896]{4,3,2,1,0:T(8,128)S(1)}, f32[2,4,2,40,896]{4,3,2,1,0:T(8,128)S(1)}, u32[]{:S(2)}, u32[]{:S(2)}) collective-permute-start(f32[2,4,2,40,896]{4,3,2,1,0:T(8,128)S(1)} %get-tuple-element.59), channel_id=1, source_target_pairs={{0,1},{1,0},{2,3},{3,2},{4,5},{5,4},{6,7},{7,6},{8,9},{9,8},{10,11... | collective-permute-start | bytes 6881288 | tf_op jit(solution)/shard_map/ppermute | solution.py:24
  17.8 28.1 %collective-permute-start.2 = (f32[2,2,4,40,896]{4,3,2,1,0:T(8,128)S(1)}, f32[2,2,4,40,896]{4,3,2,1,0:T(8,128)S(1)}, u32[]{:S(2)}, u32[]{:S(2)}) collective-permute-start(f32[2,2,4,40,896]{4,3,2,1,0:T(8,128)S(1)} %get-tuple-element.58), channel_id=1, source_target_pairs={{0,4},{1,5},{2,6},{3,7},{4,0},{5,1},{6,2},{7,3},{8,12},{9,13},{10,... | collective-permute-start | bytes 6881288 | tf_op jit(solution)/shard_map/ppermute | solution.py:24
  32.3 39.4 %collective-permute-start = (f32[2,4,2,40,896]{4,3,2,1,0:T(8,128)S(1)}, f32[2,4,2,40,896]{4,3,2,1,0:T(8,128)S(1)}, u32[]{:S(2)}, u32[]{:S(2)}) collective-permute-start(f32[2,4,2,40,896]{4,3,2,1,0:T(8,128)S(1)} %get-tuple-element.56), channel_id=1, source_target_pairs={{0,1},{1,0},{2,3},{3,2},{4,5},{5,4},{6,7},{7,6},{8,9},{9,8},{10,11... | collective-permute-start | bytes 6881288 | tf_op jit(solution)/shard_map/ppermute | solution.py:24
  33.0 43.3 %collective-permute-start.8 = (f32[2,2,4,40,896]{4,3,2,1,0:T(8,128)S(1)}, f32[2,2,4,40,896]{4,3,2,1,0:T(8,128)S(1)}, u32[]{:S(2)}, u32[]{:S(2)}) collective-permute-start(f32[2,2,4,40,896]{4,3,2,1,0:T(8,128)S(1)} %get-tuple-element.67), channel_id=1, source_target_pairs={{0,4},{1,5},{2,6},{3,7},{4,0},{5,1},{6,2},{7,3},{8,12},{9,13},{10,... | collective-permute-start | bytes 6881288 | tf_op jit(solution)/shard_map/ppermute | solution.py:24
  60.8 27.1 %collective-permute-start.7 = (f32[648,768]{1,0:T(8,128)S(1)}, f32[648,768]{1,0:T(8,128)S(1)}, u32[]{:S(2)}, u32[]{:S(2)}) collective-permute-start(f32[648,768]{1,0:T(8,128)S(1)} %pad_maximum_fusion), channel_id=1, source_target_pairs={{0,48},{1,49},{2,50},{3,51},{4,52},{5,53},{6,54},{7,55},{8,56},{9,... | collective-permute-start | bytes 5971976 | tf_op jit(solution)/shard_map/ppermute | solution.py:24
  65.2 20.6 %collective-permute-start.6 = (f32[2,4,40,896]{3,2,1,0:T(8,128)S(1)}, f32[2,4,40,896]{3,2,1,0:T(8,128)S(1)}, u32[]{:S(2)}, u32[]{:S(2)}) collective-permute-start(f32[2,4,40,896]{3,2,1,0:T(8,128)S(1)} %add_bitcast_fusion.1), channel_id=1, source_target_pairs={{0,12},{1,13},{2,14},{3,15},{4,8},{5,9},{6,10},{7,11},{8,4},{9,5},... | collective-permute-start | bytes 3440648 | tf_op jit(solution)/shard_map/ppermute | solution.py:24
  68.4 17.4 %collective-permute-start.5 = (f32[4,2,40,896]{3,2,1,0:T(8,128)S(1)}, f32[4,2,40,896]{3,2,1,0:T(8,128)S(1)}, u32[]{:S(2)}, u32[]{:S(2)}) collective-permute-start(f32[4,2,40,896]{3,2,1,0:T(8,128)S(1)} %fusion.2), channel_id=1, source_target_pairs={{0,3},{1,2},{2,1},{3,0},{4,7},{5,6},{6,5},{7,4},{8,11},{9,10},{10,... | collective-permute-start | bytes 3440648 | tf_op jit(solution)/shard_map/ppermute | solution.py:24
  76.4 25.5 %collective-permute-start.4 = (f32[4,2,40,896]{3,2,1,0:T(8,128)S(1)}, f32[4,2,40,896]{3,2,1,0:T(8,128)S(1)}, u32[]{:S(2)}, u32[]{:S(2)}) collective-permute-start(f32[4,2,40,896]{3,2,1,0:T(8,128)S(1)} %add_bitcast_fusion.2), channel_id=1, source_target_pairs={{0,3},{1,2},{2,1},{3,0},{4,7},{5,6},{6,5},{7,4},{8,11},{9,10},{10,... | collective-permute-start | bytes 3440648 | tf_op jit(solution)/shard_map/ppermute | solution.py:24
  78.0 23.9 %collective-permute-start.13 = (f32[2,4,40,896]{3,2,1,0:T(8,128)S(1)}, f32[2,4,40,896]{3,2,1,0:T(8,128)S(1)}, u32[]{:S(2)}, u32[]{:S(2)}) collective-permute-start(f32[2,4,40,896]{3,2,1,0:T(8,128)S(1)} %add_bitcast_fusion), channel_id=1, source_target_pairs={{0,12},{1,13},{2,14},{3,15},{4,8},{5,9},{6,10},{7,11},{8,4},{9,5},... | collective-permute-start | bytes 3440648 | tf_op jit(solution)/shard_map/ppermute | solution.py:24
  88.2 15.9 %collective-permute-start.12 = (f32[2,4,40,896]{3,2,1,0:T(8,128)S(1)}, f32[2,4,40,896]{3,2,1,0:T(8,128)S(1)}, u32[]{:S(2)}, u32[]{:S(2)}) collective-permute-start(f32[2,4,40,896]{3,2,1,0:T(8,128)S(1)} %bitcast_add_fusion.1), channel_id=1, source_target_pairs={{0,16},{1,17},{2,18},{3,19},{4,20},{5,21},{6,22},{7,23},{8,24},{9,... | collective-permute-start | bytes 3440648 | tf_op jit(solution)/shard_map/ppermute | solution.py:24
  88.9 15.5 %collective-permute-start.11 = (f32[328,768]{1,0:T(8,128)S(1)}, f32[328,768]{1,0:T(8,128)S(1)}, u32[]{:S(2)}, u32[]{:S(2)}) collective-permute-start(f32[328,768]{1,0:T(8,128)S(1)} %pad_maximum_fusion.1), channel_id=1, source_target_pairs={{0,1},{1,0},{2,3},{3,2},{4,5},{5,4},{6,7},{7,6},{8,9},{9,8},{10,11... | collective-permute-start | bytes 3022856 | tf_op jit(solution)/shard_map/ppermute | solution.py:24
  90.9 19.5 %collective-permute-start.10 = (f32[2,2,40,896]{3,2,1,0:T(8,128)S(1)}, f32[2,2,40,896]{3,2,1,0:T(8,128)S(1)}, u32[]{:S(2)}, u32[]{:S(2)}) collective-permute-start(f32[2,2,40,896]{3,2,1,0:T(8,128)S(1)} %slice.270), channel_id=1, source_target_pairs={{0,4},{1,5},{2,6},{3,7},{4,0},{5,1},{6,2},{7,3},{8,12},{9,13},{10,... | collective-permute-start | bytes 1720328 | tf_op jit(solution)/shard_map/ppermute | solution.py:24
  102.2 9.8 %collective-permute-start.9 = (f32[2,2,40,896]{3,2,1,0:T(8,128)S(1)}, f32[2,2,40,896]{3,2,1,0:T(8,128)S(1)}, u32[]{:S(2)}, u32[]{:S(2)}) collective-permute-start(f32[2,2,40,896]{3,2,1,0:T(8,128)S(1)} %slice.268), channel_id=1, source_target_pairs={{0,4},{1,5},{2,6},{3,7},{4,0},{5,1},{6,2},{7,3},{8,12},{9,13},{10,... | collective-permute-start | bytes 1720328 | tf_op jit(solution)/shard_map/ppermute | solution.py:24
  104.5 11.0 %collective-permute-start.16 = (f32[4,40,896]{2,1,0:T(8,128)S(1)}, f32[4,40,896]{2,1,0:T(8,128)S(1)}, u32[]{:S(2)}, u32[]{:S(2)}) collective-permute-start(f32[4,40,896]{2,1,0:T(8,128)S(1)} %fusion.5), channel_id=1, source_target_pairs={{0,48},{1,49},{2,50},{3,51},{4,52},{5,53},{6,54},{7,55},{8,56},{9,... | collective-permute-start | bytes 1720328 | tf_op jit(solution)/shard_map/ppermute | solution.py:24
  107.6 10.4 %collective-permute-start.15 = (f32[168,768]{1,0:T(8,128)S(1)}, f32[168,768]{1,0:T(8,128)S(1)}, u32[]{:S(2)}, u32[]{:S(2)}) collective-permute-start(f32[168,768]{1,0:T(8,128)S(1)} %pad_maximum_fusion.3), channel_id=1, source_target_pairs={{0,3},{1,2},{2,1},{3,0},{4,7},{5,6},{6,5},{7,4},{8,11},{9,10},{10,... | collective-permute-start | bytes 1548296 | tf_op jit(solution)/shard_map/ppermute | solution.py:24
  112.1 11.0 %collective-permute-start.14 = (f32[4,40,896]{2,1,0:T(8,128)S(1)}, f32[4,40,896]{2,1,0:T(8,128)S(1)}, u32[]{:S(2)}, u32[]{:S(2)}) collective-permute-start(f32[4,40,896]{2,1,0:T(8,128)S(1)} %pad_maximum_fusion.2), channel_id=1, source_target_pairs={{0,12},{1,13},{2,14},{3,15},{4,8},{5,9},{6,10},{7,11},{8,4},{9,5},... | collective-permute-start | bytes 1720328 | tf_op jit(solution)/shard_map/ppermute | solution.py:24
  118.2 6.7 %collective-permute-start.19 = (f32[2,40,896]{2,1,0:T(8,128)S(1)}, f32[2,40,896]{2,1,0:T(8,128)S(1)}, u32[]{:S(2)}, u32[]{:S(2)}) collective-permute-start(f32[2,40,896]{2,1,0:T(8,128)S(1)} %slice.281), channel_id=1, source_target_pairs={{0,1},{1,0},{2,3},{3,2},{4,5},{5,4},{6,7},{7,6},{8,9},{9,8},{10,11... | collective-permute-start | bytes 860168 | tf_op jit(solution)/shard_map/ppermute | solution.py:24
  123.1 6.5 %collective-permute-start.18 = (f32[88,768]{1,0:T(8,128)S(1)}, f32[88,768]{1,0:T(8,128)S(1)}, u32[]{:S(2)}, u32[]{:S(2)}) collective-permute-start(f32[88,768]{1,0:T(8,128)S(1)} %pad_maximum_fusion.4), channel_id=1, source_target_pairs={{0,4},{1,5},{2,6},{3,7},{4,0},{5,1},{6,2},{7,3},{8,12},{9,13},{10,... | collective-permute-start | bytes 811016 | tf_op jit(solution)/shard_map/ppermute | solution.py:24
  123.2 12.2 %collective-permute-start.17 = (f32[2,40,896]{2,1,0:T(8,128)S(1)}, f32[2,40,896]{2,1,0:T(8,128)S(1)}, u32[]{:S(2)}, u32[]{:S(2)}) collective-permute-start(f32[2,40,896]{2,1,0:T(8,128)S(1)} %get-tuple-element.89), channel_id=1, source_target_pairs={{0,16},{1,17},{2,18},{3,19},{4,20},{5,21},{6,22},{7,23},{8,24},{9,... | collective-permute-start | bytes 860168 | tf_op jit(solution)/shard_map/ppermute | solution.py:24
  129.5 8.9 %collective-permute-start.20 = (f32[40,896]{1,0:T(8,128)S(1)}, f32[40,896]{1,0:T(8,128)S(1)}, u32[]{:S(2)}, u32[]{:S(2)}) collective-permute-start(f32[40,896]{1,0:T(8,128)S(1)} %fusion.16), channel_id=1, source_target_pairs={{0,3},{1,2},{2,1},{3,0},{4,7},{5,6},{6,5},{7,4},{8,11},{9,10},{10,... | collective-permute-start | bytes 430088 | tf_op jit(solution)/shard_map/ppermute | solution.py:24
  135.4 6.4 %collective-permute-start.21 = (f32[48,768]{1,0:T(8,128)S(1)}, f32[48,768]{1,0:T(8,128)S(1)}, u32[]{:S(2)}, u32[]{:S(2)}) collective-permute-start(f32[48,768]{1,0:T(8,128)S(1)} %pad_maximum_fusion.5), channel_id=1, source_target_pairs={{0,12},{1,13},{2,14},{3,15},{4,8},{5,9},{6,10},{7,11},{8,4},{9,5},... | collective-permute-start | bytes 442376 | tf_op jit(solution)/shard_map/ppermute | solution.py:24
  138.4 6.4 %collective-permute-start.22 = (f32[40,896]{1,0:T(8,128)S(1)}, f32[40,896]{1,0:T(8,128)S(1)}, u32[]{:S(2)}, u32[]{:S(2)}) collective-permute-start(f32[40,896]{1,0:T(8,128)S(1)} %fusion.15), channel_id=1, source_target_pairs={{0,48},{1,49},{2,50},{3,51},{4,52},{5,53},{6,54},{7,55},{8,56},{9,... | collective-permute-start | bytes 430088 | tf_op jit(solution)/shard_map/ppermute | solution.py:24

commit v8 on v7

--- a/solution.py
+++ b/solution.py
@@ -14,10 +14,10 @@
 COLUMNS = {"A": (0, 896), "B": (896, 896), "C": (1792, 768)}
 
 
-def exchange(value, axis, turn):
+def exchange(value, axis, turn, other=False):
     pairs = []
     for section in range(2):
-        flip, stride = 1 if section == turn else 3, STRIDE[axis]
+        flip, stride = 1 if (section == turn) != other else 3, STRIDE[axis]
         for d in range(64):
             p = d // stride % 4
             pairs.append((section * 64 + d, section * 64 + d + ((p ^ flip) - p) * stride))
@@ -28,7 +28,11 @@
     outs, (acts, cots, total, asked, sems) = refs[:-5], refs[-5:]
     section, me = lax.axis_index("section"), lax.axis_index("dp")
     flips = (0, 3 - 2 * section, 1 + 2 * section, 2)
-    xs, ys, zs = ([place ^ flip for flip in flips] for place in (me % 4, me // 4 % 4, me // 16))
+    others = (0, 1 + 2 * section, 3 - 2 * section, 2)
+    x, y, z = me % 4, me // 4 % 4, me // 16
+    zs = [z ^ flip for flip in flips]
+    xs = {group: [x ^ flip for flip in (flips if group == "A" else others)] for group in "ABC"}
+    ys = {group: [y ^ flip for flip in (flips if group == "B" else others)] for group in "ABC"}
     fetch = [
         pltpu.make_async_copy(
             act.at[0, :, :, pl.ds(pl.multiple_of(zs[half + g] * TILE, 128), TILE)], acts.at[g], sems.at[g])
@@ -71,7 +75,8 @@
                 column, columns = COLUMNS[group]
                 for i in range(4):
                     for j in range(4):
-                        start = ys[i] * 160 + xs[j] * ROWS if group == "B" else xs[i] * ROWS + ys[j] * 160
+                        start = (ys if group == "B" else xs)[group][i] * (160 if group == "B" else ROWS)
+                        start += (xs if group == "B" else ys)[group][j] * (ROWS if group == "B" else 160)
                         block = total[pl.ds(pl.multiple_of(start, 8), ROWS), column - first:column - first + columns]
                         if group == "A":
                             outs[i // 2][i % 2, j, g] = block
@@ -138,39 +143,39 @@
     a2f, b2f, c2, _ = together([a2f, b2f, c2, taken])
     taken = c2
     a_far = (a_keep_far[0] + a1f[0]) + a2f
-    a3f = exchange(a_far[2:4], "y", 0)
+    a3f = exchange(a_far[2:4], "y", 0, True)
     b_far = (b_keep_far[0] + b1f[0]) + b2f
     b3 = exchange(b_far, "z", 0)
     c_whole, c_total = c_stay + c2[:TILE], c_total + c2[TILE:]
-    c3 = exchange(jnp.concatenate([c_whole[320:], c_total], axis=0), "x", 0)
+    c3 = exchange(jnp.concatenate([c_whole[320:], c_total], axis=0), "x", 0, True)
     a2n = take(a2n)
     a_near = (a_keep_near[0] + a1n[0]) + a2n
-    a3n = exchange(a_near[2:4], "y", 0)
+    a3n = exchange(a_near[2:4], "y", 0, True)
     b2n = take(b2n)
     b_near = (b_keep_near[0] + b1n[0]) + b2n
     b3 = take(b3)
     b4 = exchange(b_near[1] + b3[1], "z", 1)
     c3 = take(c3)
     c_out, c_stay, c_total = both(c_whole[:320], c3, c_total, 160)
-    c4 = exchange(c_out, "x", 1)
+    c4 = exchange(c_out, "x", 1, True)
     a3f = take(a3f)
     a3n = take(a3n)
-    a4 = exchange(jnp.concatenate([a_far[1] + a3f[1], a_near[1] + a3n[1]], axis=0), "y", 1)
+    a4 = exchange(jnp.concatenate([a_far[1] + a3f[1], a_near[1] + a3n[1]], axis=0), "y", 1, True)
     b4 = take(b4)
     b_whole = (b_near[0] + b3[0]) + b4
-    b5 = exchange(b_whole[2:4], "x", 0)
+    b5 = exchange(b_whole[2:4], "x", 0, True)
     c4 = take(c4)
     c_whole, c_total = c_stay + c4[:160], c_total + c4[160:]
-    c5 = exchange(jnp.concatenate([c_whole[80:], c_total], axis=0), "y", 0)
+    c5 = exchange(jnp.concatenate([c_whole[80:], c_total], axis=0), "y", 0, True)
     a4 = take(a4)
     a_far, a_near = (a_far[0] + a3f[0]) + a4[:2], (a_near[0] + a3n[0]) + a4[2:]
     a5 = exchange(a_far, "z", 0)
     b5 = take(b5)
-    b6 = exchange(b_whole[1] + b5[1], "x", 1)
+    b6 = exchange(b_whole[1] + b5[1], "x", 1, True)
     c5 = take(c5)
     c_out, c_stay, c_total = both(c_whole[:80], c5, c_total, 40)
-    c6 = exchange(c_out, "y", 1)
-    a5 = together([take(a5), b6])[0]
+    c6 = exchange(c_out, "y", 1, True)
+    a5 = take(a5)
     a6 = exchange(a_near[1] + a5[1], "z", 1)
     b6, c6, a6 = together([b6, c6, a6])
     a = (a_near[0] + a5[0]) + a6

time: 146 us -> 140 us (0.959)
  waiting for transfers between devices: 75.6 us -> 69.4 us
    ppermute x23, waiting for transfers between devices: 75.6 us -> 69.4 us  [exchange(): return lax.ppermute(value, ('section', 'dp'), pairs)]
  transfers between devices with their start and end apart: 23 -> 23, of which waited for: 19 -> 16; matrix products, arithmetic and copies ran while one was open for 2% -> 2% of each run, Pallas kernels for 9% -> 9%
where the time goes in v8:
time: 140 us; the launch traced here: 139 us
  waiting for transfers between devices  69.4 us (50%)
  starting transfers between devices  37.8 us (27%)
  Pallas kernels  25.9 us (18%)
  other arithmetic  4.04 us (3%)
  between operations  1.53 us (1%)
    ppermute x23, waiting for transfers between devices, exchange(): return lax.ppermute(value, ('section', 'dp'), pairs)  69.4 us
    ppermute x23, starting transfers between devices, exchange(): return lax.ppermute(value, ('section', 'dp'), pairs)  37.8 us
    pallas_call x2, Pallas kernels, partials(): pl.pallas_call(functools.partial(products, half), out_shape=[jax.ShapeDty...  25.9 us
  transfers between devices with their start and end apart: 23, of which 16 were waited for; matrix products, arithmetic and copies ran while one was open for 2% of the time, Pallas kernels for 9%

profile of v8, /device:TPU:0, one launch (start us, length us, event | category | flops | bytes accessed | tf_op | source)
XLA Modules:
  0.0 138.9 jit_solution(3503667404827959121)
XLA Ops:
  1.3 12.9 %shard_map.55 = (f32[2,4,2,40,896]{4,3,2,1,0:T(8,128)S(1)}, f32[2,4,2,40,896]{4,3,2,1,0:T(8,128)S(1)}, f32[2,2,4,40,896]{4,3,2,1,0:T(8,128)S(1)}, f32[2,2,4,40,8...) custom-call(s32[1]{0:T(128)S(6)} %copy.6.failed, s32[1]{0:T(128)S(6)} %copy.7.counts, ...), custom_call_target="tpu_custom_call" | custom-call | flops 1024 | bytes 1024 | tf_op jit(solution)/shard_map/pallas_call | solution.py:93
  14.2 2.1 %collective-permute-start.1 = (f32[1288,768]{1,0:T(8,128)S(1)}, f32[1288,768]{1,0:T(8,128)S(1)}, u32[]{:S(2)}, u32[]{:S(2)}) collective-permute-start(f32[1288,768]{1,0:T(8,128)S(1)} %get-tuple-element.56), channel_id=1, source_target_pairs={{0,16},{1,17},{2,18},{3,19},{4,20},{5,21},{6,22},{7,23},{8,24},{9,... | collective-permute-start | bytes 11870216 | tf_op jit(solution)/shard_map/ppermute | solution.py:24
  16.3 1.5 %collective-permute-start.3 = (f32[2,4,2,40,896]{4,3,2,1,0:T(8,128)S(1)}, f32[2,4,2,40,896]{4,3,2,1,0:T(8,128)S(1)}, u32[]{:S(2)}, u32[]{:S(2)}) collective-permute-start(f32[2,4,2,40,896]{4,3,2,1,0:T(8,128)S(1)} %get-tuple-element.58), channel_id=1, source_target_pairs={{0,1},{1,0},{2,3},{3,2},{4,5},{5,4},{6,7},{7,6},{8,9},{9,8},{10,11... | collective-permute-start | bytes 6881288 | tf_op jit(solution)/shard_map/ppermute | solution.py:24
  17.8 1.6 %collective-permute-start.2 = (f32[2,2,4,40,896]{4,3,2,1,0:T(8,128)S(1)}, f32[2,2,4,40,896]{4,3,2,1,0:T(8,128)S(1)}, u32[]{:S(2)}, u32[]{:S(2)}) collective-permute-start(f32[2,2,4,40,896]{4,3,2,1,0:T(8,128)S(1)} %get-tuple-element.57), channel_id=1, source_target_pairs={{0,4},{1,5},{2,6},{3,7},{4,0},{5,1},{6,2},{7,3},{8,12},{9,13},{10,... | collective-permute-start | bytes 6881288 | tf_op jit(solution)/shard_map/ppermute | solution.py:24
  19.4 12.9 %shard_map.56 = (f32[2,4,2,40,896]{4,3,2,1,0:T(8,128)S(1)}, f32[2,4,2,40,896]{4,3,2,1,0:T(8,128)S(1)}, f32[2,2,4,40,896]{4,3,2,1,0:T(8,128)S(1)}, f32[2,2,4,40,896]{4,3,2,1,0:T(8,128)S(1)}, f32[1280,768]{1,0:T(8,128)S(1)}) custom-call(s32[1]{0:T(128)S(6)} %copy.6.failed, s32[1]{0:T(128)S(6)} %copy.7.counts, s32[1,6]{1,0:T(1,128)} %order.3, ...), custom_call_target="tpu_custom_call" | custom-call | flops 1024 | bytes 1024 | tf_op jit(solution)/shard_map/pallas_call | solution.py:93
  33.4 11.1 %collective-permute-done.3 = f32[2,4,2,40,896]{4,3,2,1,0:T(8,128)S(1)} collective-permute-done((f32[2,4,2,40,896]{4,3,2,1,0:T(8,128)S(1)}, f32[2,4,2,40,896]{4,3,2,1,0:T(8,128)S(1)}, u32[]{:S(2)}, u32[]{:S(2)}) %collective-permute-start.3) | collective-permute-done | bytes 2293792 | tf_op jit(solution)/shard_map/ppermute | solution.py:24
  44.5 1.5 %collective-permute-done.2 = f32[2,2,4,40,896]{4,3,2,1,0:T(8,128)S(1)} collective-permute-done((f32[2,2,4,40,896]{4,3,2,1,0:T(8,128)S(1)}, f32[2,2,4,40,896]{4,3,2,1,0:T(8,128)S(1)}, u32[]{:S(2)}, u32[]{:S(2)}) %collective-permute-start.2) | collective-permute-done | bytes 2293792 | tf_op jit(solution)/shard_map/ppermute | solution.py:24
  46.0 14.3 %collective-permute-done.1 = f32[1288,768]{1,0:T(8,128)S(1)} collective-permute-done((f32[1288,768]{1,0:T(8,128)S(1)}, f32[1288,768]{1,0:T(8,128)S(1)}, u32[]{:S(2)}, u32[]{:S(2)}) %collective-permute-start.1) | collective-permute-done | bytes 3956768 | tf_op jit(solution)/shard_map/ppermute | solution.py:24
  60.8 4.3 %collective-permute-start.7 = (f32[648,768]{1,0:T(8,128)S(1)}, f32[648,768]{1,0:T(8,128)S(1)}, u32[]{:S(2)}, u32[]{:S(2)}) collective-permute-start(f32[648,768]{1,0:T(8,128)S(1)} %pad_maximum_fusion), channel_id=1, source_target_pairs={{0,48},{1,49},{2,50},{3,51},{4,52},{5,53},{6,54},{7,55},{8,56},{9,... | collective-permute-start | bytes 5971976 | tf_op jit(solution)/shard_map/ppermute | solution.py:24
  65.2 3.1 %collective-permute-start.6 = (f32[2,4,40,896]{3,2,1,0:T(8,128)S(1)}, f32[2,4,40,896]{3,2,1,0:T(8,128)S(1)}, u32[]{:S(2)}, u32[]{:S(2)}) collective-permute-start(f32[2,4,40,896]{3,2,1,0:T(8,128)S(1)} %add_bitcast_fusion.1), channel_id=1, source_target_pairs={{0,12},{1,13},{2,14},{3,15},{4,8},{5,9},{6,10},{7,11},{8,4},{9,5},... | collective-permute-start | bytes 3440648 | tf_op jit(solution)/shard_map/ppermute | solution.py:24
  68.4 2.8 %collective-permute-start.5 = (f32[4,2,40,896]{3,2,1,0:T(8,128)S(1)}, f32[4,2,40,896]{3,2,1,0:T(8,128)S(1)}, u32[]{:S(2)}, u32[]{:S(2)}) collective-permute-start(f32[4,2,40,896]{3,2,1,0:T(8,128)S(1)} %fusion.2), channel_id=1, source_target_pairs={{0,3},{1,2},{2,1},{3,0},{4,7},{5,6},{6,5},{7,4},{8,11},{9,10},{10,... | collective-permute-start | bytes 3440648 | tf_op jit(solution)/shard_map/ppermute | solution.py:24
  71.8 4.5 %collective-permute-done.8 = f32[2,2,4,40,896]{4,3,2,1,0:T(8,128)S(1)} collective-permute-done((f32[2,2,4,40,896]{4,3,2,1,0:T(8,128)S(1)}, f32[2,2,4,40,896]{4,3,2,1,0:T(8,128)S(1)}, u32[]{:S(2)}, u32[]{:S(2)}) %collective-permute-start.8) | collective-permute-done | bytes 2293792 | tf_op jit(solution)/shard_map/ppermute | solution.py:24
  76.4 1.5 %collective-permute-start.4 = (f32[4,2,40,896]{3,2,1,0:T(8,128)S(1)}, f32[4,2,40,896]{3,2,1,0:T(8,128)S(1)}, u32[]{:S(2)}, u32[]{:S(2)}) collective-permute-start(f32[4,2,40,896]{3,2,1,0:T(8,128)S(1)} %add_bitcast_fusion.2), channel_id=1, source_target_pairs={{0,3},{1,2},{2,1},{3,0},{4,7},{5,6},{6,5},{7,4},{8,11},{9,10},{10,... | collective-permute-start | bytes 3440648 | tf_op jit(solution)/shard_map/ppermute | solution.py:24
  78.0 3.1 %collective-permute-start.13 = (f32[2,4,40,896]{3,2,1,0:T(8,128)S(1)}, f32[2,4,40,896]{3,2,1,0:T(8,128)S(1)}, u32[]{:S(2)}, u32[]{:S(2)}) collective-permute-start(f32[2,4,40,896]{3,2,1,0:T(8,128)S(1)} %add_bitcast_fusion), channel_id=1, source_target_pairs={{0,12},{1,13},{2,14},{3,15},{4,8},{5,9},{6,10},{7,11},{8,4},{9,5},... | collective-permute-start | bytes 3440648 | tf_op jit(solution)/shard_map/ppermute | solution.py:24
  81.1 4.7 %collective-permute-done.6 = f32[2,4,40,896]{3,2,1,0:T(8,128)S(1)} collective-permute-done((f32[2,4,40,896]{3,2,1,0:T(8,128)S(1)}, f32[2,4,40,896]{3,2,1,0:T(8,128)S(1)}, u32[]{:S(2)}, u32[]{:S(2)}) %collective-permute-start.6) | collective-permute-done | bytes 1146912 | tf_op jit(solution)/shard_map/ppermute | solution.py:24
  85.8 2.2 %collective-permute-done.7 = f32[648,768]{1,0:T(8,128)S(1)} collective-permute-done((f32[648,768]{1,0:T(8,128)S(1)}, f32[648,768]{1,0:T(8,128)S(1)}, u32[]{:S(2)}, u32[]{:S(2)}) %collective-permute-start.7) | collective-permute-done | bytes 1990688 | tf_op jit(solution)/shard_map/ppermute | solution.py:24
  88.9 3.1 %collective-permute-start.11 = (f32[328,768]{1,0:T(8,128)S(1)}, f32[328,768]{1,0:T(8,128)S(1)}, u32[]{:S(2)}, u32[]{:S(2)}) collective-permute-start(f32[328,768]{1,0:T(8,128)S(1)} %pad_maximum_fusion.1), channel_id=1, source_target_pairs={{0,3},{1,2},{2,1},{3,0},{4,7},{5,6},{6,5},{7,4},{8,11},{9,10},{10,... | collective-permute-start | bytes 3022856 | tf_op jit(solution)/shard_map/ppermute | solution.py:24
  92.2 3.1 %collective-permute-start.10 = (f32[2,2,40,896]{3,2,1,0:T(8,128)S(1)}, f32[2,2,40,896]{3,2,1,0:T(8,128)S(1)}, u32[]{:S(2)}, u32[]{:S(2)}) collective-permute-start(f32[2,2,40,896]{3,2,1,0:T(8,128)S(1)} %slice.270), channel_id=1, source_target_pairs={{0,12},{1,13},{2,14},{3,15},{4,8},{5,9},{6,10},{7,11},{8,4},{9,5},... | collective-permute-start | bytes 1720328 | tf_op jit(solution)/shard_map/ppermute | solution.py:24
  95.3 2.5 %collective-permute-done.4 = f32[4,2,40,896]{3,2,1,0:T(8,128)S(1)} collective-permute-done((f32[4,2,40,896]{3,2,1,0:T(8,128)S(1)}, f32[4,2,40,896]{3,2,1,0:T(8,128)S(1)}, u32[]{:S(2)}, u32[]{:S(2)}) %collective-permute-start.4) | collective-permute-done | bytes 1146912 | tf_op jit(solution)/shard_map/ppermute | solution.py:24
  98.3 3.0 %collective-permute-start.9 = (f32[2,2,40,896]{3,2,1,0:T(8,128)S(1)}, f32[2,2,40,896]{3,2,1,0:T(8,128)S(1)}, u32[]{:S(2)}, u32[]{:S(2)}) collective-permute-start(f32[2,2,40,896]{3,2,1,0:T(8,128)S(1)} %slice.268), channel_id=1, source_target_pairs={{0,12},{1,13},{2,14},{3,15},{4,8},{5,9},{6,10},{7,11},{8,4},{9,5},... | collective-permute-start | bytes 1720328 | tf_op jit(solution)/shard_map/ppermute | solution.py:24
  101.6 2.5 %collective-permute-done.12 = f32[2,4,40,896]{3,2,1,0:T(8,128)S(1)} collective-permute-done((f32[2,4,40,896]{3,2,1,0:T(8,128)S(1)}, f32[2,4,40,896]{3,2,1,0:T(8,128)S(1)}, u32[]{:S(2)}, u32[]{:S(2)}) %collective-permute-start.12) | collective-permute-done | bytes 1146912 | tf_op jit(solution)/shard_map/ppermute | solution.py:24
  104.1 4.5 %collective-permute-done.11 = f32[328,768]{1,0:T(8,128)S(1)} collective-permute-done((f32[328,768]{1,0:T(8,128)S(1)}, f32[328,768]{1,0:T(8,128)S(1)}, u32[]{:S(2)}, u32[]{:S(2)}) %collective-permute-start.11) | collective-permute-done | bytes 1007648 | tf_op jit(solution)/shard_map/ppermute | solution.py:24
  109.3 1.1 collective-permute-done.9
  111.0 8.7 %collective-permute-done.16 = f32[4,40,896]{2,1,0:T(8,128)S(1)} collective-permute-done((f32[4,40,896]{2,1,0:T(8,128)S(1)}, f32[4,40,896]{2,1,0:T(8,128)S(1)}, u32[]{:S(2)}, u32[]{:S(2)}) %collective-permute-start.16) | collective-permute-done | bytes 573472 | tf_op jit(solution)/shard_map/ppermute | solution.py:24
  120.0 2.8 %collective-permute-start.19 = (f32[2,40,896]{2,1,0:T(8,128)S(1)}, f32[2,40,896]{2,1,0:T(8,128)S(1)}, u32[]{:S(2)}, u32[]{:S(2)}) collective-permute-start(f32[2,40,896]{2,1,0:T(8,128)S(1)} %slice.281), channel_id=1, source_target_pairs={{0,3},{1,2},{2,1},{3,0},{4,7},{5,6},{6,5},{7,4},{8,11},{9,10},{10,... | collective-permute-start | bytes 860168 | tf_op jit(solution)/shard_map/ppermute | solution.py:24
  122.8 1.0 collective-permute-start.18
  123.9 1.5 %collective-permute-start.17 = (f32[2,40,896]{2,1,0:T(8,128)S(1)}, f32[2,40,896]{2,1,0:T(8,128)S(1)}, u32[]{:S(2)}, u32[]{:S(2)}) collective-permute-start(f32[2,40,896]{2,1,0:T(8,128)S(1)} %get-tuple-element.87), channel_id=1, source_target_pairs={{0,16},{1,17},{2,18},{3,19},{4,20},{5,21},{6,22},{7,23},{8,24},{9,... | collective-permute-start | bytes 860168 | tf_op jit(solution)/shard_map/ppermute | solution.py:24
  125.4 2.5 %collective-permute-done.19 = f32[2,40,896]{2,1,0:T(8,128)S(1)} collective-permute-done((f32[2,40,896]{2,1,0:T(8,128)S(1)}, f32[2,40,896]{2,1,0:T(8,128)S(1)}, u32[]{:S(2)}, u32[]{:S(2)}) %collective-permute-start.19) | collective-permute-done | bytes 286752 | tf_op jit(solution)/shard_map/ppermute | solution.py:24
  127.9 3.4 %collective-permute-done.18 = f32[88,768]{1,0:T(8,128)S(1)} collective-permute-done((f32[88,768]{1,0:T(8,128)S(1)}, f32[88,768]{1,0:T(8,128)S(1)}, u32[]{:S(2)}, u32[]{:S(2)}) %collective-permute-start.18) | collective-permute-done | bytes 270368 | tf_op jit(solution)/shard_map/ppermute | solution.py:24
  131.5 1.1 collective-permute-start.22
  132.8 5.2 %collective-permute-done.22 = f32[40,896]{1,0:T(8,128)S(1)} collective-permute-done((f32[40,896]{1,0:T(8,128)S(1)}, f32[40,896]{1,0:T(8,128)S(1)}, u32[]{:S(2)}, u32[]{:S(2)}) %collective-permute-start.22) | collective-permute-done | bytes 143392 | tf_op jit(solution)/shard_map/ppermute | solution.py:24
  138.1 0.8 maximum_divide_fusion
  (58 shorter events, 6.5 us)
Async XLA Ops:
  14.2 46.0 %collective-permute-start.1 = (f32[1288,768]{1,0:T(8,128)S(1)}, f32[1288,768]{1,0:T(8,128)S(1)}, u32[]{:S(2)}, u32[]{:S(2)}) collective-permute-start(f32[1288,768]{1,0:T(8,128)S(1)} %get-tuple-element.56), channel_id=1, source_target_pairs={{0,16},{1,17},{2,18},{3,19},{4,20},{5,21},{6,22},{7,23},{8,24},{9,... | collective-permute-start | bytes 11870216 | tf_op jit(solution)/shard_map/ppermute | solution.py:24
  16.3 28.1 %collective-permute-start.3 = (f32[2,4,2,40,896]{4,3,2,1,0:T(8,128)S(1)}, f32[2,4,2,40,896]{4,3,2,1,0:T(8,128)S(1)}, u32[]{:S(2)}, u32[]{:S(2)}) collective-permute-start(f32[2,4,2,40,896]{4,3,2,1,0:T(8,128)S(1)} %get-tuple-element.58), channel_id=1, source_target_pairs={{0,1},{1,0},{2,3},{3,2},{4,5},{5,4},{6,7},{7,6},{8,9},{9,8},{10,11... | collective-permute-start | bytes 6881288 | tf_op jit(solution)/shard_map/ppermute | solution.py:24
  17.8 28.1 %collective-permute-start.2 = (f32[2,2,4,40,896]{4,3,2,1,0:T(8,128)S(1)}, f32[2,2,4,40,896]{4,3,2,1,0:T(8,128)S(1)}, u32[]{:S(2)}, u32[]{:S(2)}) collective-permute-start(f32[2,2,4,40,896]{4,3,2,1,0:T(8,128)S(1)} %get-tuple-element.57), channel_id=1, source_target_pairs={{0,4},{1,5},{2,6},{3,7},{4,0},{5,1},{6,2},{7,3},{8,12},{9,13},{10,... | collective-permute-start | bytes 6881288 | tf_op jit(solution)/shard_map/ppermute | solution.py:24
  32.3 39.4 %collective-permute-start = (f32[2,4,2,40,896]{4,3,2,1,0:T(8,128)S(1)}, f32[2,4,2,40,896]{4,3,2,1,0:T(8,128)S(1)}, u32[]{:S(2)}, u32[]{:S(2)}) collective-permute-start(f32[2,4,2,40,896]{4,3,2,1,0:T(8,128)S(1)} %get-tuple-element.55), channel_id=1, source_target_pairs={{0,1},{1,0},{2,3},{3,2},{4,5},{5,4},{6,7},{7,6},{8,9},{9,8},{10,11... | collective-permute-start | bytes 6881288 | tf_op jit(solution)/shard_map/ppermute | solution.py:24
  33.0 43.3 %collective-permute-start.8 = (f32[2,2,4,40,896]{4,3,2,1,0:T(8,128)S(1)}, f32[2,2,4,40,896]{4,3,2,1,0:T(8,128)S(1)}, u32[]{:S(2)}, u32[]{:S(2)}) collective-permute-start(f32[2,2,4,40,896]{4,3,2,1,0:T(8,128)S(1)} %get-tuple-element.66), channel_id=1, source_target_pairs={{0,4},{1,5},{2,6},{3,7},{4,0},{5,1},{6,2},{7,3},{8,12},{9,13},{10,... | collective-permute-start | bytes 6881288 | tf_op jit(solution)/shard_map/ppermute | solution.py:24
  60.8 27.1 %collective-permute-start.7 = (f32[648,768]{1,0:T(8,128)S(1)}, f32[648,768]{1,0:T(8,128)S(1)}, u32[]{:S(2)}, u32[]{:S(2)}) collective-permute-start(f32[648,768]{1,0:T(8,128)S(1)} %pad_maximum_fusion), channel_id=1, source_target_pairs={{0,48},{1,49},{2,50},{3,51},{4,52},{5,53},{6,54},{7,55},{8,56},{9,... | collective-permute-start | bytes 5971976 | tf_op jit(solution)/shard_map/ppermute | solution.py:24
  65.2 20.6 %collective-permute-start.6 = (f32[2,4,40,896]{3,2,1,0:T(8,128)S(1)}, f32[2,4,40,896]{3,2,1,0:T(8,128)S(1)}, u32[]{:S(2)}, u32[]{:S(2)}) collective-permute-start(f32[2,4,40,896]{3,2,1,0:T(8,128)S(1)} %add_bitcast_fusion.1), channel_id=1, source_target_pairs={{0,12},{1,13},{2,14},{3,15},{4,8},{5,9},{6,10},{7,11},{8,4},{9,5},... | collective-permute-start | bytes 3440648 | tf_op jit(solution)/shard_map/ppermute | solution.py:24
  68.4 17.4 %collective-permute-start.5 = (f32[4,2,40,896]{3,2,1,0:T(8,128)S(1)}, f32[4,2,40,896]{3,2,1,0:T(8,128)S(1)}, u32[]{:S(2)}, u32[]{:S(2)}) collective-permute-start(f32[4,2,40,896]{3,2,1,0:T(8,128)S(1)} %fusion.2), channel_id=1, source_target_pairs={{0,3},{1,2},{2,1},{3,0},{4,7},{5,6},{6,5},{7,4},{8,11},{9,10},{10,... | collective-permute-start | bytes 3440648 | tf_op jit(solution)/shard_map/ppermute | solution.py:24
  76.4 21.5 %collective-permute-start.4 = (f32[4,2,40,896]{3,2,1,0:T(8,128)S(1)}, f32[4,2,40,896]{3,2,1,0:T(8,128)S(1)}, u32[]{:S(2)}, u32[]{:S(2)}) collective-permute-start(f32[4,2,40,896]{3,2,1,0:T(8,128)S(1)} %add_bitcast_fusion.2), channel_id=1, source_target_pairs={{0,3},{1,2},{2,1},{3,0},{4,7},{5,6},{6,5},{7,4},{8,11},{9,10},{10,... | collective-permute-start | bytes 3440648 | tf_op jit(solution)/shard_map/ppermute | solution.py:24
  78.0 20.1 %collective-permute-start.13 = (f32[2,4,40,896]{3,2,1,0:T(8,128)S(1)}, f32[2,4,40,896]{3,2,1,0:T(8,128)S(1)}, u32[]{:S(2)}, u32[]{:S(2)}) collective-permute-start(f32[2,4,40,896]{3,2,1,0:T(8,128)S(1)} %add_bitcast_fusion), channel_id=1, source_target_pairs={{0,12},{1,13},{2,14},{3,15},{4,8},{5,9},{6,10},{7,11},{8,4},{9,5},... | collective-permute-start | bytes 3440648 | tf_op jit(solution)/shard_map/ppermute | solution.py:24
  88.2 15.9 %collective-permute-start.12 = (f32[2,4,40,896]{3,2,1,0:T(8,128)S(1)}, f32[2,4,40,896]{3,2,1,0:T(8,128)S(1)}, u32[]{:S(2)}, u32[]{:S(2)}) collective-permute-start(f32[2,4,40,896]{3,2,1,0:T(8,128)S(1)} %bitcast_add_fusion.1), channel_id=1, source_target_pairs={{0,16},{1,17},{2,18},{3,19},{4,20},{5,21},{6,22},{7,23},{8,24},{9,... | collective-permute-start | bytes 3440648 | tf_op jit(solution)/shard_map/ppermute | solution.py:24
  88.9 19.7 %collective-permute-start.11 = (f32[328,768]{1,0:T(8,128)S(1)}, f32[328,768]{1,0:T(8,128)S(1)}, u32[]{:S(2)}, u32[]{:S(2)}) collective-permute-start(f32[328,768]{1,0:T(8,128)S(1)} %pad_maximum_fusion.1), channel_id=1, source_target_pairs={{0,3},{1,2},{2,1},{3,0},{4,7},{5,6},{6,5},{7,4},{8,11},{9,10},{10,... | collective-permute-start | bytes 3022856 | tf_op jit(solution)/shard_map/ppermute | solution.py:24
  92.2 17.1 %collective-permute-start.10 = (f32[2,2,40,896]{3,2,1,0:T(8,128)S(1)}, f32[2,2,40,896]{3,2,1,0:T(8,128)S(1)}, u32[]{:S(2)}, u32[]{:S(2)}) collective-permute-start(f32[2,2,40,896]{3,2,1,0:T(8,128)S(1)} %slice.270), channel_id=1, source_target_pairs={{0,12},{1,13},{2,14},{3,15},{4,8},{5,9},{6,10},{7,11},{8,4},{9,5},... | collective-permute-start | bytes 1720328 | tf_op jit(solution)/shard_map/ppermute | solution.py:24
  98.3 12.0 %collective-permute-start.9 = (f32[2,2,40,896]{3,2,1,0:T(8,128)S(1)}, f32[2,2,40,896]{3,2,1,0:T(8,128)S(1)}, u32[]{:S(2)}, u32[]{:S(2)}) collective-permute-start(f32[2,2,40,896]{3,2,1,0:T(8,128)S(1)} %slice.268), channel_id=1, source_target_pairs={{0,12},{1,13},{2,14},{3,15},{4,8},{5,9},{6,10},{7,11},{8,4},{9,5},... | collective-permute-start | bytes 1720328 | tf_op jit(solution)/shard_map/ppermute | solution.py:24
  108.7 11.0 %collective-permute-start.16 = (f32[4,40,896]{2,1,0:T(8,128)S(1)}, f32[4,40,896]{2,1,0:T(8,128)S(1)}, u32[]{:S(2)}, u32[]{:S(2)}) collective-permute-start(f32[4,40,896]{2,1,0:T(8,128)S(1)} %fusion.5), channel_id=1, source_target_pairs={{0,48},{1,49},{2,50},{3,51},{4,52},{5,53},{6,54},{7,55},{8,56},{9,... | collective-permute-start | bytes 1720328 | tf_op jit(solution)/shard_map/ppermute | solution.py:24
  108.9 10.8 %collective-permute-start.15 = (f32[168,768]{1,0:T(8,128)S(1)}, f32[168,768]{1,0:T(8,128)S(1)}, u32[]{:S(2)}, u32[]{:S(2)}) collective-permute-start(f32[168,768]{1,0:T(8,128)S(1)} %pad_maximum_fusion.3), channel_id=1, source_target_pairs={{0,1},{1,0},{2,3},{3,2},{4,5},{5,4},{6,7},{7,6},{8,9},{9,8},{10,11... | collective-permute-start | bytes 1548296 | tf_op jit(solution)/shard_map/ppermute | solution.py:24
  110.5 12.3 %collective-permute-start.14 = (f32[4,40,896]{2,1,0:T(8,128)S(1)}, f32[4,40,896]{2,1,0:T(8,128)S(1)}, u32[]{:S(2)}, u32[]{:S(2)}) collective-permute-start(f32[4,40,896]{2,1,0:T(8,128)S(1)} %pad_maximum_fusion.2), channel_id=1, source_target_pairs={{0,4},{1,5},{2,6},{3,7},{4,0},{5,1},{6,2},{7,3},{8,12},{9,13},{10,... | collective-permute-start | bytes 1720328 | tf_op jit(solution)/shard_map/ppermute | solution.py:24
  120.0 7.9 %collective-permute-start.19 = (f32[2,40,896]{2,1,0:T(8,128)S(1)}, f32[2,40,896]{2,1,0:T(8,128)S(1)}, u32[]{:S(2)}, u32[]{:S(2)}) collective-permute-start(f32[2,40,896]{2,1,0:T(8,128)S(1)} %slice.281), channel_id=1, source_target_pairs={{0,3},{1,2},{2,1},{3,0},{4,7},{5,6},{6,5},{7,4},{8,11},{9,10},{10,... | collective-permute-start | bytes 860168 | tf_op jit(solution)/shard_map/ppermute | solution.py:24
  122.8 8.5 %collective-permute-start.18 = (f32[88,768]{1,0:T(8,128)S(1)}, f32[88,768]{1,0:T(8,128)S(1)}, u32[]{:S(2)}, u32[]{:S(2)}) collective-permute-start(f32[88,768]{1,0:T(8,128)S(1)} %pad_maximum_fusion.4), channel_id=1, source_target_pairs={{0,12},{1,13},{2,14},{3,15},{4,8},{5,9},{6,10},{7,11},{8,4},{9,5},... | collective-permute-start | bytes 811016 | tf_op jit(solution)/shard_map/ppermute | solution.py:24
  123.9 7.5 %collective-permute-start.17 = (f32[2,40,896]{2,1,0:T(8,128)S(1)}, f32[2,40,896]{2,1,0:T(8,128)S(1)}, u32[]{:S(2)}, u32[]{:S(2)}) collective-permute-start(f32[2,40,896]{2,1,0:T(8,128)S(1)} %get-tuple-element.87), channel_id=1, source_target_pairs={{0,16},{1,17},{2,18},{3,19},{4,20},{5,21},{6,22},{7,23},{8,24},{9,... | collective-permute-start | bytes 860168 | tf_op jit(solution)/shard_map/ppermute | solution.py:24
  131.4 6.5 %collective-permute-start.21 = (f32[48,768]{1,0:T(8,128)S(1)}, f32[48,768]{1,0:T(8,128)S(1)}, u32[]{:S(2)}, u32[]{:S(2)}) collective-permute-start(f32[48,768]{1,0:T(8,128)S(1)} %pad_maximum_fusion.5), channel_id=1, source_target_pairs={{0,4},{1,5},{2,6},{3,7},{4,0},{5,1},{6,2},{7,3},{8,12},{9,13},{10,... | collective-permute-start | bytes 442376 | tf_op jit(solution)/shard_map/ppermute | solution.py:24
  131.5 6.4 %collective-permute-start.22 = (f32[40,896]{1,0:T(8,128)S(1)}, f32[40,896]{1,0:T(8,128)S(1)}, u32[]{:S(2)}, u32[]{:S(2)}) collective-permute-start(f32[40,896]{1,0:T(8,128)S(1)} %fusion.15), channel_id=1, source_target_pairs={{0,48},{1,49},{2,50},{3,51},{4,52},{5,53},{6,54},{7,55},{8,56},{9,... | collective-permute-start | bytes 430088 | tf_op jit(solution)/shard_map/ppermute | solution.py:24
  132.7 5.3 %collective-permute-start.20 = (f32[40,896]{1,0:T(8,128)S(1)}, f32[40,896]{1,0:T(8,128)S(1)}, u32[]{:S(2)}, u32[]{:S(2)}) collective-permute-start(f32[40,896]{1,0:T(8,128)S(1)} %fusion.16), channel_id=1, source_target_pairs={{0,1},{1,0},{2,3},{3,2},{4,5},{5,4},{6,7},{7,6},{8,9},{9,8},{10,11... | collective-permute-start | bytes 430088 | tf_op jit(solution)/shard_map/ppermute | solution.py:24

commit v9 on v8

--- a/solution.py
+++ b/solution.py
@@ -22,6 +22,12 @@
             p = d // stride % 4
             pairs.append((section * 64 + d, section * 64 + d + ((p ^ flip) - p) * stride))
     return lax.ppermute(value, ("section", "dp"), pairs)
+
+
+def opposite(value, axis):
+    stride = STRIDE[axis]
+    places = [(d, d + ((d // stride % 4 ^ 2) - d // stride % 4) * stride) for d in range(64)]
+    return lax.ppermute(value, "dp", places)
 
 
 def products(half, failed, counts, order, act, cot, *refs):
@@ -163,25 +169,22 @@
     a4 = exchange(jnp.concatenate([a_far[1] + a3f[1], a_near[1] + a3n[1]], axis=0), "y", 1, True)
     b4 = take(b4)
     b_whole = (b_near[0] + b3[0]) + b4
-    b5 = exchange(b_whole[2:4], "x", 0, True)
+    b5 = [exchange(b_whole[2], "x", 0, True), exchange(b_whole[1], "x", 1, True), opposite(b_whole[3], "x")]
     c4 = take(c4)
     c_whole, c_total = c_stay + c4[:160], c_total + c4[160:]
-    c5 = exchange(jnp.concatenate([c_whole[80:], c_total], axis=0), "y", 0, True)
-    a4 = take(a4)
+    outs = [jnp.concatenate([c_whole[40 * k:40 * (k + 1)], c_total], axis=0) for k in range(4)]
+    c5 = [exchange(outs[2], "y", 0, True), exchange(outs[1], "y", 1, True), opposite(outs[3], "y")]
+    a4 = together([a4, b5[0], taken])[0]
     a_far, a_near = (a_far[0] + a3f[0]) + a4[:2], (a_near[0] + a3n[0]) + a4[2:]
-    a5 = exchange(a_far, "z", 0)
-    b5 = take(b5)
-    b6 = exchange(b_whole[1] + b5[1], "x", 1, True)
-    c5 = take(c5)
-    c_out, c_stay, c_total = both(c_whole[:80], c5, c_total, 40)
-    c6 = exchange(c_out, "y", 1, True)
-    a5 = take(a5)
-    a6 = exchange(a_near[1] + a5[1], "z", 1)
-    b6, c6, a6 = together([b6, c6, a6])
-    a = (a_near[0] + a5[0]) + a6
-    b = (b_whole[0] + b5[0]) + b6
-    c = c_stay + c6[:40]
-    total = c_total + c6[40:]
+    a5 = [exchange(a_far[0], "z", 0), exchange(a_near[1], "z", 1), opposite(a_far[1], "z")]
+    *b5, taken = together([*b5, taken])
+    *c5, taken = together([*c5, b5[2]])
+    *a5, taken = together([*a5, c5[2]])
+    a = ((a_near[0] + a5[0]) + a5[1]) + a5[2]
+    b = ((b_whole[0] + b5[0]) + b5[1]) + b5[2]
+    c = ((outs[0] + c5[0]) + c5[1]) + c5[2]
+    total = c[40:]
+    c = c[:40]
     total = jnp.concatenate([total, total, total, total[:, :256]], axis=1)
     gradient = jnp.concatenate([a, b, c], axis=1)
     return (gradient.reshape(5, 8, 2560) / total).reshape(40, 2560)

time: 140 us -> 140 us (level)
  starting transfers between devices: 37.8 us -> 43.8 us
  waiting for transfers between devices: 69.4 us -> 64.4 us
    ppermute x23, waiting for transfers between devices: 69.4 us -> 62 us  [exchange(): return lax.ppermute(value, ('section', 'dp'), pairs)]
    ppermute x0 -> x3, starting transfers between devices: none -> 6.5 us  [opposite(): return lax.ppermute(value, 'dp', places)]
    ppermute x0 -> x3, waiting for transfers between devices: none -> 2.34 us  [opposite(): return lax.ppermute(value, 'dp', places)]
  transfers between devices with their start and end apart: 23 -> 26, of which waited for: 16 -> 18; matrix products, arithmetic and copies ran while one was open for 2% -> 2% of each run, Pallas kernels for 9% -> 9%
where the time goes in v9:
time: 140 us
  waiting for transfers between devices  64.4 us (46%)
  starting transfers between devices  43.8 us (31%)
  Pallas kernels  25.9 us (18%)
  other arithmetic  3.99 us (3%)
  between operations  1.53 us (1%)
    ppermute x23, waiting for transfers between devices, exchange(): return lax.ppermute(value, ('section', 'dp'), pairs)  62 us
    ppermute x23, starting transfers between devices, exchange(): return lax.ppermute(value, ('section', 'dp'), pairs)  37.3 us
    pallas_call x2, Pallas kernels, partials(): pl.pallas_call(functools.partial(products, half), out_shape=[jax.ShapeDty...  25.9 us
    ppermute x3, starting transfers between devices, opposite(): return lax.ppermute(value, 'dp', places)  6.5 us
  transfers between devices with their start and end apart: 26, of which 18 were waited for; matrix products, arithmetic and copies ran while one was open for 2% of the time, Pallas kernels for 9%

profile of v9, /device:TPU:0, one launch (start us, length us, event | category | flops | bytes accessed | tf_op | source)
XLA Modules:
  0.0 139.8 jit_solution(15913012104369841296)
XLA Ops:
  1.3 12.9 %shard_map.55 = (f32[2,4,2,40,896]{4,3,2,1,0:T(8,128)S(1)}, f32[2,4,2,40,896]{4,3,2,1,0:T(8,128)S(1)}, f32[2,2,4,40,896]{4,3,2,1,0:T(8,128)S(1)}, f32[2,2,4,40,8...) custom-call(s32[1]{0:T(128)S(6)} %copy.6.failed, s32[1]{0:T(128)S(6)} %copy.7.counts, ...), custom_call_target="tpu_custom_call" | custom-call | flops 1024 | bytes 1024 | tf_op jit(solution)/shard_map/pallas_call | solution.py:99
  14.2 2.1 %collective-permute-start.1 = (f32[1288,768]{1,0:T(8,128)S(1)}, f32[1288,768]{1,0:T(8,128)S(1)}, u32[]{:S(2)}, u32[]{:S(2)}) collective-permute-start(f32[1288,768]{1,0:T(8,128)S(1)} %get-tuple-element.59), channel_id=1, source_target_pairs={{0,16},{1,17},{2,18},{3,19},{4,20},{5,21},{6,22},{7,23},{8,24},{9,... | collective-permute-start | bytes 11870216 | tf_op jit(solution)/shard_map/ppermute | solution.py:24
  16.3 1.5 %collective-permute-start.3 = (f32[2,4,2,40,896]{4,3,2,1,0:T(8,128)S(1)}, f32[2,4,2,40,896]{4,3,2,1,0:T(8,128)S(1)}, u32[]{:S(2)}, u32[]{:S(2)}) collective-permute-start(f32[2,4,2,40,896]{4,3,2,1,0:T(8,128)S(1)} %get-tuple-element.61), channel_id=1, source_target_pairs={{0,1},{1,0},{2,3},{3,2},{4,5},{5,4},{6,7},{7,6},{8,9},{9,8},{10,11... | collective-permute-start | bytes 6881288 | tf_op jit(solution)/shard_map/ppermute | solution.py:24
  17.8 1.6 %collective-permute-start.2 = (f32[2,2,4,40,896]{4,3,2,1,0:T(8,128)S(1)}, f32[2,2,4,40,896]{4,3,2,1,0:T(8,128)S(1)}, u32[]{:S(2)}, u32[]{:S(2)}) collective-permute-start(f32[2,2,4,40,896]{4,3,2,1,0:T(8,128)S(1)} %get-tuple-element.60), channel_id=1, source_target_pairs={{0,4},{1,5},{2,6},{3,7},{4,0},{5,1},{6,2},{7,3},{8,12},{9,13},{10,... | collective-permute-start | bytes 6881288 | tf_op jit(solution)/shard_map/ppermute | solution.py:24
  19.4 12.9 %shard_map.56 = (f32[2,4,2,40,896]{4,3,2,1,0:T(8,128)S(1)}, f32[2,4,2,40,896]{4,3,2,1,0:T(8,128)S(1)}, f32[2,2,4,40,896]{4,3,2,1,0:T(8,128)S(1)}, f32[2,2,4,40,896]{4,3,2,1,0:T(8,128)S(1)}, f32[1280,768]{1,0:T(8,128)S(1)}) custom-call(s32[1]{0:T(128)S(6)} %copy.6.failed, s32[1]{0:T(128)S(6)} %copy.7.counts, s32[1,6]{1,0:T(1,128)} %order.3, ...), custom_call_target="tpu_custom_call" | custom-call | flops 1024 | bytes 1024 | tf_op jit(solution)/shard_map/pallas_call | solution.py:99
  33.4 11.1 %collective-permute-done.3 = f32[2,4,2,40,896]{4,3,2,1,0:T(8,128)S(1)} collective-permute-done((f32[2,4,2,40,896]{4,3,2,1,0:T(8,128)S(1)}, f32[2,4,2,40,896]{4,3,2,1,0:T(8,128)S(1)}, u32[]{:S(2)}, u32[]{:S(2)}) %collective-permute-start.3) | collective-permute-done | bytes 2293792 | tf_op jit(solution)/shard_map/ppermute | solution.py:24
  44.5 1.5 %collective-permute-done.2 = f32[2,2,4,40,896]{4,3,2,1,0:T(8,128)S(1)} collective-permute-done((f32[2,2,4,40,896]{4,3,2,1,0:T(8,128)S(1)}, f32[2,2,4,40,896]{4,3,2,1,0:T(8,128)S(1)}, u32[]{:S(2)}, u32[]{:S(2)}) %collective-permute-start.2) | collective-permute-done | bytes 2293792 | tf_op jit(solution)/shard_map/ppermute | solution.py:24
  46.0 14.3 %collective-permute-done.1 = f32[1288,768]{1,0:T(8,128)S(1)} collective-permute-done((f32[1288,768]{1,0:T(8,128)S(1)}, f32[1288,768]{1,0:T(8,128)S(1)}, u32[]{:S(2)}, u32[]{:S(2)}) %collective-permute-start.1) | collective-permute-done | bytes 3956768 | tf_op jit(solution)/shard_map/ppermute | solution.py:24
  60.8 4.3 %collective-permute-start.7 = (f32[648,768]{1,0:T(8,128)S(1)}, f32[648,768]{1,0:T(8,128)S(1)}, u32[]{:S(2)}, u32[]{:S(2)}) collective-permute-start(f32[648,768]{1,0:T(8,128)S(1)} %pad_maximum_fusion), channel_id=1, source_target_pairs={{0,48},{1,49},{2,50},{3,51},{4,52},{5,53},{6,54},{7,55},{8,56},{9,... | collective-permute-start | bytes 5971976 | tf_op jit(solution)/shard_map/ppermute | solution.py:24
  65.2 3.1 %collective-permute-start.6 = (f32[2,4,40,896]{3,2,1,0:T(8,128)S(1)}, f32[2,4,40,896]{3,2,1,0:T(8,128)S(1)}, u32[]{:S(2)}, u32[]{:S(2)}) collective-permute-start(f32[2,4,40,896]{3,2,1,0:T(8,128)S(1)} %add_bitcast_fusion.1), channel_id=1, source_target_pairs={{0,12},{1,13},{2,14},{3,15},{4,8},{5,9},{6,10},{7,11},{8,4},{9,5},... | collective-permute-start | bytes 3440648 | tf_op jit(solution)/shard_map/ppermute | solution.py:24
  68.4 2.8 %collective-permute-start.5 = (f32[4,2,40,896]{3,2,1,0:T(8,128)S(1)}, f32[4,2,40,896]{3,2,1,0:T(8,128)S(1)}, u32[]{:S(2)}, u32[]{:S(2)}) collective-permute-start(f32[4,2,40,896]{3,2,1,0:T(8,128)S(1)} %fusion.2), channel_id=1, source_target_pairs={{0,3},{1,2},{2,1},{3,0},{4,7},{5,6},{6,5},{7,4},{8,11},{9,10},{10,... | collective-permute-start | bytes 3440648 | tf_op jit(solution)/shard_map/ppermute | solution.py:24
  71.8 4.5 %collective-permute-done.8 = f32[2,2,4,40,896]{4,3,2,1,0:T(8,128)S(1)} collective-permute-done((f32[2,2,4,40,896]{4,3,2,1,0:T(8,128)S(1)}, f32[2,2,4,40,896]{4,3,2,1,0:T(8,128)S(1)}, u32[]{:S(2)}, u32[]{:S(2)}) %collective-permute-start.8) | collective-permute-done | bytes 2293792 | tf_op jit(solution)/shard_map/ppermute | solution.py:24
  76.4 1.5 %collective-permute-start.4 = (f32[4,2,40,896]{3,2,1,0:T(8,128)S(1)}, f32[4,2,40,896]{3,2,1,0:T(8,128)S(1)}, u32[]{:S(2)}, u32[]{:S(2)}) collective-permute-start(f32[4,2,40,896]{3,2,1,0:T(8,128)S(1)} %add_bitcast_fusion.2), channel_id=1, source_target_pairs={{0,3},{1,2},{2,1},{3,0},{4,7},{5,6},{6,5},{7,4},{8,11},{9,10},{10,... | collective-permute-start | bytes 3440648 | tf_op jit(solution)/shard_map/ppermute | solution.py:24
  78.0 3.1 %collective-permute-start.13 = (f32[2,4,40,896]{3,2,1,0:T(8,128)S(1)}, f32[2,4,40,896]{3,2,1,0:T(8,128)S(1)}, u32[]{:S(2)}, u32[]{:S(2)}) collective-permute-start(f32[2,4,40,896]{3,2,1,0:T(8,128)S(1)} %add_bitcast_fusion), channel_id=1, source_target_pairs={{0,12},{1,13},{2,14},{3,15},{4,8},{5,9},{6,10},{7,11},{8,4},{9,5},... | collective-permute-start | bytes 3440648 | tf_op jit(solution)/shard_map/ppermute | solution.py:24
  81.1 4.7 %collective-permute-done.6 = f32[2,4,40,896]{3,2,1,0:T(8,128)S(1)} collective-permute-done((f32[2,4,40,896]{3,2,1,0:T(8,128)S(1)}, f32[2,4,40,896]{3,2,1,0:T(8,128)S(1)}, u32[]{:S(2)}, u32[]{:S(2)}) %collective-permute-start.6) | collective-permute-done | bytes 1146912 | tf_op jit(solution)/shard_map/ppermute | solution.py:24
  85.8 2.2 %collective-permute-done.7 = f32[648,768]{1,0:T(8,128)S(1)} collective-permute-done((f32[648,768]{1,0:T(8,128)S(1)}, f32[648,768]{1,0:T(8,128)S(1)}, u32[]{:S(2)}, u32[]{:S(2)}) %collective-permute-start.7) | collective-permute-done | bytes 1990688 | tf_op jit(solution)/shard_map/ppermute | solution.py:24
  88.9 3.1 %collective-permute-start.11 = (f32[328,768]{1,0:T(8,128)S(1)}, f32[328,768]{1,0:T(8,128)S(1)}, u32[]{:S(2)}, u32[]{:S(2)}) collective-permute-start(f32[328,768]{1,0:T(8,128)S(1)} %pad_maximum_fusion.1), channel_id=1, source_target_pairs={{0,3},{1,2},{2,1},{3,0},{4,7},{5,6},{6,5},{7,4},{8,11},{9,10},{10,... | collective-permute-start | bytes 3022856 | tf_op jit(solution)/shard_map/ppermute | solution.py:24
  92.2 3.1 %collective-permute-start.10 = (f32[2,2,40,896]{3,2,1,0:T(8,128)S(1)}, f32[2,2,40,896]{3,2,1,0:T(8,128)S(1)}, u32[]{:S(2)}, u32[]{:S(2)}) collective-permute-start(f32[2,2,40,896]{3,2,1,0:T(8,128)S(1)} %slice.256), channel_id=1, source_target_pairs={{0,12},{1,13},{2,14},{3,15},{4,8},{5,9},{6,10},{7,11},{8,4},{9,5},... | collective-permute-start | bytes 1720328 | tf_op jit(solution)/shard_map/ppermute | solution.py:24
  95.3 2.5 %collective-permute-done.4 = f32[4,2,40,896]{3,2,1,0:T(8,128)S(1)} collective-permute-done((f32[4,2,40,896]{3,2,1,0:T(8,128)S(1)}, f32[4,2,40,896]{3,2,1,0:T(8,128)S(1)}, u32[]{:S(2)}, u32[]{:S(2)}) %collective-permute-start.4) | collective-permute-done | bytes 1146912 | tf_op jit(solution)/shard_map/ppermute | solution.py:24
  98.3 3.0 %collective-permute-start.9 = (f32[2,2,40,896]{3,2,1,0:T(8,128)S(1)}, f32[2,2,40,896]{3,2,1,0:T(8,128)S(1)}, u32[]{:S(2)}, u32[]{:S(2)}) collective-permute-start(f32[2,2,40,896]{3,2,1,0:T(8,128)S(1)} %slice.254), channel_id=1, source_target_pairs={{0,12},{1,13},{2,14},{3,15},{4,8},{5,9},{6,10},{7,11},{8,4},{9,5},... | collective-permute-start | bytes 1720328 | tf_op jit(solution)/shard_map/ppermute | solution.py:24
  101.6 2.5 %collective-permute-done.12 = f32[2,4,40,896]{3,2,1,0:T(8,128)S(1)} collective-permute-done((f32[2,4,40,896]{3,2,1,0:T(8,128)S(1)}, f32[2,4,40,896]{3,2,1,0:T(8,128)S(1)}, u32[]{:S(2)}, u32[]{:S(2)}) %collective-permute-start.12) | collective-permute-done | bytes 1146912 | tf_op jit(solution)/shard_map/ppermute | solution.py:24
  104.2 4.4 %collective-permute-done.11 = f32[328,768]{1,0:T(8,128)S(1)} collective-permute-done((f32[328,768]{1,0:T(8,128)S(1)}, f32[328,768]{1,0:T(8,128)S(1)}, u32[]{:S(2)}, u32[]{:S(2)}) %collective-permute-start.11) | collective-permute-done | bytes 1007648 | tf_op jit(solution)/shard_map/ppermute | solution.py:24
  108.7 1.6 %collective-permute-done.9 = f32[2,2,40,896]{3,2,1,0:T(8,128)S(1)} collective-permute-done((f32[2,2,40,896]{3,2,1,0:T(8,128)S(1)}, f32[2,2,40,896]{3,2,1,0:T(8,128)S(1)}, u32[]{:S(2)}, u32[]{:S(2)}) %collective-permute-start.9) | collective-permute-done | bytes 573472 | tf_op jit(solution)/shard_map/ppermute | solution.py:24
  111.2 8.3 %collective-permute-done.15 = f32[4,40,896]{2,1,0:T(8,128)S(1)} collective-permute-done((f32[4,40,896]{2,1,0:T(8,128)S(1)}, f32[4,40,896]{2,1,0:T(8,128)S(1)}, u32[]{:S(2)}, u32[]{:S(2)}) %collective-permute-start.15) | collective-permute-done | bytes 573472 | tf_op jit(solution)/shard_map/ppermute | solution.py:24
  119.7 2.8 %collective-permute-start.16 = (f32[40,896]{1,0:T(8,128)S(1)}, f32[40,896]{1,0:T(8,128)S(1)}, u32[]{:S(2)}, u32[]{:S(2)}) collective-permute-start(f32[40,896]{1,0:T(8,128)S(1)} %get-tuple-element.97), channel_id=1, source_target_pairs={{0,3},{1,2},{2,1},{3,0},{4,7},{5,6},{6,5},{7,4},{8,11},{9,10},{10,... | collective-permute-start | bytes 430088 | tf_op jit(solution)/shard_map/ppermute | solution.py:24
  122.5 1.9 %collective-permute-start.25 = (f32[40,896]{1,0:T(8,128)S(1)}, f32[40,896]{1,0:T(8,128)S(1)}, u32[]{:S(2)}, u32[]{:S(2)}) collective-permute-start(f32[40,896]{1,0:T(8,128)S(1)} %get-tuple-element.95), channel_id=1, source_target_pairs={{0,2},{1,3},{2,0},{3,1},{4,6},{5,7},{6,4},{7,5},{8,10},{9,11},{10,... | collective-permute-start | bytes 430088 | tf_op jit(solution)/shard_map/ppermute | solution.py:30
  126.2 1.4 %collective-permute-done.24 = f32[40,896]{1,0:T(8,128)S(1)} collective-permute-done((f32[40,896]{1,0:T(8,128)S(1)}, f32[40,896]{1,0:T(8,128)S(1)}, u32[]{:S(2)}, u32[]{:S(2)}) %collective-permute-start.24) | collective-permute-done | bytes 143392 | tf_op jit(solution)/shard_map/ppermute | solution.py:24
  127.6 1.8 %collective-permute-start.23 = (f32[48,768]{1,0:T(8,128)S(1)}, f32[48,768]{1,0:T(8,128)S(1)}, u32[]{:S(2)}, u32[]{:S(2)}) collective-permute-start(f32[48,768]{1,0:T(8,128)S(1)} %get-tuple-element.104), channel_id=1, source_target_pairs={{0,8},{1,9},{2,10},{3,11},{4,12},{5,13},{6,14},{7,15},{8,0},{9,1},... | collective-permute-start | bytes 442376 | tf_op jit(solution)/shard_map/ppermute | solution.py:30
  129.8 2.8 %collective-permute-start.20 = (f32[40,896]{1,0:T(8,128)S(1)}, f32[40,896]{1,0:T(8,128)S(1)}, u32[]{:S(2)}, u32[]{:S(2)}) collective-permute-start(f32[40,896]{1,0:T(8,128)S(1)} %get-tuple-element.102), channel_id=1, source_target_pairs={{0,32},{1,33},{2,34},{3,35},{4,36},{5,37},{6,38},{7,39},{8,40},{9,... | collective-permute-start | bytes 430088 | tf_op jit(solution)/shard_map/ppermute | solution.py:30
  132.6 2.0 %collective-permute-start.19 = (f32[40,896]{1,0:T(8,128)S(1)}, f32[40,896]{1,0:T(8,128)S(1)}, u32[]{:S(2)}, u32[]{:S(2)}) collective-permute-start(f32[40,896]{1,0:T(8,128)S(1)} %slice_bitcast_fusion.4), channel_id=1, source_target_pairs={{0,48},{1,49},{2,50},{3,51},{4,52},{5,53},{6,54},{7,55},{8,56},{9,... | collective-permute-start | bytes 430088 | tf_op jit(solution)/shard_map/ppermute | solution.py:24
  134.8 2.3 %collective-permute-done.20 = f32[40,896]{1,0:T(8,128)S(1)} collective-permute-done((f32[40,896]{1,0:T(8,128)S(1)}, f32[40,896]{1,0:T(8,128)S(1)}, u32[]{:S(2)}, u32[]{:S(2)}) %collective-permute-start.20) | collective-permute-done | bytes 143392 | tf_op jit(solution)/shard_map/ppermute | solution.py:30
  137.1 1.9 %collective-permute-done.19 = f32[40,896]{1,0:T(8,128)S(1)} collective-permute-done((f32[40,896]{1,0:T(8,128)S(1)}, f32[40,896]{1,0:T(8,128)S(1)}, u32[]{:S(2)}, u32[]{:S(2)}) %collective-permute-start.19) | collective-permute-done | bytes 143392 | tf_op jit(solution)/shard_map/ppermute | solution.py:24
  (62 shorter events, 8.7 us)
Async XLA Ops:
  14.2 46.0 %collective-permute-start.1 = (f32[1288,768]{1,0:T(8,128)S(1)}, f32[1288,768]{1,0:T(8,128)S(1)}, u32[]{:S(2)}, u32[]{:S(2)}) collective-permute-start(f32[1288,768]{1,0:T(8,128)S(1)} %get-tuple-element.59), channel_id=1, source_target_pairs={{0,16},{1,17},{2,18},{3,19},{4,20},{5,21},{6,22},{7,23},{8,24},{9,... | collective-permute-start | bytes 11870216 | tf_op jit(solution)/shard_map/ppermute | solution.py:24
  16.3 28.1 %collective-permute-start.3 = (f32[2,4,2,40,896]{4,3,2,1,0:T(8,128)S(1)}, f32[2,4,2,40,896]{4,3,2,1,0:T(8,128)S(1)}, u32[]{:S(2)}, u32[]{:S(2)}) collective-permute-start(f32[2,4,2,40,896]{4,3,2,1,0:T(8,128)S(1)} %get-tuple-element.61), channel_id=1, source_target_pairs={{0,1},{1,0},{2,3},{3,2},{4,5},{5,4},{6,7},{7,6},{8,9},{9,8},{10,11... | collective-permute-start | bytes 6881288 | tf_op jit(solution)/shard_map/ppermute | solution.py:24
  17.8 28.1 %collective-permute-start.2 = (f32[2,2,4,40,896]{4,3,2,1,0:T(8,128)S(1)}, f32[2,2,4,40,896]{4,3,2,1,0:T(8,128)S(1)}, u32[]{:S(2)}, u32[]{:S(2)}) collective-permute-start(f32[2,2,4,40,896]{4,3,2,1,0:T(8,128)S(1)} %get-tuple-element.60), channel_id=1, source_target_pairs={{0,4},{1,5},{2,6},{3,7},{4,0},{5,1},{6,2},{7,3},{8,12},{9,13},{10,... | collective-permute-start | bytes 6881288 | tf_op jit(solution)/shard_map/ppermute | solution.py:24
  32.3 39.4 %collective-permute-start = (f32[2,4,2,40,896]{4,3,2,1,0:T(8,128)S(1)}, f32[2,4,2,40,896]{4,3,2,1,0:T(8,128)S(1)}, u32[]{:S(2)}, u32[]{:S(2)}) collective-permute-start(f32[2,4,2,40,896]{4,3,2,1,0:T(8,128)S(1)} %get-tuple-element.58), channel_id=1, source_target_pairs={{0,1},{1,0},{2,3},{3,2},{4,5},{5,4},{6,7},{7,6},{8,9},{9,8},{10,11... | collective-permute-start | bytes 6881288 | tf_op jit(solution)/shard_map/ppermute | solution.py:24
  33.0 43.3 %collective-permute-start.8 = (f32[2,2,4,40,896]{4,3,2,1,0:T(8,128)S(1)}, f32[2,2,4,40,896]{4,3,2,1,0:T(8,128)S(1)}, u32[]{:S(2)}, u32[]{:S(2)}) collective-permute-start(f32[2,2,4,40,896]{4,3,2,1,0:T(8,128)S(1)} %get-tuple-element.69), channel_id=1, source_target_pairs={{0,4},{1,5},{2,6},{3,7},{4,0},{5,1},{6,2},{7,3},{8,12},{9,13},{10,... | collective-permute-start | bytes 6881288 | tf_op jit(solution)/shard_map/ppermute | solution.py:24
  60.8 27.1 %collective-permute-start.7 = (f32[648,768]{1,0:T(8,128)S(1)}, f32[648,768]{1,0:T(8,128)S(1)}, u32[]{:S(2)}, u32[]{:S(2)}) collective-permute-start(f32[648,768]{1,0:T(8,128)S(1)} %pad_maximum_fusion), channel_id=1, source_target_pairs={{0,48},{1,49},{2,50},{3,51},{4,52},{5,53},{6,54},{7,55},{8,56},{9,... | collective-permute-start | bytes 5971976 | tf_op jit(solution)/shard_map/ppermute | solution.py:24
  65.2 20.6 %collective-permute-start.6 = (f32[2,4,40,896]{3,2,1,0:T(8,128)S(1)}, f32[2,4,40,896]{3,2,1,0:T(8,128)S(1)}, u32[]{:S(2)}, u32[]{:S(2)}) collective-permute-start(f32[2,4,40,896]{3,2,1,0:T(8,128)S(1)} %add_bitcast_fusion.1), channel_id=1, source_target_pairs={{0,12},{1,13},{2,14},{3,15},{4,8},{5,9},{6,10},{7,11},{8,4},{9,5},... | collective-permute-start | bytes 3440648 | tf_op jit(solution)/shard_map/ppermute | solution.py:24
  68.4 17.4 %collective-permute-start.5 = (f32[4,2,40,896]{3,2,1,0:T(8,128)S(1)}, f32[4,2,40,896]{3,2,1,0:T(8,128)S(1)}, u32[]{:S(2)}, u32[]{:S(2)}) collective-permute-start(f32[4,2,40,896]{3,2,1,0:T(8,128)S(1)} %fusion.2), channel_id=1, source_target_pairs={{0,3},{1,2},{2,1},{3,0},{4,7},{5,6},{6,5},{7,4},{8,11},{9,10},{10,... | collective-permute-start | bytes 3440648 | tf_op jit(solution)/shard_map/ppermute | solution.py:24
  76.4 21.5 %collective-permute-start.4 = (f32[4,2,40,896]{3,2,1,0:T(8,128)S(1)}, f32[4,2,40,896]{3,2,1,0:T(8,128)S(1)}, u32[]{:S(2)}, u32[]{:S(2)}) collective-permute-start(f32[4,2,40,896]{3,2,1,0:T(8,128)S(1)} %add_bitcast_fusion.2), channel_id=1, source_target_pairs={{0,3},{1,2},{2,1},{3,0},{4,7},{5,6},{6,5},{7,4},{8,11},{9,10},{10,... | collective-permute-start | bytes 3440648 | tf_op jit(solution)/shard_map/ppermute | solution.py:24
  78.0 20.1 %collective-permute-start.13 = (f32[2,4,40,896]{3,2,1,0:T(8,128)S(1)}, f32[2,4,40,896]{3,2,1,0:T(8,128)S(1)}, u32[]{:S(2)}, u32[]{:S(2)}) collective-permute-start(f32[2,4,40,896]{3,2,1,0:T(8,128)S(1)} %add_bitcast_fusion), channel_id=1, source_target_pairs={{0,12},{1,13},{2,14},{3,15},{4,8},{5,9},{6,10},{7,11},{8,4},{9,5},... | collective-permute-start | bytes 3440648 | tf_op jit(solution)/shard_map/ppermute | solution.py:24
  88.2 15.9 %collective-permute-start.12 = (f32[2,4,40,896]{3,2,1,0:T(8,128)S(1)}, f32[2,4,40,896]{3,2,1,0:T(8,128)S(1)}, u32[]{:S(2)}, u32[]{:S(2)}) collective-permute-start(f32[2,4,40,896]{3,2,1,0:T(8,128)S(1)} %bitcast_add_fusion.1), channel_id=1, source_target_pairs={{0,16},{1,17},{2,18},{3,19},{4,20},{5,21},{6,22},{7,23},{8,24},{9,... | collective-permute-start | bytes 3440648 | tf_op jit(solution)/shard_map/ppermute | solution.py:24
  88.9 19.7 %collective-permute-start.11 = (f32[328,768]{1,0:T(8,128)S(1)}, f32[328,768]{1,0:T(8,128)S(1)}, u32[]{:S(2)}, u32[]{:S(2)}) collective-permute-start(f32[328,768]{1,0:T(8,128)S(1)} %pad_maximum_fusion.1), channel_id=1, source_target_pairs={{0,3},{1,2},{2,1},{3,0},{4,7},{5,6},{6,5},{7,4},{8,11},{9,10},{10,... | collective-permute-start | bytes 3022856 | tf_op jit(solution)/shard_map/ppermute | solution.py:24
  92.2 16.5 %collective-permute-start.10 = (f32[2,2,40,896]{3,2,1,0:T(8,128)S(1)}, f32[2,2,40,896]{3,2,1,0:T(8,128)S(1)}, u32[]{:S(2)}, u32[]{:S(2)}) collective-permute-start(f32[2,2,40,896]{3,2,1,0:T(8,128)S(1)} %slice.256), channel_id=1, source_target_pairs={{0,12},{1,13},{2,14},{3,15},{4,8},{5,9},{6,10},{7,11},{8,4},{9,5},... | collective-permute-start | bytes 1720328 | tf_op jit(solution)/shard_map/ppermute | solution.py:24
  98.3 12.0 %collective-permute-start.9 = (f32[2,2,40,896]{3,2,1,0:T(8,128)S(1)}, f32[2,2,40,896]{3,2,1,0:T(8,128)S(1)}, u32[]{:S(2)}, u32[]{:S(2)}) collective-permute-start(f32[2,2,40,896]{3,2,1,0:T(8,128)S(1)} %slice.254), channel_id=1, source_target_pairs={{0,12},{1,13},{2,14},{3,15},{4,8},{5,9},{6,10},{7,11},{8,4},{9,5},... | collective-permute-start | bytes 1720328 | tf_op jit(solution)/shard_map/ppermute | solution.py:24
  108.6 10.9 %collective-permute-start.15 = (f32[4,40,896]{2,1,0:T(8,128)S(1)}, f32[4,40,896]{2,1,0:T(8,128)S(1)}, u32[]{:S(2)}, u32[]{:S(2)}) collective-permute-start(f32[4,40,896]{2,1,0:T(8,128)S(1)} %fusion.3), channel_id=1, source_target_pairs={{0,48},{1,49},{2,50},{3,51},{4,52},{5,53},{6,54},{7,55},{8,56},{9,... | collective-permute-start | bytes 1720328 | tf_op jit(solution)/shard_map/ppermute | solution.py:24
  110.4 14.1 %collective-permute-start.17 = (f32[168,768]{1,0:T(8,128)S(1)}, f32[168,768]{1,0:T(8,128)S(1)}, u32[]{:S(2)}, u32[]{:S(2)}) collective-permute-start(f32[168,768]{1,0:T(8,128)S(1)} %pad_maximum_fusion.3), channel_id=1, source_target_pairs={{0,1},{1,0},{2,3},{3,2},{4,5},{5,4},{6,7},{7,6},{8,9},{9,8},{10,11... | collective-permute-start | bytes 1548296 | tf_op jit(solution)/shard_map/ppermute | solution.py:24
  110.8 18.6 %collective-permute-start.14 = (f32[4,40,896]{2,1,0:T(8,128)S(1)}, f32[4,40,896]{2,1,0:T(8,128)S(1)}, u32[]{:S(2)}, u32[]{:S(2)}) collective-permute-start(f32[4,40,896]{2,1,0:T(8,128)S(1)} %pad_maximum_fusion.2), channel_id=1, source_target_pairs={{0,4},{1,5},{2,6},{3,7},{4,0},{5,1},{6,2},{7,3},{8,12},{9,13},{10,... | collective-permute-start | bytes 1720328 | tf_op jit(solution)/shard_map/ppermute | solution.py:24
  119.7 6.4 %collective-permute-start.16 = (f32[40,896]{1,0:T(8,128)S(1)}, f32[40,896]{1,0:T(8,128)S(1)}, u32[]{:S(2)}, u32[]{:S(2)}) collective-permute-start(f32[40,896]{1,0:T(8,128)S(1)} %get-tuple-element.97), channel_id=1, source_target_pairs={{0,3},{1,2},{2,1},{3,0},{4,7},{5,6},{6,5},{7,4},{8,11},{9,10},{10,... | collective-permute-start | bytes 430088 | tf_op jit(solution)/shard_map/ppermute | solution.py:24
  122.5 5.1 %collective-permute-start.24 = (f32[40,896]{1,0:T(8,128)S(1)}, f32[40,896]{1,0:T(8,128)S(1)}, u32[]{:S(2)}, u32[]{:S(2)}) collective-permute-start(f32[40,896]{1,0:T(8,128)S(1)} %get-tuple-element.96), channel_id=1, source_target_pairs={{0,1},{1,0},{2,3},{3,2},{4,5},{5,4},{6,7},{7,6},{8,9},{9,8},{10,11... | collective-permute-start | bytes 430088 | tf_op jit(solution)/shard_map/ppermute | solution.py:24
  122.5 6.9 %collective-permute-start.25 = (f32[40,896]{1,0:T(8,128)S(1)}, f32[40,896]{1,0:T(8,128)S(1)}, u32[]{:S(2)}, u32[]{:S(2)}) collective-permute-start(f32[40,896]{1,0:T(8,128)S(1)} %get-tuple-element.95), channel_id=1, source_target_pairs={{0,2},{1,3},{2,0},{3,1},{4,6},{5,7},{6,4},{7,5},{8,10},{9,11},{10,... | collective-permute-start | bytes 430088 | tf_op jit(solution)/shard_map/ppermute | solution.py:30
  124.7 7.9 %collective-permute-start.21 = (f32[48,768]{1,0:T(8,128)S(1)}, f32[48,768]{1,0:T(8,128)S(1)}, u32[]{:S(2)}, u32[]{:S(2)}) collective-permute-start(f32[48,768]{1,0:T(8,128)S(1)} %get-tuple-element.106), channel_id=1, source_target_pairs={{0,12},{1,13},{2,14},{3,15},{4,8},{5,9},{6,10},{7,11},{8,4},{9,5},... | collective-permute-start | bytes 442376 | tf_op jit(solution)/shard_map/ppermute | solution.py:24
  126.1 8.5 %collective-permute-start.22 = (f32[48,768]{1,0:T(8,128)S(1)}, f32[48,768]{1,0:T(8,128)S(1)}, u32[]{:S(2)}, u32[]{:S(2)}) collective-permute-start(f32[48,768]{1,0:T(8,128)S(1)} %get-tuple-element.105), channel_id=1, source_target_pairs={{0,4},{1,5},{2,6},{3,7},{4,0},{5,1},{6,2},{7,3},{8,12},{9,13},{10,... | collective-permute-start | bytes 442376 | tf_op jit(solution)/shard_map/ppermute | solution.py:24
  127.6 6.9 %collective-permute-start.23 = (f32[48,768]{1,0:T(8,128)S(1)}, f32[48,768]{1,0:T(8,128)S(1)}, u32[]{:S(2)}, u32[]{:S(2)}) collective-permute-start(f32[48,768]{1,0:T(8,128)S(1)} %get-tuple-element.104), channel_id=1, source_target_pairs={{0,8},{1,9},{2,10},{3,11},{4,12},{5,13},{6,14},{7,15},{8,0},{9,1},... | collective-permute-start | bytes 442376 | tf_op jit(solution)/shard_map/ppermute | solution.py:30
  129.6 5.2 %collective-permute-start.18 = (f32[40,896]{1,0:T(8,128)S(1)}, f32[40,896]{1,0:T(8,128)S(1)}, u32[]{:S(2)}, u32[]{:S(2)}) collective-permute-start(f32[40,896]{1,0:T(8,128)S(1)} %get-tuple-element.103), channel_id=1, source_target_pairs={{0,16},{1,17},{2,18},{3,19},{4,20},{5,21},{6,22},{7,23},{8,24},{9,... | collective-permute-start | bytes 430088 | tf_op jit(solution)/shard_map/ppermute | solution.py:24
  129.8 7.4 %collective-permute-start.20 = (f32[40,896]{1,0:T(8,128)S(1)}, f32[40,896]{1,0:T(8,128)S(1)}, u32[]{:S(2)}, u32[]{:S(2)}) collective-permute-start(f32[40,896]{1,0:T(8,128)S(1)} %get-tuple-element.102), channel_id=1, source_target_pairs={{0,32},{1,33},{2,34},{3,35},{4,36},{5,37},{6,38},{7,39},{8,40},{9,... | collective-permute-start | bytes 430088 | tf_op jit(solution)/shard_map/ppermute | solution.py:30
  132.6 6.4 %collective-permute-start.19 = (f32[40,896]{1,0:T(8,128)S(1)}, f32[40,896]{1,0:T(8,128)S(1)}, u32[]{:S(2)}, u32[]{:S(2)}) collective-permute-start(f32[40,896]{1,0:T(8,128)S(1)} %slice_bitcast_fusion.4), channel_id=1, source_target_pairs={{0,48},{1,49},{2,50},{3,51},{4,52},{5,53},{6,54},{7,55},{8,56},{9,... | collective-permute-start | bytes 430088 | tf_op jit(solution)/shard_map/ppermute | solution.py:24

commit v10 on v8

--- a/solution.py
+++ b/solution.py
@@ -22,6 +22,12 @@
             p = d // stride % 4
             pairs.append((section * 64 + d, section * 64 + d + ((p ^ flip) - p) * stride))
     return lax.ppermute(value, ("section", "dp"), pairs)
+
+
+def opposite(value, axis):
+    stride = STRIDE[axis]
+    places = [(d, d + ((d // stride % 4 ^ 2) - d // stride % 4) * stride) for d in range(64)]
+    return lax.ppermute(value, "dp", places)
 
 
 def products(half, failed, counts, order, act, cot, *refs):
@@ -35,7 +41,8 @@
     ys = {group: [y ^ flip for flip in (flips if group == "B" else others)] for group in "ABC"}
     fetch = [
         pltpu.make_async_copy(
-            act.at[0, :, :, pl.ds(pl.multiple_of(zs[half + g] * TILE, 128), TILE)], acts.at[g], sems.at[g])
+            act.at[0, :, :, pl.ds(pl.multiple_of(zs[half + g] * TILE, 128), TILE)],
+            acts.at[:, :, pl.ds(g * TILE, TILE)], sems.at[g])
         for g in range(2)
     ]
     load = {}
@@ -46,6 +53,8 @@
     ask.start()
     load["C"].start()
     fetch[0].start()
+    if half == 2:
+        fetch[1].start()
     ask.wait()
     alive = jnp.where(me == failed[0], 0, counts[0])
     live = [jnp.float32(0)] * SLOTS
@@ -56,34 +65,39 @@
         alive_rows = jnp.full((8, COLUMNS["C"][1]), alive.astype(jnp.float32))
         outs[4][2 * TILE:, :] = alive_rows
         outs[5][...] = alive_rows
-    for g in range(2):
-        fetch[g].wait()
-        rows = acts[g].reshape(K, TILE)
+    tiles = 2 if half == 2 else 1
+    for step in range(2 // tiles):
+        for g in range(step * tiles, step * tiles + tiles):
+            fetch[g].wait()
+        rows = acts[:, :, step * TILE:(step + tiles) * TILE].reshape(K, tiles * TILE)
         for pack in ("C", "AB"):
             first, last = COLUMNS[pack[0]][0], sum(COLUMNS[pack[-1]])
-            if g == 0:
+            if step == 0:
                 load[pack].wait()
                 if pack == "C":
                     load["AB"].start()
-                    fetch[1].start()
+                    if tiles == 1:
+                        fetch[1].start()
                 for k in range(SLOTS):
                     cots[k, :, first:last] = cots[k, :, first:last] * live[k].astype(jnp.bfloat16)
             total[:, :last - first] = lax.dot_general(
                 rows, cots[:, :, first:last].reshape(K, last - first), (((0,), (0,)), ((), ())),
                 preferred_element_type=jnp.float32)
-            for group in pack:
-                column, columns = COLUMNS[group]
-                for i in range(4):
-                    for j in range(4):
-                        start = (ys if group == "B" else xs)[group][i] * (160 if group == "B" else ROWS)
-                        start += (xs if group == "B" else ys)[group][j] * (ROWS if group == "B" else 160)
-                        block = total[pl.ds(pl.multiple_of(start, 8), ROWS), column - first:column - first + columns]
-                        if group == "A":
-                            outs[i // 2][i % 2, j, g] = block
-                        elif group == "B":
-                            outs[2 + i // 2][i % 2, g, j] = block
-                        else:
-                            outs[4][pl.ds(((g * 4 + i) * 4 + j) * ROWS, ROWS), :] = block
+            for g in range(step * tiles, step * tiles + tiles):
+                for group in pack:
+                    column, columns = COLUMNS[group]
+                    for i in range(4):
+                        for j in range(4):
+                            start = (ys if group == "B" else xs)[group][i] * (160 if group == "B" else ROWS)
+                            start += (xs if group == "B" else ys)[group][j] * (ROWS if group == "B" else 160)
+                            start += g % tiles * TILE
+                            block = total[pl.ds(pl.multiple_of(start, 8), ROWS), column - first:column - first + columns]
+                            if group == "A":
+                                outs[i // 2][i % 2, j, g] = block
+                            elif group == "B":
+                                outs[2 + i // 2][i % 2, g, j] = block
+                            else:
+                                outs[4][pl.ds(((g * 4 + i) * 4 + j) * ROWS, ROWS), :] = block
 
 
 def partials(half, activations, cotangents, failed, counts, order):
@@ -96,13 +110,13 @@
         in_specs=[pl.BlockSpec(memory_space=pltpu.SMEM)] * 2 + [pl.BlockSpec(memory_space=pltpu.HBM)] * 3,
         out_specs=[pl.BlockSpec(memory_space=pltpu.VMEM)] * len(shapes),
         scratch_shapes=[
-            pltpu.VMEM((2, SLOTS, TOKENS, TILE), jnp.bfloat16),
+            pltpu.VMEM((SLOTS, TOKENS, 2 * TILE), jnp.bfloat16),
             pltpu.VMEM((SLOTS, TOKENS, a + b + c), jnp.bfloat16),
-            pltpu.VMEM((TILE, max(a + b, c)), jnp.float32),
+            pltpu.VMEM((TILE * (2 if half == 2 else 1), max(a + b, c)), jnp.float32),
             pltpu.SMEM((1, SLOTS), jnp.int32),
             pltpu.SemaphoreType.DMA((5,)),
         ],
-        compiler_params=pltpu.CompilerParams(vmem_limit_bytes=28 << 20),
+        compiler_params=pltpu.CompilerParams(vmem_limit_bytes=(33 if half == 2 else 28) << 20),
         cost_estimate=pl.CostEstimate(flops=1024, bytes_accessed=1024, transcendentals=0),
     )(failed, counts, *(pltpu.with_memory_space_constraint(x, pltpu.HBM) for x in (order, activations, cotangents)))
 
@@ -169,16 +183,14 @@
     c5 = exchange(jnp.concatenate([c_whole[80:], c_total], axis=0), "y", 0, True)
     a4 = take(a4)
     a_far, a_near = (a_far[0] + a3f[0]) + a4[:2], (a_near[0] + a3n[0]) + a4[2:]
-    a5 = exchange(a_far, "z", 0)
+    a5 = [exchange(a_far[0], "z", 0), exchange(a_near[1], "z", 1), opposite(a_far[1], "z")]
     b5 = take(b5)
     b6 = exchange(b_whole[1] + b5[1], "x", 1, True)
     c5 = take(c5)
     c_out, c_stay, c_total = both(c_whole[:80], c5, c_total, 40)
     c6 = exchange(c_out, "y", 1, True)
-    a5 = take(a5)
-    a6 = exchange(a_near[1] + a5[1], "z", 1)
-    b6, c6, a6 = together([b6, c6, a6])
-    a = (a_near[0] + a5[0]) + a6
+    b6, c6, *a5 = together([b6, c6, *a5])
+    a = ((a_near[0] + a5[0]) + a5[1]) + a5[2]
     b = (b_whole[0] + b5[0]) + b6
     c = c_stay + c6[:40]
     total = c_total + c6[40:]

time: 140 us -> 143 us (1.021)
  the two profiles are of different devices: /device:TPU:0 before, /device:TPU:72 now
where the time goes in v10:
time: 143 us; the launch traced here: 142 us
  waiting for transfers between devices  74.1 us (52%)
  starting transfers between devices  33.2 us (23%)
  Pallas kernels  27 us (19%)
  other arithmetic  6.45 us (5%)
  between operations  1.54 us (1%)
    ppermute x23, waiting for transfers between devices, exchange(): return lax.ppermute(value, ('section', 'dp'), pairs)  74.1 us
    ppermute x23, starting transfers between devices, exchange(): return lax.ppermute(value, ('section', 'dp'), pairs)  31.4 us
    pallas_call x2, Pallas kernels, partials(): pl.pallas_call(functools.partial(products, half), out_shape=[jax.ShapeDty...  27 us
  transfers between devices with their start and end apart: 24, of which 15 were waited for; matrix products, arithmetic and copies ran while one was open for 4% of the time, Pallas kernels for 9%

profile of v10, /device:TPU:72, one launch (start us, length us, event | category | flops | bytes accessed | tf_op | source)
XLA Modules:
  0.0 142.5 jit_solution(11371749195097373574)
XLA Ops:
  1.3 14.0 %shard_map.55 = (f32[2,4,2,40,896]{4,3,2,1,0:T(8,128)S(1)}, f32[2,4,2,40,896]{4,3,2,1,0:T(8,128)S(1)}, f32[2,2,4,40,896]{4,3,2,1,0:T(8,128)S(1)}, f32[2,2,4,40,8...) custom-call(s32[1]{0:T(128)S(6)} %copy.6.failed, s32[1]{0:T(128)S(6)} %copy.7.counts, ...), custom_call_target="tpu_custom_call" | custom-call | flops 1024 | bytes 1024 | tf_op jit(solution)/shard_map/pallas_call | solution.py:107
  15.3 1.7 %collective-permute-start.1 = (f32[1288,768]{1,0:T(8,128)S(1)}, f32[1288,768]{1,0:T(8,128)S(1)}, u32[]{:S(2)}, u32[]{:S(2)}) collective-permute-start(f32[1288,768]{1,0:T(8,128)S(1)} %get-tuple-element.57), channel_id=1, source_target_pairs={{0,16},{1,17},{2,18},{3,19},{4,20},{5,21},{6,22},{7,23},{8,24},{9,... | collective-permute-start | bytes 11870216 | tf_op jit(solution)/shard_map/ppermute | solution.py:24
  17.0 1.5 %collective-permute-start.3 = (f32[2,4,2,40,896]{4,3,2,1,0:T(8,128)S(1)}, f32[2,4,2,40,896]{4,3,2,1,0:T(8,128)S(1)}, u32[]{:S(2)}, u32[]{:S(2)}) collective-permute-start(f32[2,4,2,40,896]{4,3,2,1,0:T(8,128)S(1)} %get-tuple-element.59), channel_id=1, source_target_pairs={{0,1},{1,0},{2,3},{3,2},{4,5},{5,4},{6,7},{7,6},{8,9},{9,8},{10,11... | collective-permute-start | bytes 6881288 | tf_op jit(solution)/shard_map/ppermute | solution.py:24
  18.9 13.0 %shard_map.56 = (f32[2,4,2,40,896]{4,3,2,1,0:T(8,128)S(1)}, f32[2,4,2,40,896]{4,3,2,1,0:T(8,128)S(1)}, f32[2,2,4,40,896]{4,3,2,1,0:T(8,128)S(1)}, f32[2,2,4,40,896]{4,3,2,1,0:T(8,128)S(1)}, f32[1280,768]{1,0:T(8,128)S(1)}) custom-call(s32[1]{0:T(128)S(6)} %copy.6.failed, s32[1]{0:T(128)S(6)} %copy.7.counts, s32[1,6]{1,0:T(1,128)} %order.3, ...), custom_call_target="tpu_custom_call" | custom-call | flops 1024 | bytes 1024 | tf_op jit(solution)/shard_map/pallas_call | solution.py:107
  32.6 1.6 %collective-permute-start.8 = (f32[2,2,4,40,896]{4,3,2,1,0:T(8,128)S(1)}, f32[2,2,4,40,896]{4,3,2,1,0:T(8,128)S(1)}, u32[]{:S(2)}, u32[]{:S(2)}) collective-permute-start(f32[2,2,4,40,896]{4,3,2,1,0:T(8,128)S(1)} %get-tuple-element.67), channel_id=1, source_target_pairs={{0,4},{1,5},{2,6},{3,7},{4,0},{5,1},{6,2},{7,3},{8,12},{9,13},{10,... | collective-permute-start | bytes 6881288 | tf_op jit(solution)/shard_map/ppermute | solution.py:24
  34.1 11.0 %collective-permute-done.3 = f32[2,4,2,40,896]{4,3,2,1,0:T(8,128)S(1)} collective-permute-done((f32[2,4,2,40,896]{4,3,2,1,0:T(8,128)S(1)}, f32[2,4,2,40,896]{4,3,2,1,0:T(8,128)S(1)}, u32[]{:S(2)}, u32[]{:S(2)}) %collective-permute-start.3) | collective-permute-done | bytes 2293792 | tf_op jit(solution)/shard_map/ppermute | solution.py:24
  45.1 1.6 %collective-permute-done.2 = f32[2,2,4,40,896]{4,3,2,1,0:T(8,128)} collective-permute-done((f32[2,2,4,40,896]{4,3,2,1,0:T(8,128)S(1)}, f32[2,2,4,40,896]{4,3,2,1,0:T(8,128)}, u32[]{:S(2)}, u32[]{:S(2)}) %collective-permute-start.2) | collective-permute-done | bytes 2293792 | tf_op jit(solution)/shard_map/ppermute | solution.py:24
  46.7 14.6 %collective-permute-done.1 = f32[1288,768]{1,0:T(8,128)S(1)} collective-permute-done((f32[1288,768]{1,0:T(8,128)S(1)}, f32[1288,768]{1,0:T(8,128)S(1)}, u32[]{:S(2)}, u32[]{:S(2)}) %collective-permute-start.1) | collective-permute-done | bytes 3956768 | tf_op jit(solution)/shard_map/ppermute | solution.py:24
  63.3 1.7 %collective-permute-start.6 = (f32[2,4,40,896]{3,2,1,0:T(8,128)S(1)}, f32[2,4,40,896]{3,2,1,0:T(8,128)S(1)}, u32[]{:S(2)}, u32[]{:S(2)}) collective-permute-start(f32[2,4,40,896]{3,2,1,0:T(8,128)S(1)} %add_bitcast_fusion.1), channel_id=1, source_target_pairs={{0,12},{1,13},{2,14},{3,15},{4,8},{5,9},{6,10},{7,11},{8,4},{9,5},... | collective-permute-start | bytes 3440648 | tf_op jit(solution)/shard_map/ppermute | solution.py:24
  65.1 2.8 %collective-permute-start.5 = (f32[4,2,40,896]{3,2,1,0:T(8,128)S(1)}, f32[4,2,40,896]{3,2,1,0:T(8,128)S(1)}, u32[]{:S(2)}, u32[]{:S(2)}) collective-permute-start(f32[4,2,40,896]{3,2,1,0:T(8,128)S(1)} %fusion.2), channel_id=1, source_target_pairs={{0,3},{1,2},{2,1},{3,0},{4,7},{5,6},{6,5},{7,4},{8,11},{9,10},{10,... | collective-permute-start | bytes 3440648 | tf_op jit(solution)/shard_map/ppermute | solution.py:24
  67.9 3.9 %collective-permute-done = f32[2,4,2,40,896]{4,3,2,1,0:T(8,128)S(1)} collective-permute-done((f32[2,4,2,40,896]{4,3,2,1,0:T(8,128)S(1)}, f32[2,4,2,40,896]{4,3,2,1,0:T(8,128)S(1)}, u32[]{:S(2)}, u32[]{:S(2)}) %collective-permute-start) | collective-permute-done | bytes 2293792 | tf_op jit(solution)/shard_map/ppermute | solution.py:24
  71.9 3.4 %collective-permute-done.8 = f32[2,2,4,40,896]{4,3,2,1,0:T(8,128)S(1)} collective-permute-done((f32[2,2,4,40,896]{4,3,2,1,0:T(8,128)S(1)}, f32[2,2,4,40,896]{4,3,2,1,0:T(8,128)S(1)}, u32[]{:S(2)}, u32[]{:S(2)}) %collective-permute-start.8) | collective-permute-done | bytes 2293792 | tf_op jit(solution)/shard_map/ppermute | solution.py:24
  75.4 1.5 %collective-permute-start.4 = (f32[4,2,40,896]{3,2,1,0:T(8,128)S(1)}, f32[4,2,40,896]{3,2,1,0:T(8,128)S(1)}, u32[]{:S(2)}, u32[]{:S(2)}) collective-permute-start(f32[4,2,40,896]{3,2,1,0:T(8,128)S(1)} %add_bitcast_fusion.2), channel_id=1, source_target_pairs={{0,3},{1,2},{2,1},{3,0},{4,7},{5,6},{6,5},{7,4},{8,11},{9,10},{10,... | collective-permute-start | bytes 3440648 | tf_op jit(solution)/shard_map/ppermute | solution.py:24
  77.1 1.7 %collective-permute-start.13 = (f32[2,4,40,896]{3,2,1,0:T(8,128)S(1)}, f32[2,4,40,896]{3,2,1,0:T(8,128)S(1)}, u32[]{:S(2)}, u32[]{:S(2)}) collective-permute-start(f32[2,4,40,896]{3,2,1,0:T(8,128)S(1)} %add_bitcast_fusion), channel_id=1, source_target_pairs={{0,12},{1,13},{2,14},{3,15},{4,8},{5,9},{6,10},{7,11},{8,4},{9,5},... | collective-permute-start | bytes 3440648 | tf_op jit(solution)/shard_map/ppermute | solution.py:24
  78.7 3.1 %collective-permute-done.6 = f32[2,4,40,896]{3,2,1,0:T(8,128)S(1)} collective-permute-done((f32[2,4,40,896]{3,2,1,0:T(8,128)S(1)}, f32[2,4,40,896]{3,2,1,0:T(8,128)S(1)}, u32[]{:S(2)}, u32[]{:S(2)}) %collective-permute-start.6) | collective-permute-done | bytes 1146912 | tf_op jit(solution)/shard_map/ppermute | solution.py:24
  82.2 4.5 %collective-permute-done.7 = f32[648,768]{1,0:T(8,128)S(1)} collective-permute-done((f32[648,768]{1,0:T(8,128)S(1)}, f32[648,768]{1,0:T(8,128)S(1)}, u32[]{:S(2)}, u32[]{:S(2)}) %collective-permute-start.7) | collective-permute-done | bytes 1990688 | tf_op jit(solution)/shard_map/ppermute | solution.py:24
  86.7 1.5 %bitcast_add_fusion.1 = f32[2,4,40,896]{3,2,1,0:T(8,128)S(1)} fusion(f32[2,4,40,896]{3,2,1,0:T(8,128)S(1)} %collective-permute-done.6, f32[2,2,4,40,896]{4,3,2,1,0:T(8,128)} %collective-permute-done.2, f32[2,2,4,40,896]{4,3,2,1,0:T(8,128)S(1)} %get-tuple-element.64), kind=kLoop, calls=%fused_computation.9 | loop fusion | flops 573440 | bytes 4587520 | tf_op jit(solution)/shard_map/add | solution.py:161
  88.2 2.9 %collective-permute-start.12 = (f32[2,4,40,896]{3,2,1,0:T(8,128)S(1)}, f32[2,4,40,896]{3,2,1,0:T(8,128)S(1)}, u32[]{:S(2)}, u32[]{:S(2)}) collective-permute-start(f32[2,4,40,896]{3,2,1,0:T(8,128)S(1)} %bitcast_add_fusion.1), channel_id=1, source_target_pairs={{0,16},{1,17},{2,18},{3,19},{4,20},{5,21},{6,22},{7,23},{8,24},{9,... | collective-permute-start | bytes 3440648 | tf_op jit(solution)/shard_map/ppermute | solution.py:24
  91.7 3.1 %collective-permute-start.11 = (f32[328,768]{1,0:T(8,128)S(1)}, f32[328,768]{1,0:T(8,128)S(1)}, u32[]{:S(2)}, u32[]{:S(2)}) collective-permute-start(f32[328,768]{1,0:T(8,128)S(1)} %pad_maximum_fusion.1), channel_id=1, source_target_pairs={{0,3},{1,2},{2,1},{3,0},{4,7},{5,6},{6,5},{7,4},{8,11},{9,10},{10,... | collective-permute-start | bytes 3022856 | tf_op jit(solution)/shard_map/ppermute | solution.py:24
  95.0 1.7 %collective-permute-start.10 = (f32[2,2,40,896]{3,2,1,0:T(8,128)S(1)}, f32[2,2,40,896]{3,2,1,0:T(8,128)S(1)}, u32[]{:S(2)}, u32[]{:S(2)}) collective-permute-start(f32[2,2,40,896]{3,2,1,0:T(8,128)S(1)} %slice.270), channel_id=1, source_target_pairs={{0,12},{1,13},{2,14},{3,15},{4,8},{5,9},{6,10},{7,11},{8,4},{9,5},... | collective-permute-start | bytes 1720328 | tf_op jit(solution)/shard_map/ppermute | solution.py:24
  97.6 7.3 %collective-permute-done.12 = f32[2,4,40,896]{3,2,1,0:T(8,128)S(1)} collective-permute-done((f32[2,4,40,896]{3,2,1,0:T(8,128)S(1)}, f32[2,4,40,896]{3,2,1,0:T(8,128)S(1)}, u32[]{:S(2)}, u32[]{:S(2)}) %collective-permute-start.12) | collective-permute-done | bytes 1146912 | tf_op jit(solution)/shard_map/ppermute | solution.py:24
  105.0 2.6 %collective-permute-done.11 = f32[328,768]{1,0:T(8,128)S(1)} collective-permute-done((f32[328,768]{1,0:T(8,128)S(1)}, f32[328,768]{1,0:T(8,128)S(1)}, u32[]{:S(2)}, u32[]{:S(2)}) %collective-permute-start.11) | collective-permute-done | bytes 1007648 | tf_op jit(solution)/shard_map/ppermute | solution.py:24
  108.2 2.7 %collective-permute-done.9 = f32[2,2,40,896]{3,2,1,0:T(8,128)S(1)} collective-permute-done((f32[2,2,40,896]{3,2,1,0:T(8,128)S(1)}, f32[2,2,40,896]{3,2,1,0:T(8,128)S(1)}, u32[]{:S(2)}, u32[]{:S(2)}) %collective-permute-start.9) | collective-permute-done | bytes 573472 | tf_op jit(solution)/shard_map/ppermute | solution.py:24
  111.0 1.7 %collective-permute-start.14 = (f32[4,40,896]{2,1,0:T(8,128)S(1)}, f32[4,40,896]{2,1,0:T(8,128)S(1)}, u32[]{:S(2)}, u32[]{:S(2)}) collective-permute-start(f32[4,40,896]{2,1,0:T(8,128)S(1)} %pad_maximum_fusion.2), channel_id=1, source_target_pairs={{0,4},{1,5},{2,6},{3,7},{4,0},{5,1},{6,2},{7,3},{8,12},{9,13},{10,... | collective-permute-start | bytes 1720328 | tf_op jit(solution)/shard_map/ppermute | solution.py:24
  112.8 4.6 %collective-permute-done.16 = f32[4,40,896]{2,1,0:T(8,128)S(1)} collective-permute-done((f32[4,40,896]{2,1,0:T(8,128)S(1)}, f32[4,40,896]{2,1,0:T(8,128)S(1)}, u32[]{:S(2)}, u32[]{:S(2)}) %collective-permute-start.16) | collective-permute-done | bytes 573472 | tf_op jit(solution)/shard_map/ppermute | solution.py:24
  117.6 3.9 %collective-permute-done.14 = f32[4,40,896]{2,1,0:T(8,128)S(1)} collective-permute-done((f32[4,40,896]{2,1,0:T(8,128)S(1)}, f32[4,40,896]{2,1,0:T(8,128)S(1)}, u32[]{:S(2)}, u32[]{:S(2)}) %collective-permute-start.14) | collective-permute-done | bytes 573472 | tf_op jit(solution)/shard_map/ppermute | solution.py:24
  121.7 2.1 %collective-permute-start.19 = (f32[88,768]{1,0:T(8,128)S(1)}, f32[88,768]{1,0:T(8,128)S(1)}, u32[]{:S(2)}, u32[]{:S(2)}) collective-permute-start(f32[88,768]{1,0:T(8,128)S(1)} %pad_maximum_fusion.4), channel_id=1, source_target_pairs={{0,12},{1,13},{2,14},{3,15},{4,8},{5,9},{6,10},{7,11},{8,4},{9,5},... | collective-permute-start | bytes 811016 | tf_op jit(solution)/shard_map/ppermute | solution.py:24
  124.0 1.7 %collective-permute-start.21 = (f32[40,896]{1,0:T(8,128)S(1)}, f32[40,896]{1,0:T(8,128)S(1)}, u32[]{:S(2)}, u32[]{:S(2)}) collective-permute-start(f32[40,896]{1,0:T(8,128)S(1)} %get-tuple-element.92), channel_id=1, source_target_pairs={{0,16},{1,17},{2,18},{3,19},{4,20},{5,21},{6,22},{7,23},{8,24},{9,... | collective-permute-start | bytes 430088 | tf_op jit(solution)/shard_map/ppermute | solution.py:24
  125.7 1.8 %collective-permute-start.23 = (f32[40,896]{1,0:T(8,128)S(1)}, f32[40,896]{1,0:T(8,128)S(1)}, u32[]{:S(2)}, u32[]{:S(2)}) collective-permute-start(f32[40,896]{1,0:T(8,128)S(1)} %get-tuple-element.91), channel_id=1, source_target_pairs={{0,32},{1,33},{2,34},{3,35},{4,36},{5,37},{6,38},{7,39},{8,40},{9,... | collective-permute-start | bytes 430088 | tf_op jit(solution)/shard_map/ppermute | solution.py:30
  127.6 5.5 %collective-permute-done.17 = f32[2,40,896]{2,1,0:T(8,128)S(1)} collective-permute-done((f32[2,40,896]{2,1,0:T(8,128)S(1)}, f32[2,40,896]{2,1,0:T(8,128)S(1)}, u32[]{:S(2)}, u32[]{:S(2)}) %collective-permute-start.17) | collective-permute-done | bytes 286752 | tf_op jit(solution)/shard_map/ppermute | solution.py:24
  133.2 3.2 %collective-permute-start.20 = (f32[48,768]{1,0:T(8,128)S(1)}, f32[48,768]{1,0:T(8,128)S(1)}, u32[]{:S(2)}, u32[]{:S(2)}) collective-permute-start(f32[48,768]{1,0:T(8,128)S(1)} %pad_maximum_fusion.5), channel_id=1, source_target_pairs={{0,4},{1,5},{2,6},{3,7},{4,0},{5,1},{6,2},{7,3},{8,12},{9,13},{10,... | collective-permute-start | bytes 442376 | tf_op jit(solution)/shard_map/ppermute | solution.py:24
  136.5 5.1 %collective-permute-done.18 = f32[40,896]{1,0:T(8,128)S(1)} collective-permute-done((f32[40,896]{1,0:T(8,128)S(1)}, f32[40,896]{1,0:T(8,128)S(1)}, u32[]{:S(2)}, u32[]{:S(2)}) %collective-permute-start.18) | collective-permute-done | bytes 143392 | tf_op jit(solution)/shard_map/ppermute | solution.py:24
  (61 shorter events, 8.1 us)
Async XLA Ops:
  15.3 46.0 %collective-permute-start.1 = (f32[1288,768]{1,0:T(8,128)S(1)}, f32[1288,768]{1,0:T(8,128)S(1)}, u32[]{:S(2)}, u32[]{:S(2)}) collective-permute-start(f32[1288,768]{1,0:T(8,128)S(1)} %get-tuple-element.57), channel_id=1, source_target_pairs={{0,16},{1,17},{2,18},{3,19},{4,20},{5,21},{6,22},{7,23},{8,24},{9,... | collective-permute-start | bytes 11870216 | tf_op jit(solution)/shard_map/ppermute | solution.py:24
  17.0 28.1 %collective-permute-start.3 = (f32[2,4,2,40,896]{4,3,2,1,0:T(8,128)S(1)}, f32[2,4,2,40,896]{4,3,2,1,0:T(8,128)S(1)}, u32[]{:S(2)}, u32[]{:S(2)}) collective-permute-start(f32[2,4,2,40,896]{4,3,2,1,0:T(8,128)S(1)} %get-tuple-element.59), channel_id=1, source_target_pairs={{0,1},{1,0},{2,3},{3,2},{4,5},{5,4},{6,7},{7,6},{8,9},{9,8},{10,11... | collective-permute-start | bytes 6881288 | tf_op jit(solution)/shard_map/ppermute | solution.py:24
  18.5 28.2 %collective-permute-start.2 = (f32[2,2,4,40,896]{4,3,2,1,0:T(8,128)S(1)}, f32[2,2,4,40,896]{4,3,2,1,0:T(8,128)}, u32[]{:S(2)}, u32[]{:S(2)}) collective-permute-start(f32[2,2,4,40,896]{4,3,2,1,0:T(8,128)S(1)} %get-tuple-element.58), channel_id=1, source_target_pairs={{0,4},{1,5},{2,6},{3,7},{4,0},{5,1},{6,2},{7,3},{8,12},{9,13},{10,... | collective-permute-start | bytes 6881288 | tf_op jit(solution)/shard_map/ppermute | solution.py:24
  32.0 39.9 %collective-permute-start = (f32[2,4,2,40,896]{4,3,2,1,0:T(8,128)S(1)}, f32[2,4,2,40,896]{4,3,2,1,0:T(8,128)S(1)}, u32[]{:S(2)}, u32[]{:S(2)}) collective-permute-start(f32[2,4,2,40,896]{4,3,2,1,0:T(8,128)S(1)} %get-tuple-element.56), channel_id=1, source_target_pairs={{0,1},{1,0},{2,3},{3,2},{4,5},{5,4},{6,7},{7,6},{8,9},{9,8},{10,11... | collective-permute-start | bytes 6881288 | tf_op jit(solution)/shard_map/ppermute | solution.py:24
  32.6 42.7 %collective-permute-start.8 = (f32[2,2,4,40,896]{4,3,2,1,0:T(8,128)S(1)}, f32[2,2,4,40,896]{4,3,2,1,0:T(8,128)S(1)}, u32[]{:S(2)}, u32[]{:S(2)}) collective-permute-start(f32[2,2,4,40,896]{4,3,2,1,0:T(8,128)S(1)} %get-tuple-element.67), channel_id=1, source_target_pairs={{0,4},{1,5},{2,6},{3,7},{4,0},{5,1},{6,2},{7,3},{8,12},{9,13},{10,... | collective-permute-start | bytes 6881288 | tf_op jit(solution)/shard_map/ppermute | solution.py:24
  61.7 25.0 %collective-permute-start.7 = (f32[648,768]{1,0:T(8,128)S(1)}, f32[648,768]{1,0:T(8,128)S(1)}, u32[]{:S(2)}, u32[]{:S(2)}) collective-permute-start(f32[648,768]{1,0:T(8,128)S(1)} %pad_maximum_fusion), channel_id=1, source_target_pairs={{0,48},{1,49},{2,50},{3,51},{4,52},{5,53},{6,54},{7,55},{8,56},{9,... | collective-permute-start | bytes 5971976 | tf_op jit(solution)/shard_map/ppermute | solution.py:24
  63.3 18.5 %collective-permute-start.6 = (f32[2,4,40,896]{3,2,1,0:T(8,128)S(1)}, f32[2,4,40,896]{3,2,1,0:T(8,128)S(1)}, u32[]{:S(2)}, u32[]{:S(2)}) collective-permute-start(f32[2,4,40,896]{3,2,1,0:T(8,128)S(1)} %add_bitcast_fusion.1), channel_id=1, source_target_pairs={{0,12},{1,13},{2,14},{3,15},{4,8},{5,9},{6,10},{7,11},{8,4},{9,5},... | collective-permute-start | bytes 3440648 | tf_op jit(solution)/shard_map/ppermute | solution.py:24
  65.1 17.1 %collective-permute-start.5 = (f32[4,2,40,896]{3,2,1,0:T(8,128)S(1)}, f32[4,2,40,896]{3,2,1,0:T(8,128)S(1)}, u32[]{:S(2)}, u32[]{:S(2)}) collective-permute-start(f32[4,2,40,896]{3,2,1,0:T(8,128)S(1)} %fusion.2), channel_id=1, source_target_pairs={{0,3},{1,2},{2,1},{3,0},{4,7},{5,6},{6,5},{7,4},{8,11},{9,10},{10,... | collective-permute-start | bytes 3440648 | tf_op jit(solution)/shard_map/ppermute | solution.py:24
  75.4 21.2 %collective-permute-start.4 = (f32[4,2,40,896]{3,2,1,0:T(8,128)S(1)}, f32[4,2,40,896]{3,2,1,0:T(8,128)S(1)}, u32[]{:S(2)}, u32[]{:S(2)}) collective-permute-start(f32[4,2,40,896]{3,2,1,0:T(8,128)S(1)} %add_bitcast_fusion.2), channel_id=1, source_target_pairs={{0,3},{1,2},{2,1},{3,0},{4,7},{5,6},{6,5},{7,4},{8,11},{9,10},{10,... | collective-permute-start | bytes 3440648 | tf_op jit(solution)/shard_map/ppermute | solution.py:24
  77.1 19.6 %collective-permute-start.13 = (f32[2,4,40,896]{3,2,1,0:T(8,128)S(1)}, f32[2,4,40,896]{3,2,1,0:T(8,128)S(1)}, u32[]{:S(2)}, u32[]{:S(2)}) collective-permute-start(f32[2,4,40,896]{3,2,1,0:T(8,128)S(1)} %add_bitcast_fusion), channel_id=1, source_target_pairs={{0,12},{1,13},{2,14},{3,15},{4,8},{5,9},{6,10},{7,11},{8,4},{9,5},... | collective-permute-start | bytes 3440648 | tf_op jit(solution)/shard_map/ppermute | solution.py:24
  88.2 16.7 %collective-permute-start.12 = (f32[2,4,40,896]{3,2,1,0:T(8,128)S(1)}, f32[2,4,40,896]{3,2,1,0:T(8,128)S(1)}, u32[]{:S(2)}, u32[]{:S(2)}) collective-permute-start(f32[2,4,40,896]{3,2,1,0:T(8,128)S(1)} %bitcast_add_fusion.1), channel_id=1, source_target_pairs={{0,16},{1,17},{2,18},{3,19},{4,20},{5,21},{6,22},{7,23},{8,24},{9,... | collective-permute-start | bytes 3440648 | tf_op jit(solution)/shard_map/ppermute | solution.py:24
  91.7 15.9 %collective-permute-start.11 = (f32[328,768]{1,0:T(8,128)S(1)}, f32[328,768]{1,0:T(8,128)S(1)}, u32[]{:S(2)}, u32[]{:S(2)}) collective-permute-start(f32[328,768]{1,0:T(8,128)S(1)} %pad_maximum_fusion.1), channel_id=1, source_target_pairs={{0,3},{1,2},{2,1},{3,0},{4,7},{5,6},{6,5},{7,4},{8,11},{9,10},{10,... | collective-permute-start | bytes 3022856 | tf_op jit(solution)/shard_map/ppermute | solution.py:24
  95.0 13.2 %collective-permute-start.10 = (f32[2,2,40,896]{3,2,1,0:T(8,128)S(1)}, f32[2,2,40,896]{3,2,1,0:T(8,128)S(1)}, u32[]{:S(2)}, u32[]{:S(2)}) collective-permute-start(f32[2,2,40,896]{3,2,1,0:T(8,128)S(1)} %slice.270), channel_id=1, source_target_pairs={{0,12},{1,13},{2,14},{3,15},{4,8},{5,9},{6,10},{7,11},{8,4},{9,5},... | collective-permute-start | bytes 1720328 | tf_op jit(solution)/shard_map/ppermute | solution.py:24
  96.9 14.0 %collective-permute-start.9 = (f32[2,2,40,896]{3,2,1,0:T(8,128)S(1)}, f32[2,2,40,896]{3,2,1,0:T(8,128)S(1)}, u32[]{:S(2)}, u32[]{:S(2)}) collective-permute-start(f32[2,2,40,896]{3,2,1,0:T(8,128)S(1)} %slice.268), channel_id=1, source_target_pairs={{0,12},{1,13},{2,14},{3,15},{4,8},{5,9},{6,10},{7,11},{8,4},{9,5},... | collective-permute-start | bytes 1720328 | tf_op jit(solution)/shard_map/ppermute | solution.py:24
  107.6 9.8 %collective-permute-start.16 = (f32[4,40,896]{2,1,0:T(8,128)S(1)}, f32[4,40,896]{2,1,0:T(8,128)S(1)}, u32[]{:S(2)}, u32[]{:S(2)}) collective-permute-start(f32[4,40,896]{2,1,0:T(8,128)S(1)} %fusion.5), channel_id=1, source_target_pairs={{0,48},{1,49},{2,50},{3,51},{4,52},{5,53},{6,54},{7,55},{8,56},{9,... | collective-permute-start | bytes 1720328 | tf_op jit(solution)/shard_map/ppermute | solution.py:24
  107.8 9.6 %collective-permute-start.15 = (f32[168,768]{1,0:T(8,128)S(1)}, f32[168,768]{1,0:T(8,128)S(1)}, u32[]{:S(2)}, u32[]{:S(2)}) collective-permute-start(f32[168,768]{1,0:T(8,128)S(1)} %pad_maximum_fusion.3), channel_id=1, source_target_pairs={{0,1},{1,0},{2,3},{3,2},{4,5},{5,4},{6,7},{7,6},{8,9},{9,8},{10,11... | collective-permute-start | bytes 1548296 | tf_op jit(solution)/shard_map/ppermute | solution.py:24
  111.0 10.4 %collective-permute-start.14 = (f32[4,40,896]{2,1,0:T(8,128)S(1)}, f32[4,40,896]{2,1,0:T(8,128)S(1)}, u32[]{:S(2)}, u32[]{:S(2)}) collective-permute-start(f32[4,40,896]{2,1,0:T(8,128)S(1)} %pad_maximum_fusion.2), channel_id=1, source_target_pairs={{0,4},{1,5},{2,6},{3,7},{4,0},{5,1},{6,2},{7,3},{8,12},{9,13},{10,... | collective-permute-start | bytes 1720328 | tf_op jit(solution)/shard_map/ppermute | solution.py:24
  121.7 11.4 %collective-permute-start.19 = (f32[88,768]{1,0:T(8,128)S(1)}, f32[88,768]{1,0:T(8,128)S(1)}, u32[]{:S(2)}, u32[]{:S(2)}) collective-permute-start(f32[88,768]{1,0:T(8,128)S(1)} %pad_maximum_fusion.4), channel_id=1, source_target_pairs={{0,12},{1,13},{2,14},{3,15},{4,8},{5,9},{6,10},{7,11},{8,4},{9,5},... | collective-permute-start | bytes 811016 | tf_op jit(solution)/shard_map/ppermute | solution.py:24
  123.8 9.3 %collective-permute-start.17 = (f32[2,40,896]{2,1,0:T(8,128)S(1)}, f32[2,40,896]{2,1,0:T(8,128)S(1)}, u32[]{:S(2)}, u32[]{:S(2)}) collective-permute-start(f32[2,40,896]{2,1,0:T(8,128)S(1)} %slice.279), channel_id=1, source_target_pairs={{0,3},{1,2},{2,1},{3,0},{4,7},{5,6},{6,5},{7,4},{8,11},{9,10},{10,... | collective-permute-start | bytes 860168 | tf_op jit(solution)/shard_map/ppermute | solution.py:24
  124.0 12.5 %collective-permute-start.21 = (f32[40,896]{1,0:T(8,128)S(1)}, f32[40,896]{1,0:T(8,128)S(1)}, u32[]{:S(2)}, u32[]{:S(2)}) collective-permute-start(f32[40,896]{1,0:T(8,128)S(1)} %get-tuple-element.92), channel_id=1, source_target_pairs={{0,16},{1,17},{2,18},{3,19},{4,20},{5,21},{6,22},{7,23},{8,24},{9,... | collective-permute-start | bytes 430088 | tf_op jit(solution)/shard_map/ppermute | solution.py:24
  125.7 10.8 %collective-permute-start.23 = (f32[40,896]{1,0:T(8,128)S(1)}, f32[40,896]{1,0:T(8,128)S(1)}, u32[]{:S(2)}, u32[]{:S(2)}) collective-permute-start(f32[40,896]{1,0:T(8,128)S(1)} %get-tuple-element.91), channel_id=1, source_target_pairs={{0,32},{1,33},{2,34},{3,35},{4,36},{5,37},{6,38},{7,39},{8,40},{9,... | collective-permute-start | bytes 430088 | tf_op jit(solution)/shard_map/ppermute | solution.py:30
  127.5 9.0 %collective-permute-start.22 = (f32[40,896]{1,0:T(8,128)S(1)}, f32[40,896]{1,0:T(8,128)S(1)}, u32[]{:S(2)}, u32[]{:S(2)}) collective-permute-start(f32[40,896]{1,0:T(8,128)S(1)} %slice_bitcast_fusion.1), channel_id=1, source_target_pairs={{0,48},{1,49},{2,50},{3,51},{4,52},{5,53},{6,54},{7,55},{8,56},{9,... | collective-permute-start | bytes 430088 | tf_op jit(solution)/shard_map/ppermute | solution.py:24
  133.2 8.4 %collective-permute-start.20 = (f32[48,768]{1,0:T(8,128)S(1)}, f32[48,768]{1,0:T(8,128)S(1)}, u32[]{:S(2)}, u32[]{:S(2)}) collective-permute-start(f32[48,768]{1,0:T(8,128)S(1)} %pad_maximum_fusion.5), channel_id=1, source_target_pairs={{0,4},{1,5},{2,6},{3,7},{4,0},{5,1},{6,2},{7,3},{8,12},{9,13},{10,... | collective-permute-start | bytes 442376 | tf_op jit(solution)/shard_map/ppermute | solution.py:24
  136.4 5.2 %collective-permute-start.18 = (f32[40,896]{1,0:T(8,128)S(1)}, f32[40,896]{1,0:T(8,128)S(1)}, u32[]{:S(2)}, u32[]{:S(2)}) collective-permute-start(f32[40,896]{1,0:T(8,128)S(1)} %fusion.15), channel_id=1, source_target_pairs={{0,1},{1,0},{2,3},{3,2},{4,5},{5,4},{6,7},{7,6},{8,9},{9,8},{10,11... | collective-permute-start | bytes 430088 | tf_op jit(solution)/shard_map/ppermute | solution.py:24

commit v11 on v8

--- a/solution.py
+++ b/solution.py
@@ -17,7 +17,7 @@
 def exchange(value, axis, turn, other=False):
     pairs = []
     for section in range(2):
-        flip, stride = 1 if (section == turn) != other else 3, STRIDE[axis]
+        flip, stride = 1 if (section == turn) == other else 3, STRIDE[axis]
         for d in range(64):
             p = d // stride % 4
             pairs.append((section * 64 + d, section * 64 + d + ((p ^ flip) - p) * stride))
@@ -27,8 +27,8 @@
 def products(half, failed, counts, order, act, cot, *refs):
     outs, (acts, cots, total, asked, sems) = refs[:-5], refs[-5:]
     section, me = lax.axis_index("section"), lax.axis_index("dp")
-    flips = (0, 3 - 2 * section, 1 + 2 * section, 2)
-    others = (0, 1 + 2 * section, 3 - 2 * section, 2)
+    flips = (0, 1 + 2 * section, 3 - 2 * section, 2)
+    others = (0, 3 - 2 * section, 1 + 2 * section, 2)
     x, y, z = me % 4, me // 4 % 4, me // 16
     zs = [z ^ flip for flip in flips]
     xs = {group: [x ^ flip for flip in (flips if group == "A" else others)] for group in "ABC"}

time: 140 us -> 143 us (1.021)
  waiting for transfers between devices: 69.4 us -> 75.4 us
  starting transfers between devices: 37.8 us -> 35.5 us
    ppermute x23, waiting for transfers between devices: 69.4 us -> 75.4 us  [exchange(): return lax.ppermute(value, ('section', 'dp'), pairs)]
    ppermute x23, starting transfers between devices: 37.8 us -> 35.5 us  [exchange(): return lax.ppermute(value, ('section', 'dp'), pairs)]
  transfers between devices with their start and end apart: 23 -> 23, of which waited for: 16 -> 18; matrix products, arithmetic and copies ran while one was open for 2% -> 2% of each run, Pallas kernels for 9% -> 9%
where the time goes in v11:
time: 143 us
  waiting for transfers between devices  75.4 us (53%)
  starting transfers between devices  35.5 us (25%)
  Pallas kernels  25.9 us (18%)
  other arithmetic  4.04 us (3%)
  between operations  1.54 us (1%)
    ppermute x23, waiting for transfers between devices, exchange(): return lax.ppermute(value, ('section', 'dp'), pairs)  75.4 us
    ppermute x23, starting transfers between devices, exchange(): return lax.ppermute(value, ('section', 'dp'), pairs)  35.5 us
    pallas_call x2, Pallas kernels, partials(): pl.pallas_call(functools.partial(products, half), out_shape=[jax.ShapeDty...  25.9 us
  transfers between devices with their start and end apart: 23, of which 18 were waited for; matrix products, arithmetic and copies ran while one was open for 2% of the time, Pallas kernels for 9%

profile of v11, /device:TPU:0, one launch (start us, length us, event | category | flops | bytes accessed | tf_op | source)
XLA Modules:
  0.0 142.5 jit_solution(17138350956829909480)
XLA Ops:
  1.3 12.9 %shard_map.55 = (f32[2,4,2,40,896]{4,3,2,1,0:T(8,128)S(1)}, f32[2,4,2,40,896]{4,3,2,1,0:T(8,128)S(1)}, f32[2,2,4,40,896]{4,3,2,1,0:T(8,128)S(1)}, f32[2,2,4,40,8...) custom-call(s32[1]{0:T(128)S(6)} %copy.6.failed, s32[1]{0:T(128)S(6)} %copy.7.counts, ...), custom_call_target="tpu_custom_call" | custom-call | flops 1024 | bytes 1024 | tf_op jit(solution)/shard_map/pallas_call | solution.py:93
  14.2 4.2 %collective-permute-start.1 = (f32[1288,768]{1,0:T(8,128)S(1)}, f32[1288,768]{1,0:T(8,128)S(1)}, u32[]{:S(2)}, u32[]{:S(2)}) collective-permute-start(f32[1288,768]{1,0:T(8,128)S(1)} %get-tuple-element.56), channel_id=1, source_target_pairs={{0,48},{1,49},{2,50},{3,51},{4,52},{5,53},{6,54},{7,55},{8,56},{9,... | collective-permute-start | bytes 11870216 | tf_op jit(solution)/shard_map/ppermute | solution.py:24
  18.4 2.7 %collective-permute-start.3 = (f32[2,4,2,40,896]{4,3,2,1,0:T(8,128)S(1)}, f32[2,4,2,40,896]{4,3,2,1,0:T(8,128)S(1)}, u32[]{:S(2)}, u32[]{:S(2)}) collective-permute-start(f32[2,4,2,40,896]{4,3,2,1,0:T(8,128)S(1)} %get-tuple-element.58), channel_id=1, source_target_pairs={{0,3},{1,2},{2,1},{3,0},{4,7},{5,6},{6,5},{7,4},{8,11},{9,10},{10,... | collective-permute-start | bytes 6881288 | tf_op jit(solution)/shard_map/ppermute | solution.py:24
  21.2 3.0 %collective-permute-start.2 = (f32[2,2,4,40,896]{4,3,2,1,0:T(8,128)S(1)}, f32[2,2,4,40,896]{4,3,2,1,0:T(8,128)S(1)}, u32[]{:S(2)}, u32[]{:S(2)}) collective-permute-start(f32[2,2,4,40,896]{4,3,2,1,0:T(8,128)S(1)} %get-tuple-element.57), channel_id=1, source_target_pairs={{0,12},{1,13},{2,14},{3,15},{4,8},{5,9},{6,10},{7,11},{8,4},{9,5},... | collective-permute-start | bytes 6881288 | tf_op jit(solution)/shard_map/ppermute | solution.py:24
  24.2 12.9 %shard_map.56 = (f32[2,4,2,40,896]{4,3,2,1,0:T(8,128)S(1)}, f32[2,4,2,40,896]{4,3,2,1,0:T(8,128)S(1)}, f32[2,2,4,40,896]{4,3,2,1,0:T(8,128)S(1)}, f32[2,2,4,40,896]{4,3,2,1,0:T(8,128)S(1)}, f32[1280,768]{1,0:T(8,128)S(1)}) custom-call(s32[1]{0:T(128)S(6)} %copy.6.failed, s32[1]{0:T(128)S(6)} %copy.7.counts, s32[1,6]{1,0:T(1,128)} %order.3, ...), custom_call_target="tpu_custom_call" | custom-call | flops 1024 | bytes 1024 | tf_op jit(solution)/shard_map/pallas_call | solution.py:93
  37.9 9.9 %collective-permute-done.3 = f32[2,4,2,40,896]{4,3,2,1,0:T(8,128)S(1)} collective-permute-done((f32[2,4,2,40,896]{4,3,2,1,0:T(8,128)S(1)}, f32[2,4,2,40,896]{4,3,2,1,0:T(8,128)S(1)}, u32[]{:S(2)}, u32[]{:S(2)}) %collective-permute-start.3) | collective-permute-done | bytes 2293792 | tf_op jit(solution)/shard_map/ppermute | solution.py:24
  47.8 2.8 %collective-permute-done.2 = f32[2,2,4,40,896]{4,3,2,1,0:T(8,128)S(1)} collective-permute-done((f32[2,2,4,40,896]{4,3,2,1,0:T(8,128)S(1)}, f32[2,2,4,40,896]{4,3,2,1,0:T(8,128)S(1)}, u32[]{:S(2)}, u32[]{:S(2)}) %collective-permute-start.2) | collective-permute-done | bytes 2293792 | tf_op jit(solution)/shard_map/ppermute | solution.py:24
  50.6 11.8 %collective-permute-done.1 = f32[1288,768]{1,0:T(8,128)S(1)} collective-permute-done((f32[1288,768]{1,0:T(8,128)S(1)}, f32[1288,768]{1,0:T(8,128)S(1)}, u32[]{:S(2)}, u32[]{:S(2)}) %collective-permute-start.1) | collective-permute-done | bytes 3956768 | tf_op jit(solution)/shard_map/ppermute | solution.py:24
  63.1 1.7 %collective-permute-start.6 = (f32[2,4,40,896]{3,2,1,0:T(8,128)S(1)}, f32[2,4,40,896]{3,2,1,0:T(8,128)S(1)}, u32[]{:S(2)}, u32[]{:S(2)}) collective-permute-start(f32[2,4,40,896]{3,2,1,0:T(8,128)S(1)} %add_bitcast_fusion.1), channel_id=1, source_target_pairs={{0,4},{1,5},{2,6},{3,7},{4,0},{5,1},{6,2},{7,3},{8,12},{9,13},{10,... | collective-permute-start | bytes 3440648 | tf_op jit(solution)/shard_map/ppermute | solution.py:24
  64.9 1.6 %collective-permute-start.5 = (f32[4,2,40,896]{3,2,1,0:T(8,128)S(1)}, f32[4,2,40,896]{3,2,1,0:T(8,128)S(1)}, u32[]{:S(2)}, u32[]{:S(2)}) collective-permute-start(f32[4,2,40,896]{3,2,1,0:T(8,128)S(1)} %fusion.2), channel_id=1, source_target_pairs={{0,1},{1,0},{2,3},{3,2},{4,5},{5,4},{6,7},{7,6},{8,9},{9,8},{10,11... | collective-permute-start | bytes 3440648 | tf_op jit(solution)/shard_map/ppermute | solution.py:24
  66.5 7.5 %collective-permute-done = f32[2,4,2,40,896]{4,3,2,1,0:T(8,128)S(1)} collective-permute-done((f32[2,4,2,40,896]{4,3,2,1,0:T(8,128)S(1)}, f32[2,4,2,40,896]{4,3,2,1,0:T(8,128)S(1)}, u32[]{:S(2)}, u32[]{:S(2)}) %collective-permute-start) | collective-permute-done | bytes 2293792 | tf_op jit(solution)/shard_map/ppermute | solution.py:24
  74.0 8.4 %collective-permute-done.8 = f32[2,2,4,40,896]{4,3,2,1,0:T(8,128)S(1)} collective-permute-done((f32[2,2,4,40,896]{4,3,2,1,0:T(8,128)S(1)}, f32[2,2,4,40,896]{4,3,2,1,0:T(8,128)S(1)}, u32[]{:S(2)}, u32[]{:S(2)}) %collective-permute-start.8) | collective-permute-done | bytes 2293792 | tf_op jit(solution)/shard_map/ppermute | solution.py:24
  83.2 4.7 %collective-permute-done.7 = f32[648,768]{1,0:T(8,128)S(1)} collective-permute-done((f32[648,768]{1,0:T(8,128)S(1)}, f32[648,768]{1,0:T(8,128)S(1)}, u32[]{:S(2)}, u32[]{:S(2)}) %collective-permute-start.7) | collective-permute-done | bytes 1990688 | tf_op jit(solution)/shard_map/ppermute | solution.py:24
  88.1 3.3 %collective-permute-start.12 = (f32[2,4,40,896]{3,2,1,0:T(8,128)S(1)}, f32[2,4,40,896]{3,2,1,0:T(8,128)S(1)}, u32[]{:S(2)}, u32[]{:S(2)}) collective-permute-start(f32[2,4,40,896]{3,2,1,0:T(8,128)S(1)} %bitcast_add_fusion.1), channel_id=1, source_target_pairs={{0,48},{1,49},{2,50},{3,51},{4,52},{5,53},{6,54},{7,55},{8,56},{9,... | collective-permute-start | bytes 3440648 | tf_op jit(solution)/shard_map/ppermute | solution.py:24
  92.1 1.8 %collective-permute-start.11 = (f32[328,768]{1,0:T(8,128)S(1)}, f32[328,768]{1,0:T(8,128)S(1)}, u32[]{:S(2)}, u32[]{:S(2)}) collective-permute-start(f32[328,768]{1,0:T(8,128)S(1)} %pad_maximum_fusion.1), channel_id=1, source_target_pairs={{0,1},{1,0},{2,3},{3,2},{4,5},{5,4},{6,7},{7,6},{8,9},{9,8},{10,11... | collective-permute-start | bytes 3022856 | tf_op jit(solution)/shard_map/ppermute | solution.py:24
  94.1 1.7 %collective-permute-start.10 = (f32[2,2,40,896]{3,2,1,0:T(8,128)S(1)}, f32[2,2,40,896]{3,2,1,0:T(8,128)S(1)}, u32[]{:S(2)}, u32[]{:S(2)}) collective-permute-start(f32[2,2,40,896]{3,2,1,0:T(8,128)S(1)} %slice.270), channel_id=1, source_target_pairs={{0,4},{1,5},{2,6},{3,7},{4,0},{5,1},{6,2},{7,3},{8,12},{9,13},{10,... | collective-permute-start | bytes 1720328 | tf_op jit(solution)/shard_map/ppermute | solution.py:24
  95.7 2.7 %collective-permute-done.4 = f32[4,2,40,896]{3,2,1,0:T(8,128)S(1)} collective-permute-done((f32[4,2,40,896]{3,2,1,0:T(8,128)S(1)}, f32[4,2,40,896]{3,2,1,0:T(8,128)S(1)}, u32[]{:S(2)}, u32[]{:S(2)}) %collective-permute-start.4) | collective-permute-done | bytes 1146912 | tf_op jit(solution)/shard_map/ppermute | solution.py:24
  99.7 5.6 %collective-permute-done.12 = f32[2,4,40,896]{3,2,1,0:T(8,128)S(1)} collective-permute-done((f32[2,4,40,896]{3,2,1,0:T(8,128)S(1)}, f32[2,4,40,896]{3,2,1,0:T(8,128)S(1)}, u32[]{:S(2)}, u32[]{:S(2)}) %collective-permute-start.12) | collective-permute-done | bytes 1146912 | tf_op jit(solution)/shard_map/ppermute | solution.py:24
  105.3 3.9 %collective-permute-done.11 = f32[328,768]{1,0:T(8,128)S(1)} collective-permute-done((f32[328,768]{1,0:T(8,128)S(1)}, f32[328,768]{1,0:T(8,128)S(1)}, u32[]{:S(2)}, u32[]{:S(2)}) %collective-permute-start.11) | collective-permute-done | bytes 1007648 | tf_op jit(solution)/shard_map/ppermute | solution.py:24
  109.9 1.1 collective-permute-done.9
  111.1 3.2 %collective-permute-start.14 = (f32[4,40,896]{2,1,0:T(8,128)S(1)}, f32[4,40,896]{2,1,0:T(8,128)S(1)}, u32[]{:S(2)}, u32[]{:S(2)}) collective-permute-start(f32[4,40,896]{2,1,0:T(8,128)S(1)} %pad_maximum_fusion.2), channel_id=1, source_target_pairs={{0,12},{1,13},{2,14},{3,15},{4,8},{5,9},{6,10},{7,11},{8,4},{9,5},... | collective-permute-start | bytes 1720328 | tf_op jit(solution)/shard_map/ppermute | solution.py:24
  114.2 4.8 %collective-permute-done.16 = f32[4,40,896]{2,1,0:T(8,128)S(1)} collective-permute-done((f32[4,40,896]{2,1,0:T(8,128)S(1)}, f32[4,40,896]{2,1,0:T(8,128)S(1)}, u32[]{:S(2)}, u32[]{:S(2)}) %collective-permute-start.16) | collective-permute-done | bytes 573472 | tf_op jit(solution)/shard_map/ppermute | solution.py:24
  119.1 0.8 collective-permute-done.15
  120.2 1.8 %collective-permute-done.14 = f32[4,40,896]{2,1,0:T(8,128)S(1)} collective-permute-done((f32[4,40,896]{2,1,0:T(8,128)S(1)}, f32[4,40,896]{2,1,0:T(8,128)S(1)}, u32[]{:S(2)}, u32[]{:S(2)}) %collective-permute-start.14) | collective-permute-done | bytes 573472 | tf_op jit(solution)/shard_map/ppermute | solution.py:24
  122.2 1.4 collective-permute-start.17
  123.6 3.2 %collective-permute-done.19 = f32[2,40,896]{2,1,0:T(8,128)S(1)} collective-permute-done((f32[2,40,896]{2,1,0:T(8,128)S(1)}, f32[2,40,896]{2,1,0:T(8,128)S(1)}, u32[]{:S(2)}, u32[]{:S(2)}) %collective-permute-start.19) | collective-permute-done | bytes 286752 | tf_op jit(solution)/shard_map/ppermute | solution.py:24
  126.8 1.7 %collective-permute-done.18 = f32[88,768]{1,0:T(8,128)S(1)} collective-permute-done((f32[88,768]{1,0:T(8,128)S(1)}, f32[88,768]{1,0:T(8,128)S(1)}, u32[]{:S(2)}, u32[]{:S(2)}) %collective-permute-start.18) | collective-permute-done | bytes 270368 | tf_op jit(solution)/shard_map/ppermute | solution.py:24
  128.6 1.5 %collective-permute-done.17 = f32[2,40,896]{2,1,0:T(8,128)S(1)} collective-permute-done((f32[2,40,896]{2,1,0:T(8,128)S(1)}, f32[2,40,896]{2,1,0:T(8,128)S(1)}, u32[]{:S(2)}, u32[]{:S(2)}) %collective-permute-start.17) | collective-permute-done | bytes 286752 | tf_op jit(solution)/shard_map/ppermute | solution.py:24
  130.1 3.2 %collective-permute-start.21 = (f32[48,768]{1,0:T(8,128)S(1)}, f32[48,768]{1,0:T(8,128)S(1)}, u32[]{:S(2)}, u32[]{:S(2)}) collective-permute-start(f32[48,768]{1,0:T(8,128)S(1)} %pad_maximum_fusion.5), channel_id=1, source_target_pairs={{0,12},{1,13},{2,14},{3,15},{4,8},{5,9},{6,10},{7,11},{8,4},{9,5},... | collective-permute-start | bytes 442376 | tf_op jit(solution)/shard_map/ppermute | solution.py:24
  133.3 0.9 collective-permute-start.22
  134.2 4.3 %collective-permute-start.20 = (f32[40,896]{1,0:T(8,128)S(1)}, f32[40,896]{1,0:T(8,128)S(1)}, u32[]{:S(2)}, u32[]{:S(2)}) collective-permute-start(f32[40,896]{1,0:T(8,128)S(1)} %fusion.16), channel_id=1, source_target_pairs={{0,3},{1,2},{2,1},{3,0},{4,7},{5,6},{6,5},{7,4},{8,11},{9,10},{10,... | collective-permute-start | bytes 430088 | tf_op jit(solution)/shard_map/ppermute | solution.py:24
  138.5 3.1 %collective-permute-done.20 = f32[40,896]{1,0:T(8,128)S(1)} collective-permute-done((f32[40,896]{1,0:T(8,128)S(1)}, f32[40,896]{1,0:T(8,128)S(1)}, u32[]{:S(2)}, u32[]{:S(2)}) %collective-permute-start.20) | collective-permute-done | bytes 143392 | tf_op jit(solution)/shard_map/ppermute | solution.py:24
  (58 shorter events, 7.0 us)
Async XLA Ops:
  14.2 48.1 %collective-permute-start.1 = (f32[1288,768]{1,0:T(8,128)S(1)}, f32[1288,768]{1,0:T(8,128)S(1)}, u32[]{:S(2)}, u32[]{:S(2)}) collective-permute-start(f32[1288,768]{1,0:T(8,128)S(1)} %get-tuple-element.56), channel_id=1, source_target_pairs={{0,48},{1,49},{2,50},{3,51},{4,52},{5,53},{6,54},{7,55},{8,56},{9,... | collective-permute-start | bytes 11870216 | tf_op jit(solution)/shard_map/ppermute | solution.py:24
  18.4 29.4 %collective-permute-start.3 = (f32[2,4,2,40,896]{4,3,2,1,0:T(8,128)S(1)}, f32[2,4,2,40,896]{4,3,2,1,0:T(8,128)S(1)}, u32[]{:S(2)}, u32[]{:S(2)}) collective-permute-start(f32[2,4,2,40,896]{4,3,2,1,0:T(8,128)S(1)} %get-tuple-element.58), channel_id=1, source_target_pairs={{0,3},{1,2},{2,1},{3,0},{4,7},{5,6},{6,5},{7,4},{8,11},{9,10},{10,... | collective-permute-start | bytes 6881288 | tf_op jit(solution)/shard_map/ppermute | solution.py:24
  21.2 29.4 %collective-permute-start.2 = (f32[2,2,4,40,896]{4,3,2,1,0:T(8,128)S(1)}, f32[2,2,4,40,896]{4,3,2,1,0:T(8,128)S(1)}, u32[]{:S(2)}, u32[]{:S(2)}) collective-permute-start(f32[2,2,4,40,896]{4,3,2,1,0:T(8,128)S(1)} %get-tuple-element.57), channel_id=1, source_target_pairs={{0,12},{1,13},{2,14},{3,15},{4,8},{5,9},{6,10},{7,11},{8,4},{9,5},... | collective-permute-start | bytes 6881288 | tf_op jit(solution)/shard_map/ppermute | solution.py:24
  37.2 36.8 %collective-permute-start = (f32[2,4,2,40,896]{4,3,2,1,0:T(8,128)S(1)}, f32[2,4,2,40,896]{4,3,2,1,0:T(8,128)S(1)}, u32[]{:S(2)}, u32[]{:S(2)}) collective-permute-start(f32[2,4,2,40,896]{4,3,2,1,0:T(8,128)S(1)} %get-tuple-element.55), channel_id=1, source_target_pairs={{0,3},{1,2},{2,1},{3,0},{4,7},{5,6},{6,5},{7,4},{8,11},{9,10},{10,... | collective-permute-start | bytes 6881288 | tf_op jit(solution)/shard_map/ppermute | solution.py:24
  37.7 44.6 %collective-permute-start.8 = (f32[2,2,4,40,896]{4,3,2,1,0:T(8,128)S(1)}, f32[2,2,4,40,896]{4,3,2,1,0:T(8,128)S(1)}, u32[]{:S(2)}, u32[]{:S(2)}) collective-permute-start(f32[2,2,4,40,896]{4,3,2,1,0:T(8,128)S(1)} %get-tuple-element.66), channel_id=1, source_target_pairs={{0,12},{1,13},{2,14},{3,15},{4,8},{5,9},{6,10},{7,11},{8,4},{9,5},... | collective-permute-start | bytes 6881288 | tf_op jit(solution)/shard_map/ppermute | solution.py:24
  62.9 25.0 %collective-permute-start.7 = (f32[648,768]{1,0:T(8,128)S(1)}, f32[648,768]{1,0:T(8,128)S(1)}, u32[]{:S(2)}, u32[]{:S(2)}) collective-permute-start(f32[648,768]{1,0:T(8,128)S(1)} %pad_maximum_fusion), channel_id=1, source_target_pairs={{0,16},{1,17},{2,18},{3,19},{4,20},{5,21},{6,22},{7,23},{8,24},{9,... | collective-permute-start | bytes 5971976 | tf_op jit(solution)/shard_map/ppermute | solution.py:24
  63.1 20.1 %collective-permute-start.6 = (f32[2,4,40,896]{3,2,1,0:T(8,128)S(1)}, f32[2,4,40,896]{3,2,1,0:T(8,128)S(1)}, u32[]{:S(2)}, u32[]{:S(2)}) collective-permute-start(f32[2,4,40,896]{3,2,1,0:T(8,128)S(1)} %add_bitcast_fusion.1), channel_id=1, source_target_pairs={{0,4},{1,5},{2,6},{3,7},{4,0},{5,1},{6,2},{7,3},{8,12},{9,13},{10,... | collective-permute-start | bytes 3440648 | tf_op jit(solution)/shard_map/ppermute | solution.py:24
  64.9 18.3 %collective-permute-start.5 = (f32[4,2,40,896]{3,2,1,0:T(8,128)S(1)}, f32[4,2,40,896]{3,2,1,0:T(8,128)S(1)}, u32[]{:S(2)}, u32[]{:S(2)}) collective-permute-start(f32[4,2,40,896]{3,2,1,0:T(8,128)S(1)} %fusion.2), channel_id=1, source_target_pairs={{0,1},{1,0},{2,3},{3,2},{4,5},{5,4},{6,7},{7,6},{8,9},{9,8},{10,11... | collective-permute-start | bytes 3440648 | tf_op jit(solution)/shard_map/ppermute | solution.py:24
  82.5 15.9 %collective-permute-start.4 = (f32[4,2,40,896]{3,2,1,0:T(8,128)S(1)}, f32[4,2,40,896]{3,2,1,0:T(8,128)S(1)}, u32[]{:S(2)}, u32[]{:S(2)}) collective-permute-start(f32[4,2,40,896]{3,2,1,0:T(8,128)S(1)} %add_bitcast_fusion.2), channel_id=1, source_target_pairs={{0,1},{1,0},{2,3},{3,2},{4,5},{5,4},{6,7},{7,6},{8,9},{9,8},{10,11... | collective-permute-start | bytes 3440648 | tf_op jit(solution)/shard_map/ppermute | solution.py:24
  82.7 15.9 %collective-permute-start.13 = (f32[2,4,40,896]{3,2,1,0:T(8,128)S(1)}, f32[2,4,40,896]{3,2,1,0:T(8,128)S(1)}, u32[]{:S(2)}, u32[]{:S(2)}) collective-permute-start(f32[2,4,40,896]{3,2,1,0:T(8,128)S(1)} %add_bitcast_fusion), channel_id=1, source_target_pairs={{0,4},{1,5},{2,6},{3,7},{4,0},{5,1},{6,2},{7,3},{8,12},{9,13},{10,... | collective-permute-start | bytes 3440648 | tf_op jit(solution)/shard_map/ppermute | solution.py:24
  88.1 17.1 %collective-permute-start.12 = (f32[2,4,40,896]{3,2,1,0:T(8,128)S(1)}, f32[2,4,40,896]{3,2,1,0:T(8,128)S(1)}, u32[]{:S(2)}, u32[]{:S(2)}) collective-permute-start(f32[2,4,40,896]{3,2,1,0:T(8,128)S(1)} %bitcast_add_fusion.1), channel_id=1, source_target_pairs={{0,48},{1,49},{2,50},{3,51},{4,52},{5,53},{6,54},{7,55},{8,56},{9,... | collective-permute-start | bytes 3440648 | tf_op jit(solution)/shard_map/ppermute | solution.py:24
  92.1 17.1 %collective-permute-start.11 = (f32[328,768]{1,0:T(8,128)S(1)}, f32[328,768]{1,0:T(8,128)S(1)}, u32[]{:S(2)}, u32[]{:S(2)}) collective-permute-start(f32[328,768]{1,0:T(8,128)S(1)} %pad_maximum_fusion.1), channel_id=1, source_target_pairs={{0,1},{1,0},{2,3},{3,2},{4,5},{5,4},{6,7},{7,6},{8,9},{9,8},{10,11... | collective-permute-start | bytes 3022856 | tf_op jit(solution)/shard_map/ppermute | solution.py:24
  94.1 15.8 %collective-permute-start.10 = (f32[2,2,40,896]{3,2,1,0:T(8,128)S(1)}, f32[2,2,40,896]{3,2,1,0:T(8,128)S(1)}, u32[]{:S(2)}, u32[]{:S(2)}) collective-permute-start(f32[2,2,40,896]{3,2,1,0:T(8,128)S(1)} %slice.270), channel_id=1, source_target_pairs={{0,4},{1,5},{2,6},{3,7},{4,0},{5,1},{6,2},{7,3},{8,12},{9,13},{10,... | collective-permute-start | bytes 1720328 | tf_op jit(solution)/shard_map/ppermute | solution.py:24
  98.9 12.0 %collective-permute-start.9 = (f32[2,2,40,896]{3,2,1,0:T(8,128)S(1)}, f32[2,2,40,896]{3,2,1,0:T(8,128)S(1)}, u32[]{:S(2)}, u32[]{:S(2)}) collective-permute-start(f32[2,2,40,896]{3,2,1,0:T(8,128)S(1)} %slice.268), channel_id=1, source_target_pairs={{0,4},{1,5},{2,6},{3,7},{4,0},{5,1},{6,2},{7,3},{8,12},{9,13},{10,... | collective-permute-start | bytes 1720328 | tf_op jit(solution)/shard_map/ppermute | solution.py:24
  109.3 9.8 %collective-permute-start.16 = (f32[4,40,896]{2,1,0:T(8,128)S(1)}, f32[4,40,896]{2,1,0:T(8,128)S(1)}, u32[]{:S(2)}, u32[]{:S(2)}) collective-permute-start(f32[4,40,896]{2,1,0:T(8,128)S(1)} %fusion.5), channel_id=1, source_target_pairs={{0,16},{1,17},{2,18},{3,19},{4,20},{5,21},{6,22},{7,23},{8,24},{9,... | collective-permute-start | bytes 1720328 | tf_op jit(solution)/shard_map/ppermute | solution.py:24
  109.5 10.4 %collective-permute-start.15 = (f32[168,768]{1,0:T(8,128)S(1)}, f32[168,768]{1,0:T(8,128)S(1)}, u32[]{:S(2)}, u32[]{:S(2)}) collective-permute-start(f32[168,768]{1,0:T(8,128)S(1)} %pad_maximum_fusion.3), channel_id=1, source_target_pairs={{0,3},{1,2},{2,1},{3,0},{4,7},{5,6},{6,5},{7,4},{8,11},{9,10},{10,... | collective-permute-start | bytes 1548296 | tf_op jit(solution)/shard_map/ppermute | solution.py:24
  111.1 11.0 %collective-permute-start.14 = (f32[4,40,896]{2,1,0:T(8,128)S(1)}, f32[4,40,896]{2,1,0:T(8,128)S(1)}, u32[]{:S(2)}, u32[]{:S(2)}) collective-permute-start(f32[4,40,896]{2,1,0:T(8,128)S(1)} %pad_maximum_fusion.2), channel_id=1, source_target_pairs={{0,12},{1,13},{2,14},{3,15},{4,8},{5,9},{6,10},{7,11},{8,4},{9,5},... | collective-permute-start | bytes 1720328 | tf_op jit(solution)/shard_map/ppermute | solution.py:24
  120.1 6.7 %collective-permute-start.19 = (f32[2,40,896]{2,1,0:T(8,128)S(1)}, f32[2,40,896]{2,1,0:T(8,128)S(1)}, u32[]{:S(2)}, u32[]{:S(2)}) collective-permute-start(f32[2,40,896]{2,1,0:T(8,128)S(1)} %slice.281), channel_id=1, source_target_pairs={{0,1},{1,0},{2,3},{3,2},{4,5},{5,4},{6,7},{7,6},{8,9},{9,8},{10,11... | collective-permute-start | bytes 860168 | tf_op jit(solution)/shard_map/ppermute | solution.py:24
  122.1 6.5 %collective-permute-start.18 = (f32[88,768]{1,0:T(8,128)S(1)}, f32[88,768]{1,0:T(8,128)S(1)}, u32[]{:S(2)}, u32[]{:S(2)}) collective-permute-start(f32[88,768]{1,0:T(8,128)S(1)} %pad_maximum_fusion.4), channel_id=1, source_target_pairs={{0,4},{1,5},{2,6},{3,7},{4,0},{5,1},{6,2},{7,3},{8,12},{9,13},{10,... | collective-permute-start | bytes 811016 | tf_op jit(solution)/shard_map/ppermute | solution.py:24
  122.2 7.9 %collective-permute-start.17 = (f32[2,40,896]{2,1,0:T(8,128)S(1)}, f32[2,40,896]{2,1,0:T(8,128)S(1)}, u32[]{:S(2)}, u32[]{:S(2)}) collective-permute-start(f32[2,40,896]{2,1,0:T(8,128)S(1)} %get-tuple-element.87), channel_id=1, source_target_pairs={{0,48},{1,49},{2,50},{3,51},{4,52},{5,53},{6,54},{7,55},{8,56},{9,... | collective-permute-start | bytes 860168 | tf_op jit(solution)/shard_map/ppermute | solution.py:24
  130.1 11.5 %collective-permute-start.21 = (f32[48,768]{1,0:T(8,128)S(1)}, f32[48,768]{1,0:T(8,128)S(1)}, u32[]{:S(2)}, u32[]{:S(2)}) collective-permute-start(f32[48,768]{1,0:T(8,128)S(1)} %pad_maximum_fusion.5), channel_id=1, source_target_pairs={{0,12},{1,13},{2,14},{3,15},{4,8},{5,9},{6,10},{7,11},{8,4},{9,5},... | collective-permute-start | bytes 442376 | tf_op jit(solution)/shard_map/ppermute | solution.py:24
  133.3 5.2 %collective-permute-start.22 = (f32[40,896]{1,0:T(8,128)S(1)}, f32[40,896]{1,0:T(8,128)S(1)}, u32[]{:S(2)}, u32[]{:S(2)}) collective-permute-start(f32[40,896]{1,0:T(8,128)S(1)} %fusion.15), channel_id=1, source_target_pairs={{0,16},{1,17},{2,18},{3,19},{4,20},{5,21},{6,22},{7,23},{8,24},{9,... | collective-permute-start | bytes 430088 | tf_op jit(solution)/shard_map/ppermute | solution.py:24
  134.2 7.4 %collective-permute-start.20 = (f32[40,896]{1,0:T(8,128)S(1)}, f32[40,896]{1,0:T(8,128)S(1)}, u32[]{:S(2)}, u32[]{:S(2)}) collective-permute-start(f32[40,896]{1,0:T(8,128)S(1)} %fusion.16), channel_id=1, source_target_pairs={{0,3},{1,2},{2,1},{3,0},{4,7},{5,6},{6,5},{7,4},{8,11},{9,10},{10,... | collective-permute-start | bytes 430088 | tf_op jit(solution)/shard_map/ppermute | solution.py:24
